TPU v7x, 1024 devices: a whole 4x8x16 slice. The times are simulated.
1024 devices in a mesh: row: 64 (over x, z), col: 16 (over y, core).
Axes of the slice: x: 4, y: 8, z: 16, core: 2. Of those that a mesh axis runs over, the one named last changes fastest.
Arguments:
- table: float32 [131072, 256], P(('row', 'col')), may hold values from -3 to 3
- blocks: float32 [1024, 16, 128, 128], P(('row', 'col')), may hold values from 0 to 0.05
- block_ids: int32 [1024, 16], P(('row', 'col')), may hold values from 0 to 1023, as said below
- counts: int32 [1024], P(('row', 'col')), may hold values from 4 to 16, as said below
- users: int32 [1024, 64], P(('row', 'col')), may hold values from 0 to 127
- positives: int32 [1024, 64], P(('row', 'col')), may hold values from 0 to 127
- neg_index: int32 [1024, 64], P(('row', 'col')), may hold values from 0 to 63
- popular: int32 [1024, 64], P(('row', 'col')), may hold values from 0 to 127
Outputs:
- gradient: float32 [131072, 256], P(('row', 'col'))
- span_loss: float32 [1024], P(('row', 'col'))
Inputs may be any that keep to these rules, and one draw needn't show every extreme that they name: `block_ids`: each row names 16 different positions rb * 64 + cb of one device's 16 x 64 grid of blocks. `counts`: some device has all 16 slots live.
All inputs are finite; a program needn't handle non-finite values.
Results may differ from a plain program's by a relative error of at most 0.0003.
Values sent between devices are 32-bit elements; how exact they have to be, the bound alone decides.
No kernel may reach another device: no remote copies, remote signals or barrier semaphores. Data moves between devices by JAX's collectives and lax.ppermute only.
A program may use at most 64 MiB of HBM per device.

v0:
```python
import jax
import jax.numpy as jnp
from jax import lax
from jax.sharding import PartitionSpec as P

BLOCK = 128
LAYERS = 1


precise = lax.Precision.HIGHEST


def slot_tables(positions, live_count, row_blocks, col_blocks):
    slot_count = positions.shape[0]
    live_mask = (jnp.arange(slot_count, dtype=jnp.int32) < live_count).astype(jnp.float32)
    row_hot = (
        positions[:, None] // col_blocks == jnp.arange(row_blocks, dtype=jnp.int32)[None, :]
    ).astype(jnp.float32)
    col_hot = (
        positions[:, None] % col_blocks == jnp.arange(col_blocks, dtype=jnp.int32)[None, :]
    ).astype(jnp.float32)
    return (live_mask, row_hot, col_hot)


def padded_product(source, values, positions, live_count, row_blocks, col_blocks, transpose):
    feature_width = source.shape[1]
    live_mask, row_hot, col_hot = slot_tables(positions, live_count, row_blocks, col_blocks)
    if transpose:
        stacked = source.reshape(row_blocks, BLOCK, feature_width)
        picked = jnp.einsum("kr,rbd->kbd", row_hot * live_mask[:, None], stacked, precision=precise)
        products = jnp.einsum("kab,kad->kbd", values, picked, precision=precise)
        placed = jnp.einsum("kc,kbd->cbd", col_hot, products, precision=precise)
        return placed.reshape(col_blocks * BLOCK, feature_width)
    stacked = source.reshape(col_blocks, BLOCK, feature_width)
    picked = jnp.einsum("kc,cbd->kbd", col_hot * live_mask[:, None], stacked, precision=precise)
    products = jnp.einsum("kab,kbd->kad", values, picked, precision=precise)
    placed = jnp.einsum("kr,kad->rad", row_hot, products, precision=precise)
    return placed.reshape(row_blocks * BLOCK, feature_width)


def one_hot(indices, span_rows):
    return (indices[:, None] == jnp.arange(span_rows, dtype=jnp.int32)[None, :]).astype(jnp.float32)


def per_device(table, blocks, block_ids, counts, users, positives, neg_index, popular):
    values = blocks[0]
    positions = block_ids[0]
    live_count = counts[0]
    span_rows = table.shape[0]
    feature_width = table.shape[1]
    group_size = lax.axis_size("col")
    row_devices = lax.axis_size("row")
    row_blocks = group_size * span_rows // BLOCK
    col_blocks = row_devices * span_rows // BLOCK

    def multiply(source, transpose):
        return padded_product(
            source, values, positions, live_count, row_blocks, col_blocks, transpose
        )

    current = table
    layer_sum = table
    column_slab = lax.all_gather(current, "row", axis=0, tiled=True)
    partial_rows = multiply(column_slab, False)
    pieces = lax.all_to_all(
        partial_rows.reshape(group_size, span_rows, feature_width),
        "col",
        split_axis=0,
        concat_axis=0,
        tiled=True,
    )
    current = jnp.sum(pieces, axis=0)
    layer_sum = layer_sum + current
    final_rows = layer_sum / (LAYERS + 1)
    pick_user = one_hot(users[0], span_rows)
    pick_item = one_hot(positives[0], span_rows)
    pick_batch = one_hot(jnp.take(positives[0], neg_index[0]), span_rows)
    pick_popular = one_hot(popular[0], span_rows)

    def pair_losses(table_rows):
        user_rows = jnp.dot(pick_user, table_rows, precision=precise)
        item_rows = jnp.dot(pick_item, table_rows, precision=precise)
        batch_rows = jnp.dot(pick_batch, table_rows, precision=precise)
        popular_rows = jnp.dot(pick_popular, table_rows, precision=precise)
        positive_score = jnp.sum(user_rows * item_rows, axis=-1)
        first_terms = jax.nn.softplus(jnp.sum(user_rows * batch_rows, axis=-1) - positive_score)
        second_terms = jax.nn.softplus(jnp.sum(user_rows * popular_rows, axis=-1) - positive_score)
        return first_terms + second_terms

    losses, pull = jax.vjp(pair_losses, final_rows)
    final_grad = pull(jnp.ones_like(losses))[0]
    span_loss = (jnp.sum(losses) / losses.shape[0]).reshape(1)
    scaled = final_grad / (LAYERS + 1)
    gradient = scaled
    row_slab = lax.all_gather(gradient, "col", axis=0, tiled=True)
    partial_cols = multiply(row_slab, True)
    pieces = lax.all_to_all(
        partial_cols.reshape(row_devices, span_rows, feature_width),
        "row",
        split_axis=0,
        concat_axis=0,
        tiled=True,
    )
    returned = jnp.sum(pieces, axis=0)
    gradient = scaled + returned
    return (gradient, span_loss)


def solution(mesh):
    in_specs = (
        P(("row", "col"), None),
        P(("row", "col"), None, None, None),
        P(("row", "col"), None),
        P(("row", "col")),
        P(("row", "col"), None),
        P(("row", "col"), None),
        P(("row", "col"), None),
        P(("row", "col"), None),
    )
    out_specs = (P(("row", "col"), None), P(("row", "col")))
    return jax.shard_map(
        per_device, mesh=mesh, in_specs=in_specs, out_specs=out_specs, check_vma=False
    )
```

profile of v0, /device:TPU:1, one launch (start us, length us, event | category | flops | bytes accessed | tf_op | source)
XLA Modules:
  0.0 728.0 jit_solution(13092670068086928673)
XLA Ops:
  7.2 0.0 copy-start
  7.2 0.0 all-gather.3.cloned.1.call-start
  7.2 0.7 all-gather.3.cloned.1.call-update
  8.6 0.7 and_select_fusion.2
  9.2 167.7 %all-gather.3.cloned.1.call-done = f32[8192,256]{1,0:T(8,128)} async-done(((f32[128,256]{1,0:T(8,128)}), f32[8192,256]{1,0:T(8,128)}) %all-gather.3.cloned.1.call-update) | async-done | bytes 8388624 | tf_op jit(solution)/shard_map/all_gather | solution.py:63
  176.9 12.3 %fusion = f32[16,128,256]{2,0,1:T(8,128)S(1)} fusion(f32[64,128,256]{2,1,0:T(8,128)} %bitcast.59, f32[16]{0:T(128)S(1)} %compare_convert_fusion, s32[16]{0:T(128)S(1)} %get-tuple-element.20), kind=kOutput, calls=%fused_computation.1 | convolution fusion | flops 402655232 | bytes 10485888 | tf_op jit(solution)/shard_map/kc,cbd->kbd/dot_general | solution.py:35
  189.2 0.0 copy-done
  189.3 6.0 fusion.8
  195.2 2.4 copy.21
  197.6 1.2 fusion.50
  198.9 2.5 copy.22
  201.4 0.0 copy-start.6
  201.4 0.0 copy-start.1
  201.4 15.1 %all-to-all-start = ((f32[16,128,256]{2,1,0:T(8,128)}), f32[16,128,256]{2,1,0:T(8,128)S(1)}, u32[]{:S(2)}, u32[]{:S(2)}) async-start(f32[16,128,256]{2,1,0:T(8,128)} %copy.22), calls=%async_computation | async-start | bytes 4194304 | tf_op jit(solution)/shard_map/all_to_all | solution.py:65
  216.5 0.0 copy-start.3
  216.5 0.0 copy-start.4
  216.5 0.0 copy-start.5
  216.5 0.0 all-gather.5.cloned.1.call-start
  216.6 0.0 copy-done.6
  216.6 0.0 copy-done.1
  216.6 0.8 gather_fusion
  217.4 48.0 %all-to-all-done = f32[16,128,256]{2,1,0:T(8,128)S(1)} async-done(((f32[16,128,256]{2,1,0:T(8,128)}), f32[16,128,256]{2,1,0:T(8,128)S(1)}, u32[]{:S(2)}, u32[]{:S(2)}) %all-to-all-start) | async-done | bytes 2097184 | tf_op jit(solution)/shard_map/all_to_all | solution.py:65
  265.5 0.1 reduce_sum.54
  265.6 0.0 copy-done.3
  265.6 0.2 fusion.33
  265.9 0.2 fusion.30
  266.1 0.0 copy-done.4
  266.1 0.2 fusion.35
  266.3 0.0 copy-done.5
  266.4 0.4 multiply_reduce_fusion
  266.7 0.6 add_reduce_fusion
  267.4 0.3 fusion.24
  267.7 0.3 convolution_add_fusion.2
  268.0 0.3 convolution_add_fusion.1
  268.4 1.0 fusion.14
  269.4 0.0 all-gather.5.cloned.1.call-update
  269.4 39.6 %all-gather.5.cloned.1.call-done = f32[2048,256]{1,0:T(8,128)} async-done(((f32[128,256]{1,0:T(8,128)}), f32[2048,256]{1,0:T(8,128)}) %all-gather.5.cloned.1.call-update) | async-done | bytes 2097168 | tf_op jit(solution)/shard_map/all_gather | solution.py:95
  309.0 4.4 fusion.4
  313.4 4.6 fusion.11
  318.0 2.3 copy.25
  320.3 5.1 fusion.52
  325.4 8.1 %copy.26 = f32[64,128,256]{2,1,0:T(8,128)} copy(f32[64,128,256]{2,0,1:T(8,128)S(1)} %fusion.52) | data formatting | bytes 16777216 | tf_op jit(solution)/shard_map/kc,kbd->cbd/dot_general | solution.py:32
  333.5 16.4 %all-to-all-start.1 = ((f32[64,128,256]{2,1,0:T(8,128)}), f32[64,128,256]{2,1,0:T(8,128)}, u32[]{:S(2)}, u32[]{:S(2)}) async-start(f32[64,128,256]{2,1,0:T(8,128)} %copy.26), calls=%async_computation.1 | async-start | bytes 16777216 | tf_op jit(solution)/shard_map/all_to_all | solution.py:97
  350.5 0.0 copy-start.2
  350.5 364.9 %all-to-all-done.1 = f32[64,128,256]{2,1,0:T(8,128)} async-done(((f32[64,128,256]{2,1,0:T(8,128)}), f32[64,128,256]{2,1,0:T(8,128)}, u32[]{:S(2)}, u32[]{:S(2)}) %all-to-all-start.1) | async-done | bytes 8388640 | tf_op jit(solution)/shard_map/all_to_all | solution.py:97
  715.4 3.9 reduce_sum.58
  719.3 0.0 copy-done.2
  719.3 0.7 add.61
  (6 shorter events, 0.1 us)
Async XLA Ops:
  7.2 182.1 %copy-start = (f32[1,16,128,128]{3,2,1,0:T(8,128)S(1)}, f32[1,16,128,128]{3,2,1,0:T(8,128)}, u32[]{:S(2)}) copy-start(f32[1,16,128,128]{3,2,1,0:T(8,128)} %param.10) | copy-start | bytes 3145732
  7.2 169.7 %all-gather.3.cloned.1.call-start = ((), (), s32[]{:S(2)}) async-start(), calls=%async_computation.2 | async-start | bytes 8519680 | tf_op jit(solution)/shard_map/all_gather | solution.py:63
  201.4 15.2 %copy-start.6 = (s32[1,64]{1,0:T(1,128)S(1)}, s32[1,64]{1,0:T(1,128)}, u32[]{:S(2)}) copy-start(s32[1,64]{1,0:T(1,128)} %param.15) | copy-start | bytes 772
  201.4 15.2 %copy-start.1 = (s32[1,64]{1,0:T(1,128)S(1)}, s32[1,64]{1,0:T(1,128)}, u32[]{:S(2)}) copy-start(s32[1,64]{1,0:T(1,128)} %param.14) | copy-start | bytes 772
  201.4 64.0 %all-to-all-start = ((f32[16,128,256]{2,1,0:T(8,128)}), f32[16,128,256]{2,1,0:T(8,128)S(1)}, u32[]{:S(2)}, u32[]{:S(2)}) async-start(f32[16,128,256]{2,1,0:T(8,128)} %copy.22), calls=%async_computation | async-start | bytes 4194304 | tf_op jit(solution)/shard_map/all_to_all | solution.py:65
  216.5 49.1 %copy-start.3 = (f32[128,256]{1,0:T(8,128)S(1)}, f32[128,256]{1,0:T(8,128)}, u32[]{:S(2)}) copy-start(f32[128,256]{1,0:T(8,128)} %param.9) | copy-start | bytes 393220
  216.5 49.6 %copy-start.4 = (s32[1,64]{1,0:T(1,128)S(1)}, s32[1,64]{1,0:T(1,128)}, u32[]{:S(2)}) copy-start(s32[1,64]{1,0:T(1,128)} %param.16) | copy-start | bytes 772
  216.5 49.8 %copy-start.5 = (s32[1,64]{1,0:T(1,128)S(1)}, s32[1,64]{1,0:T(1,128)}, u32[]{:S(2)}) copy-start(s32[1,64]{1,0:T(1,128)} %param.13) | copy-start | bytes 772
  216.5 92.5 %all-gather.5.cloned.1.call-start = ((), (), s32[]{:S(2)}) async-start(), calls=%async_computation.3 | async-start | bytes 2228224 | tf_op jit(solution)/shard_map/all_gather | solution.py:95
  333.5 382.0 %all-to-all-start.1 = ((f32[64,128,256]{2,1,0:T(8,128)}), f32[64,128,256]{2,1,0:T(8,128)}, u32[]{:S(2)}, u32[]{:S(2)}) async-start(f32[64,128,256]{2,1,0:T(8,128)} %copy.26), calls=%async_computation.1 | async-start | bytes 16777216 | tf_op jit(solution)/shard_map/all_to_all | solution.py:97
  350.5 368.8 %copy-start.2 = (f32[128,256]{1,0:T(8,128)S(1)}, f32[128,256]{1,0:T(8,128)}, u32[]{:S(2)}) copy-start(f32[128,256]{1,0:T(8,128)} %fusion.14) | copy-start | bytes 393220
Sparse Core Ops, SparseCore 0:
  12.1 164.7 all-gather.2
  269.5 39.4 all-gather.4
where the time goes:
time: 730 us; the launch traced here: 728 us
  waiting for transfers between devices  621 us (85%)
  matrix products  36.6 us (5%)
  starting transfers between devices  31.6 us (4%)
  between operations  16.7 us (2%)
  local copies, waits for them, and re-layouts  16.1 us (2%)
    all_to_all x1, waiting for transfers between devices, per_device(): lax.all_to_all(partial_cols.reshape(row_devices, span_rows, feature_width...  365 us
    all_gather x1, waiting for transfers between devices, per_device(): column_slab = lax.all_gather(current, 'row', axis=0, tiled=True)  168 us
    all_to_all x1, waiting for transfers between devices, per_device(): lax.all_to_all(partial_rows.reshape(group_size, span_rows, feature_width)...  48 us
    all_gather x1, waiting for transfers between devices, per_device(): row_slab = lax.all_gather(gradient, 'col', axis=0, tiled=True)  39.6 us
    all_to_all x1, starting transfers between devices, per_device(): lax.all_to_all(partial_cols.reshape(row_devices, span_rows, feature_width...  16.4 us
    all_to_all x1, starting transfers between devices, per_device(): lax.all_to_all(partial_rows.reshape(group_size, span_rows, feature_width)...  15.1 us
  transfers between devices with their start and end apart: 4, of which 4 were waited for; matrix products, arithmetic and copies ran while one was open for 0% of the time, Pallas kernels for 0%

commit v1 on v0

v1 whole, which is shorter than its diff:
```python
import functools

import jax
import jax.numpy as jnp
from jax import lax
from jax.experimental import pallas as pl
from jax.experimental.pallas import tpu as pltpu
from jax.sharding import PartitionSpec as P

BLOCK = 128
NX = 4
NZ = 16
NY = 8
HALF = 128
SLOTS = 16
RB = 16
CB = 64
HEAD = 8
VMEM_LIMIT = 48 * 1024 * 1024

precise = lax.Precision.HIGHEST

X_GROUPS = [[x * NZ + z for x in range(NX)] for z in range(NZ)]
Y_GROUPS = [[y * 2 + k for y in range(NY)] for k in range(2)]
CORE_GROUPS = [[2 * y, 2 * y + 1] for y in range(NY)]
Z_GROUPS = [[x * NZ + z for z in range(NZ)] for x in range(NX)]
Z_NEAR = [[x * NZ + 4 * a + b for b in range(4)] for x in range(NX) for a in range(4)]
Z_FAR = [[x * NZ + 4 * a + b for a in range(4)] for x in range(NX) for b in range(4)]
CORE_SWAP = [(i, i ^ 1) for i in range(2 * NY)]


def x_shift(step):
    return [(x * NZ + z, ((x + step) % NX) * NZ + z) for x in range(NX) for z in range(NZ)]


def exchange(values, axis, groups):
    return lax.all_to_all(
        values, axis, split_axis=0, concat_axis=0, tiled=True, axis_index_groups=groups
    )


def split_bf16(values):
    high = values.astype(jnp.bfloat16)
    low = (values - high.astype(jnp.float32)).astype(jnp.bfloat16)
    return high, low


def product(left, right_high, right_low, contract):
    left_high, left_low = split_bf16(left)
    dims = (((contract,), (0,)), ((), ()))

    def dot(a, b):
        return lax.dot_general(a, b, dims, preferred_element_type=jnp.float32)

    return dot(left_high, right_high) + (dot(left_high, right_low) + dot(left_low, right_high))


def block_kernel(transpose, place_ref, ids_ref, *refs):
    sources = refs[: 2 * NX]
    right_ref, out_ref, high_ref, low_ref = refs[2 * NX :]
    own_x = place_ref[0]
    out_ref[...] = jnp.zeros_like(out_ref)

    @pl.loop(0, right_ref.shape[0])
    def _(i):
        high, low = split_bf16(right_ref[i])
        high_ref[i] = high
        low_ref[i] = low

    for number, source in enumerate(sources):
        step, core = number // 2, number % 2
        row_x = lax.rem(own_x + (NX - step), NX)
        column_core = place_ref[1] if core == 0 else 1 - place_ref[1]

        @pl.loop(0, SLOTS)
        def _(slot):
            position = ids_ref[number * SLOTS + slot]
            column = lax.rem(jnp.maximum(position, 0), CB)
            live = jnp.logical_and(position >= 0, column // NZ == own_x)

            @pl.when(live)
            def _():
                row = row_x * RB + position // CB
                near = lax.rem(column, NZ) * 2 + column_core
                block = source[pl.ds(pl.multiple_of(slot * BLOCK, BLOCK), BLOCK), :]
                if transpose:
                    out_ref[near] += product(block, high_ref[row], low_ref[row], 0)
                else:
                    out_ref[row] += product(block, high_ref[near], low_ref[near], 1)


def multiply(place, ids, sources, right, transpose):
    rows = 2 * NZ if transpose else NX * RB
    return pl.pallas_call(
        functools.partial(block_kernel, transpose),
        out_shape=jax.ShapeDtypeStruct((rows, BLOCK, HALF), jnp.float32),
        in_specs=[pl.BlockSpec(memory_space=pltpu.SMEM)] * 2
        + [pl.BlockSpec(memory_space=pltpu.VMEM)] * (2 * NX + 1),
        out_specs=pl.BlockSpec(memory_space=pltpu.VMEM),
        scratch_shapes=[
            pltpu.VMEM(right.shape, jnp.bfloat16),
            pltpu.VMEM(right.shape, jnp.bfloat16),
        ],
        compiler_params=pltpu.CompilerParams(vmem_limit_bytes=VMEM_LIMIT),
    )(place, ids, *sources, right)


def swap_halves(rows):
    halves = rows.reshape(BLOCK, 2, HALF).transpose(1, 0, 2)
    return exchange(halves, "col", CORE_GROUPS)


def join_halves(pieces):
    halves = exchange(pieces, "col", CORE_GROUPS)
    return halves.transpose(1, 0, 2).reshape(BLOCK, 2 * HALF)


def one_hot(indices, span_rows):
    return (indices[:, None] == jnp.arange(span_rows, dtype=jnp.int32)[None, :]).astype(jnp.float32)


def per_device(table, blocks, block_ids, counts, users, positives, neg_index, popular):
    place = jnp.stack([lax.axis_index("row") // NZ, lax.axis_index("col") % 2]).astype(jnp.int32)

    halves = swap_halves(table)
    gathered = lax.all_gather(halves, "row", axis=0, tiled=True, axis_index_groups=Z_GROUPS)

    live = jnp.arange(SLOTS, dtype=jnp.int32) < counts[0]
    marked = jnp.where(live, block_ids[0], -1).astype(jnp.float32)
    header = jnp.pad(marked[None, :], ((0, HEAD - 1), (0, BLOCK - SLOTS)))
    packed = jnp.concatenate([blocks.reshape(SLOTS * BLOCK, BLOCK), header], axis=0)
    sources = []
    for step in range(NX):
        moved = packed if step == 0 else lax.ppermute(packed, "row", x_shift(step))
        sources += [moved, lax.ppermute(moved, "col", CORE_SWAP)]
    ids = jnp.concatenate([s[SLOTS * BLOCK, :SLOTS] for s in sources]).astype(jnp.int32)

    partial_rows = multiply(place, ids, sources, gathered, False)
    pieces = exchange(partial_rows.reshape(NX, RB * BLOCK, HALF), "row", X_GROUPS)
    summed = jnp.sum(pieces, axis=0).reshape(NY, 2 * BLOCK, HALF)
    pieces = exchange(summed, "col", Y_GROUPS)
    summed = jnp.sum(pieces, axis=0).reshape(2, BLOCK, HALF)
    current = join_halves(summed)

    final_rows = (table + current) / 2
    span_rows = table.shape[0]
    pick_user = one_hot(users[0], span_rows)
    pick_item = one_hot(positives[0], span_rows)
    pick_batch = one_hot(jnp.take(positives[0], neg_index[0]), span_rows)
    pick_popular = one_hot(popular[0], span_rows)

    def pair_losses(table_rows):
        user_rows = jnp.dot(pick_user, table_rows, precision=precise)
        item_rows = jnp.dot(pick_item, table_rows, precision=precise)
        batch_rows = jnp.dot(pick_batch, table_rows, precision=precise)
        popular_rows = jnp.dot(pick_popular, table_rows, precision=precise)
        positive_score = jnp.sum(user_rows * item_rows, axis=-1)
        first_terms = jax.nn.softplus(jnp.sum(user_rows * batch_rows, axis=-1) - positive_score)
        second_terms = jax.nn.softplus(jnp.sum(user_rows * popular_rows, axis=-1) - positive_score)
        return first_terms + second_terms

    losses, pull = jax.vjp(pair_losses, final_rows)
    final_grad = pull(jnp.ones_like(losses))[0]
    span_loss = (jnp.sum(losses) / losses.shape[0]).reshape(1)
    scaled = final_grad / 2

    halves = swap_halves(scaled).reshape(1, 2 * BLOCK, HALF)
    column = exchange(jnp.broadcast_to(halves, (NY, 2 * BLOCK, HALF)), "col", Y_GROUPS)
    column = column.reshape(1, RB * BLOCK, HALF)
    slab = exchange(jnp.broadcast_to(column, (NX, RB * BLOCK, HALF)), "row", X_GROUPS)
    partial_cols = multiply(place, ids, sources, slab.reshape(NX * RB, BLOCK, HALF), True)
    by_near = partial_cols.reshape(4, 4, 2 * BLOCK, HALF).transpose(1, 0, 2, 3)
    summed = jnp.sum(exchange(by_near, "row", Z_NEAR), axis=0)
    summed = jnp.sum(exchange(summed, "row", Z_FAR), axis=0)
    returned = join_halves(summed.reshape(2, BLOCK, HALF))
    return (scaled + returned, span_loss)


def solution(mesh):
    in_specs = (
        P(("row", "col"), None),
        P(("row", "col"), None, None, None),
        P(("row", "col"), None),
        P(("row", "col")),
        P(("row", "col"), None),
        P(("row", "col"), None),
        P(("row", "col"), None),
        P(("row", "col"), None),
    )
    out_specs = (P(("row", "col"), None), P(("row", "col")))
    return jax.shard_map(
        per_device, mesh=mesh, in_specs=in_specs, out_specs=out_specs, check_vma=False
    )
```

time: 730 us -> 405 us (0.55)
  waiting for transfers between devices: 621 us -> 80.9 us
  blocking collectives: 0 us -> 221 us
  matrix products: 36.6 us -> 2.37 us
  Pallas kernels: 0 us -> 23.8 us
    all_to_all x2, waiting for transfers between devices: 413 us -> 43.8 us  [exchange(): lax.all_to_all(values, axis, split_axis=0, concat_axis=0, tiled=True, axi...]
    all_to_all x0 -> x8, blocking collectives: none -> 221 us  [exchange(): lax.all_to_all(values, axis, split_axis=0, concat_axis=0, tiled=True, axi...]
    all_gather x2 -> x1, waiting for transfers between devices: 207 us -> 1.19 us  [per_device(): lax.all_gather(halves, 'row', axis=0, tiled=True, axis_index_groups=Z_GRO...]
    ppermute x0 -> x7, waiting for transfers between devices: none -> 36 us  [the longest x3 35.8 us: per_device(): moved = packed if step == 0 else lax.ppermute(packed, 'row', x_shift(step))]
    dot_general x6 -> x0, matrix products: 33.6 us -> none  [the longest x1 12.3 us: padded_product(): jnp.einsum('kc,cbd->kbd', col_hot * live_mask[:, None], stacked, precisio...]
    pallas_call x0 -> x2, Pallas kernels: none -> 23.8 us  [multiply(): pl.pallas_call(functools.partial(block_kernel, transpose), out_shape=jax....]
    ppermute x0 -> x7, starting transfers between devices: none -> 19.5 us  [the longest x4 12.3 us: per_device(): sources += [moved, lax.ppermute(moved, 'col', CORE_SWAP)]]
    dot_general x4 -> x0, local copies, waits for them, and re-layouts: 15.3 us -> none  [the longest x1 8.08 us: padded_product(): placed = jnp.einsum('kc,kbd->cbd', col_hot, products, precision=precise)]
  transfers between devices with their start and end apart: 4 -> 10, of which waited for: 4 -> 6; matrix products, arithmetic and copies ran while one was open for 0% -> 1% of each run, Pallas kernels for 0% -> 0%
where the time goes in v1:
time: 405 us; the launch traced here: 404 us
  blocking collectives  221 us (55%)
  waiting for transfers between devices  80.9 us (20%)
  starting transfers between devices  37.7 us (9%)
  Pallas kernels  23.8 us (6%)
  between operations  16.7 us (4%)
  other arithmetic  10.8 us (3%)
  local copies, waits for them, and re-layouts  9.84 us (2%)
    all_to_all x8, blocking collectives, exchange(): lax.all_to_all(values, axis, split_axis=0, concat_axis=0, tiled=True, axi...  221 us
    all_to_all x2, waiting for transfers between devices, exchange(): lax.all_to_all(values, axis, split_axis=0, concat_axis=0, tiled=True, axi...  43.8 us
    ppermute x3, waiting for transfers between devices, per_device(): moved = packed if step == 0 else lax.ppermute(packed, 'row', x_shift(step))  35.8 us
    pallas_call x2, Pallas kernels, multiply(): pl.pallas_call(functools.partial(block_kernel, transpose), out_shape=jax....  23.8 us
    all_to_all x2, starting transfers between devices, exchange(): lax.all_to_all(values, axis, split_axis=0, concat_axis=0, tiled=True, axi...  18.2 us
    ppermute x4, starting transfers between devices, per_device(): sources += [moved, lax.ppermute(moved, 'col', CORE_SWAP)]  12.3 us
  transfers between devices with their start and end apart: 10, of which 6 were waited for; matrix products, arithmetic and copies ran while one was open for 1% of the time, Pallas kernels for 0%

profile of v1, /device:TPU:1, one launch (start us, length us, event | category | flops | bytes accessed | tf_op | source)
XLA Modules:
  0.0 403.6 jit_solution(15541946171560658765)
XLA Ops:
  7.2 1.0 copy.21
  8.2 17.6 %all_to_all.50 = f32[2,128,128]{1,2,0:T(8,128)S(1)} all-to-all(f32[2,128,128]{1,2,0:T(8,128)S(1)} %bitcast.83), channel_id=1, replica_groups={{0,1},{2,3},{4,5},{6,7},{8,9},{10,11},{12,13},{14,15},{16,17},{18,19},{..., dimensions={0} | all-to-all | bytes 262144 | tf_op jit(solution)/shard_map/all_to_all | solution.py:37
  25.9 0.8 copy.22
  27.3 0.7 fusion.30
  27.9 1.3 select_maximum_fusion.refs_0_
  29.3 1.9 collective-permute-start.5
  31.2 1.9 collective-permute-start.3
  33.1 3.4 collective-permute-start.1
  36.5 2.8 collective-permute-start
  39.3 16.4 %collective-permute-done.5.refs_6_ = f32[2056,128]{1,0:T(8,128)} collective-permute-done((f32[2056,128]{1,0:T(8,128)S(1)}, f32[2056,128]{1,0:T(8,128)}, u32[]{:S(2)}, u32[]{:S(2)}) %collective-permute-start.5) | collective-permute-done | bytes 1052704 | tf_op jit(solution)/shard_map/ppermute | solution.py:134
  55.7 3.9 collective-permute-start.6
  59.7 3.2 collective-permute-start.4
  63.0 19.3 %collective-permute-done.1.refs_2_ = f32[2056,128]{1,0:T(8,128)S(1)} collective-permute-done((f32[2056,128]{1,0:T(8,128)S(1)}, f32[2056,128]{1,0:T(8,128)S(1)}, u32[]{:S(2)}, u32[]{:S(2)}) %collective-permute-start.1) | collective-permute-done | bytes 1052704 | tf_op jit(solution)/shard_map/ppermute | solution.py:134
  82.3 2.4 collective-permute-start.2
  84.7 0.7 slice_bitcast_fusion.1
  85.4 0.7 slice_bitcast_fusion.6
  86.1 0.7 slice_bitcast_fusion
  87.0 0.8 copy-done.4
  87.8 1.0 copy-done
  88.9 1.2 all-gather.2.cloned.1.call-done.refs_8_
  90.1 1.2 copy-done.1
  91.3 11.4 %shard_map.95 = f32[64,128,128]{2,1,0:T(8,128)} custom-call(s32[2]{0:T(128)S(1)} %pad_add_fusion.place_ref, s32[128]{0:T(128)S(1)} %convert_element_type.18.ids_ref, f32[2056,128]{1,0:T(8,128)S(1)} %select_maximum_fusion.refs_0_, f32[2056,128]{1,0:T(8,128)} %collective-permute-done.refs_1_, f32[2056,128]{1,0:T(8,128)S(1)} %collective-permute-done.1.refs_2_, ...), custom_call_target="tpu_custom_call" | custom-call | tf_op jit(solution)/shard_map/pallas_call | solution.py:94
  102.7 45.2 %all_to_all.51 = f32[4,2048,128]{2,1,0:T(8,128)} all-to-all(f32[4,2048,128]{2,1,0:T(8,128)} %bitcast.75), channel_id=1, replica_groups={{0,256,512,768},{16,272,528,784},{32,288,544,800},{48,304,560,816},{64,..., dimensions={0} | all-to-all | bytes 8388608 | tf_op jit(solution)/shard_map/all_to_all | solution.py:37
  147.9 3.5 reduce_sum.72
  151.4 8.5 %all-to-all-start.2 = ((f32[8,256,128]{2,1,0:T(8,128)}), f32[8,256,128]{2,1,0:T(8,128)}, u32[]{:S(2)}, u32[]{:S(2)}) async-start(f32[8,256,128]{2,1,0:T(8,128)} %bitcast.79), calls=%async_computation.2 | async-start | bytes 2097152 | tf_op jit(solution)/shard_map/all_to_all | solution.py:37
  159.9 0.8 gather_fusion
  160.7 15.9 %all-to-all-done.2 = f32[8,256,128]{2,1,0:T(8,128)} async-done(((f32[8,256,128]{2,1,0:T(8,128)}), f32[8,256,128]{2,1,0:T(8,128)}, u32[]{:S(2)}, u32[]{:S(2)}) %all-to-all-start.2) | async-done | bytes 1048608 | tf_op jit(solution)/shard_map/all_to_all | solution.py:37
  176.6 1.3 reduce_sum.73
  177.9 16.7 %all_to_all.52 = f32[2,128,128]{2,1,0:T(8,128)S(1)} all-to-all(f32[2,128,128]{2,1,0:T(8,128)S(1)} %bitcast.81), channel_id=1, replica_groups={{0,1},{2,3},{4,5},{6,7},{8,9},{10,11},{12,13},{14,15},{16,17},{18,19},{..., dimensions={0} | all-to-all | bytes 262144 | tf_op jit(solution)/shard_map/all_to_all | solution.py:37
  194.6 0.2 fusion.18
  195.3 0.4 multiply_reduce_fusion
  195.7 0.6 add_reduce_fusion
  196.3 0.3 fusion.9
  196.7 0.3 convolution_add_fusion.2
  197.0 0.3 convolution_add_fusion.1
  197.3 0.3 fusion
  197.7 3.8 all_to_all.53
  201.6 31.6 %all_to_all.54 = f32[8,256,128]{2,1,0:T(8,128)S(1)} all-to-all(f32[8,256,128]{2,1,0:T(8,128)S(1)} %broadcast_in_dim.49), channel_id=1, replica_groups={{0,2,4,6,8,10,12,14},{1,3,5,7,9,11,13,15},{16,18,20,22,24,26,28,30},{17..., dimensions={0} | all-to-all | bytes 2097152 | tf_op jit(solution)/shard_map/all_to_all | solution.py:37
  233.2 0.3 broadcast_in_dim.51
  233.5 52.0 %all_to_all.55 = f32[4,2048,128]{2,1,0:T(8,128)} all-to-all(f32[4,2048,128]{2,1,0:T(8,128)S(1)} %broadcast_in_dim.51), channel_id=1, replica_groups={{0,256,512,768},{16,272,528,784},{32,288,544,800},{48,304,560,816},{64,..., dimensions={0} | all-to-all | bytes 8388608 | tf_op jit(solution)/shard_map/all_to_all | solution.py:37
  285.5 12.4 %shard_map.96 = f32[32,128,128]{2,1,0:T(8,128)} custom-call(s32[2]{0:T(128)S(1)} %pad_add_fusion.place_ref, s32[128]{0:T(128)S(1)} %convert_element_type.18.ids_ref, f32[2056,128]{1,0:T(8,128)S(1)} %select_maximum_fusion.refs_0_, f32[2056,128]{1,0:T(8,128)} %collective-permute-done.refs_1_, f32[2056,128]{1,0:T(8,128)S(1)} %collective-permute-done.1.refs_2_, ...), custom_call_target="tpu_custom_call" | custom-call | tf_op jit(solution)/shard_map/pallas_call | solution.py:94
  297.9 1.7 copy.34
  299.7 50.5 %all_to_all.56 = f32[4,4,256,128]{3,2,1,0:T(8,128)} all-to-all(f32[4,4,256,128]{3,2,1,0:T(8,128)S(1)} %bitcast.76), channel_id=1, replica_groups={{0,16,32,48},{64,80,96,112},{128,144,160,176},{192,208,224,240},{256,27..., dimensions={0} | all-to-all | bytes 4194304 | tf_op jit(solution)/shard_map/all_to_all | solution.py:37
  350.2 2.6 reduce_sum.77
  352.7 9.7 %all-to-all-start.8 = ((f32[4,256,128]{2,1,0:T(8,128)}), f32[4,256,128]{2,1,0:T(8,128)S(1)}, u32[]{:S(2)}, u32[]{:S(2)}) async-start(f32[4,256,128]{2,1,0:T(8,128)} %reduce_sum.77), calls=%async_computation.8 | async-start | bytes 1048576 | tf_op jit(solution)/shard_map/all_to_all | solution.py:37
  363.0 27.9 %all-to-all-done.8 = f32[4,256,128]{2,1,0:T(8,128)S(1)} async-done(((f32[4,256,128]{2,1,0:T(8,128)}), f32[4,256,128]{2,1,0:T(8,128)S(1)}, u32[]{:S(2)}, u32[]{:S(2)}) %all-to-all-start.8) | async-done | bytes 524320 | tf_op jit(solution)/shard_map/all_to_all | solution.py:37
  391.0 4.0 all_to_all.57
  394.9 0.7 bitcast_add_fusion
  (42 shorter events, 1.1 us)
Async XLA Ops:
  7.2 82.9 %all-gather.2.cloned.1.call-start = ((), (), s32[]{:S(2)}) async-start(), calls=%async_computation.10 | async-start | bytes 2228224 | tf_op jit(solution)/shard_map/all_gather | solution.py:126
  27.9 31.7 %copy-start.8 = (s32[1,16]{1,0:T(1,128)S(1)}, s32[1,16]{1,0:T(1,128)}, u32[]{:S(2)}) copy-start(s32[1,16]{1,0:T(1,128)} %param.11) | copy-start | bytes 196
  29.3 26.5 %collective-permute-start.5 = (f32[2056,128]{1,0:T(8,128)S(1)}, f32[2056,128]{1,0:T(8,128)}, u32[]{:S(2)}, u32[]{:S(2)}) collective-permute-start(f32[2056,128]{1,0:T(8,128)S(1)} %select_maximum_fusion.refs_0_), channel_id=1, source_target_pairs={{0,768},{16,784},{32,800},{48,816},{64,832},{80,848},{96,864},{112... | collective-permute-start | bytes 3158024 | tf_op jit(solution)/shard_map/ppermute | solution.py:134
  31.2 28.5 %collective-permute-start.3 = (f32[2056,128]{1,0:T(8,128)S(1)}, f32[2056,128]{1,0:T(8,128)S(1)}, u32[]{:S(2)}, u32[]{:S(2)}) collective-permute-start(f32[2056,128]{1,0:T(8,128)S(1)} %select_maximum_fusion.refs_0_), channel_id=1, source_target_pairs={{0,512},{16,528},{32,544},{48,560},{64,576},{80,592},{96,608},{112... | collective-permute-start | bytes 3158024 | tf_op jit(solution)/shard_map/ppermute | solution.py:134
  33.1 49.2 %collective-permute-start.1 = (f32[2056,128]{1,0:T(8,128)S(1)}, f32[2056,128]{1,0:T(8,128)S(1)}, u32[]{:S(2)}, u32[]{:S(2)}) collective-permute-start(f32[2056,128]{1,0:T(8,128)S(1)} %select_maximum_fusion.refs_0_), channel_id=1, source_target_pairs={{0,256},{16,272},{32,288},{48,304},{64,320},{80,336},{96,352},{112... | collective-permute-start | bytes 3158024 | tf_op jit(solution)/shard_map/ppermute | solution.py:134
  36.5 48.9 %collective-permute-start = (f32[2056,128]{1,0:T(8,128)S(1)}, f32[2056,128]{1,0:T(8,128)}, u32[]{:S(2)}, u32[]{:S(2)}) collective-permute-start(f32[2056,128]{1,0:T(8,128)S(1)} %select_maximum_fusion.refs_0_), channel_id=1, source_target_pairs={{0,1},{1,0},{2,3},{3,2},{4,5},{5,4},{6,7},{7,6},{8,9},{9,8},{10,11... | collective-permute-start | bytes 3158024 | tf_op jit(solution)/shard_map/ppermute | solution.py:135
  55.7 30.4 %collective-permute-start.6 = (f32[2056,128]{1,0:T(8,128)}, f32[2056,128]{1,0:T(8,128)}, u32[]{:S(2)}, u32[]{:S(2)}) collective-permute-start(f32[2056,128]{1,0:T(8,128)} %collective-permute-done.5.refs_6_), channel_id=1, source_target_pairs={{0,1},{1,0},{2,3},{3,2},{4,5},{5,4},{6,7},{7,6},{8,9},{9,8},{10,11... | collective-permute-start | bytes 3158024 | tf_op jit(solution)/shard_map/ppermute | solution.py:135
  59.7 27.0 %collective-permute-start.4 = (f32[2056,128]{1,0:T(8,128)S(1)}, f32[2056,128]{1,0:T(8,128)S(1)}, u32[]{:S(2)}, u32[]{:S(2)}) collective-permute-start(f32[2056,128]{1,0:T(8,128)S(1)} %collective-permute-done.3.refs_4_), channel_id=1, source_target_pairs={{0,1},{1,0},{2,3},{3,2},{4,5},{5,4},{6,7},{7,6},{8,9},{9,8},{10,11... | collective-permute-start | bytes 3158024 | tf_op jit(solution)/shard_map/ppermute | solution.py:135
  82.3 4.7 %collective-permute-start.2 = (f32[2056,128]{1,0:T(8,128)S(1)}, f32[2056,128]{1,0:T(8,128)S(1)}, u32[]{:S(2)}, u32[]{:S(2)}) collective-permute-start(f32[2056,128]{1,0:T(8,128)S(1)} %collective-permute-done.1.refs_2_), channel_id=1, source_target_pairs={{0,1},{1,0},{2,3},{3,2},{4,5},{5,4},{6,7},{7,6},{8,9},{9,8},{10,11... | collective-permute-start | bytes 3158024 | tf_op jit(solution)/shard_map/ppermute | solution.py:135
  86.8 1.0 copy-start.4
  87.8 1.0 copy-start
  90.1 1.2 copy-start.1
  151.4 8.5 %copy-start.9 = (s32[1,64]{1,0:T(1,128)S(1)}, s32[1,64]{1,0:T(1,128)}, u32[]{:S(2)}) copy-start(s32[1,64]{1,0:T(1,128)} %param.15) | copy-start | bytes 772
  151.4 8.5 %copy-start.3 = (s32[1,64]{1,0:T(1,128)S(1)}, s32[1,64]{1,0:T(1,128)}, u32[]{:S(2)}) copy-start(s32[1,64]{1,0:T(1,128)} %param.14) | copy-start | bytes 772
  151.4 25.2 %all-to-all-start.2 = ((f32[8,256,128]{2,1,0:T(8,128)}), f32[8,256,128]{2,1,0:T(8,128)}, u32[]{:S(2)}, u32[]{:S(2)}) async-start(f32[8,256,128]{2,1,0:T(8,128)} %bitcast.79), calls=%async_computation.2 | async-start | bytes 2097152 | tf_op jit(solution)/shard_map/all_to_all | solution.py:37
  159.8 34.7 %copy-start.5 = (f32[128,256]{1,0:T(8,128)S(1)}, f32[128,256]{1,0:T(8,128)}, u32[]{:S(2)}) copy-start(f32[128,256]{1,0:T(8,128)} %param.9) | copy-start | bytes 393220
  160.7 34.4 %copy-start.6 = (s32[1,64]{1,0:T(1,128)S(1)}, s32[1,64]{1,0:T(1,128)}, u32[]{:S(2)}) copy-start(s32[1,64]{1,0:T(1,128)} %param.16) | copy-start | bytes 772
  160.7 34.6 %copy-start.7 = (s32[1,64]{1,0:T(1,128)S(1)}, s32[1,64]{1,0:T(1,128)}, u32[]{:S(2)}) copy-start(s32[1,64]{1,0:T(1,128)} %param.13) | copy-start | bytes 772
  233.5 52.0 %copy-start.2 = (f32[2056,128]{1,0:T(8,128)S(1)}, f32[2056,128]{1,0:T(8,128)}, u32[]{:S(2)}) copy-start(f32[2056,128]{1,0:T(8,128)} %copy-done) | copy-start | bytes 3158020
  352.7 38.2 %all-to-all-start.8 = ((f32[4,256,128]{2,1,0:T(8,128)}), f32[4,256,128]{2,1,0:T(8,128)S(1)}, u32[]{:S(2)}, u32[]{:S(2)}) async-start(f32[4,256,128]{2,1,0:T(8,128)} %reduce_sum.77), calls=%async_computation.8 | async-start | bytes 1048576 | tf_op jit(solution)/shard_map/all_to_all | solution.py:37
Sparse Core Ops, SparseCore 0:
  26.8 63.2 all-gather.1

commit v2 on v1

v2 whole, which is shorter than its diff:
```python
import functools

import jax
import jax.numpy as jnp
from jax import lax
from jax.experimental import pallas as pl
from jax.experimental.pallas import tpu as pltpu
from jax.sharding import PartitionSpec as P

BLOCK = 128
NX = 4
NZ = 16
NY = 8
HALF = 128
SLOTS = 16
CB = 64
HEAD = 8
PAIRS = 64
VMEM_LIMIT = 48 * 1024 * 1024

precise = lax.Precision.HIGHEST

Y_GROUPS = [[y * 2 + k for y in range(NY)] for k in range(2)]
CORE_SWAP = [(i, i ^ 1) for i in range(2 * NY)]


def send_x(values, step):
    pairs = [(x * NZ + z, ((x + step) % NX) * NZ + z) for x in range(NX) for z in range(NZ)]
    return lax.ppermute(values, "row", pairs)


def send_z(values, step):
    pairs = [(x * NZ + z, x * NZ + (z + step) % NZ) for x in range(NX) for z in range(NZ)]
    return lax.ppermute(values, "row", pairs)


def swap_cores(values):
    return lax.ppermute(values, "col", CORE_SWAP)


def exchange_y(values):
    return lax.all_to_all(
        values, "col", split_axis=0, concat_axis=0, tiled=True, axis_index_groups=Y_GROUPS
    )


def split_bf16(values):
    high = values.astype(jnp.bfloat16)
    low = (values - high.astype(jnp.float32)).astype(jnp.bfloat16)
    return high, low


def product(left, right, contract):
    left_high, left_low = split_bf16(left)
    right_high, right_low = split_bf16(right)
    dims = (((contract,), (0,)), ((), ()))

    def dot(a, b):
        return lax.dot_general(a, b, dims, preferred_element_type=jnp.float32)

    return dot(left_high, right_high) + (dot(left_high, right_low) + dot(left_low, right_high))


def for_live_slots(place_ref, ids_ref, sources, body):
    own_x, own_z = place_ref[0], place_ref[1]
    for number, source in enumerate(sources):
        step, core = number // 2, number % 2

        @pl.loop(0, SLOTS)
        def _(slot):
            position = ids_ref[number * SLOTS + slot]
            column = jnp.bitwise_and(position, CB - 1)
            live = jnp.logical_and(position >= 0, column // NZ == own_x)

            @pl.when(live)
            def _():
                near = jnp.bitwise_and(column - own_z, NZ - 1) * 2 + core
                block = source[pl.ds(pl.multiple_of(slot * BLOCK, BLOCK), BLOCK), :]
                body(step, block, position // CB, near)


OWN = (0, 4, 8, 12)
AFTER = (1, 5, 9, 13)
BEFORE = (15, 3, 7, 11)
TWO_AFTER = (2, 6)
TWO_BEFORE = (14, 10)
PARTS = (OWN, AFTER, BEFORE, TWO_AFTER, TWO_BEFORE)


def forward_kernel(place_ref, ids_ref, *refs):
    sources, parts = refs[: 2 * NX], refs[2 * NX : 2 * NX + len(PARTS)]
    outs, rows_ref = refs[2 * NX + len(PARTS) : -1], refs[-1]
    for out in outs:
        out[...] = jnp.zeros_like(out)
    for part, distances in zip(parts, PARTS):
        for index, distance in enumerate(distances):
            rows_ref[pl.ds(2 * distance, 2)] = part[pl.ds(2 * index, 2)]

    def body(step, block, rb, near):
        value = product(block, rows_ref[near], 1)
        for half in range(2):

            @pl.when(rb % 2 == half)
            def _():
                outs[2 * step + half][rb // 2] += value

    for_live_slots(place_ref, ids_ref, sources, body)


def backward_kernel(place_ref, ids_ref, *refs):
    sources, slabs = refs[: 2 * NX], refs[2 * NX : 4 * NX]
    outs, total_ref = refs[4 * NX : -1], refs[-1]
    total_ref[...] = jnp.zeros_like(total_ref)

    def body(step, block, rb, near):
        first, second = slabs[2 * step], slabs[2 * step + 1]
        rows = jnp.where(rb % 2 == 0, first[rb // 2], second[rb // 2])
        total_ref[near] += product(block, rows, 0)

    for_live_slots(place_ref, ids_ref, sources, body)
    for out, distances in zip(outs, PARTS):
        for index, distance in enumerate(distances):
            out[pl.ds(2 * index, 2)] = total_ref[pl.ds(2 * distance, 2)]


def call_kernel(body, place, ids, arrays, out_blocks):
    whole = pl.BlockSpec(memory_space=pltpu.VMEM)
    return pl.pallas_call(
        body,
        out_shape=[jax.ShapeDtypeStruct((n, BLOCK, HALF), jnp.float32) for n in out_blocks],
        in_specs=[pl.BlockSpec(memory_space=pltpu.SMEM)] * 2 + [whole] * len(arrays),
        out_specs=[whole] * len(out_blocks),
        scratch_shapes=[pltpu.VMEM((2 * NZ, BLOCK, HALF), jnp.float32)],
        compiler_params=pltpu.CompilerParams(vmem_limit_bytes=VMEM_LIMIT),
    )(place, ids, *arrays)


def one_hot(indices, span_rows):
    return (indices[..., None] == jnp.arange(span_rows, dtype=jnp.int32)).astype(jnp.float32)


def per_device(table, blocks, block_ids, counts, users, positives, neg_index, popular):
    own_row = lax.axis_index("row")
    core = jnp.bitwise_and(lax.axis_index("col"), 1)
    place = jnp.stack([own_row // NZ, jnp.bitwise_and(own_row, NZ - 1)]).astype(jnp.int32)

    left, right = table[:, :HALF], table[:, HALF:]
    own_half = jnp.where(core == 0, left, right)
    other_half = swap_cores(jnp.where(core == 0, right, left))
    pair = jnp.stack([own_half, other_half])

    near_4 = jnp.concatenate([pair, send_z(pair, -4), send_z(pair, 8), send_z(pair, 4)])
    ends_after = near_4[:4]
    ends_before = jnp.concatenate([near_4[:2], near_4[6:]])

    live = jnp.arange(SLOTS, dtype=jnp.int32) < counts[0]
    marked = jnp.where(live, block_ids[0], -1).astype(jnp.float32)
    header = jnp.pad(marked[None, :], ((0, HEAD - 1), (0, BLOCK - SLOTS)))
    packed = jnp.concatenate([blocks.reshape(SLOTS * BLOCK, BLOCK), header], axis=0)
    sources = []
    for step in range(NX):
        moved = packed if step == 0 else send_x(packed, step)
        sources += [moved, swap_cores(moved)]
    ids = jnp.concatenate([s[SLOTS * BLOCK, :SLOTS] for s in sources]).astype(jnp.int32)

    parts = [
        near_4,
        send_z(near_4, -1),
        send_z(near_4, 1),
        send_z(ends_after, -2),
        send_z(ends_before, 2),
    ]
    partial_rows = call_kernel(forward_kernel, place, ids, sources + parts, [NY] * (2 * NX))
    current = []
    for half in range(2):
        summed = partial_rows[half]
        for step in range(1, NX):
            summed = summed + send_x(partial_rows[2 * step + half], -step)
        current.append(jnp.sum(exchange_y(summed), axis=0))

    picks = jnp.stack([users[0], positives[0], jnp.take(positives[0], neg_index[0]), popular[0]])
    other_picks = swap_cores(picks)
    is_first = core == 0
    span_picks = [jnp.where(is_first, picks, other_picks), jnp.where(is_first, other_picks, picks)]
    span_table = [
        jnp.where(is_first, own_half, other_half),
        jnp.where(is_first, other_half, own_half),
    ]
    final_rows = jnp.stack([(t + c) / 2 for t, c in zip(span_table, current)])
    hot = one_hot(jnp.stack(span_picks), BLOCK)
    rows = jnp.einsum("hpij,hjd->hpid", hot, final_rows, precision=precise)
    user_rows, item_rows, batch_rows, popular_rows = (rows[:, i] for i in range(4))
    scores = jnp.stack(
        [
            jnp.sum(user_rows * item_rows, axis=-1),
            jnp.sum(user_rows * batch_rows, axis=-1),
            jnp.sum(user_rows * popular_rows, axis=-1),
        ],
        axis=1,
    )
    scores = scores + swap_cores(scores)
    first = scores[:, 1] - scores[:, 0]
    second = scores[:, 2] - scores[:, 0]
    losses = jax.nn.softplus(first) + jax.nn.softplus(second)
    span_losses = jnp.sum(losses, axis=1) / PAIRS
    span_loss = jnp.where(is_first, span_losses[0], span_losses[1]).reshape(1)
    pull_first = jax.nn.sigmoid(first)[..., None] / 2
    pull_second = jax.nn.sigmoid(second)[..., None] / 2
    pull_item = -(pull_first + pull_second)
    row_grads = jnp.stack(
        [
            pull_item * item_rows + pull_first * batch_rows + pull_second * popular_rows,
            pull_item * user_rows,
            pull_first * user_rows,
            pull_second * user_rows,
        ],
        axis=1,
    )
    scaled = jnp.einsum("hpij,hpid->hjd", hot, row_grads, precision=precise)

    slabs = [None] * (2 * NX)
    for half in range(2):
        slab = exchange_y(jnp.broadcast_to(scaled[half][None], (NY, BLOCK, HALF)))
        slabs[half] = slab
        for step in range(1, NX):
            slabs[2 * step + half] = send_x(slab, step)
    own, after, before, two_after, two_before = call_kernel(
        backward_kernel, place, ids, sources + slabs, [2 * len(p) for p in PARTS]
    )
    after = send_z(after, 1)
    before = send_z(before, -1)
    two_after = send_z(two_after, 2)
    two_before = send_z(two_before, -2)
    sums = [own[2 * m : 2 * m + 2] + after[2 * m : 2 * m + 2] + before[2 * m : 2 * m + 2] for m in range(4)]
    sums[0] = sums[0] + two_after[:2] + two_before[:2]
    sums[1] = sums[1] + two_after[2:]
    sums[3] = sums[3] + two_before[2:]
    returned = sums[0] + send_z(sums[1], 4) + send_z(sums[3], -4) + send_z(sums[2], 8)

    scaled_own = jnp.where(is_first, scaled[0], scaled[1])
    scaled_other = jnp.where(is_first, scaled[1], scaled[0])
    own_grad = scaled_own + returned[0]
    other_grad = swap_cores(scaled_other + returned[1])
    gradient = jnp.where(
        is_first,
        jnp.concatenate([own_grad, other_grad], axis=1),
        jnp.concatenate([other_grad, own_grad], axis=1),
    )
    return (gradient, span_loss)


def solution(mesh):
    in_specs = (
        P(("row", "col"), None),
        P(("row", "col"), None, None, None),
        P(("row", "col"), None),
        P(("row", "col")),
        P(("row", "col"), None),
        P(("row", "col"), None),
        P(("row", "col"), None),
        P(("row", "col"), None),
    )
    out_specs = (P(("row", "col"), None), P(("row", "col")))
    return jax.shard_map(
        per_device, mesh=mesh, in_specs=in_specs, out_specs=out_specs, check_vma=False
    )
```

time: 405 us -> 392 us (0.968)
  blocking collectives: 221 us -> 20.4 us
  starting transfers between devices: 37.7 us -> 158 us
  waiting for transfers between devices: 80.9 us -> 176 us
  between operations: 16.7 us -> 4.47 us
  other arithmetic: 10.8 us -> 5.32 us
  Pallas kernels: 23.8 us -> 19.1 us
    all_to_all x8 -> x1, blocking collectives: 221 us -> 20.4 us  [exchange_y(): lax.all_to_all(values, 'col', split_axis=0, concat_axis=0, tiled=True, ax...]
    ppermute x7 -> x37, starting transfers between devices: 19.5 us -> 144 us  [the longest x14 69.6 us: send_z(): return lax.ppermute(values, 'row', pairs)]
    ppermute x7 -> x37, waiting for transfers between devices: 36 us -> 149 us  [the longest x15 77.2 us: send_x(): return lax.ppermute(values, 'row', pairs)]
    all_to_all x2 -> x3, waiting for transfers between devices: 43.8 us -> 27.1 us  [exchange_y(): lax.all_to_all(values, 'col', split_axis=0, concat_axis=0, tiled=True, ax...]
    reduce_sum x5 -> x3, other arithmetic: 7.99 us -> 0.19 us  [the longest x1 0.13 us: per_device(): jnp.sum(user_rows * item_rows, axis=-1)]
    pallas_call x2, Pallas kernels: 23.8 us -> 19.1 us  [call_kernel(): pl.pallas_call(body, out_shape=[jax.ShapeDtypeStruct((n, BLOCK, HALF), jn...]
    all_to_all x2 -> x3, starting transfers between devices: 18.2 us -> 14 us  [exchange_y(): lax.all_to_all(values, 'col', split_axis=0, concat_axis=0, tiled=True, ax...]
  transfers between devices with their start and end apart: 10 -> 40, of which waited for: 6 -> 23; matrix products, arithmetic and copies ran while one was open for 1% -> 1% of each run, Pallas kernels for 0% -> 0%
where the time goes in v2:
time: 392 us; the launch traced here: 391 us
  waiting for transfers between devices  176 us (45%)
  starting transfers between devices  158 us (40%)
  blocking collectives  20.4 us (5%)
  Pallas kernels  19.1 us (5%)
  local copies, waits for them, and re-layouts  7.01 us (2%)
  other arithmetic  5.32 us (1%)
  between operations  4.47 us (1%)
    ppermute x15, waiting for transfers between devices, send_x(): return lax.ppermute(values, 'row', pairs)  77.2 us
    ppermute x14, starting transfers between devices, send_z(): return lax.ppermute(values, 'row', pairs)  69.6 us
    ppermute x14, waiting for transfers between devices, send_z(): return lax.ppermute(values, 'row', pairs)  69 us
    ppermute x15, starting transfers between devices, send_x(): return lax.ppermute(values, 'row', pairs)  42.4 us
    ppermute x8, starting transfers between devices, swap_cores(): return lax.ppermute(values, 'col', CORE_SWAP)  31.9 us
    all_to_all x3, waiting for transfers between devices, exchange_y(): lax.all_to_all(values, 'col', split_axis=0, concat_axis=0, tiled=True, ax...  27.1 us
    all_to_all x1, blocking collectives, exchange_y(): lax.all_to_all(values, 'col', split_axis=0, concat_axis=0, tiled=True, ax...  20.4 us
    pallas_call x2, Pallas kernels, call_kernel(): pl.pallas_call(body, out_shape=[jax.ShapeDtypeStruct((n, BLOCK, HALF), jn...  19.1 us
  transfers between devices with their start and end apart: 40, of which 23 were waited for; matrix products, arithmetic and copies ran while one was open for 1% of the time, Pallas kernels for 0%

profile of v2, /device:TPU:1, one launch (start us, length us, event | category | flops | bytes accessed | tf_op | source)
XLA Modules:
  0.0 390.8 jit_solution(12716983709639524528)
XLA Ops:
  3.3 5.2 %collective-permute-start.7 = (f32[2056,128]{1,0:T(8,128)S(1)}, f32[2056,128]{1,0:T(8,128)}, u32[]{:S(2)}, u32[]{:S(2)}) collective-permute-start(f32[2056,128]{1,0:T(8,128)S(1)} %select_maximum_fusion.refs_0_), channel_id=1, source_target_pairs={{0,768},{16,784},{32,800},{48,816},{64,832},{80,848},{96,864},{112... | collective-permute-start | bytes 3158024 | tf_op jit(solution)/shard_map/ppermute | solution.py:29
  8.5 2.4 collective-permute-start.5
  10.9 2.5 collective-permute-start.3
  13.5 13.7 %collective-permute-start.1 = (f32[128,128]{1,0:T(8,128)S(1)}, f32[128,128]{1,0:T(8,128)S(1)}, u32[]{:S(2)}, u32[]{:S(2)}) collective-permute-start(f32[128,128]{1,0:T(8,128)S(1)} %slice_select_fusion), channel_id=1, source_target_pairs={{0,1},{1,0},{2,3},{3,2},{4,5},{5,4},{6,7},{7,6},{8,9},{9,8},{10,11... | collective-permute-start | bytes 196616 | tf_op jit(solution)/shard_map/ppermute | solution.py:38
  28.1 7.7 %collective-permute-start.9 = (f32[2,128,128]{2,1,0:T(8,128)S(1)}, f32[2,128,128]{2,1,0:T(8,128)S(1)}, u32[]{:S(2)}, u32[]{:S(2)}) collective-permute-start(f32[2,128,128]{2,1,0:T(8,128)S(1)} %pad_maximum_fusion.2), channel_id=1, source_target_pairs={{0,192},{16,208},{32,224},{48,240},{64,0},{80,16},{96,32},{112,48}... | collective-permute-start | bytes 393224 | tf_op jit(solution)/shard_map/ppermute | solution.py:34
  35.8 3.1 collective-permute-start.10
  38.9 3.8 collective-permute-done.9
  42.7 2.5 collective-permute-start.2
  45.2 11.2 %collective-permute-done.10 = f32[2,128,128]{2,1,0:T(8,128)S(1)} collective-permute-done((f32[2,128,128]{2,1,0:T(8,128)S(1)}, f32[2,128,128]{2,1,0:T(8,128)S(1)}, u32[]{:S(2)}, u32[]{:S(2)}) %collective-permute-start.10) | collective-permute-done | bytes 131104 | tf_op jit(solution)/shard_map/ppermute | solution.py:34
  58.4 3.4 collective-permute-start.8
  61.8 4.3 %collective-permute-done.11 = f32[2,128,128]{2,1,0:T(8,128)S(1)} collective-permute-done((f32[2,128,128]{2,1,0:T(8,128)S(1)}, f32[2,128,128]{2,1,0:T(8,128)S(1)}, u32[]{:S(2)}, u32[]{:S(2)}) %collective-permute-start.11) | collective-permute-done | bytes 131104 | tf_op jit(solution)/shard_map/ppermute | solution.py:34
  66.2 8.2 %collective-permute-start.12 = (f32[8,128,128]{2,1,0:T(8,128)S(1)}, f32[8,128,128]{2,1,0:T(8,128)S(1)}, u32[]{:S(2)}, u32[]{:S(2)}) collective-permute-start(f32[8,128,128]{2,1,0:T(8,128)S(1)} %constant_dynamic-update-slice_fusion.refs_8_), channel_id=1, source_target_pairs={{0,240},{16,0},{32,16},{48,32},{64,48},{80,64},{96,80},{112,96},{1... | collective-permute-start | bytes 1572872 | tf_op jit(solution)/shard_map/ppermute | solution.py:34
  80.9 7.2 %collective-permute-start.13 = (f32[8,128,128]{2,1,0:T(8,128)S(1)}, f32[8,128,128]{2,1,0:T(8,128)}, u32[]{:S(2)}, u32[]{:S(2)}) collective-permute-start(f32[8,128,128]{2,1,0:T(8,128)S(1)} %constant_dynamic-update-slice_fusion.refs_8_), channel_id=1, source_target_pairs={{0,16},{16,32},{32,48},{48,64},{64,80},{80,96},{96,112},{112,128},... | collective-permute-start | bytes 1572872 | tf_op jit(solution)/shard_map/ppermute | solution.py:34
  88.1 3.0 collective-permute-start.14
  91.2 3.2 collective-permute-start.15
  95.5 7.1 %collective-permute-done.14.refs_11_ = f32[4,128,128]{2,1,0:T(8,128)S(1)} collective-permute-done((f32[4,128,128]{2,1,0:T(8,128)S(1)}, f32[4,128,128]{2,1,0:T(8,128)S(1)}, u32[]{:S(2)}, u32[]{:S(2)}) %collective-permute-start.14) | collective-permute-done | bytes 262176 | tf_op jit(solution)/shard_map/ppermute | solution.py:34
  102.6 9.2 %collective-permute-done.15.refs_12_ = f32[4,128,128]{2,1,0:T(8,128)S(1)} collective-permute-done((f32[4,128,128]{2,1,0:T(8,128)S(1)}, f32[4,128,128]{2,1,0:T(8,128)S(1)}, u32[]{:S(2)}, u32[]{:S(2)}) %collective-permute-start.15) | collective-permute-done | bytes 262176 | tf_op jit(solution)/shard_map/ppermute | solution.py:34
  111.8 9.3 %shard_map.95 = (f32[8,128,128]{2,1,0:T(8,128)S(1)}, f32[8,128,128]{2,1,0:T(8,128)S(1)}, f32[8,128,128]{2,1,0:T(8,128)S(1)}, f32[8,128,128]{2,1,0:T(8,128)S(1)},...) custom-call(s32[2]{0:T(128)S(1)} %pad_add_fusion.2.place_ref, ...), custom_call_target="tpu_custom_call" | custom-call | tf_op jit(solution)/shard_map/pallas_call | solution.py:128
  121.9 5.5 %collective-permute-start.19 = (f32[8,128,128]{2,1,0:T(8,128)S(1)}, f32[8,128,128]{2,1,0:T(8,128)S(1)}, u32[]{:S(2)}, u32[]{:S(2)}) collective-permute-start(f32[8,128,128]{2,1,0:T(8,128)S(1)} %get-tuple-element.20), channel_id=1, source_target_pairs={{0,768},{16,784},{32,800},{48,816},{64,832},{80,848},{96,864},{112... | collective-permute-start | bytes 1572872 | tf_op jit(solution)/shard_map/ppermute | solution.py:29
  129.7 2.8 collective-permute-start.21
  132.4 5.6 %collective-permute-done.19 = f32[8,128,128]{2,1,0:T(8,128)S(1)} collective-permute-done((f32[8,128,128]{2,1,0:T(8,128)S(1)}, f32[8,128,128]{2,1,0:T(8,128)S(1)}, u32[]{:S(2)}, u32[]{:S(2)}) %collective-permute-start.19) | collective-permute-done | bytes 524320 | tf_op jit(solution)/shard_map/ppermute | solution.py:29
  138.0 4.7 %collective-permute-done.20 = f32[8,128,128]{2,1,0:T(8,128)S(1)} collective-permute-done((f32[8,128,128]{2,1,0:T(8,128)S(1)}, f32[8,128,128]{2,1,0:T(8,128)S(1)}, u32[]{:S(2)}, u32[]{:S(2)}) %collective-permute-start.20) | collective-permute-done | bytes 524320 | tf_op jit(solution)/shard_map/ppermute | solution.py:29
  142.7 13.2 %collective-permute-done.21 = f32[8,128,128]{2,1,0:T(8,128)S(1)} collective-permute-done((f32[8,128,128]{2,1,0:T(8,128)S(1)}, f32[8,128,128]{2,1,0:T(8,128)S(1)}, u32[]{:S(2)}, u32[]{:S(2)}) %collective-permute-start.21) | collective-permute-done | bytes 524320 | tf_op jit(solution)/shard_map/ppermute | solution.py:29
  156.9 3.7 all-to-all-start.1
  164.8 3.1 collective-permute-start.18
  167.8 7.3 %collective-permute-done.16 = f32[8,128,128]{2,1,0:T(8,128)S(1)} collective-permute-done((f32[8,128,128]{2,1,0:T(8,128)S(1)}, f32[8,128,128]{2,1,0:T(8,128)S(1)}, u32[]{:S(2)}, u32[]{:S(2)}) %collective-permute-start.16) | collective-permute-done | bytes 524320 | tf_op jit(solution)/shard_map/ppermute | solution.py:29
  175.2 2.8 collective-permute-done.17
  178.0 13.0 %collective-permute-done.18 = f32[8,128,128]{2,1,0:T(8,128)S(1)} collective-permute-done((f32[8,128,128]{2,1,0:T(8,128)S(1)}, f32[8,128,128]{2,1,0:T(8,128)S(1)}, u32[]{:S(2)}, u32[]{:S(2)}) %collective-permute-start.18) | collective-permute-done | bytes 524320 | tf_op jit(solution)/shard_map/ppermute | solution.py:29
  191.9 6.8 %all-to-all-start = ((f32[8,128,128]{2,1,0:T(8,128)}), f32[8,128,128]{2,1,0:T(8,128)S(1)}, u32[]{:S(2)}, u32[]{:S(2)}) async-start(f32[8,128,128]{2,1,0:T(8,128)} %add_add_fusion.1), calls=%async_computation | async-start | bytes 1048576 | tf_op jit(solution)/shard_map/all_to_all | solution.py:42
  199.6 2.7 collective-permute-start
  203.1 13.5 %all-to-all-done = f32[8,128,128]{2,1,0:T(8,128)S(1)} async-done(((f32[8,128,128]{2,1,0:T(8,128)}), f32[8,128,128]{2,1,0:T(8,128)S(1)}, u32[]{:S(2)}, u32[]{:S(2)}) %all-to-all-start) | async-done | bytes 524320 | tf_op jit(solution)/shard_map/all_to_all | solution.py:42
  221.3 20.4 %all_to_all.20.refs_8_ = f32[8,128,128]{2,1,0:T(8,128)S(1)} all-to-all(f32[8,128,128]{2,1,0:T(8,128)S(1)} %broadcast_in_dim.30), channel_id=1, replica_groups={{0,2,4,6,8,10,12,14},{1,3,5,7,9,11,13,15},{16,18,20,22,24,26,28,30},{17..., dimensions={0} | all-to-all | bytes 1048576 | tf_op jit(solution)/shard_map/all_to_all | solution.py:42
  242.5 3.5 all-to-all-start.3
  250.3 13.6 %all-to-all-done.3.refs_9_ = f32[8,128,128]{2,1,0:T(8,128)S(1)} async-done(((f32[8,128,128]{2,1,0:T(8,128)}), f32[8,128,128]{2,1,0:T(8,128)S(1)}, u32[]{:S(2)}, u32[]{:S(2)}) %all-to-all-start.3) | async-done | bytes 524320 | tf_op jit(solution)/shard_map/all_to_all | solution.py:42
  268.1 4.1 %collective-permute-start.27 = (f32[8,128,128]{2,1,0:T(8,128)S(1)}, f32[8,128,128]{2,1,0:T(8,128)S(1)}, u32[]{:S(2)}, u32[]{:S(2)}) collective-permute-start(f32[8,128,128]{2,1,0:T(8,128)S(1)} %all_to_all.20.refs_8_), channel_id=1, source_target_pairs={{0,768},{16,784},{32,800},{48,816},{64,832},{80,848},{96,864},{112... | collective-permute-start | bytes 1572872 | tf_op jit(solution)/shard_map/ppermute | solution.py:29
  275.3 20.6 %collective-permute-done.24.refs_11_ = f32[8,128,128]{2,1,0:T(8,128)S(1)} collective-permute-done((f32[8,128,128]{2,1,0:T(8,128)S(1)}, f32[8,128,128]{2,1,0:T(8,128)S(1)}, u32[]{:S(2)}, u32[]{:S(2)}) %collective-permute-start.24) | collective-permute-done | bytes 524320 | tf_op jit(solution)/shard_map/ppermute | solution.py:29
  295.8 8.9 %collective-permute-done.28.refs_15_ = f32[8,128,128]{2,1,0:T(8,128)S(1)} collective-permute-done((f32[8,128,128]{2,1,0:T(8,128)S(1)}, f32[8,128,128]{2,1,0:T(8,128)S(1)}, u32[]{:S(2)}, u32[]{:S(2)}) %collective-permute-start.28) | collective-permute-done | bytes 524320 | tf_op jit(solution)/shard_map/ppermute | solution.py:29
  305.5 9.8 %shard_map.96 = (f32[8,128,128]{2,1,0:T(8,128)S(1)}, f32[8,128,128]{2,1,0:T(8,128)S(1)}, f32[8,128,128]{2,1,0:T(8,128)S(1)}, f32[4,128,128]{2,1,0:T(8,128)S(1)}, f32[4,128,128]{2,1,0:T(8,128)S(1)}) custom-call(s32[2]{0:T(128)S(1)} %pad_add_fusion.2.place_ref, s32[128]{0:T(128)S(1)} %convert_element_type.15.ids_ref, f32[2056,128]{1,0:T(8,128)} %copy-done.3, ...), custom_call_target="tpu_custom_call" | custom-call | tf_op jit(solution)/shard_map/pallas_call | solution.py:128
  315.3 10.8 %collective-permute-start.29 = (f32[8,128,128]{2,1,0:T(8,128)S(1)}, f32[8,128,128]{2,1,0:T(8,128)S(1)}, u32[]{:S(2)}, u32[]{:S(2)}) collective-permute-start(f32[8,128,128]{2,1,0:T(8,128)S(1)} %get-tuple-element.24), channel_id=1, source_target_pairs={{0,16},{16,32},{32,48},{48,64},{64,80},{80,96},{96,112},{112,128},... | collective-permute-start | bytes 1572872 | tf_op jit(solution)/shard_map/ppermute | solution.py:34
  328.1 3.1 collective-permute-start.31
  331.2 4.3 %collective-permute-start.32 = (f32[4,128,128]{2,1,0:T(8,128)S(1)}, f32[4,128,128]{2,1,0:T(8,128)S(1)}, u32[]{:S(2)}, u32[]{:S(2)}) collective-permute-start(f32[4,128,128]{2,1,0:T(8,128)S(1)} %get-tuple-element.27), channel_id=1, source_target_pairs={{0,224},{16,240},{32,0},{48,16},{64,32},{80,48},{96,64},{112,80},{... | collective-permute-start | bytes 786440 | tf_op jit(solution)/shard_map/ppermute | solution.py:34
  335.5 11.5 %collective-permute-done.31 = f32[4,128,128]{2,1,0:T(8,128)S(1)} collective-permute-done((f32[4,128,128]{2,1,0:T(8,128)S(1)}, f32[4,128,128]{2,1,0:T(8,128)S(1)}, u32[]{:S(2)}, u32[]{:S(2)}) %collective-permute-start.31) | collective-permute-done | bytes 262176 | tf_op jit(solution)/shard_map/ppermute | solution.py:34
  347.0 3.9 collective-permute-done.32
  352.9 7.3 %collective-permute-start.34 = (f32[2,128,128]{2,1,0:T(8,128)S(1)}, f32[2,128,128]{2,1,0:T(8,128)S(1)}, u32[]{:S(2)}, u32[]{:S(2)}) collective-permute-start(f32[2,128,128]{2,1,0:T(8,128)S(1)} %get-tuple-element.38), channel_id=1, source_target_pairs={{0,192},{16,208},{32,224},{48,240},{64,0},{80,16},{96,32},{112,48}... | collective-permute-start | bytes 393224 | tf_op jit(solution)/shard_map/ppermute | solution.py:34
  360.2 6.0 %collective-permute-start.35 = (f32[2,128,128]{2,1,0:T(8,128)S(1)}, f32[2,128,128]{2,1,0:T(8,128)S(1)}, u32[]{:S(2)}, u32[]{:S(2)}) collective-permute-start(f32[2,128,128]{2,1,0:T(8,128)S(1)} %get-tuple-element.37), channel_id=1, source_target_pairs={{0,128},{16,144},{32,160},{48,176},{64,192},{80,208},{96,224},{112... | collective-permute-start | bytes 393224 | tf_op jit(solution)/shard_map/ppermute | solution.py:34
  366.2 5.6 %collective-permute-done.34 = f32[2,128,128]{2,1,0:T(8,128)S(1)} collective-permute-done((f32[2,128,128]{2,1,0:T(8,128)S(1)}, f32[2,128,128]{2,1,0:T(8,128)S(1)}, u32[]{:S(2)}, u32[]{:S(2)}) %collective-permute-start.34) | collective-permute-done | bytes 131104 | tf_op jit(solution)/shard_map/ppermute | solution.py:34
  371.8 12.3 %collective-permute-done.35 = f32[2,128,128]{2,1,0:T(8,128)S(1)} collective-permute-done((f32[2,128,128]{2,1,0:T(8,128)S(1)}, f32[2,128,128]{2,1,0:T(8,128)S(1)}, u32[]{:S(2)}, u32[]{:S(2)}) %collective-permute-start.35) | collective-permute-done | bytes 131104 | tf_op jit(solution)/shard_map/ppermute | solution.py:34
  384.2 2.9 collective-permute-start.36
  (112 shorter events, 45.8 us)
Async XLA Ops:
  1.9 11.5 %copy-start.9 = (f32[128,256]{1,0:T(8,128)S(1)}, f32[128,256]{1,0:T(8,128)}, u32[]{:S(2)}) copy-start(f32[128,256]{1,0:T(8,128)} %param.8) | copy-start | bytes 393220
  1.9 25.3 %copy-start.12 = (s32[1,16]{1,0:T(1,128)S(1)}, s32[1,16]{1,0:T(1,128)}, u32[]{:S(2)}) copy-start(s32[1,16]{1,0:T(1,128)} %param.10) | copy-start | bytes 196
  3.3 71.2 %copy-start.3 = (f32[2056,128]{1,0:T(8,128)}, f32[2056,128]{1,0:T(8,128)S(1)}, u32[]{:S(2)}) copy-start(f32[2056,128]{1,0:T(8,128)S(1)} %select_maximum_fusion.refs_0_) | copy-start | bytes 3158020
  3.3 55.1 %collective-permute-start.7 = (f32[2056,128]{1,0:T(8,128)S(1)}, f32[2056,128]{1,0:T(8,128)}, u32[]{:S(2)}, u32[]{:S(2)}) collective-permute-start(f32[2056,128]{1,0:T(8,128)S(1)} %select_maximum_fusion.refs_0_), channel_id=1, source_target_pairs={{0,768},{16,784},{32,800},{48,816},{64,832},{80,848},{96,864},{112... | collective-permute-start | bytes 3158024 | tf_op jit(solution)/shard_map/ppermute | solution.py:29
  8.5 66.0 %collective-permute-start.5 = (f32[2056,128]{1,0:T(8,128)S(1)}, f32[2056,128]{1,0:T(8,128)}, u32[]{:S(2)}, u32[]{:S(2)}) collective-permute-start(f32[2056,128]{1,0:T(8,128)S(1)} %select_maximum_fusion.refs_0_), channel_id=1, source_target_pairs={{0,512},{16,528},{32,544},{48,560},{64,576},{80,592},{96,608},{112... | collective-permute-start | bytes 3158024 | tf_op jit(solution)/shard_map/ppermute | solution.py:29
  10.9 65.8 %collective-permute-start.3 = (f32[2056,128]{1,0:T(8,128)S(1)}, f32[2056,128]{1,0:T(8,128)}, u32[]{:S(2)}, u32[]{:S(2)}) collective-permute-start(f32[2056,128]{1,0:T(8,128)S(1)} %select_maximum_fusion.refs_0_), channel_id=1, source_target_pairs={{0,256},{16,272},{32,288},{48,304},{64,320},{80,336},{96,352},{112... | collective-permute-start | bytes 3158024 | tf_op jit(solution)/shard_map/ppermute | solution.py:29
  13.5 14.6 %collective-permute-start.1 = (f32[128,128]{1,0:T(8,128)S(1)}, f32[128,128]{1,0:T(8,128)S(1)}, u32[]{:S(2)}, u32[]{:S(2)}) collective-permute-start(f32[128,128]{1,0:T(8,128)S(1)} %slice_select_fusion), channel_id=1, source_target_pairs={{0,1},{1,0},{2,3},{3,2},{4,5},{5,4},{6,7},{7,6},{8,9},{9,8},{10,11... | collective-permute-start | bytes 196616 | tf_op jit(solution)/shard_map/ppermute | solution.py:38
  28.1 14.6 %collective-permute-start.9 = (f32[2,128,128]{2,1,0:T(8,128)S(1)}, f32[2,128,128]{2,1,0:T(8,128)S(1)}, u32[]{:S(2)}, u32[]{:S(2)}) collective-permute-start(f32[2,128,128]{2,1,0:T(8,128)S(1)} %pad_maximum_fusion.2), channel_id=1, source_target_pairs={{0,192},{16,208},{32,224},{48,240},{64,0},{80,16},{96,32},{112,48}... | collective-permute-start | bytes 393224 | tf_op jit(solution)/shard_map/ppermute | solution.py:34
  35.8 20.7 %collective-permute-start.10 = (f32[2,128,128]{2,1,0:T(8,128)S(1)}, f32[2,128,128]{2,1,0:T(8,128)S(1)}, u32[]{:S(2)}, u32[]{:S(2)}) collective-permute-start(f32[2,128,128]{2,1,0:T(8,128)S(1)} %pad_maximum_fusion.2), channel_id=1, source_target_pairs={{0,128},{16,144},{32,160},{48,176},{64,192},{80,208},{96,224},{112... | collective-permute-start | bytes 393224 | tf_op jit(solution)/shard_map/ppermute | solution.py:34
  42.7 38.2 %collective-permute-start.2 = (f32[2056,128]{1,0:T(8,128)S(1)}, f32[2056,128]{1,0:T(8,128)S(1)}, u32[]{:S(2)}, u32[]{:S(2)}) collective-permute-start(f32[2056,128]{1,0:T(8,128)S(1)} %select_maximum_fusion.refs_0_), channel_id=1, source_target_pairs={{0,1},{1,0},{2,3},{3,2},{4,5},{5,4},{6,7},{7,6},{8,9},{9,8},{10,11... | collective-permute-start | bytes 3158024 | tf_op jit(solution)/shard_map/ppermute | solution.py:38
  56.5 9.7 %collective-permute-start.11 = (f32[2,128,128]{2,1,0:T(8,128)S(1)}, f32[2,128,128]{2,1,0:T(8,128)S(1)}, u32[]{:S(2)}, u32[]{:S(2)}) collective-permute-start(f32[2,128,128]{2,1,0:T(8,128)S(1)} %pad_maximum_fusion.2), channel_id=1, source_target_pairs={{0,64},{16,80},{32,96},{48,112},{64,128},{80,144},{96,160},{112,17... | collective-permute-start | bytes 393224 | tf_op jit(solution)/shard_map/ppermute | solution.py:34
  58.4 29.7 %collective-permute-start.8 = (f32[2056,128]{1,0:T(8,128)}, f32[2056,128]{1,0:T(8,128)S(1)}, u32[]{:S(2)}, u32[]{:S(2)}) collective-permute-start(f32[2056,128]{1,0:T(8,128)} %collective-permute-done.7.refs_6_), channel_id=1, source_target_pairs={{0,1},{1,0},{2,3},{3,2},{4,5},{5,4},{6,7},{7,6},{8,9},{9,8},{10,11... | collective-permute-start | bytes 3158024 | tf_op jit(solution)/shard_map/ppermute | solution.py:38
  66.2 45.6 %collective-permute-start.12 = (f32[8,128,128]{2,1,0:T(8,128)S(1)}, f32[8,128,128]{2,1,0:T(8,128)S(1)}, u32[]{:S(2)}, u32[]{:S(2)}) collective-permute-start(f32[8,128,128]{2,1,0:T(8,128)S(1)} %constant_dynamic-update-slice_fusion.refs_8_), channel_id=1, source_target_pairs={{0,240},{16,0},{32,16},{48,32},{64,48},{80,64},{96,80},{112,96},{1... | collective-permute-start | bytes 1572872 | tf_op jit(solution)/shard_map/ppermute | solution.py:34
  74.5 16.7 %collective-permute-start.6 = (f32[2056,128]{1,0:T(8,128)}, f32[2056,128]{1,0:T(8,128)S(1)}, u32[]{:S(2)}, u32[]{:S(2)}) collective-permute-start(f32[2056,128]{1,0:T(8,128)} %collective-permute-done.5.refs_4_), channel_id=1, source_target_pairs={{0,1},{1,0},{2,3},{3,2},{4,5},{5,4},{6,7},{7,6},{8,9},{9,8},{10,11... | collective-permute-start | bytes 3158024 | tf_op jit(solution)/shard_map/ppermute | solution.py:38
  76.7 17.7 %collective-permute-start.4 = (f32[2056,128]{1,0:T(8,128)}, f32[2056,128]{1,0:T(8,128)S(1)}, u32[]{:S(2)}, u32[]{:S(2)}) collective-permute-start(f32[2056,128]{1,0:T(8,128)} %collective-permute-done.3.refs_2_), channel_id=1, source_target_pairs={{0,1},{1,0},{2,3},{3,2},{4,5},{5,4},{6,7},{7,6},{8,9},{9,8},{10,11... | collective-permute-start | bytes 3158024 | tf_op jit(solution)/shard_map/ppermute | solution.py:38
  80.9 10.3 %copy-start.4 = (f32[2056,128]{1,0:T(8,128)}, f32[2056,128]{1,0:T(8,128)S(1)}, u32[]{:S(2)}) copy-start(f32[2056,128]{1,0:T(8,128)S(1)} %collective-permute-done.2.refs_1_) | copy-start | bytes 3158020
  80.9 30.9 %collective-permute-start.13 = (f32[8,128,128]{2,1,0:T(8,128)S(1)}, f32[8,128,128]{2,1,0:T(8,128)}, u32[]{:S(2)}, u32[]{:S(2)}) collective-permute-start(f32[8,128,128]{2,1,0:T(8,128)S(1)} %constant_dynamic-update-slice_fusion.refs_8_), channel_id=1, source_target_pairs={{0,16},{16,32},{32,48},{48,64},{64,80},{80,96},{96,112},{112,128},... | collective-permute-start | bytes 1572872 | tf_op jit(solution)/shard_map/ppermute | solution.py:34
  88.1 14.4 %collective-permute-start.14 = (f32[4,128,128]{2,1,0:T(8,128)S(1)}, f32[4,128,128]{2,1,0:T(8,128)S(1)}, u32[]{:S(2)}, u32[]{:S(2)}) collective-permute-start(f32[4,128,128]{2,1,0:T(8,128)S(1)} %get-tuple-element.50), channel_id=1, source_target_pairs={{0,224},{16,240},{32,0},{48,16},{64,32},{80,48},{96,64},{112,80},{... | collective-permute-start | bytes 786440 | tf_op jit(solution)/shard_map/ppermute | solution.py:34
  91.2 20.6 %collective-permute-start.15 = (f32[4,128,128]{2,1,0:T(8,128)S(1)}, f32[4,128,128]{2,1,0:T(8,128)S(1)}, u32[]{:S(2)}, u32[]{:S(2)}) collective-permute-start(f32[4,128,128]{2,1,0:T(8,128)S(1)} %get-tuple-element.49), channel_id=1, source_target_pairs={{0,32},{16,48},{32,64},{48,80},{64,96},{80,112},{96,128},{112,144}... | collective-permute-start | bytes 786440 | tf_op jit(solution)/shard_map/ppermute | solution.py:34
  121.9 16.1 %collective-permute-start.19 = (f32[8,128,128]{2,1,0:T(8,128)S(1)}, f32[8,128,128]{2,1,0:T(8,128)S(1)}, u32[]{:S(2)}, u32[]{:S(2)}) collective-permute-start(f32[8,128,128]{2,1,0:T(8,128)S(1)} %get-tuple-element.20), channel_id=1, source_target_pairs={{0,768},{16,784},{32,800},{48,816},{64,832},{80,848},{96,864},{112... | collective-permute-start | bytes 1572872 | tf_op jit(solution)/shard_map/ppermute | solution.py:29
  127.5 15.2 %collective-permute-start.20 = (f32[8,128,128]{2,1,0:T(8,128)S(1)}, f32[8,128,128]{2,1,0:T(8,128)S(1)}, u32[]{:S(2)}, u32[]{:S(2)}) collective-permute-start(f32[8,128,128]{2,1,0:T(8,128)S(1)} %get-tuple-element.21), channel_id=1, source_target_pairs={{0,512},{16,528},{32,544},{48,560},{64,576},{80,592},{96,608},{112... | collective-permute-start | bytes 1572872 | tf_op jit(solution)/shard_map/ppermute | solution.py:29
  129.7 26.3 %collective-permute-start.21 = (f32[8,128,128]{2,1,0:T(8,128)S(1)}, f32[8,128,128]{2,1,0:T(8,128)S(1)}, u32[]{:S(2)}, u32[]{:S(2)}) collective-permute-start(f32[8,128,128]{2,1,0:T(8,128)S(1)} %get-tuple-element.22), channel_id=1, source_target_pairs={{0,256},{16,272},{32,288},{48,304},{64,320},{80,336},{96,352},{112... | collective-permute-start | bytes 1572872 | tf_op jit(solution)/shard_map/ppermute | solution.py:29
  156.9 35.1 %all-to-all-start.1 = ((f32[8,128,128]{2,1,0:T(8,128)}), f32[8,128,128]{2,1,0:T(8,128)S(1)}, u32[]{:S(2)}, u32[]{:S(2)}) async-start(f32[8,128,128]{2,1,0:T(8,128)} %add_add_fusion), calls=%async_computation.1 | async-start | bytes 1048576 | tf_op jit(solution)/shard_map/all_to_all | solution.py:42
  160.6 14.6 %collective-permute-start.16 = (f32[8,128,128]{2,1,0:T(8,128)S(1)}, f32[8,128,128]{2,1,0:T(8,128)S(1)}, u32[]{:S(2)}, u32[]{:S(2)}) collective-permute-start(f32[8,128,128]{2,1,0:T(8,128)S(1)} %copy-done.1), channel_id=1, source_target_pairs={{0,768},{16,784},{32,800},{48,816},{64,832},{80,848},{96,864},{112... | collective-permute-start | bytes 1572872 | tf_op jit(solution)/shard_map/ppermute | solution.py:29
  162.5 15.5 %collective-permute-start.17 = (f32[8,128,128]{2,1,0:T(8,128)S(1)}, f32[8,128,128]{2,1,0:T(8,128)S(1)}, u32[]{:S(2)}, u32[]{:S(2)}) collective-permute-start(f32[8,128,128]{2,1,0:T(8,128)S(1)} %get-tuple-element.17), channel_id=1, source_target_pairs={{0,512},{16,528},{32,544},{48,560},{64,576},{80,592},{96,608},{112... | collective-permute-start | bytes 1572872 | tf_op jit(solution)/shard_map/ppermute | solution.py:29
  164.8 26.3 %collective-permute-start.18 = (f32[8,128,128]{2,1,0:T(8,128)S(1)}, f32[8,128,128]{2,1,0:T(8,128)S(1)}, u32[]{:S(2)}, u32[]{:S(2)}) collective-permute-start(f32[8,128,128]{2,1,0:T(8,128)S(1)} %get-tuple-element.18), channel_id=1, source_target_pairs={{0,256},{16,272},{32,288},{48,304},{64,320},{80,336},{96,352},{112... | collective-permute-start | bytes 1572872 | tf_op jit(solution)/shard_map/ppermute | solution.py:29
  191.0 7.7 %copy-start.13 = (s32[1,64]{1,0:T(1,128)S(1)}, s32[1,64]{1,0:T(1,128)}, u32[]{:S(2)}) copy-start(s32[1,64]{1,0:T(1,128)} %param.14) | copy-start | bytes 772
  191.9 6.8 %copy-start.2 = (s32[1,64]{1,0:T(1,128)S(1)}, s32[1,64]{1,0:T(1,128)}, u32[]{:S(2)}) copy-start(s32[1,64]{1,0:T(1,128)} %param.13) | copy-start | bytes 772
  191.9 7.6 %copy-start.10 = (s32[1,64]{1,0:T(1,128)S(1)}, s32[1,64]{1,0:T(1,128)}, u32[]{:S(2)}) copy-start(s32[1,64]{1,0:T(1,128)} %param.15) | copy-start | bytes 772
  191.9 7.6 %copy-start.11 = (s32[1,64]{1,0:T(1,128)S(1)}, s32[1,64]{1,0:T(1,128)}, u32[]{:S(2)}) copy-start(s32[1,64]{1,0:T(1,128)} %param.12) | copy-start | bytes 772
  191.9 24.7 %all-to-all-start = ((f32[8,128,128]{2,1,0:T(8,128)}), f32[8,128,128]{2,1,0:T(8,128)S(1)}, u32[]{:S(2)}, u32[]{:S(2)}) async-start(f32[8,128,128]{2,1,0:T(8,128)} %add_add_fusion.1), calls=%async_computation | async-start | bytes 1048576 | tf_op jit(solution)/shard_map/all_to_all | solution.py:42
  199.6 3.5 collective-permute-start
  217.2 3.2 collective-permute-start.22
  242.5 21.4 %all-to-all-start.3 = ((f32[8,128,128]{2,1,0:T(8,128)}), f32[8,128,128]{2,1,0:T(8,128)S(1)}, u32[]{:S(2)}, u32[]{:S(2)}) async-start(f32[8,128,128]{2,1,0:T(8,128)} %broadcast_in_dim.31), calls=%async_computation.3 | async-start | bytes 1048576 | tf_op jit(solution)/shard_map/all_to_all | solution.py:42
  246.0 27.4 %collective-permute-start.23 = (f32[8,128,128]{2,1,0:T(8,128)S(1)}, f32[8,128,128]{2,1,0:T(8,128)S(1)}, u32[]{:S(2)}, u32[]{:S(2)}) collective-permute-start(f32[8,128,128]{2,1,0:T(8,128)S(1)} %all_to_all.20.refs_8_), channel_id=1, source_target_pairs={{0,256},{16,272},{32,288},{48,304},{64,320},{80,336},{96,352},{112... | collective-permute-start | bytes 1572872 | tf_op jit(solution)/shard_map/ppermute | solution.py:29
  247.9 47.9 %collective-permute-start.25 = (f32[8,128,128]{2,1,0:T(8,128)S(1)}, f32[8,128,128]{2,1,0:T(8,128)S(1)}, u32[]{:S(2)}, u32[]{:S(2)}) collective-permute-start(f32[8,128,128]{2,1,0:T(8,128)S(1)} %all_to_all.20.refs_8_), channel_id=1, source_target_pairs={{0,512},{16,528},{32,544},{48,560},{64,576},{80,592},{96,608},{112... | collective-permute-start | bytes 1572872 | tf_op jit(solution)/shard_map/ppermute | solution.py:29
  263.9 32.0 %collective-permute-start.24 = (f32[8,128,128]{2,1,0:T(8,128)S(1)}, f32[8,128,128]{2,1,0:T(8,128)S(1)}, u32[]{:S(2)}, u32[]{:S(2)}) collective-permute-start(f32[8,128,128]{2,1,0:T(8,128)S(1)} %all-to-all-done.3.refs_9_), channel_id=1, source_target_pairs={{0,256},{16,272},{32,288},{48,304},{64,320},{80,336},{96,352},{112... | collective-permute-start | bytes 1572872 | tf_op jit(solution)/shard_map/ppermute | solution.py:29
  265.8 30.0 %collective-permute-start.26 = (f32[8,128,128]{2,1,0:T(8,128)S(1)}, f32[8,128,128]{2,1,0:T(8,128)S(1)}, u32[]{:S(2)}, u32[]{:S(2)}) collective-permute-start(f32[8,128,128]{2,1,0:T(8,128)S(1)} %all-to-all-done.3.refs_9_), channel_id=1, source_target_pairs={{0,512},{16,528},{32,544},{48,560},{64,576},{80,592},{96,608},{112... | collective-permute-start | bytes 1572872 | tf_op jit(solution)/shard_map/ppermute | solution.py:29
  268.1 27.7 %collective-permute-start.27 = (f32[8,128,128]{2,1,0:T(8,128)S(1)}, f32[8,128,128]{2,1,0:T(8,128)S(1)}, u32[]{:S(2)}, u32[]{:S(2)}) collective-permute-start(f32[8,128,128]{2,1,0:T(8,128)S(1)} %all_to_all.20.refs_8_), channel_id=1, source_target_pairs={{0,768},{16,784},{32,800},{48,816},{64,832},{80,848},{96,864},{112... | collective-permute-start | bytes 1572872 | tf_op jit(solution)/shard_map/ppermute | solution.py:29
  273.4 31.4 %collective-permute-start.28 = (f32[8,128,128]{2,1,0:T(8,128)S(1)}, f32[8,128,128]{2,1,0:T(8,128)S(1)}, u32[]{:S(2)}, u32[]{:S(2)}) collective-permute-start(f32[8,128,128]{2,1,0:T(8,128)S(1)} %all-to-all-done.3.refs_9_), channel_id=1, source_target_pairs={{0,768},{16,784},{32,800},{48,816},{64,832},{80,848},{96,864},{112... | collective-permute-start | bytes 1572872 | tf_op jit(solution)/shard_map/ppermute | solution.py:29
  315.3 35.6 %collective-permute-start.29 = (f32[8,128,128]{2,1,0:T(8,128)S(1)}, f32[8,128,128]{2,1,0:T(8,128)S(1)}, u32[]{:S(2)}, u32[]{:S(2)}) collective-permute-start(f32[8,128,128]{2,1,0:T(8,128)S(1)} %get-tuple-element.24), channel_id=1, source_target_pairs={{0,16},{16,32},{32,48},{48,64},{64,80},{80,96},{96,112},{112,128},... | collective-permute-start | bytes 1572872 | tf_op jit(solution)/shard_map/ppermute | solution.py:34
  326.2 24.8 %collective-permute-start.30 = (f32[8,128,128]{2,1,0:T(8,128)S(1)}, f32[8,128,128]{2,1,0:T(8,128)S(1)}, u32[]{:S(2)}, u32[]{:S(2)}) collective-permute-start(f32[8,128,128]{2,1,0:T(8,128)S(1)} %get-tuple-element.25), channel_id=1, source_target_pairs={{0,240},{16,0},{32,16},{48,32},{64,48},{80,64},{96,80},{112,96},{1... | collective-permute-start | bytes 1572872 | tf_op jit(solution)/shard_map/ppermute | solution.py:34
  328.1 18.9 %collective-permute-start.31 = (f32[4,128,128]{2,1,0:T(8,128)S(1)}, f32[4,128,128]{2,1,0:T(8,128)S(1)}, u32[]{:S(2)}, u32[]{:S(2)}) collective-permute-start(f32[4,128,128]{2,1,0:T(8,128)S(1)} %get-tuple-element.26), channel_id=1, source_target_pairs={{0,32},{16,48},{32,64},{48,80},{64,96},{80,112},{96,128},{112,144}... | collective-permute-start | bytes 786440 | tf_op jit(solution)/shard_map/ppermute | solution.py:34
  331.2 19.7 %collective-permute-start.32 = (f32[4,128,128]{2,1,0:T(8,128)S(1)}, f32[4,128,128]{2,1,0:T(8,128)S(1)}, u32[]{:S(2)}, u32[]{:S(2)}) collective-permute-start(f32[4,128,128]{2,1,0:T(8,128)S(1)} %get-tuple-element.27), channel_id=1, source_target_pairs={{0,224},{16,240},{32,0},{48,16},{64,32},{80,48},{96,64},{112,80},{... | collective-permute-start | bytes 786440 | tf_op jit(solution)/shard_map/ppermute | solution.py:34
  351.0 15.2 %collective-permute-start.33 = (f32[2,128,128]{2,1,0:T(8,128)S(1)}, f32[2,128,128]{2,1,0:T(8,128)S(1)}, u32[]{:S(2)}, u32[]{:S(2)}) collective-permute-start(f32[2,128,128]{2,1,0:T(8,128)S(1)} %get-tuple-element.36), channel_id=1, source_target_pairs={{0,64},{16,80},{32,96},{48,112},{64,128},{80,144},{96,160},{112,17... | collective-permute-start | bytes 393224 | tf_op jit(solution)/shard_map/ppermute | solution.py:34
  352.9 18.9 %collective-permute-start.34 = (f32[2,128,128]{2,1,0:T(8,128)S(1)}, f32[2,128,128]{2,1,0:T(8,128)S(1)}, u32[]{:S(2)}, u32[]{:S(2)}) collective-permute-start(f32[2,128,128]{2,1,0:T(8,128)S(1)} %get-tuple-element.38), channel_id=1, source_target_pairs={{0,192},{16,208},{32,224},{48,240},{64,0},{80,16},{96,32},{112,48}... | collective-permute-start | bytes 393224 | tf_op jit(solution)/shard_map/ppermute | solution.py:34
  360.2 23.9 %collective-permute-start.35 = (f32[2,128,128]{2,1,0:T(8,128)S(1)}, f32[2,128,128]{2,1,0:T(8,128)S(1)}, u32[]{:S(2)}, u32[]{:S(2)}) collective-permute-start(f32[2,128,128]{2,1,0:T(8,128)S(1)} %get-tuple-element.37), channel_id=1, source_target_pairs={{0,128},{16,144},{32,160},{48,176},{64,192},{80,208},{96,224},{112... | collective-permute-start | bytes 393224 | tf_op jit(solution)/shard_map/ppermute | solution.py:34
  384.2 4.8 %collective-permute-start.36 = (f32[128,128]{1,0:T(8,128)S(1)}, f32[128,128]{1,0:T(8,128)S(1)}, u32[]{:S(2)}, u32[]{:S(2)}) collective-permute-start(f32[128,128]{1,0:T(8,128)S(1)} %get-tuple-element.44), channel_id=1, source_target_pairs={{0,1},{1,0},{2,3},{3,2},{4,5},{5,4},{6,7},{7,6},{8,9},{9,8},{10,11... | collective-permute-start | bytes 196616 | tf_op jit(solution)/shard_map/ppermute | solution.py:38
  (6 other events, 13.5 us)

commit v3 on v2

--- a/solution.py
+++ b/solution.py
@@ -1,5 +1,3 @@
-import functools
-
 import jax
 import jax.numpy as jnp
 from jax import lax
@@ -20,13 +18,10 @@
 
 precise = lax.Precision.HIGHEST
 
+X_GROUPS = [[x * NZ + z for x in range(NX)] for z in range(NZ)]
+Z_FAR = [[x * NZ + 4 * a + b for a in range(4)] for x in range(NX) for b in range(4)]
 Y_GROUPS = [[y * 2 + k for y in range(NY)] for k in range(2)]
 CORE_SWAP = [(i, i ^ 1) for i in range(2 * NY)]
-
-
-def send_x(values, step):
-    pairs = [(x * NZ + z, ((x + step) % NX) * NZ + z) for x in range(NX) for z in range(NZ)]
-    return lax.ppermute(values, "row", pairs)
 
 
 def send_z(values, step):
@@ -38,9 +33,9 @@
     return lax.ppermute(values, "col", CORE_SWAP)
 
 
-def exchange_y(values):
+def exchange(values, axis, groups):
     return lax.all_to_all(
-        values, "col", split_axis=0, concat_axis=0, tiled=True, axis_index_groups=Y_GROUPS
+        values, axis, split_axis=0, concat_axis=0, tiled=True, axis_index_groups=groups
     )
 
 
@@ -63,64 +58,63 @@
 
 def for_live_slots(place_ref, ids_ref, sources, body):
     own_x, own_z = place_ref[0], place_ref[1]
-    for number, source in enumerate(sources):
-        step, core = number // 2, number % 2
-
-        @pl.loop(0, SLOTS)
-        def _(slot):
-            position = ids_ref[number * SLOTS + slot]
+    for core, source in enumerate(sources):
+
+        @pl.loop(0, NX * SLOTS)
+        def _(number):
+            position = ids_ref[core * NX * SLOTS + number]
             column = jnp.bitwise_and(position, CB - 1)
             live = jnp.logical_and(position >= 0, column // NZ == own_x)
 
             @pl.when(live)
             def _():
-                near = jnp.bitwise_and(column - own_z, NZ - 1) * 2 + core
-                block = source[pl.ds(pl.multiple_of(slot * BLOCK, BLOCK), BLOCK), :]
+                z = jnp.bitwise_and(column, NZ - 1)
+                near = jnp.bitwise_and(z - own_z, 3) * 8 + (z // 4) * 2 + core
+                step = number // SLOTS
+                slot = jnp.bitwise_and(number, SLOTS - 1)
+                start = step * (SLOTS * BLOCK + HEAD) + slot * BLOCK
+                block = source[pl.ds(pl.multiple_of(start, 8), BLOCK), :]
                 body(step, block, position // CB, near)
 
 
-OWN = (0, 4, 8, 12)
-AFTER = (1, 5, 9, 13)
-BEFORE = (15, 3, 7, 11)
-TWO_AFTER = (2, 6)
-TWO_BEFORE = (14, 10)
-PARTS = (OWN, AFTER, BEFORE, TWO_AFTER, TWO_BEFORE)
-
-
-def forward_kernel(place_ref, ids_ref, *refs):
-    sources, parts = refs[: 2 * NX], refs[2 * NX : 2 * NX + len(PARTS)]
-    outs, rows_ref = refs[2 * NX + len(PARTS) : -1], refs[-1]
-    for out in outs:
+def forward_kernel(place_ref, ids_ref, source_ref, other_ref, own, after, two, two_far, before, *refs):
+    by_span, rows_ref = refs[:2], refs[2]
+    for out in by_span:
         out[...] = jnp.zeros_like(out)
-    for part, distances in zip(parts, PARTS):
-        for index, distance in enumerate(distances):
-            rows_ref[pl.ds(2 * distance, 2)] = part[pl.ds(2 * index, 2)]
+    start = 0
+    for part in (own, after, two, two_far, before):
+        rows_ref[pl.ds(start, part.shape[0])] = part[...]
+        start += part.shape[0]
 
     def body(step, block, rb, near):
         value = product(block, rows_ref[near], 1)
-        for half in range(2):
-
-            @pl.when(rb % 2 == half)
-            def _():
-                outs[2 * step + half][rb // 2] += value
-
-    for_live_slots(place_ref, ids_ref, sources, body)
-
-
-def backward_kernel(place_ref, ids_ref, *refs):
-    sources, slabs = refs[: 2 * NX], refs[2 * NX : 4 * NX]
-    outs, total_ref = refs[4 * NX : -1], refs[-1]
+
+        @pl.when(rb % 2 == 0)
+        def _():
+            by_span[0][(rb // 2) * NX + step] += value
+
+        @pl.when(rb % 2 == 1)
+        def _():
+            by_span[1][step * NY + rb // 2] += value
+
+    for_live_slots(place_ref, ids_ref, (source_ref, other_ref), body)
+
+
+def backward_kernel(place_ref, ids_ref, source_ref, other_ref, first, second, *refs):
+    outs, total_ref = refs[:-1], refs[-1]
     total_ref[...] = jnp.zeros_like(total_ref)
 
     def body(step, block, rb, near):
-        first, second = slabs[2 * step], slabs[2 * step + 1]
-        rows = jnp.where(rb % 2 == 0, first[rb // 2], second[rb // 2])
+        rows = jnp.where(
+            rb % 2 == 0, first[(rb // 2) * NX + step], second[step * NY + rb // 2]
+        )
         total_ref[near] += product(block, rows, 0)
 
-    for_live_slots(place_ref, ids_ref, sources, body)
-    for out, distances in zip(outs, PARTS):
-        for index, distance in enumerate(distances):
-            out[pl.ds(2 * index, 2)] = total_ref[pl.ds(2 * distance, 2)]
+    for_live_slots(place_ref, ids_ref, (source_ref, other_ref), body)
+    start = 0
+    for out in outs:
+        out[...] = total_ref[pl.ds(start, out.shape[0])]
+        start += out.shape[0]
 
 
 def call_kernel(body, place, ids, arrays, out_blocks):
@@ -149,34 +143,34 @@
     other_half = swap_cores(jnp.where(core == 0, right, left))
     pair = jnp.stack([own_half, other_half])
 
-    near_4 = jnp.concatenate([pair, send_z(pair, -4), send_z(pair, 8), send_z(pair, 4)])
-    ends_after = near_4[:4]
-    ends_before = jnp.concatenate([near_4[:2], near_4[6:]])
-
     live = jnp.arange(SLOTS, dtype=jnp.int32) < counts[0]
     marked = jnp.where(live, block_ids[0], -1).astype(jnp.float32)
     header = jnp.pad(marked[None, :], ((0, HEAD - 1), (0, BLOCK - SLOTS)))
     packed = jnp.concatenate([blocks.reshape(SLOTS * BLOCK, BLOCK), header], axis=0)
-    sources = []
-    for step in range(NX):
-        moved = packed if step == 0 else send_x(packed, step)
-        sources += [moved, swap_cores(moved)]
-    ids = jnp.concatenate([s[SLOTS * BLOCK, :SLOTS] for s in sources]).astype(jnp.int32)
-
-    parts = [
-        near_4,
-        send_z(near_4, -1),
-        send_z(near_4, 1),
-        send_z(ends_after, -2),
-        send_z(ends_before, 2),
-    ]
-    partial_rows = call_kernel(forward_kernel, place, ids, sources + parts, [NY] * (2 * NX))
-    current = []
-    for half in range(2):
-        summed = partial_rows[half]
-        for step in range(1, NX):
-            summed = summed + send_x(partial_rows[2 * step + half], -step)
-        current.append(jnp.sum(exchange_y(summed), axis=0))
+    source = lax.all_gather(packed, "row", axis=0, tiled=True, axis_index_groups=X_GROUPS)
+    other = swap_cores(source)
+    ids = jnp.concatenate(
+        [s.reshape(NX, -1, BLOCK)[:, SLOTS * BLOCK, :SLOTS].reshape(-1) for s in (source, other)]
+    ).astype(jnp.int32)
+
+    far = exchange(jnp.broadcast_to(pair[None], (4, 2, BLOCK, HALF)), "row", Z_FAR)
+    far = far.reshape(8, BLOCK, HALF)
+    parts = [far, send_z(far, -1), send_z(far[:4], -2), send_z(far[4:], 2), send_z(far, 1)]
+    first, second = call_kernel(
+        forward_kernel, place, ids, [source, other] + parts, [NX * NY] * 2
+    )
+
+    first = lax.psum_scatter(
+        first.reshape(NY * NX, BLOCK, HALF),
+        "col",
+        scatter_dimension=0,
+        tiled=True,
+        axis_index_groups=Y_GROUPS,
+    )
+    second = jnp.sum(exchange(second.reshape(NX, NY, BLOCK, HALF), "row", X_GROUPS), axis=0)
+    second = jnp.sum(exchange(second, "col", Y_GROUPS), axis=0)
+    first = jnp.sum(exchange(first, "row", X_GROUPS), axis=0)
+    current = [first, second]
 
     picks = jnp.stack([users[0], positives[0], jnp.take(positives[0], neg_index[0]), popular[0]])
     other_picks = swap_cores(picks)
@@ -218,24 +212,17 @@
     )
     scaled = jnp.einsum("hpij,hpid->hjd", hot, row_grads, precision=precise)
 
-    slabs = [None] * (2 * NX)
-    for half in range(2):
-        slab = exchange_y(jnp.broadcast_to(scaled[half][None], (NY, BLOCK, HALF)))
-        slabs[half] = slab
-        for step in range(1, NX):
-            slabs[2 * step + half] = send_x(slab, step)
-    own, after, before, two_after, two_before = call_kernel(
-        backward_kernel, place, ids, sources + slabs, [2 * len(p) for p in PARTS]
-    )
-    after = send_z(after, 1)
-    before = send_z(before, -1)
-    two_after = send_z(two_after, 2)
-    two_before = send_z(two_before, -2)
-    sums = [own[2 * m : 2 * m + 2] + after[2 * m : 2 * m + 2] + before[2 * m : 2 * m + 2] for m in range(4)]
-    sums[0] = sums[0] + two_after[:2] + two_before[:2]
-    sums[1] = sums[1] + two_after[2:]
-    sums[3] = sums[3] + two_before[2:]
-    returned = sums[0] + send_z(sums[1], 4) + send_z(sums[3], -4) + send_z(sums[2], 8)
+    first = exchange(jnp.broadcast_to(scaled[0][None], (NX, BLOCK, HALF)), "row", X_GROUPS)
+    first = lax.all_gather(first, "col", axis=0, tiled=True, axis_index_groups=Y_GROUPS)
+    second = exchange(jnp.broadcast_to(scaled[1][None], (NY, BLOCK, HALF)), "col", Y_GROUPS)
+    second = jnp.broadcast_to(second[None], (NX, NY, BLOCK, HALF))
+    second = exchange(second, "row", X_GROUPS).reshape(NX * NY, BLOCK, HALF)
+    own, after, two, two_far, before = call_kernel(
+        backward_kernel, place, ids, [source, other, first, second], [8, 8, 4, 4, 8]
+    )
+    two = jnp.concatenate([send_z(two, 2), send_z(two_far, -2)])
+    near = own + send_z(after, 1) + send_z(before, -1) + two
+    returned = jnp.sum(exchange(near.reshape(4, 2, BLOCK, HALF), "row", Z_FAR), axis=0)
 
     scaled_own = jnp.where(is_first, scaled[0], scaled[1])
     scaled_other = jnp.where(is_first, scaled[1], scaled[0])

time: 392 us -> 393 us (level)
  blocking collectives: 20.4 us -> 121 us
  starting transfers between devices: 158 us -> 83.7 us
  waiting for transfers between devices: 176 us -> 134 us
  between operations: 4.47 us -> 17.2 us
  Pallas kernels: 19.1 us -> 24.1 us
    all_to_all x1 -> x5, blocking collectives: 20.4 us -> 121 us  [exchange(): lax.all_to_all(values, axis, split_axis=0, concat_axis=0, tiled=True, axi...]
    ppermute x15 -> x0, waiting for transfers between devices: 77.2 us -> none  [send_x(): return lax.ppermute(values, 'row', pairs)]
    all_gather x0 -> x2, waiting for transfers between devices: none -> 67.8 us  [the longest x1 67.8 us: per_device(): lax.all_gather(packed, 'row', axis=0, tiled=True, axis_index_groups=X_GRO...]
    ppermute x14 -> x8, waiting for transfers between devices: 69 us -> 19.8 us  [send_z(): return lax.ppermute(values, 'row', pairs)]
    ppermute x15 -> x0, starting transfers between devices: 42.4 us -> none  [send_x(): return lax.ppermute(values, 'row', pairs)]
    ppermute x14 -> x8, starting transfers between devices: 69.6 us -> 33.6 us  [send_z(): return lax.ppermute(values, 'row', pairs)]
    all_to_all x3, waiting for transfers between devices: 27.1 us -> 37.4 us  [exchange(): lax.all_to_all(values, axis, split_axis=0, concat_axis=0, tiled=True, axi...]
    all_to_all x3, starting transfers between devices: 14 us -> 20 us  [exchange(): lax.all_to_all(values, axis, split_axis=0, concat_axis=0, tiled=True, axi...]
  transfers between devices with their start and end apart: 40 -> 19, of which waited for: 23 -> 11; matrix products, arithmetic and copies ran while one was open for 1% -> 1% of each run, Pallas kernels for 0% -> 0%
where the time goes in v3:
time: 393 us; the launch traced here: 392 us
  waiting for transfers between devices  134 us (34%)
  blocking collectives  121 us (31%)
  starting transfers between devices  83.7 us (21%)
  Pallas kernels  24.1 us (6%)
  between operations  17.2 us (4%)
  other arithmetic  6.22 us (2%)
  local copies, waits for them, and re-layouts  4.97 us (1%)
    all_to_all x5, blocking collectives, exchange(): lax.all_to_all(values, axis, split_axis=0, concat_axis=0, tiled=True, axi...  121 us
    all_gather x1, waiting for transfers between devices, per_device(): lax.all_gather(packed, 'row', axis=0, tiled=True, axis_index_groups=X_GRO...  67.8 us
    all_to_all x3, waiting for transfers between devices, exchange(): lax.all_to_all(values, axis, split_axis=0, concat_axis=0, tiled=True, axi...  37.4 us
    ppermute x8, starting transfers between devices, send_z(): return lax.ppermute(values, 'row', pairs)  33.6 us
    ppermute x5, starting transfers between devices, swap_cores(): return lax.ppermute(values, 'col', CORE_SWAP)  29.9 us
    pallas_call x2, Pallas kernels, call_kernel(): pl.pallas_call(body, out_shape=[jax.ShapeDtypeStruct((n, BLOCK, HALF), jn...  24.1 us
    all_to_all x3, starting transfers between devices, exchange(): lax.all_to_all(values, axis, split_axis=0, concat_axis=0, tiled=True, axi...  20 us
    ppermute x8, waiting for transfers between devices, send_z(): return lax.ppermute(values, 'row', pairs)  19.8 us
  transfers between devices with their start and end apart: 19, of which 11 were waited for; matrix products, arithmetic and copies ran while one was open for 1% of the time, Pallas kernels for 0%

profile of v3, /device:TPU:1, one launch (start us, length us, event | category | flops | bytes accessed | tf_op | source)
XLA Modules:
  0.0 392.3 jit_solution(9730327363780830637)
XLA Ops:
  7.9 0.7 fusion.18
  8.6 2.3 select_maximum_fusion
  10.9 67.8 %all-gather.3.cloned.1.call-done.source_ref = f32[8224,128]{1,0:T(8,128)} async-done(((f32[2056,128]{1,0:T(8,128)}), f32[8224,128]{1,0:T(8,128)}) %all-gather.3.cloned.1.call-update) | async-done | bytes 4210704 | tf_op jit(solution)/shard_map/all_gather | solution.py:150
  78.7 2.6 collective-permute-start.2
  81.3 1.9 collective-permute-start.1
  83.2 4.9 %collective-permute-done.1 = f32[128,128]{1,0:T(8,128)S(1)} collective-permute-done((f32[128,128]{1,0:T(8,128)S(1)}, f32[128,128]{1,0:T(8,128)S(1)}, u32[]{:S(2)}, u32[]{:S(2)}) %collective-permute-start.1) | collective-permute-done | bytes 65568 | tf_op jit(solution)/shard_map/ppermute | solution.py:33
  88.2 40.0 %all_to_all.40 = f32[4,2,128,128]{3,2,1,0:T(8,128)S(1)} all-to-all(f32[4,2,128,128]{3,2,1,0:T(8,128)S(1)} %broadcast_in_dim.20), channel_id=1, replica_groups={{0,64,128,192},{16,80,144,208},{32,96,160,224},{48,112,176,240},{256,32..., dimensions={0} | all-to-all | bytes 1048576 | tf_op jit(solution)/shard_map/all_to_all | solution.py:37
  128.2 1.9 collective-permute-start.3
  130.1 7.0 %collective-permute-start.6 = (f32[8,128,128]{2,1,0:T(8,128)S(1)}, f32[8,128,128]{2,1,0:T(8,128)S(1)}, u32[]{:S(2)}, u32[]{:S(2)}) collective-permute-start(f32[8,128,128]{2,1,0:T(8,128)S(1)} %bitcast.87), channel_id=1, source_target_pairs={{0,16},{16,32},{32,48},{48,64},{64,80},{80,96},{96,112},{112,128},... | collective-permute-start | bytes 1572872 | tf_op jit(solution)/shard_map/ppermute | solution.py:29
  137.2 2.2 collective-permute-start.4
  139.4 4.0 %collective-permute-start.5 = (f32[4,128,128]{2,1,0:T(8,128)S(1)}, f32[4,128,128]{2,1,0:T(8,128)S(1)}, u32[]{:S(2)}, u32[]{:S(2)}) collective-permute-start(f32[4,128,128]{2,1,0:T(8,128)S(1)} %bitcast.94), channel_id=1, source_target_pairs={{0,32},{16,48},{32,64},{48,80},{64,96},{80,112},{96,128},{112,144}... | collective-permute-start | bytes 786440 | tf_op jit(solution)/shard_map/ppermute | solution.py:29
  143.5 0.7 slice.91
  144.3 0.7 slice.92
  145.2 10.8 %collective-permute-done.4.two = f32[4,128,128]{2,1,0:T(8,128)S(1)} collective-permute-done((f32[4,128,128]{2,1,0:T(8,128)S(1)}, f32[4,128,128]{2,1,0:T(8,128)S(1)}, u32[]{:S(2)}, u32[]{:S(2)}) %collective-permute-start.4) | collective-permute-done | bytes 262176 | tf_op jit(solution)/shard_map/ppermute | solution.py:29
  156.0 0.3 collective-permute-done.5.two_far
  156.3 12.4 %shard_map.95 = (f32[32,128,128]{2,1,0:T(8,128)}, f32[32,128,128]{2,1,0:T(8,128)}) custom-call(s32[2]{0:T(128)S(1)} %pad_add_fusion.2.place_ref, s32[128]{0:T(128)S(1)} %maximum_convert_fusion.ids_ref, f32[8224,128]{1,0:T(8,128)} %all-gather.3.cloned.1.call-done.source_ref, f32[8224,128]{1,0:T(8,128)} %collective-permute-done.2.other_ref, ...), custom_call_target="tpu_custom_call" | custom-call | tf_op jit(solution)/shard_map/pallas_call | solution.py:122
  168.8 24.6 %all_to_all.41 = f32[4,8,128,128]{3,2,1,0:T(8,128)S(1)} all-to-all(f32[4,8,128,128]{3,2,1,0:T(8,128)} %bitcast.92), channel_id=1, replica_groups={{0,256,512,768},{16,272,528,784},{32,288,544,800},{48,304,560,816},{64,..., dimensions={0} | all-to-all | bytes 4194304 | tf_op jit(solution)/shard_map/all_to_all | solution.py:37
  193.4 1.0 reduce_sum.73
  194.3 6.3 %all-to-all-start.3 = ((f32[8,128,128]{2,1,0:T(8,128)}), f32[8,128,128]{2,1,0:T(8,128)S(1)}, u32[]{:S(2)}, u32[]{:S(2)}) async-start(f32[8,128,128]{2,1,0:T(8,128)} %reduce_sum.73), calls=%async_computation.4 | async-start | bytes 1048576 | tf_op jit(solution)/shard_map/all_to_all | solution.py:37
  200.7 0.8 gather_fusion
  201.5 8.3 %collective-permute-start = (s32[4,64]{1,0:T(4,128)S(1)}, s32[4,64]{1,0:T(4,128)S(1)}, u32[]{:S(2)}, u32[]{:S(2)}) collective-permute-start(s32[4,64]{1,0:T(4,128)S(1)} %pad_add_fusion.1), channel_id=1, source_target_pairs={{0,1},{1,0},{2,3},{3,2},{4,5},{5,4},{6,7},{7,6},{8,9},{9,8},{10,11... | collective-permute-start | bytes 3080 | tf_op jit(solution)/shard_map/ppermute | solution.py:33
  209.8 9.5 %all-to-all-done.3 = f32[8,128,128]{2,1,0:T(8,128)S(1)} async-done(((f32[8,128,128]{2,1,0:T(8,128)}), f32[8,128,128]{2,1,0:T(8,128)S(1)}, u32[]{:S(2)}, u32[]{:S(2)}) %all-to-all-start.3) | async-done | bytes 524320 | tf_op jit(solution)/shard_map/all_to_all | solution.py:37
  219.3 3.4 reduce-scatter.2.cloned.1.call-done
  222.8 4.1 %all-to-all-start.1 = ((f32[4,128,128]{2,1,0:T(8,128)}), f32[4,128,128]{2,1,0:T(8,128)S(1)}, u32[]{:S(2)}, u32[]{:S(2)}) async-start(f32[4,128,128]{2,1,0:T(8,128)} %reduce-scatter.2.cloned.1.call-done), calls=%async_computation.2 | async-start | bytes 524288 | tf_op jit(solution)/shard_map/all_to_all | solution.py:37
  226.9 5.5 %all-to-all-done.1 = f32[4,128,128]{2,1,0:T(8,128)S(1)} async-done(((f32[4,128,128]{2,1,0:T(8,128)}), f32[4,128,128]{2,1,0:T(8,128)S(1)}, u32[]{:S(2)}, u32[]{:S(2)}) %all-to-all-start.1) | async-done | bytes 262176 | tf_op jit(solution)/shard_map/all_to_all | solution.py:37
  232.4 0.3 fusion.7
  232.9 5.9 %collective-permute-start.7 = (f32[2,3,64]{2,0,1:T(2,128)S(1)}, f32[2,3,64]{2,0,1:T(2,128)S(1)}, u32[]{:S(2)}, u32[]{:S(2)}) collective-permute-start(f32[2,3,64]{2,0,1:T(2,128)S(1)} %pad_maximum_fusion.1), channel_id=1, source_target_pairs={{0,1},{1,0},{2,3},{3,2},{4,5},{5,4},{6,7},{7,6},{8,9},{9,8},{10,11... | collective-permute-start | bytes 4616 | tf_op jit(solution)/shard_map/ppermute | solution.py:33
  238.8 0.8 collective-permute-done.7
  239.7 0.1 add_negate_fusion
  239.9 0.5 convolution_bitcast_fusion
  240.5 9.5 %all_to_all.42 = f32[4,128,128]{2,1,0:T(8,128)} all-to-all(f32[4,128,128]{2,1,0:T(8,128)S(1)} %broadcast_in_dim.21), channel_id=1, replica_groups={{0,256,512,768},{16,272,528,784},{32,288,544,800},{48,304,560,816},{64,..., dimensions={0} | all-to-all | bytes 524288 | tf_op jit(solution)/shard_map/all_to_all | solution.py:37
  250.1 20.5 %all_to_all.43 = f32[8,128,128]{2,1,0:T(8,128)S(1)} all-to-all(f32[8,128,128]{2,1,0:T(8,128)S(1)} %broadcast_in_dim.22), channel_id=1, replica_groups={{0,2,4,6,8,10,12,14},{1,3,5,7,9,11,13,15},{16,18,20,22,24,26,28,30},{17..., dimensions={0} | all-to-all | bytes 1048576 | tf_op jit(solution)/shard_map/all_to_all | solution.py:37
  270.5 0.2 broadcast_in_dim.23
  270.8 26.6 %all_to_all.44 = f32[4,8,128,128]{3,2,1,0:T(8,128)} all-to-all(f32[4,8,128,128]{3,2,1,0:T(8,128)S(1)} %broadcast_in_dim.23), channel_id=1, replica_groups={{0,256,512,768},{16,272,528,784},{32,288,544,800},{48,304,560,816},{64,..., dimensions={0} | all-to-all | bytes 4194304 | tf_op jit(solution)/shard_map/all_to_all | solution.py:37
  297.4 1.6 copy-done
  298.9 11.6 %shard_map.96 = (f32[8,128,128]{2,1,0:T(8,128)S(1)}, f32[8,128,128]{2,1,0:T(8,128)S(1)}, f32[4,128,128]{2,1,0:T(8,128)S(1)}, f32[4,128,128]{2,1,0:T(8,128)S(1)}, f32[8,128,128]{2,1,0:T(8,128)S(1)}) custom-call(s32[2]{0:T(128)S(1)} %pad_add_fusion.2.place_ref, s32[128]{0:T(128)S(1)} %maximum_convert_fusion.ids_ref, ...), custom_call_target="tpu_custom_call" | custom-call | tf_op jit(solution)/shard_map/pallas_call | solution.py:122
  310.6 2.7 collective-permute-start.8
  313.3 8.5 %collective-permute-start.9 = (f32[8,128,128]{2,1,0:T(8,128)S(1)}, f32[8,128,128]{2,1,0:T(8,128)S(1)}, u32[]{:S(2)}, u32[]{:S(2)}) collective-permute-start(f32[8,128,128]{2,1,0:T(8,128)S(1)} %get-tuple-element.13), channel_id=1, source_target_pairs={{0,240},{16,0},{32,16},{48,32},{64,48},{80,64},{96,80},{112,96},{1... | collective-permute-start | bytes 1572872 | tf_op jit(solution)/shard_map/ppermute | solution.py:29
  321.8 1.9 collective-permute-start.10
  323.7 5.5 %collective-permute-start.11 = (f32[4,128,128]{2,1,0:T(8,128)S(1)}, f32[4,128,128]{2,1,0:T(8,128)S(1)}, u32[]{:S(2)}, u32[]{:S(2)}) collective-permute-start(f32[4,128,128]{2,1,0:T(8,128)S(1)} %get-tuple-element.15), channel_id=1, source_target_pairs={{0,224},{16,240},{32,0},{48,16},{64,32},{80,48},{96,64},{112,80},{... | collective-permute-start | bytes 786440 | tf_op jit(solution)/shard_map/ppermute | solution.py:29
  329.2 7.9 %collective-permute-done.10 = f32[4,128,128]{2,1,0:T(8,128)S(1)} collective-permute-done((f32[4,128,128]{2,1,0:T(8,128)S(1)}, f32[4,128,128]{2,1,0:T(8,128)S(1)}, u32[]{:S(2)}, u32[]{:S(2)}) %collective-permute-start.10) | collective-permute-done | bytes 262176 | tf_op jit(solution)/shard_map/ppermute | solution.py:29
  337.1 0.8 collective-permute-done.11
  337.9 0.9 maximum_add_fusion
  338.8 9.6 %all-to-all-start.7 = ((f32[4,2,128,128]{3,2,1,0:T(8,128)}), f32[4,2,128,128]{3,2,1,0:T(8,128)S(1)}, u32[]{:S(2)}, u32[]{:S(2)}) async-start(f32[4,2,128,128]{3,2,1,0:T(8,128)} %bitcast.33), calls=%async_computation.8 | async-start | bytes 1048576 | tf_op jit(solution)/shard_map/all_to_all | solution.py:37
  348.4 22.4 %all-to-all-done.7 = f32[4,2,128,128]{3,2,1,0:T(8,128)S(1)} async-done(((f32[4,2,128,128]{3,2,1,0:T(8,128)}), f32[4,2,128,128]{3,2,1,0:T(8,128)S(1)}, u32[]{:S(2)}, u32[]{:S(2)}) %all-to-all-start.7) | async-done | bytes 524320 | tf_op jit(solution)/shard_map/all_to_all | solution.py:37
  370.8 11.2 %collective-permute-start.12 = (f32[128,128]{1,0:T(8,128)S(1)}, f32[128,128]{1,0:T(8,128)S(1)}, u32[]{:S(2)}, u32[]{:S(2)}) collective-permute-start(f32[128,128]{1,0:T(8,128)S(1)} %get-tuple-element.29), channel_id=1, source_target_pairs={{0,1},{1,0},{2,3},{3,2},{4,5},{5,4},{6,7},{7,6},{8,9},{9,8},{10,11... | collective-permute-start | bytes 196616 | tf_op jit(solution)/shard_map/ppermute | solution.py:33
  382.0 0.6 fusion.25
  383.9 0.7 maximum_select_fusion
  (52 shorter events, 1.1 us)
Async XLA Ops:
  7.2 74.1 %copy-start.2 = (f32[128,256]{1,0:T(8,128)S(1)}, f32[128,256]{1,0:T(8,128)}, u32[]{:S(2)}) copy-start(f32[128,256]{1,0:T(8,128)} %param.8) | copy-start | bytes 393220
  7.2 71.5 %all-gather.3.cloned.1.call-start = ((), (), s32[]{:S(2)}) async-start(), calls=%async_computation.9 | async-start | bytes 5263360 | tf_op jit(solution)/shard_map/all_gather | solution.py:150
  10.9 211.9 %reduce-scatter.2.cloned.1.call-start = ((), (), s32[]{:S(2)}) async-start(), calls=%async_computation.10 | async-start | bytes 2359296 | tf_op jit(solution)/shard_map/reduce_scatter | solution.py:163
  78.7 65.6 %collective-permute-start.2 = (f32[8224,128]{1,0:T(8,128)}, f32[8224,128]{1,0:T(8,128)}, u32[]{:S(2)}, u32[]{:S(2)}) collective-permute-start(f32[8224,128]{1,0:T(8,128)} %all-gather.3.cloned.1.call-done.source_ref), channel_id=1, source_target_pairs={{0,1},{1,0},{2,3},{3,2},{4,5},{5,4},{6,7},{7,6},{8,9},{9,8},{10,11... | collective-permute-start | bytes 12632072 | tf_op jit(solution)/shard_map/ppermute | solution.py:33
  81.3 6.8 %collective-permute-start.1 = (f32[128,128]{1,0:T(8,128)S(1)}, f32[128,128]{1,0:T(8,128)S(1)}, u32[]{:S(2)}, u32[]{:S(2)}) collective-permute-start(f32[128,128]{1,0:T(8,128)S(1)} %get-tuple-element.35), channel_id=1, source_target_pairs={{0,1},{1,0},{2,3},{3,2},{4,5},{5,4},{6,7},{7,6},{8,9},{9,8},{10,11... | collective-permute-start | bytes 196616 | tf_op jit(solution)/shard_map/ppermute | solution.py:33
  128.2 28.1 %collective-permute-start.3 = (f32[8,128,128]{2,1,0:T(8,128)S(1)}, f32[8,128,128]{2,1,0:T(8,128)S(1)}, u32[]{:S(2)}, u32[]{:S(2)}) collective-permute-start(f32[8,128,128]{2,1,0:T(8,128)S(1)} %bitcast.86), channel_id=1, source_target_pairs={{0,240},{16,0},{32,16},{48,32},{64,48},{80,64},{96,80},{112,96},{1... | collective-permute-start | bytes 1572872 | tf_op jit(solution)/shard_map/ppermute | solution.py:29
  130.1 26.2 %collective-permute-start.6 = (f32[8,128,128]{2,1,0:T(8,128)S(1)}, f32[8,128,128]{2,1,0:T(8,128)S(1)}, u32[]{:S(2)}, u32[]{:S(2)}) collective-permute-start(f32[8,128,128]{2,1,0:T(8,128)S(1)} %bitcast.87), channel_id=1, source_target_pairs={{0,16},{16,32},{32,48},{48,64},{64,80},{80,96},{96,112},{112,128},... | collective-permute-start | bytes 1572872 | tf_op jit(solution)/shard_map/ppermute | solution.py:29
  137.2 18.8 %collective-permute-start.4 = (f32[4,128,128]{2,1,0:T(8,128)S(1)}, f32[4,128,128]{2,1,0:T(8,128)S(1)}, u32[]{:S(2)}, u32[]{:S(2)}) collective-permute-start(f32[4,128,128]{2,1,0:T(8,128)S(1)} %bitcast.95), channel_id=1, source_target_pairs={{0,224},{16,240},{32,0},{48,16},{64,32},{80,48},{96,64},{112,80},{... | collective-permute-start | bytes 786440 | tf_op jit(solution)/shard_map/ppermute | solution.py:29
  139.4 16.9 %collective-permute-start.5 = (f32[4,128,128]{2,1,0:T(8,128)S(1)}, f32[4,128,128]{2,1,0:T(8,128)S(1)}, u32[]{:S(2)}, u32[]{:S(2)}) collective-permute-start(f32[4,128,128]{2,1,0:T(8,128)S(1)} %bitcast.94), channel_id=1, source_target_pairs={{0,32},{16,48},{32,64},{48,80},{64,96},{80,112},{96,128},{112,144}... | collective-permute-start | bytes 786440 | tf_op jit(solution)/shard_map/ppermute | solution.py:29
  193.4 7.3 %copy-start.5 = (s32[1,64]{1,0:T(1,128)S(1)}, s32[1,64]{1,0:T(1,128)}, u32[]{:S(2)}) copy-start(s32[1,64]{1,0:T(1,128)} %param.14) | copy-start | bytes 772
  193.4 7.3 %copy-start.1 = (s32[1,64]{1,0:T(1,128)S(1)}, s32[1,64]{1,0:T(1,128)}, u32[]{:S(2)}) copy-start(s32[1,64]{1,0:T(1,128)} %param.13) | copy-start | bytes 772
  193.4 8.1 %copy-start.3 = (s32[1,64]{1,0:T(1,128)S(1)}, s32[1,64]{1,0:T(1,128)}, u32[]{:S(2)}) copy-start(s32[1,64]{1,0:T(1,128)} %param.15) | copy-start | bytes 772
  193.4 8.1 %copy-start.4 = (s32[1,64]{1,0:T(1,128)S(1)}, s32[1,64]{1,0:T(1,128)}, u32[]{:S(2)}) copy-start(s32[1,64]{1,0:T(1,128)} %param.12) | copy-start | bytes 772
  194.3 25.0 %all-to-all-start.3 = ((f32[8,128,128]{2,1,0:T(8,128)}), f32[8,128,128]{2,1,0:T(8,128)S(1)}, u32[]{:S(2)}, u32[]{:S(2)}) async-start(f32[8,128,128]{2,1,0:T(8,128)} %reduce_sum.73), calls=%async_computation.4 | async-start | bytes 1048576 | tf_op jit(solution)/shard_map/all_to_all | solution.py:37
  201.5 25.3 %collective-permute-start = (s32[4,64]{1,0:T(4,128)S(1)}, s32[4,64]{1,0:T(4,128)S(1)}, u32[]{:S(2)}, u32[]{:S(2)}) collective-permute-start(s32[4,64]{1,0:T(4,128)S(1)} %pad_add_fusion.1), channel_id=1, source_target_pairs={{0,1},{1,0},{2,3},{3,2},{4,5},{5,4},{6,7},{7,6},{8,9},{9,8},{10,11... | collective-permute-start | bytes 3080 | tf_op jit(solution)/shard_map/ppermute | solution.py:33
  222.8 9.6 %all-to-all-start.1 = ((f32[4,128,128]{2,1,0:T(8,128)}), f32[4,128,128]{2,1,0:T(8,128)S(1)}, u32[]{:S(2)}, u32[]{:S(2)}) async-start(f32[4,128,128]{2,1,0:T(8,128)} %reduce-scatter.2.cloned.1.call-done), calls=%async_computation.2 | async-start | bytes 524288 | tf_op jit(solution)/shard_map/all_to_all | solution.py:37
  226.8 70.5 %all-gather.5.cloned.1.call-start = ((), (), s32[]{:S(2)}) async-start(), calls=%async_computation.11 | async-start | bytes 2359296 | tf_op jit(solution)/shard_map/all_gather | solution.py:216
  232.9 6.7 %collective-permute-start.7 = (f32[2,3,64]{2,0,1:T(2,128)S(1)}, f32[2,3,64]{2,0,1:T(2,128)S(1)}, u32[]{:S(2)}, u32[]{:S(2)}) collective-permute-start(f32[2,3,64]{2,0,1:T(2,128)S(1)} %pad_maximum_fusion.1), channel_id=1, source_target_pairs={{0,1},{1,0},{2,3},{3,2},{4,5},{5,4},{6,7},{7,6},{8,9},{9,8},{10,11... | collective-permute-start | bytes 4616 | tf_op jit(solution)/shard_map/ppermute | solution.py:33
  297.4 1.6 copy-start
  310.6 27.3 %collective-permute-start.8 = (f32[8,128,128]{2,1,0:T(8,128)S(1)}, f32[8,128,128]{2,1,0:T(8,128)S(1)}, u32[]{:S(2)}, u32[]{:S(2)}) collective-permute-start(f32[8,128,128]{2,1,0:T(8,128)S(1)} %get-tuple-element.12), channel_id=1, source_target_pairs={{0,16},{16,32},{32,48},{48,64},{64,80},{80,96},{96,112},{112,128},... | collective-permute-start | bytes 1572872 | tf_op jit(solution)/shard_map/ppermute | solution.py:29
  313.3 24.6 %collective-permute-start.9 = (f32[8,128,128]{2,1,0:T(8,128)S(1)}, f32[8,128,128]{2,1,0:T(8,128)S(1)}, u32[]{:S(2)}, u32[]{:S(2)}) collective-permute-start(f32[8,128,128]{2,1,0:T(8,128)S(1)} %get-tuple-element.13), channel_id=1, source_target_pairs={{0,240},{16,0},{32,16},{48,32},{64,48},{80,64},{96,80},{112,96},{1... | collective-permute-start | bytes 1572872 | tf_op jit(solution)/shard_map/ppermute | solution.py:29
  321.8 15.3 %collective-permute-start.10 = (f32[4,128,128]{2,1,0:T(8,128)S(1)}, f32[4,128,128]{2,1,0:T(8,128)S(1)}, u32[]{:S(2)}, u32[]{:S(2)}) collective-permute-start(f32[4,128,128]{2,1,0:T(8,128)S(1)} %get-tuple-element.14), channel_id=1, source_target_pairs={{0,32},{16,48},{32,64},{48,80},{64,96},{80,112},{96,128},{112,144}... | collective-permute-start | bytes 786440 | tf_op jit(solution)/shard_map/ppermute | solution.py:29
  323.7 14.1 %collective-permute-start.11 = (f32[4,128,128]{2,1,0:T(8,128)S(1)}, f32[4,128,128]{2,1,0:T(8,128)S(1)}, u32[]{:S(2)}, u32[]{:S(2)}) collective-permute-start(f32[4,128,128]{2,1,0:T(8,128)S(1)} %get-tuple-element.15), channel_id=1, source_target_pairs={{0,224},{16,240},{32,0},{48,16},{64,32},{80,48},{96,64},{112,80},{... | collective-permute-start | bytes 786440 | tf_op jit(solution)/shard_map/ppermute | solution.py:29
  338.8 32.0 %all-to-all-start.7 = ((f32[4,2,128,128]{3,2,1,0:T(8,128)}), f32[4,2,128,128]{3,2,1,0:T(8,128)S(1)}, u32[]{:S(2)}, u32[]{:S(2)}) async-start(f32[4,2,128,128]{3,2,1,0:T(8,128)} %bitcast.33), calls=%async_computation.8 | async-start | bytes 1048576 | tf_op jit(solution)/shard_map/all_to_all | solution.py:37
  370.8 13.1 %collective-permute-start.12 = (f32[128,128]{1,0:T(8,128)S(1)}, f32[128,128]{1,0:T(8,128)S(1)}, u32[]{:S(2)}, u32[]{:S(2)}) collective-permute-start(f32[128,128]{1,0:T(8,128)S(1)} %get-tuple-element.29), channel_id=1, source_target_pairs={{0,1},{1,0},{2,3},{3,2},{4,5},{5,4},{6,7},{7,6},{8,9},{9,8},{10,11... | collective-permute-start | bytes 196616 | tf_op jit(solution)/shard_map/ppermute | solution.py:33
Sparse Core Ops, SparseCore 0:
  11.0 67.6 all-gather.2
  168.9 53.8 reduce-scatter.1
  250.2 45.7 all-gather.4

commit v4 on v3

--- a/solution.py
+++ b/solution.py
@@ -46,14 +46,12 @@
 
 
 def product(left, right, contract):
-    left_high, left_low = split_bf16(left)
-    right_high, right_low = split_bf16(right)
+    rows = jnp.concatenate(split_bf16(left), axis=1 - contract)
+    columns = jnp.concatenate(split_bf16(right), axis=1)
     dims = (((contract,), (0,)), ((), ()))
-
-    def dot(a, b):
-        return lax.dot_general(a, b, dims, preferred_element_type=jnp.float32)
-
-    return dot(left_high, right_high) + (dot(left_high, right_low) + dot(left_low, right_high))
+    all_four = lax.dot_general(rows, columns, dims, preferred_element_type=jnp.float32)
+    top, bottom = all_four[:BLOCK], all_four[BLOCK:]
+    return top[:, :HALF] + (top[:, HALF:] + bottom[:, :HALF])
 
 
 def for_live_slots(place_ref, ids_ref, sources, body):
@@ -148,14 +146,16 @@
     header = jnp.pad(marked[None, :], ((0, HEAD - 1), (0, BLOCK - SLOTS)))
     packed = jnp.concatenate([blocks.reshape(SLOTS * BLOCK, BLOCK), header], axis=0)
     source = lax.all_gather(packed, "row", axis=0, tiled=True, axis_index_groups=X_GROUPS)
+
+    far = exchange(jnp.broadcast_to(pair[None], (4, 2, BLOCK, HALF)), "row", Z_FAR)
+    far = far.reshape(8, BLOCK, HALF)
+    after, before = send_z(far, -1), send_z(far, 1)
+    parts = [far, after, send_z(far[:4], -2), send_z(far[4:], 2), before]
+    source, _, _ = lax.optimization_barrier((source, after, before))
     other = swap_cores(source)
     ids = jnp.concatenate(
         [s.reshape(NX, -1, BLOCK)[:, SLOTS * BLOCK, :SLOTS].reshape(-1) for s in (source, other)]
     ).astype(jnp.int32)
-
-    far = exchange(jnp.broadcast_to(pair[None], (4, 2, BLOCK, HALF)), "row", Z_FAR)
-    far = far.reshape(8, BLOCK, HALF)
-    parts = [far, send_z(far, -1), send_z(far[:4], -2), send_z(far[4:], 2), send_z(far, 1)]
     first, second = call_kernel(
         forward_kernel, place, ids, [source, other] + parts, [NX * NY] * 2
     )

time: 393 us -> 339 us (0.86)
  waiting for transfers between devices: 134 us -> 76.4 us
  starting transfers between devices: 83.7 us -> 101 us
  blocking collectives: 121 us -> 109 us
    all_gather x1, waiting for transfers between devices: 67.8 us -> 0.01 us  [per_device(): lax.all_gather(packed, 'row', axis=0, tiled=True, axis_index_groups=X_GRO...]
    ppermute x8, waiting for transfers between devices: 19.8 us -> 34.9 us  [send_z(): return lax.ppermute(values, 'row', pairs)]
    all_to_all x5, blocking collectives: 121 us -> 109 us  [exchange(): lax.all_to_all(values, axis, split_axis=0, concat_axis=0, tiled=True, axi...]
    ppermute x5, starting transfers between devices: 29.9 us -> 40.2 us  [swap_cores(): return lax.ppermute(values, 'col', CORE_SWAP)]
    ppermute x8, starting transfers between devices: 33.6 us -> 43.5 us  [send_z(): return lax.ppermute(values, 'row', pairs)]
    ppermute x5, waiting for transfers between devices: 5.72 us -> 1.69 us  [swap_cores(): return lax.ppermute(values, 'col', CORE_SWAP)]
where the time goes in v4:
time: 339 us; the launch traced here: 338 us
  blocking collectives  109 us (32%)
  starting transfers between devices  101 us (30%)
  waiting for transfers between devices  76.4 us (23%)
  Pallas kernels  22.3 us (7%)
  between operations  17.2 us (5%)
  other arithmetic  6.22 us (2%)
  local copies, waits for them, and re-layouts  4.97 us (1%)
    all_to_all x5, blocking collectives, exchange(): lax.all_to_all(values, axis, split_axis=0, concat_axis=0, tiled=True, axi...  109 us
    ppermute x8, starting transfers between devices, send_z(): return lax.ppermute(values, 'row', pairs)  43.5 us
    ppermute x5, starting transfers between devices, swap_cores(): return lax.ppermute(values, 'col', CORE_SWAP)  40.2 us
    all_to_all x3, waiting for transfers between devices, exchange(): lax.all_to_all(values, axis, split_axis=0, concat_axis=0, tiled=True, axi...  39.7 us
    ppermute x8, waiting for transfers between devices, send_z(): return lax.ppermute(values, 'row', pairs)  34.9 us
    pallas_call x2, Pallas kernels, call_kernel(): pl.pallas_call(body, out_shape=[jax.ShapeDtypeStruct((n, BLOCK, HALF), jn...  22.3 us
    all_to_all x3, starting transfers between devices, exchange(): lax.all_to_all(values, axis, split_axis=0, concat_axis=0, tiled=True, axi...  17.1 us
  transfers between devices with their start and end apart: 19, of which 11 were waited for; matrix products, arithmetic and copies ran while one was open for 1% of the time, Pallas kernels for 0%

profile of v4, /device:TPU:1, one launch (start us, length us, event | category | flops | bytes accessed | tf_op | source)
XLA Modules:
  0.0 337.5 jit_solution(13016631291133371264)
XLA Ops:
  7.9 0.7 fusion.18
  8.6 2.3 select_maximum_fusion
  10.9 16.1 %collective-permute-start.1 = (f32[128,128]{1,0:T(8,128)S(1)}, f32[128,128]{1,0:T(8,128)S(1)}, u32[]{:S(2)}, u32[]{:S(2)}) collective-permute-start(f32[128,128]{1,0:T(8,128)S(1)} %get-tuple-element.37), channel_id=1, source_target_pairs={{0,1},{1,0},{2,3},{3,2},{4,5},{5,4},{6,7},{7,6},{8,9},{9,8},{10,11... | collective-permute-start | bytes 196616 | tf_op jit(solution)/shard_map/ppermute | solution.py:33
  27.0 0.9 collective-permute-done.1
  27.9 25.1 %all_to_all.40 = f32[4,2,128,128]{3,2,1,0:T(8,128)S(1)} all-to-all(f32[4,2,128,128]{3,2,1,0:T(8,128)S(1)} %broadcast_in_dim.20), channel_id=1, replica_groups={{0,64,128,192},{16,80,144,208},{32,96,160,224},{48,112,176,240},{256,32..., dimensions={0} | all-to-all | bytes 1048576 | tf_op jit(solution)/shard_map/all_to_all | solution.py:37
  53.1 16.2 %collective-permute-start.2 = (f32[8,128,128]{2,1,0:T(8,128)S(1)}, f32[8,128,128]{2,1,0:T(8,128)S(1)}, u32[]{:S(2)}, u32[]{:S(2)}) collective-permute-start(f32[8,128,128]{2,1,0:T(8,128)S(1)} %bitcast.86), channel_id=1, source_target_pairs={{0,240},{16,0},{32,16},{48,32},{64,48},{80,64},{96,80},{112,96},{1... | collective-permute-start | bytes 1572872 | tf_op jit(solution)/shard_map/ppermute | solution.py:29
  69.3 1.9 collective-permute-start.3
  71.2 8.3 %collective-permute-done.2.after = f32[8,128,128]{2,1,0:T(8,128)S(1)} collective-permute-done((f32[8,128,128]{2,1,0:T(8,128)S(1)}, f32[8,128,128]{2,1,0:T(8,128)S(1)}, u32[]{:S(2)}, u32[]{:S(2)}) %collective-permute-start.2) | collective-permute-done | bytes 524320 | tf_op jit(solution)/shard_map/ppermute | solution.py:29
  79.5 5.0 %collective-permute-done.3.before = f32[8,128,128]{2,1,0:T(8,128)S(1)} collective-permute-done((f32[8,128,128]{2,1,0:T(8,128)S(1)}, f32[8,128,128]{2,1,0:T(8,128)S(1)}, u32[]{:S(2)}, u32[]{:S(2)}) %collective-permute-start.3) | collective-permute-done | bytes 524320 | tf_op jit(solution)/shard_map/ppermute | solution.py:29
  84.6 4.0 %collective-permute-start.4 = (f32[8224,128]{1,0:T(8,128)}, f32[8224,128]{1,0:T(8,128)}, u32[]{:S(2)}, u32[]{:S(2)}) collective-permute-start(f32[8224,128]{1,0:T(8,128)} %all-gather.3.cloned.1.call-done.source_ref), channel_id=1, source_target_pairs={{0,1},{1,0},{2,3},{3,2},{4,5},{5,4},{6,7},{7,6},{8,9},{9,8},{10,11... | collective-permute-start | bytes 12632072 | tf_op jit(solution)/shard_map/ppermute | solution.py:33
  88.7 1.9 collective-permute-start.5
  90.6 4.3 %collective-permute-start.6 = (f32[4,128,128]{2,1,0:T(8,128)S(1)}, f32[4,128,128]{2,1,0:T(8,128)S(1)}, u32[]{:S(2)}, u32[]{:S(2)}) collective-permute-start(f32[4,128,128]{2,1,0:T(8,128)S(1)} %bitcast.94), channel_id=1, source_target_pairs={{0,32},{16,48},{32,64},{48,80},{64,96},{80,112},{96,128},{112,144}... | collective-permute-start | bytes 786440 | tf_op jit(solution)/shard_map/ppermute | solution.py:29
  95.0 0.7 slice.91
  95.8 0.7 slice.92
  96.7 6.7 %collective-permute-done.5.two = f32[4,128,128]{2,1,0:T(8,128)S(1)} collective-permute-done((f32[4,128,128]{2,1,0:T(8,128)S(1)}, f32[4,128,128]{2,1,0:T(8,128)S(1)}, u32[]{:S(2)}, u32[]{:S(2)}) %collective-permute-start.5) | collective-permute-done | bytes 262176 | tf_op jit(solution)/shard_map/ppermute | solution.py:29
  103.4 4.0 %collective-permute-done.6.two_far = f32[4,128,128]{2,1,0:T(8,128)S(1)} collective-permute-done((f32[4,128,128]{2,1,0:T(8,128)S(1)}, f32[4,128,128]{2,1,0:T(8,128)S(1)}, u32[]{:S(2)}, u32[]{:S(2)}) %collective-permute-start.6) | collective-permute-done | bytes 262176 | tf_op jit(solution)/shard_map/ppermute | solution.py:29
  107.4 11.7 %shard_map.95 = (f32[32,128,128]{2,1,0:T(8,128)}, f32[32,128,128]{2,1,0:T(8,128)}) custom-call(s32[2]{0:T(128)S(1)} %pad_add_fusion.2.place_ref, s32[128]{0:T(128)S(1)} %maximum_convert_fusion.ids_ref, f32[8224,128]{1,0:T(8,128)} %all-gather.3.cloned.1.call-done.source_ref, f32[8224,128]{1,0:T(8,128)} %collective-permute-done.4.other_ref, ...), custom_call_target="tpu_custom_call" | custom-call | tf_op jit(solution)/shard_map/pallas_call | solution.py:120
  119.1 29.6 %all_to_all.41 = f32[4,8,128,128]{3,2,1,0:T(8,128)S(1)} all-to-all(f32[4,8,128,128]{3,2,1,0:T(8,128)} %bitcast.92), channel_id=1, replica_groups={{0,256,512,768},{16,272,528,784},{32,288,544,800},{48,304,560,816},{64,..., dimensions={0} | all-to-all | bytes 4194304 | tf_op jit(solution)/shard_map/all_to_all | solution.py:37
  148.8 1.0 reduce_sum.73
  149.7 7.5 %all-to-all-start.3 = ((f32[8,128,128]{2,1,0:T(8,128)}), f32[8,128,128]{2,1,0:T(8,128)S(1)}, u32[]{:S(2)}, u32[]{:S(2)}) async-start(f32[8,128,128]{2,1,0:T(8,128)} %reduce_sum.73), calls=%async_computation.4 | async-start | bytes 1048576 | tf_op jit(solution)/shard_map/all_to_all | solution.py:37
  157.3 0.8 gather_fusion
  158.1 4.3 %collective-permute-start = (s32[4,64]{1,0:T(4,128)S(1)}, s32[4,64]{1,0:T(4,128)S(1)}, u32[]{:S(2)}, u32[]{:S(2)}) collective-permute-start(s32[4,64]{1,0:T(4,128)S(1)} %pad_add_fusion.1), channel_id=1, source_target_pairs={{0,1},{1,0},{2,3},{3,2},{4,5},{5,4},{6,7},{7,6},{8,9},{9,8},{10,11... | collective-permute-start | bytes 3080 | tf_op jit(solution)/shard_map/ppermute | solution.py:33
  162.4 12.2 %all-to-all-done.3 = f32[8,128,128]{2,1,0:T(8,128)S(1)} async-done(((f32[8,128,128]{2,1,0:T(8,128)}), f32[8,128,128]{2,1,0:T(8,128)S(1)}, u32[]{:S(2)}, u32[]{:S(2)}) %all-to-all-start.3) | async-done | bytes 524320 | tf_op jit(solution)/shard_map/all_to_all | solution.py:37
  174.6 3.4 %all-to-all-start.1 = ((f32[4,128,128]{2,1,0:T(8,128)}), f32[4,128,128]{2,1,0:T(8,128)S(1)}, u32[]{:S(2)}, u32[]{:S(2)}) async-start(f32[4,128,128]{2,1,0:T(8,128)} %reduce-scatter.2.cloned.1.call-done), calls=%async_computation.2 | async-start | bytes 524288 | tf_op jit(solution)/shard_map/all_to_all | solution.py:37
  178.2 5.4 %all-to-all-done.1 = f32[4,128,128]{2,1,0:T(8,128)S(1)} async-done(((f32[4,128,128]{2,1,0:T(8,128)}), f32[4,128,128]{2,1,0:T(8,128)S(1)}, u32[]{:S(2)}, u32[]{:S(2)}) %all-to-all-start.1) | async-done | bytes 262176 | tf_op jit(solution)/shard_map/all_to_all | solution.py:37
  183.6 0.3 fusion.7
  184.1 5.5 %collective-permute-start.7 = (f32[2,3,64]{2,0,1:T(2,128)S(1)}, f32[2,3,64]{2,0,1:T(2,128)S(1)}, u32[]{:S(2)}, u32[]{:S(2)}) collective-permute-start(f32[2,3,64]{2,0,1:T(2,128)S(1)} %pad_maximum_fusion.1), channel_id=1, source_target_pairs={{0,1},{1,0},{2,3},{3,2},{4,5},{5,4},{6,7},{7,6},{8,9},{9,8},{10,11... | collective-permute-start | bytes 4616 | tf_op jit(solution)/shard_map/ppermute | solution.py:33
  189.6 0.8 collective-permute-done.7
  190.4 0.1 add_negate_fusion
  190.7 0.5 convolution_bitcast_fusion
  191.2 9.5 %all_to_all.42 = f32[4,128,128]{2,1,0:T(8,128)} all-to-all(f32[4,128,128]{2,1,0:T(8,128)S(1)} %broadcast_in_dim.21), channel_id=1, replica_groups={{0,256,512,768},{16,272,528,784},{32,288,544,800},{48,304,560,816},{64,..., dimensions={0} | all-to-all | bytes 524288 | tf_op jit(solution)/shard_map/all_to_all | solution.py:37
  200.8 17.8 %all_to_all.43 = f32[8,128,128]{2,1,0:T(8,128)S(1)} all-to-all(f32[8,128,128]{2,1,0:T(8,128)S(1)} %broadcast_in_dim.22), channel_id=1, replica_groups={{0,2,4,6,8,10,12,14},{1,3,5,7,9,11,13,15},{16,18,20,22,24,26,28,30},{17..., dimensions={0} | all-to-all | bytes 1048576 | tf_op jit(solution)/shard_map/all_to_all | solution.py:37
  218.6 0.2 broadcast_in_dim.23
  218.9 26.5 %all_to_all.44 = f32[4,8,128,128]{3,2,1,0:T(8,128)} all-to-all(f32[4,8,128,128]{3,2,1,0:T(8,128)S(1)} %broadcast_in_dim.23), channel_id=1, replica_groups={{0,256,512,768},{16,272,528,784},{32,288,544,800},{48,304,560,816},{64,..., dimensions={0} | all-to-all | bytes 4194304 | tf_op jit(solution)/shard_map/all_to_all | solution.py:37
  245.4 1.6 copy-done
  247.0 10.7 %shard_map.96 = (f32[8,128,128]{2,1,0:T(8,128)S(1)}, f32[8,128,128]{2,1,0:T(8,128)S(1)}, f32[4,128,128]{2,1,0:T(8,128)S(1)}, f32[4,128,128]{2,1,0:T(8,128)S(1)}, f32[8,128,128]{2,1,0:T(8,128)S(1)}) custom-call(s32[2]{0:T(128)S(1)} %pad_add_fusion.2.place_ref, s32[128]{0:T(128)S(1)} %maximum_convert_fusion.ids_ref, ...), custom_call_target="tpu_custom_call" | custom-call | tf_op jit(solution)/shard_map/pallas_call | solution.py:120
  257.6 4.8 %collective-permute-start.8 = (f32[8,128,128]{2,1,0:T(8,128)S(1)}, f32[8,128,128]{2,1,0:T(8,128)S(1)}, u32[]{:S(2)}, u32[]{:S(2)}) collective-permute-start(f32[8,128,128]{2,1,0:T(8,128)S(1)} %get-tuple-element.14), channel_id=1, source_target_pairs={{0,16},{16,32},{32,48},{48,64},{64,80},{80,96},{96,112},{112,128},... | collective-permute-start | bytes 1572872 | tf_op jit(solution)/shard_map/ppermute | solution.py:29
  262.5 7.0 %collective-permute-start.9 = (f32[8,128,128]{2,1,0:T(8,128)S(1)}, f32[8,128,128]{2,1,0:T(8,128)S(1)}, u32[]{:S(2)}, u32[]{:S(2)}) collective-permute-start(f32[8,128,128]{2,1,0:T(8,128)S(1)} %get-tuple-element.15), channel_id=1, source_target_pairs={{0,240},{16,0},{32,16},{48,32},{64,48},{80,64},{96,80},{112,96},{1... | collective-permute-start | bytes 1572872 | tf_op jit(solution)/shard_map/ppermute | solution.py:29
  269.4 1.9 collective-permute-start.10
  271.4 5.5 %collective-permute-start.11 = (f32[4,128,128]{2,1,0:T(8,128)S(1)}, f32[4,128,128]{2,1,0:T(8,128)S(1)}, u32[]{:S(2)}, u32[]{:S(2)}) collective-permute-start(f32[4,128,128]{2,1,0:T(8,128)S(1)} %get-tuple-element.17), channel_id=1, source_target_pairs={{0,224},{16,240},{32,0},{48,16},{64,32},{80,48},{96,64},{112,80},{... | collective-permute-start | bytes 786440 | tf_op jit(solution)/shard_map/ppermute | solution.py:29
  276.8 7.8 %collective-permute-done.10 = f32[4,128,128]{2,1,0:T(8,128)S(1)} collective-permute-done((f32[4,128,128]{2,1,0:T(8,128)S(1)}, f32[4,128,128]{2,1,0:T(8,128)S(1)}, u32[]{:S(2)}, u32[]{:S(2)}) %collective-permute-start.10) | collective-permute-done | bytes 262176 | tf_op jit(solution)/shard_map/ppermute | solution.py:29
  284.6 3.0 collective-permute-done.11
  287.6 0.9 maximum_add_fusion
  288.5 6.2 %all-to-all-start.7 = ((f32[4,2,128,128]{3,2,1,0:T(8,128)}), f32[4,2,128,128]{3,2,1,0:T(8,128)S(1)}, u32[]{:S(2)}, u32[]{:S(2)}) async-start(f32[4,2,128,128]{3,2,1,0:T(8,128)} %bitcast.33), calls=%async_computation.8 | async-start | bytes 1048576 | tf_op jit(solution)/shard_map/all_to_all | solution.py:37
  294.8 22.2 %all-to-all-done.7 = f32[4,2,128,128]{3,2,1,0:T(8,128)S(1)} async-done(((f32[4,2,128,128]{3,2,1,0:T(8,128)}), f32[4,2,128,128]{3,2,1,0:T(8,128)S(1)}, u32[]{:S(2)}, u32[]{:S(2)}) %all-to-all-start.7) | async-done | bytes 524320 | tf_op jit(solution)/shard_map/all_to_all | solution.py:37
  317.0 10.3 %collective-permute-start.12 = (f32[128,128]{1,0:T(8,128)S(1)}, f32[128,128]{1,0:T(8,128)S(1)}, u32[]{:S(2)}, u32[]{:S(2)}) collective-permute-start(f32[128,128]{1,0:T(8,128)S(1)} %get-tuple-element.31), channel_id=1, source_target_pairs={{0,1},{1,0},{2,3},{3,2},{4,5},{5,4},{6,7},{7,6},{8,9},{9,8},{10,11... | collective-permute-start | bytes 196616 | tf_op jit(solution)/shard_map/ppermute | solution.py:33
  327.3 0.6 fusion.25
  329.2 0.7 maximum_select_fusion
  (52 shorter events, 1.1 us)
Async XLA Ops:
  7.2 3.7 %copy-start.2 = (f32[128,256]{1,0:T(8,128)S(1)}, f32[128,256]{1,0:T(8,128)}, u32[]{:S(2)}) copy-start(f32[128,256]{1,0:T(8,128)} %param.8) | copy-start | bytes 393220
  7.2 77.4 %all-gather.3.cloned.1.call-start = ((), (), s32[]{:S(2)}) async-start(), calls=%async_computation.9 | async-start | bytes 5263360 | tf_op jit(solution)/shard_map/all_gather | solution.py:148
  10.9 163.8 %reduce-scatter.2.cloned.1.call-start = ((), (), s32[]{:S(2)}) async-start(), calls=%async_computation.10 | async-start | bytes 2359296 | tf_op jit(solution)/shard_map/reduce_scatter | solution.py:163
  10.9 17.0 %collective-permute-start.1 = (f32[128,128]{1,0:T(8,128)S(1)}, f32[128,128]{1,0:T(8,128)S(1)}, u32[]{:S(2)}, u32[]{:S(2)}) collective-permute-start(f32[128,128]{1,0:T(8,128)S(1)} %get-tuple-element.37), channel_id=1, source_target_pairs={{0,1},{1,0},{2,3},{3,2},{4,5},{5,4},{6,7},{7,6},{8,9},{9,8},{10,11... | collective-permute-start | bytes 196616 | tf_op jit(solution)/shard_map/ppermute | solution.py:33
  53.1 26.5 %collective-permute-start.2 = (f32[8,128,128]{2,1,0:T(8,128)S(1)}, f32[8,128,128]{2,1,0:T(8,128)S(1)}, u32[]{:S(2)}, u32[]{:S(2)}) collective-permute-start(f32[8,128,128]{2,1,0:T(8,128)S(1)} %bitcast.86), channel_id=1, source_target_pairs={{0,240},{16,0},{32,16},{48,32},{64,48},{80,64},{96,80},{112,96},{1... | collective-permute-start | bytes 1572872 | tf_op jit(solution)/shard_map/ppermute | solution.py:29
  69.3 15.3 %collective-permute-start.3 = (f32[8,128,128]{2,1,0:T(8,128)S(1)}, f32[8,128,128]{2,1,0:T(8,128)S(1)}, u32[]{:S(2)}, u32[]{:S(2)}) collective-permute-start(f32[8,128,128]{2,1,0:T(8,128)S(1)} %bitcast.87), channel_id=1, source_target_pairs={{0,16},{16,32},{32,48},{48,64},{64,80},{80,96},{96,112},{112,128},... | collective-permute-start | bytes 1572872 | tf_op jit(solution)/shard_map/ppermute | solution.py:29
  84.6 11.2 %collective-permute-start.4 = (f32[8224,128]{1,0:T(8,128)}, f32[8224,128]{1,0:T(8,128)}, u32[]{:S(2)}, u32[]{:S(2)}) collective-permute-start(f32[8224,128]{1,0:T(8,128)} %all-gather.3.cloned.1.call-done.source_ref), channel_id=1, source_target_pairs={{0,1},{1,0},{2,3},{3,2},{4,5},{5,4},{6,7},{7,6},{8,9},{9,8},{10,11... | collective-permute-start | bytes 12632072 | tf_op jit(solution)/shard_map/ppermute | solution.py:33
  88.7 14.7 %collective-permute-start.5 = (f32[4,128,128]{2,1,0:T(8,128)S(1)}, f32[4,128,128]{2,1,0:T(8,128)S(1)}, u32[]{:S(2)}, u32[]{:S(2)}) collective-permute-start(f32[4,128,128]{2,1,0:T(8,128)S(1)} %bitcast.95), channel_id=1, source_target_pairs={{0,224},{16,240},{32,0},{48,16},{64,32},{80,48},{96,64},{112,80},{... | collective-permute-start | bytes 786440 | tf_op jit(solution)/shard_map/ppermute | solution.py:29
  90.6 16.8 %collective-permute-start.6 = (f32[4,128,128]{2,1,0:T(8,128)S(1)}, f32[4,128,128]{2,1,0:T(8,128)S(1)}, u32[]{:S(2)}, u32[]{:S(2)}) collective-permute-start(f32[4,128,128]{2,1,0:T(8,128)S(1)} %bitcast.94), channel_id=1, source_target_pairs={{0,32},{16,48},{32,64},{48,80},{64,96},{80,112},{96,128},{112,144}... | collective-permute-start | bytes 786440 | tf_op jit(solution)/shard_map/ppermute | solution.py:29
  148.8 8.5 %copy-start.5 = (s32[1,64]{1,0:T(1,128)S(1)}, s32[1,64]{1,0:T(1,128)}, u32[]{:S(2)}) copy-start(s32[1,64]{1,0:T(1,128)} %param.14) | copy-start | bytes 772
  148.8 8.5 %copy-start.1 = (s32[1,64]{1,0:T(1,128)S(1)}, s32[1,64]{1,0:T(1,128)}, u32[]{:S(2)}) copy-start(s32[1,64]{1,0:T(1,128)} %param.13) | copy-start | bytes 772
  148.8 9.3 %copy-start.3 = (s32[1,64]{1,0:T(1,128)S(1)}, s32[1,64]{1,0:T(1,128)}, u32[]{:S(2)}) copy-start(s32[1,64]{1,0:T(1,128)} %param.15) | copy-start | bytes 772
  148.8 9.3 %copy-start.4 = (s32[1,64]{1,0:T(1,128)S(1)}, s32[1,64]{1,0:T(1,128)}, u32[]{:S(2)}) copy-start(s32[1,64]{1,0:T(1,128)} %param.12) | copy-start | bytes 772
  149.7 24.9 %all-to-all-start.3 = ((f32[8,128,128]{2,1,0:T(8,128)}), f32[8,128,128]{2,1,0:T(8,128)S(1)}, u32[]{:S(2)}, u32[]{:S(2)}) async-start(f32[8,128,128]{2,1,0:T(8,128)} %reduce_sum.73), calls=%async_computation.4 | async-start | bytes 1048576 | tf_op jit(solution)/shard_map/all_to_all | solution.py:37
  158.1 20.0 %collective-permute-start = (s32[4,64]{1,0:T(4,128)S(1)}, s32[4,64]{1,0:T(4,128)S(1)}, u32[]{:S(2)}, u32[]{:S(2)}) collective-permute-start(s32[4,64]{1,0:T(4,128)S(1)} %pad_add_fusion.1), channel_id=1, source_target_pairs={{0,1},{1,0},{2,3},{3,2},{4,5},{5,4},{6,7},{7,6},{8,9},{9,8},{10,11... | collective-permute-start | bytes 3080 | tf_op jit(solution)/shard_map/ppermute | solution.py:33
  174.6 8.9 %all-to-all-start.1 = ((f32[4,128,128]{2,1,0:T(8,128)}), f32[4,128,128]{2,1,0:T(8,128)S(1)}, u32[]{:S(2)}, u32[]{:S(2)}) async-start(f32[4,128,128]{2,1,0:T(8,128)} %reduce-scatter.2.cloned.1.call-done), calls=%async_computation.2 | async-start | bytes 524288 | tf_op jit(solution)/shard_map/all_to_all | solution.py:37
  178.0 67.4 %all-gather.5.cloned.1.call-start = ((), (), s32[]{:S(2)}) async-start(), calls=%async_computation.11 | async-start | bytes 2359296 | tf_op jit(solution)/shard_map/all_gather | solution.py:216
  184.1 6.3 %collective-permute-start.7 = (f32[2,3,64]{2,0,1:T(2,128)S(1)}, f32[2,3,64]{2,0,1:T(2,128)S(1)}, u32[]{:S(2)}, u32[]{:S(2)}) collective-permute-start(f32[2,3,64]{2,0,1:T(2,128)S(1)} %pad_maximum_fusion.1), channel_id=1, source_target_pairs={{0,1},{1,0},{2,3},{3,2},{4,5},{5,4},{6,7},{7,6},{8,9},{9,8},{10,11... | collective-permute-start | bytes 4616 | tf_op jit(solution)/shard_map/ppermute | solution.py:33
  245.4 1.6 copy-start
  257.6 30.0 %collective-permute-start.8 = (f32[8,128,128]{2,1,0:T(8,128)S(1)}, f32[8,128,128]{2,1,0:T(8,128)S(1)}, u32[]{:S(2)}, u32[]{:S(2)}) collective-permute-start(f32[8,128,128]{2,1,0:T(8,128)S(1)} %get-tuple-element.14), channel_id=1, source_target_pairs={{0,16},{16,32},{32,48},{48,64},{64,80},{80,96},{96,112},{112,128},... | collective-permute-start | bytes 1572872 | tf_op jit(solution)/shard_map/ppermute | solution.py:29
  262.5 25.2 %collective-permute-start.9 = (f32[8,128,128]{2,1,0:T(8,128)S(1)}, f32[8,128,128]{2,1,0:T(8,128)S(1)}, u32[]{:S(2)}, u32[]{:S(2)}) collective-permute-start(f32[8,128,128]{2,1,0:T(8,128)S(1)} %get-tuple-element.15), channel_id=1, source_target_pairs={{0,240},{16,0},{32,16},{48,32},{64,48},{80,64},{96,80},{112,96},{1... | collective-permute-start | bytes 1572872 | tf_op jit(solution)/shard_map/ppermute | solution.py:29
  269.4 15.2 %collective-permute-start.10 = (f32[4,128,128]{2,1,0:T(8,128)S(1)}, f32[4,128,128]{2,1,0:T(8,128)S(1)}, u32[]{:S(2)}, u32[]{:S(2)}) collective-permute-start(f32[4,128,128]{2,1,0:T(8,128)S(1)} %get-tuple-element.16), channel_id=1, source_target_pairs={{0,32},{16,48},{32,64},{48,80},{64,96},{80,112},{96,128},{112,144}... | collective-permute-start | bytes 786440 | tf_op jit(solution)/shard_map/ppermute | solution.py:29
  271.4 16.3 %collective-permute-start.11 = (f32[4,128,128]{2,1,0:T(8,128)S(1)}, f32[4,128,128]{2,1,0:T(8,128)S(1)}, u32[]{:S(2)}, u32[]{:S(2)}) collective-permute-start(f32[4,128,128]{2,1,0:T(8,128)S(1)} %get-tuple-element.17), channel_id=1, source_target_pairs={{0,224},{16,240},{32,0},{48,16},{64,32},{80,48},{96,64},{112,80},{... | collective-permute-start | bytes 786440 | tf_op jit(solution)/shard_map/ppermute | solution.py:29
  288.5 28.4 %all-to-all-start.7 = ((f32[4,2,128,128]{3,2,1,0:T(8,128)}), f32[4,2,128,128]{3,2,1,0:T(8,128)S(1)}, u32[]{:S(2)}, u32[]{:S(2)}) async-start(f32[4,2,128,128]{3,2,1,0:T(8,128)} %bitcast.33), calls=%async_computation.8 | async-start | bytes 1048576 | tf_op jit(solution)/shard_map/all_to_all | solution.py:37
  317.0 12.2 %collective-permute-start.12 = (f32[128,128]{1,0:T(8,128)S(1)}, f32[128,128]{1,0:T(8,128)S(1)}, u32[]{:S(2)}, u32[]{:S(2)}) collective-permute-start(f32[128,128]{1,0:T(8,128)S(1)} %get-tuple-element.31), channel_id=1, source_target_pairs={{0,1},{1,0},{2,3},{3,2},{4,5},{5,4},{6,7},{7,6},{8,9},{9,8},{10,11... | collective-permute-start | bytes 196616 | tf_op jit(solution)/shard_map/ppermute | solution.py:33
Sparse Core Ops, SparseCore 0:
  11.0 67.6 all-gather.2
  119.3 41.6 reduce-scatter.1
  200.9 41.8 all-gather.4

commit v5 on v4

v5 whole, which is shorter than its diff:
```python
import jax
import jax.numpy as jnp
from jax import lax
from jax.experimental import pallas as pl
from jax.experimental.pallas import tpu as pltpu
from jax.sharding import PartitionSpec as P

BLOCK = 128
NX = 4
NZ = 16
NY = 8
HALF = 128
SLOTS = 16
CB = 64
HEAD = 8
PAIRS = 64
STRIDE = SLOTS * BLOCK + HEAD
EXTRA = 32
VMEM_LIMIT = 48 * 1024 * 1024

precise = lax.Precision.HIGHEST

BOTH = ("row", "col")
X_GROUPS = [[x * NZ + z for x in range(NX)] for z in range(NZ)]
Y_GROUPS = [[y * 2 + k for y in range(NY)] for k in range(2)]
X_CORE = [
    [(x * NZ + z) * 2 * NY + 2 * y + k for x in range(NX) for k in range(2)]
    for z in range(NZ)
    for y in range(NY)
]
Z_CORE = [
    [(x * NZ + 4 * a + b) * 2 * NY + 2 * y + k for a in range(4) for k in range(2)]
    for x in range(NX)
    for b in range(4)
    for y in range(NY)
]
CORE_SWAP = [(i, i ^ 1) for i in range(2 * NY)]


def send_z(values, step):
    pairs = [(x * NZ + z, x * NZ + (z + step) % NZ) for x in range(NX) for z in range(NZ)]
    return lax.ppermute(values, "row", pairs)


def swap_cores(values):
    return lax.ppermute(values, "col", CORE_SWAP)


def exchange(values, axis, groups):
    return lax.all_to_all(
        values, axis, split_axis=0, concat_axis=0, tiled=True, axis_index_groups=groups
    )


def split_bf16(values):
    high = values.astype(jnp.bfloat16)
    low = (values - high.astype(jnp.float32)).astype(jnp.bfloat16)
    return high, low


def product(left, right, contract):
    rows = jnp.concatenate(split_bf16(left), axis=1 - contract)
    columns = jnp.concatenate(split_bf16(right), axis=1)
    dims = (((contract,), (0,)), ((), ()))
    all_four = lax.dot_general(rows, columns, dims, preferred_element_type=jnp.float32)
    top, bottom = all_four[:BLOCK], all_four[BLOCK:]
    return top[:, :HALF] + (top[:, HALF:] + bottom[:, :HALF])


def start_copies(place_ref, ids_ref, source_ref, blocks_ref, order_ref, arrived):
    def visit(number, count):
        position = ids_ref[number]
        column = jnp.bitwise_and(position, CB - 1)
        live = jnp.logical_and(position >= 0, column // NZ == place_ref[0])

        @pl.when(live)
        def _():
            order_ref[count] = number
            copy_block(number, count, source_ref, blocks_ref, arrived).start()

        return count + live.astype(jnp.int32)

    return lax.fori_loop(0, 2 * NX * SLOTS, visit, jnp.int32(0))


def copy_block(number, place, source_ref, blocks_ref, arrived):
    start = (number // SLOTS) * STRIDE + jnp.bitwise_and(number, SLOTS - 1) * BLOCK
    rows = source_ref.at[pl.ds(pl.multiple_of(start, 8), BLOCK)]
    return pltpu.make_async_copy(rows, blocks_ref.at[place], arrived.at[place])


def for_live_blocks(count, place_ref, ids_ref, source_ref, blocks_ref, order_ref, arrived, body):
    @pl.loop(0, count)
    def _(index):
        number = order_ref[index]
        position = ids_ref[number]
        z = jnp.bitwise_and(position, NZ - 1)
        near = jnp.bitwise_and(z - place_ref[1], 3) * 8 + (z // 4) * 2
        near = near + jnp.bitwise_and(number // SLOTS, 1)
        copy_block(number, index, source_ref, blocks_ref, arrived).wait()
        body(number // (2 * SLOTS), blocks_ref[index], position // CB, near)


def forward_kernel(place_ref, ids_ref, source_ref, *refs):
    parts, (first, second), rows_ref, rest = refs[:5], refs[5:7], refs[7], refs[8:]
    count = start_copies(place_ref, ids_ref, source_ref, *rest)
    first[...] = jnp.zeros_like(first)
    second[...] = jnp.zeros_like(second)
    start = 0
    for part in parts:
        rows_ref[pl.ds(start, part.shape[0])] = part[...]
        start += part.shape[0]

    def body(x, block, rb, near):
        value = product(block, rows_ref[near], 1)
        y = rb // 2

        @pl.when(rb % 2 == 0)
        def _():
            first[y * NX + x, pl.ds(0, BLOCK)] += value

        @pl.when(rb % 2 == 1)
        def _():
            first[y * NX + x, pl.ds(BLOCK, EXTRA)] += value[:EXTRA]
            second[x * NY + y] += value[EXTRA:]

    for_live_blocks(count, place_ref, ids_ref, source_ref, *rest, body)


def backward_kernel(place_ref, ids_ref, source_ref, first, second, *refs):
    outs, total_ref, rest = refs[:5], refs[5], refs[6:]
    count = start_copies(place_ref, ids_ref, source_ref, *rest)
    total_ref[...] = jnp.zeros_like(total_ref)

    def body(x, block, rb, near):
        y = rb // 2
        rows = jnp.where(rb % 2 == 0, first[y * NX + x], second[x * NY + y])
        total_ref[near] += product(block, rows, 0)

    for_live_blocks(count, place_ref, ids_ref, source_ref, *rest, body)
    start = 0
    for out in outs:
        out[...] = total_ref[pl.ds(start, out.shape[0])]
        start += out.shape[0]


def call_kernel(body, place, ids, source, arrays, out_shapes):
    whole = pl.BlockSpec(memory_space=pltpu.VMEM)
    scalars = pl.BlockSpec(memory_space=pltpu.SMEM)
    slots = 2 * NX * SLOTS
    return pl.pallas_call(
        body,
        out_shape=[jax.ShapeDtypeStruct((*shape, HALF), jnp.float32) for shape in out_shapes],
        in_specs=[scalars, scalars, pl.BlockSpec(memory_space=pl.ANY)] + [whole] * len(arrays),
        out_specs=[whole] * len(out_shapes),
        scratch_shapes=[
            pltpu.VMEM((2 * NZ, BLOCK, HALF), jnp.float32),
            pltpu.VMEM((slots, BLOCK, BLOCK), jnp.float32),
            pltpu.SMEM((slots,), jnp.int32),
            pltpu.SemaphoreType.DMA((slots,)),
        ],
        compiler_params=pltpu.CompilerParams(vmem_limit_bytes=VMEM_LIMIT),
    )(place, ids, source, *arrays)


def one_hot(indices, span_rows):
    return (indices[..., None] == jnp.arange(span_rows, dtype=jnp.int32)).astype(jnp.float32)


def per_device(table, blocks, block_ids, counts, users, positives, neg_index, popular):
    own_row = lax.axis_index("row")
    core = jnp.bitwise_and(lax.axis_index("col"), 1)
    own_z = jnp.bitwise_and(own_row, NZ - 1)
    place = jnp.stack([own_row // NZ, own_z]).astype(jnp.int32)

    live = jnp.arange(SLOTS, dtype=jnp.int32) < counts[0]
    marked = jnp.where(live, block_ids[0], -1).astype(jnp.float32)
    header = jnp.pad(marked[None, :], ((0, HEAD - 1), (0, BLOCK - SLOTS)))
    packed = jnp.concatenate([blocks.reshape(SLOTS * BLOCK, BLOCK), header], axis=0)
    source = lax.all_gather(packed, BOTH, axis=0, tiled=True, axis_index_groups=X_CORE)

    halves = jnp.stack([table[:, :HALF], table[:, HALF:]])
    halves = jnp.broadcast_to(halves[None], (4, 2, BLOCK, HALF)).reshape(8, BLOCK, HALF)
    far = exchange(halves, BOTH, Z_CORE)
    span_table = lax.dynamic_slice_in_dim(far, own_z // 4 * 2, 2)
    parts = [far, send_z(far, -1), send_z(far[:4], -2), send_z(far[4:], 2), send_z(far, 1)]
    picks = jnp.stack([users[0], positives[0], jnp.take(positives[0], neg_index[0]), popular[0]])
    other_picks = swap_cores(picks)
    source, other_picks, *parts = lax.optimization_barrier((source, other_picks, *parts))
    ids = source.reshape(2 * NX, STRIDE, BLOCK)[:, SLOTS * BLOCK, :SLOTS].reshape(-1).astype(jnp.int32)
    shapes = [(NX * NY, BLOCK + EXTRA), (NX * NY, BLOCK - EXTRA)]
    first, second = call_kernel(forward_kernel, place, ids, source, parts, shapes)

    first = lax.psum_scatter(
        first, "col", scatter_dimension=0, tiled=True, axis_index_groups=Y_GROUPS
    )
    second = second.reshape(NX, NY, BLOCK - EXTRA, HALF)
    second = jnp.sum(exchange(second, "row", X_GROUPS), axis=0)
    second = jnp.sum(exchange(second, "col", Y_GROUPS), axis=0)
    first = jnp.sum(exchange(first, "row", X_GROUPS), axis=0)
    current = jnp.concatenate([first, second]).reshape(2, BLOCK, HALF)

    is_first = core == 0
    span_picks = [jnp.where(is_first, picks, other_picks), jnp.where(is_first, other_picks, picks)]
    final_rows = (span_table + current) / 2
    hot = one_hot(jnp.stack(span_picks), BLOCK)
    rows = jnp.einsum("hpij,hjd->hpid", hot, final_rows, precision=precise)
    user_rows, item_rows, batch_rows, popular_rows = (rows[:, i] for i in range(4))
    scores = jnp.stack(
        [
            jnp.sum(user_rows * item_rows, axis=-1),
            jnp.sum(user_rows * batch_rows, axis=-1),
            jnp.sum(user_rows * popular_rows, axis=-1),
        ],
        axis=1,
    )
    scores = scores + swap_cores(scores)
    first = scores[:, 1] - scores[:, 0]
    second = scores[:, 2] - scores[:, 0]
    losses = jax.nn.softplus(first) + jax.nn.softplus(second)
    span_losses = jnp.sum(losses, axis=1) / PAIRS
    span_loss = jnp.where(is_first, span_losses[0], span_losses[1]).reshape(1)
    pull_first = jax.nn.sigmoid(first)[..., None] / 2
    pull_second = jax.nn.sigmoid(second)[..., None] / 2
    pull_item = -(pull_first + pull_second)
    row_grads = jnp.stack(
        [
            pull_item * item_rows + pull_first * batch_rows + pull_second * popular_rows,
            pull_item * user_rows,
            pull_first * user_rows,
            pull_second * user_rows,
        ],
        axis=1,
    )
    scaled = jnp.einsum("hpij,hpid->hjd", hot, row_grads, precision=precise)

    first = exchange(jnp.broadcast_to(scaled[0][None], (NX, BLOCK, HALF)), "row", X_GROUPS)
    first = lax.all_gather(first, "col", axis=0, tiled=True, axis_index_groups=Y_GROUPS)
    second = exchange(jnp.broadcast_to(scaled[1][None], (NY, BLOCK, HALF)), "col", Y_GROUPS)
    second = jnp.broadcast_to(second[None], (NX, NY, BLOCK, HALF))
    second = exchange(second, "row", X_GROUPS).reshape(NX * NY, BLOCK, HALF)
    shapes = [(n, BLOCK) for n in (8, 8, 4, 4, 8)]
    own, after, two, two_far, before = call_kernel(
        backward_kernel, place, ids, source, [first, second], shapes
    )
    two = jnp.concatenate([send_z(two, 2), send_z(two_far, -2)])
    near = (own + send_z(after, 1) + send_z(before, -1) + two).reshape(4, 2, BLOCK, HALF)
    is_own = (jnp.arange(4) == own_z // 4)[:, None, None, None]
    near = near + jnp.where(is_own, scaled[None], 0.0)
    halves = exchange(near.reshape(8, BLOCK, HALF), BOTH, Z_CORE)
    halves = jnp.sum(halves.reshape(4, 2, BLOCK, HALF), axis=0)
    gradient = jnp.concatenate([halves[0], halves[1]], axis=1)
    return (gradient, span_loss)


def solution(mesh):
    in_specs = (
        P(("row", "col"), None),
        P(("row", "col"), None, None, None),
        P(("row", "col"), None),
        P(("row", "col")),
        P(("row", "col"), None),
        P(("row", "col"), None),
        P(("row", "col"), None),
        P(("row", "col"), None),
    )
    out_specs = (P(("row", "col"), None), P(("row", "col")))
    return jax.shard_map(
        per_device, mesh=mesh, in_specs=in_specs, out_specs=out_specs, check_vma=False
    )
```

time: 339 us -> 332 us (0.979)
  the two profiles are of different devices: /device:TPU:1 before, /device:TPU:112 now
where the time goes in v5:
time: 332 us; the launch traced here: 330 us
  waiting for transfers between devices  121 us (36%)
  blocking collectives  84 us (25%)
  starting transfers between devices  74.8 us (23%)
  between operations  17.2 us (5%)
  Pallas kernels  16.6 us (5%)
  other arithmetic  8.66 us (3%)
  local copies, waits for them, and re-layouts  7.72 us (2%)
    all_to_all x4, waiting for transfers between devices, exchange(): lax.all_to_all(values, axis, split_axis=0, concat_axis=0, tiled=True, axi...  84.4 us
    all_to_all x4, blocking collectives, exchange(): lax.all_to_all(values, axis, split_axis=0, concat_axis=0, tiled=True, axi...  84 us
    all_to_all x4, starting transfers between devices, exchange(): lax.all_to_all(values, axis, split_axis=0, concat_axis=0, tiled=True, axi...  40.9 us
    ppermute x8, starting transfers between devices, send_z(): return lax.ppermute(values, 'row', pairs)  30 us
    ppermute x8, waiting for transfers between devices, send_z(): return lax.ppermute(values, 'row', pairs)  26.6 us
    pallas_call x2, Pallas kernels, call_kernel(): pl.pallas_call(body, out_shape=[jax.ShapeDtypeStruct((*shape, HALF), jnp....  16.6 us
    reduce_scatter x1, waiting for transfers between devices, per_device(): lax.psum_scatter(first, 'col', scatter_dimension=0, tiled=True, axis_inde...  7.55 us
  transfers between devices with their start and end apart: 17, of which 10 were waited for; matrix products, arithmetic and copies ran while one was open for 2% of the time, Pallas kernels for 0%

profile of v5, /device:TPU:112, one launch (start us, length us, event | category | flops | bytes accessed | tf_op | source)
XLA Modules:
  0.0 330.4 jit_solution(9208524464724026144)
XLA Ops:
  7.9 0.7 fusion.20
  8.5 2.4 select_maximum_fusion
  10.9 0.9 copy-done.4
  11.8 0.8 broadcast_in_dim.71
  12.7 17.8 %all-to-all-start = ((f32[8,128,128]{2,1,0:T(8,128)}), f32[8,128,128]{2,1,0:T(8,128)S(1)}, u32[]{:S(2)}, u32[]{:S(2)}) async-start(f32[8,128,128]{2,1,0:T(8,128)} %bitcast.10), calls=%async_computation | async-start | bytes 1048576 | tf_op jit(solution)/shard_map/all_to_all | solution.py:50
  30.6 0.8 gather_fusion
  31.4 31.0 %all-to-all-done.refs_0_ = f32[8,128,128]{2,1,0:T(8,128)S(1)} async-done(((f32[8,128,128]{2,1,0:T(8,128)}), f32[8,128,128]{2,1,0:T(8,128)S(1)}, u32[]{:S(2)}, u32[]{:S(2)}) %all-to-all-start) | async-done | bytes 524320 | tf_op jit(solution)/shard_map/all_to_all | solution.py:50
  62.4 5.0 %collective-permute-start.1 = (f32[8,128,128]{2,1,0:T(8,128)S(1)}, f32[8,128,128]{2,1,0:T(8,128)S(1)}, u32[]{:S(2)}, u32[]{:S(2)}) collective-permute-start(f32[8,128,128]{2,1,0:T(8,128)S(1)} %all-to-all-done.refs_0_), channel_id=1, source_target_pairs={{0,240},{16,0},{32,16},{48,32},{64,48},{80,64},{96,80},{112,96},{1... | collective-permute-start | bytes 1572872 | tf_op jit(solution)/shard_map/ppermute | solution.py:42
  67.4 1.9 collective-permute-start.4
  69.4 5.0 %collective-permute-start.2 = (f32[4,128,128]{2,1,0:T(8,128)S(1)}, f32[4,128,128]{2,1,0:T(8,128)S(1)}, u32[]{:S(2)}, u32[]{:S(2)}) collective-permute-start(f32[4,128,128]{2,1,0:T(8,128)S(1)} %get-tuple-element.37), channel_id=1, source_target_pairs={{0,224},{16,240},{32,0},{48,16},{64,32},{80,48},{96,64},{112,80},{... | collective-permute-start | bytes 786440 | tf_op jit(solution)/shard_map/ppermute | solution.py:42
  74.3 1.9 collective-permute-start.3
  76.3 1.9 collective-permute-start
  78.3 1.0 collective-permute-done
  79.4 11.2 %collective-permute-done.2.refs_2_ = f32[4,128,128]{2,1,0:T(8,128)S(1)} collective-permute-done((f32[4,128,128]{2,1,0:T(8,128)S(1)}, f32[4,128,128]{2,1,0:T(8,128)S(1)}, u32[]{:S(2)}, u32[]{:S(2)}) %collective-permute-start.2) | collective-permute-done | bytes 262176 | tf_op jit(solution)/shard_map/ppermute | solution.py:42
  90.5 2.0 collective-permute-done.3.refs_3_
  92.5 0.7 copy-done.1
  93.2 0.8 slice.77
  94.1 1.0 copy-done.2
  95.0 8.4 %shard_map.95 = (f32[32,160,128]{2,1,0:T(8,128)}, f32[32,96,128]{2,1,0:T(8,128)S(1)}) custom-call(s32[2]{0:T(128)S(1)} %pad_add_fusion.2.place_ref, s32[128]{0:T(128)S(1)} %convert_element_type.14.ids_ref, f32[16448,128]{1,0:T(8,128)} %all-gather.3.cloned.1.call-done.source_ref, f32[8,128,128]{2,1,0:T(8,128)S(1)} %all-to-all-done.refs_0_, ...), custom_call_target="tpu_custom_call" | custom-call | tf_op jit(solution)/shard_map/pallas_call | solution.py:151
  103.5 23.9 %all_to_all.40 = f32[4,8,96,128]{3,2,1,0:T(8,128)} all-to-all(f32[4,8,96,128]{3,2,1,0:T(8,128)S(1)} %bitcast.69), channel_id=1, replica_groups={{0,256,512,768},{16,272,528,784},{32,288,544,800},{48,304,560,816},{64,..., dimensions={0} | all-to-all | bytes 3145728 | tf_op jit(solution)/shard_map/all_to_all | solution.py:50
  127.4 2.3 reduce_sum.73
  129.8 6.3 %all-to-all-start.3 = ((f32[8,96,128]{2,1,0:T(8,128)}), f32[8,96,128]{2,1,0:T(8,128)S(1)}, u32[]{:S(2)}, u32[]{:S(2)}) async-start(f32[8,96,128]{2,1,0:T(8,128)} %reduce_sum.73), calls=%async_computation.4 | async-start | bytes 786432 | tf_op jit(solution)/shard_map/all_to_all | solution.py:50
  136.0 13.9 %all-to-all-done.3 = f32[8,96,128]{2,1,0:T(8,128)S(1)} async-done(((f32[8,96,128]{2,1,0:T(8,128)}), f32[8,96,128]{2,1,0:T(8,128)S(1)}, u32[]{:S(2)}, u32[]{:S(2)}) %all-to-all-start.3) | async-done | bytes 393248 | tf_op jit(solution)/shard_map/all_to_all | solution.py:50
  149.9 7.6 %reduce-scatter.2.cloned.1.call-done = f32[4,160,128]{2,1,0:T(8,128)} async-done(((f32[32,160,128]{2,1,0:T(8,128)}), f32[4,160,128]{2,1,0:T(8,128)}) %reduce-scatter.2.cloned.1.call-update) | async-done | bytes 327696 | tf_op jit(solution)/shard_map/reduce_scatter | solution.py:194
  157.5 4.1 %all-to-all-start.1 = ((f32[4,160,128]{2,1,0:T(8,128)}), f32[4,160,128]{2,1,0:T(8,128)S(1)}, u32[]{:S(2)}, u32[]{:S(2)}) async-start(f32[4,160,128]{2,1,0:T(8,128)} %reduce-scatter.2.cloned.1.call-done), calls=%async_computation.2 | async-start | bytes 655360 | tf_op jit(solution)/shard_map/all_to_all | solution.py:50
  161.7 7.0 %all-to-all-done.1 = f32[4,160,128]{2,1,0:T(8,128)S(1)} async-done(((f32[4,160,128]{2,1,0:T(8,128)}), f32[4,160,128]{2,1,0:T(8,128)S(1)}, u32[]{:S(2)}, u32[]{:S(2)}) %all-to-all-start.1) | async-done | bytes 327712 | tf_op jit(solution)/shard_map/all_to_all | solution.py:50
  168.7 0.3 fusion.8
  169.0 0.1 multiply_reduce_fusion.2
  169.2 1.9 collective-permute-start.5
  171.1 1.1 collective-permute-done.5
  172.3 0.1 add_negate_fusion
  172.5 0.5 convolution_bitcast_fusion
  173.1 10.3 %all_to_all.41 = f32[4,128,128]{2,1,0:T(8,128)} all-to-all(f32[4,128,128]{2,1,0:T(8,128)S(1)} %broadcast_in_dim.73), channel_id=1, replica_groups={{0,256,512,768},{16,272,528,784},{32,288,544,800},{48,304,560,816},{64,..., dimensions={0} | all-to-all | bytes 524288 | tf_op jit(solution)/shard_map/all_to_all | solution.py:50
  183.5 20.5 %all_to_all.42 = f32[8,128,128]{2,1,0:T(8,128)S(1)} all-to-all(f32[8,128,128]{2,1,0:T(8,128)S(1)} %broadcast_in_dim.75), channel_id=1, replica_groups={{0,2,4,6,8,10,12,14},{1,3,5,7,9,11,13,15},{16,18,20,22,24,26,28,30},{17..., dimensions={0} | all-to-all | bytes 1048576 | tf_op jit(solution)/shard_map/all_to_all | solution.py:50
  204.0 0.2 broadcast_in_dim.76
  204.2 29.3 %all_to_all.43 = f32[4,8,128,128]{3,2,1,0:T(8,128)} all-to-all(f32[4,8,128,128]{3,2,1,0:T(8,128)S(1)} %broadcast_in_dim.76), channel_id=1, replica_groups={{0,256,512,768},{16,272,528,784},{32,288,544,800},{48,304,560,816},{64,..., dimensions={0} | all-to-all | bytes 4194304 | tf_op jit(solution)/shard_map/all_to_all | solution.py:50
  233.5 1.6 copy-done
  235.1 8.1 %shard_map.96 = (f32[8,128,128]{2,1,0:T(8,128)S(1)}, f32[8,128,128]{2,1,0:T(8,128)S(1)}, f32[4,128,128]{2,1,0:T(8,128)S(1)}, f32[4,128,128]{2,1,0:T(8,128)S(1)}, f32[8,128,128]{2,1,0:T(8,128)S(1)}) custom-call(s32[2]{0:T(128)S(1)} %pad_add_fusion.2.place_ref, s32[128]{0:T(128)S(1)} %convert_element_type.14.ids_ref, ...), custom_call_target="tpu_custom_call" | custom-call | tf_op jit(solution)/shard_map/pallas_call | solution.py:151
  243.2 5.6 %collective-permute-start.6 = (f32[8,128,128]{2,1,0:T(8,128)S(1)}, f32[8,128,128]{2,1,0:T(8,128)S(1)}, u32[]{:S(2)}, u32[]{:S(2)}) collective-permute-start(f32[8,128,128]{2,1,0:T(8,128)S(1)} %get-tuple-element.26), channel_id=1, source_target_pairs={{0,16},{16,32},{32,48},{48,64},{64,80},{80,96},{96,112},{112,128},... | collective-permute-start | bytes 1572872 | tf_op jit(solution)/shard_map/ppermute | solution.py:42
  248.8 1.9 collective-permute-start.7
  250.8 5.1 %collective-permute-start.8 = (f32[4,128,128]{2,1,0:T(8,128)S(1)}, f32[4,128,128]{2,1,0:T(8,128)}, u32[]{:S(2)}, u32[]{:S(2)}) collective-permute-start(f32[4,128,128]{2,1,0:T(8,128)S(1)} %get-tuple-element.28), channel_id=1, source_target_pairs={{0,32},{16,48},{32,64},{48,80},{64,96},{80,112},{96,128},{112,144}... | collective-permute-start | bytes 786440 | tf_op jit(solution)/shard_map/ppermute | solution.py:42
  255.9 3.5 %collective-permute-start.9 = (f32[4,128,128]{2,1,0:T(8,128)S(1)}, f32[4,128,128]{2,1,0:T(8,128)}, u32[]{:S(2)}, u32[]{:S(2)}) collective-permute-start(f32[4,128,128]{2,1,0:T(8,128)S(1)} %get-tuple-element.29), channel_id=1, source_target_pairs={{0,224},{16,240},{32,0},{48,16},{64,32},{80,48},{96,64},{112,80},{... | collective-permute-start | bytes 786440 | tf_op jit(solution)/shard_map/ppermute | solution.py:42
  259.6 13.4 %collective-permute-done.8 = f32[4,128,128]{2,1,0:T(8,128)} collective-permute-done((f32[4,128,128]{2,1,0:T(8,128)S(1)}, f32[4,128,128]{2,1,0:T(8,128)}, u32[]{:S(2)}, u32[]{:S(2)}) %collective-permute-start.8) | collective-permute-done | bytes 262176 | tf_op jit(solution)/shard_map/ppermute | solution.py:42
  273.0 2.0 fusion
  275.0 12.6 %all-to-all-start.7 = ((f32[8,128,128]{2,1,0:T(8,128)}), f32[8,128,128]{2,1,0:T(8,128)S(1)}, u32[]{:S(2)}, u32[]{:S(2)}) async-start(f32[8,128,128]{2,1,0:T(8,128)} %fusion), calls=%async_computation.8 | async-start | bytes 1048576 | tf_op jit(solution)/shard_map/all_to_all | solution.py:50
  287.7 0.6 fusion.27
  289.5 32.5 %all-to-all-done.7 = f32[8,128,128]{2,1,0:T(8,128)S(1)} async-done(((f32[8,128,128]{2,1,0:T(8,128)}), f32[8,128,128]{2,1,0:T(8,128)S(1)}, u32[]{:S(2)}, u32[]{:S(2)}) %all-to-all-start.7) | async-done | bytes 524320 | tf_op jit(solution)/shard_map/all_to_all | solution.py:50
  322.1 0.7 pad_maximum_fusion.2
  (52 shorter events, 0.9 us)
Async XLA Ops:
  7.2 86.0 %all-gather.3.cloned.1.call-start = ((), (), s32[]{:S(2)}) async-start(), calls=%async_computation.9 | async-start | bytes 9474048 | tf_op jit(solution)/shard_map/all_gather | solution.py:180
  10.9 0.9 copy-start.4
  11.8 18.8 %copy-start.7 = (s32[1,64]{1,0:T(1,128)S(1)}, s32[1,64]{1,0:T(1,128)}, u32[]{:S(2)}) copy-start(s32[1,64]{1,0:T(1,128)} %param.14) | copy-start | bytes 772
  11.8 18.8 %copy-start.3 = (s32[1,64]{1,0:T(1,128)S(1)}, s32[1,64]{1,0:T(1,128)}, u32[]{:S(2)}) copy-start(s32[1,64]{1,0:T(1,128)} %param.13) | copy-start | bytes 772
  12.7 49.7 %all-to-all-start = ((f32[8,128,128]{2,1,0:T(8,128)}), f32[8,128,128]{2,1,0:T(8,128)S(1)}, u32[]{:S(2)}, u32[]{:S(2)}) async-start(f32[8,128,128]{2,1,0:T(8,128)} %bitcast.10), calls=%async_computation | async-start | bytes 1048576 | tf_op jit(solution)/shard_map/all_to_all | solution.py:50
  30.5 45.8 %copy-start.5 = (s32[1,64]{1,0:T(1,128)S(1)}, s32[1,64]{1,0:T(1,128)}, u32[]{:S(2)}) copy-start(s32[1,64]{1,0:T(1,128)} %param.15) | copy-start | bytes 772
  30.5 45.8 %copy-start.6 = (s32[1,64]{1,0:T(1,128)S(1)}, s32[1,64]{1,0:T(1,128)}, u32[]{:S(2)}) copy-start(s32[1,64]{1,0:T(1,128)} %param.12) | copy-start | bytes 772
  30.5 127.0 %reduce-scatter.2.cloned.1.call-start = ((), (), s32[]{:S(2)}) async-start(), calls=%async_computation.10 | async-start | bytes 2949120 | tf_op jit(solution)/shard_map/reduce_scatter | solution.py:194
  62.4 30.8 %collective-permute-start.1 = (f32[8,128,128]{2,1,0:T(8,128)S(1)}, f32[8,128,128]{2,1,0:T(8,128)S(1)}, u32[]{:S(2)}, u32[]{:S(2)}) collective-permute-start(f32[8,128,128]{2,1,0:T(8,128)S(1)} %all-to-all-done.refs_0_), channel_id=1, source_target_pairs={{0,240},{16,0},{32,16},{48,32},{64,48},{80,64},{96,80},{112,96},{1... | collective-permute-start | bytes 1572872 | tf_op jit(solution)/shard_map/ppermute | solution.py:42
  67.4 25.8 %collective-permute-start.4 = (f32[8,128,128]{2,1,0:T(8,128)S(1)}, f32[8,128,128]{2,1,0:T(8,128)S(1)}, u32[]{:S(2)}, u32[]{:S(2)}) collective-permute-start(f32[8,128,128]{2,1,0:T(8,128)S(1)} %all-to-all-done.refs_0_), channel_id=1, source_target_pairs={{0,16},{16,32},{32,48},{48,64},{64,80},{80,96},{96,112},{112,128},... | collective-permute-start | bytes 1572872 | tf_op jit(solution)/shard_map/ppermute | solution.py:42
  69.4 21.2 %collective-permute-start.2 = (f32[4,128,128]{2,1,0:T(8,128)S(1)}, f32[4,128,128]{2,1,0:T(8,128)S(1)}, u32[]{:S(2)}, u32[]{:S(2)}) collective-permute-start(f32[4,128,128]{2,1,0:T(8,128)S(1)} %get-tuple-element.37), channel_id=1, source_target_pairs={{0,224},{16,240},{32,0},{48,16},{64,32},{80,48},{96,64},{112,80},{... | collective-permute-start | bytes 786440 | tf_op jit(solution)/shard_map/ppermute | solution.py:42
  74.3 18.2 %collective-permute-start.3 = (f32[4,128,128]{2,1,0:T(8,128)S(1)}, f32[4,128,128]{2,1,0:T(8,128)S(1)}, u32[]{:S(2)}, u32[]{:S(2)}) collective-permute-start(f32[4,128,128]{2,1,0:T(8,128)S(1)} %get-tuple-element.36), channel_id=1, source_target_pairs={{0,32},{16,48},{32,64},{48,80},{64,96},{80,112},{96,128},{112,144}... | collective-permute-start | bytes 786440 | tf_op jit(solution)/shard_map/ppermute | solution.py:42
  76.3 3.1 collective-permute-start
  92.5 0.7 copy-start.1
  94.1 1.0 copy-start.2
  129.8 20.2 %all-to-all-start.3 = ((f32[8,96,128]{2,1,0:T(8,128)}), f32[8,96,128]{2,1,0:T(8,128)S(1)}, u32[]{:S(2)}, u32[]{:S(2)}) async-start(f32[8,96,128]{2,1,0:T(8,128)} %reduce_sum.73), calls=%async_computation.4 | async-start | bytes 786432 | tf_op jit(solution)/shard_map/all_to_all | solution.py:50
  157.5 11.2 %all-to-all-start.1 = ((f32[4,160,128]{2,1,0:T(8,128)}), f32[4,160,128]{2,1,0:T(8,128)S(1)}, u32[]{:S(2)}, u32[]{:S(2)}) async-start(f32[4,160,128]{2,1,0:T(8,128)} %reduce-scatter.2.cloned.1.call-done), calls=%async_computation.2 | async-start | bytes 655360 | tf_op jit(solution)/shard_map/all_to_all | solution.py:50
  161.6 71.9 %all-gather.5.cloned.1.call-start = ((), (), s32[]{:S(2)}) async-start(), calls=%async_computation.11 | async-start | bytes 2359296 | tf_op jit(solution)/shard_map/all_gather | solution.py:238
  169.2 3.1 collective-permute-start.5
  233.5 1.6 copy-start
  243.2 29.8 %collective-permute-start.6 = (f32[8,128,128]{2,1,0:T(8,128)S(1)}, f32[8,128,128]{2,1,0:T(8,128)S(1)}, u32[]{:S(2)}, u32[]{:S(2)}) collective-permute-start(f32[8,128,128]{2,1,0:T(8,128)S(1)} %get-tuple-element.26), channel_id=1, source_target_pairs={{0,16},{16,32},{32,48},{48,64},{64,80},{80,96},{96,112},{112,128},... | collective-permute-start | bytes 1572872 | tf_op jit(solution)/shard_map/ppermute | solution.py:42
  248.8 24.2 %collective-permute-start.7 = (f32[8,128,128]{2,1,0:T(8,128)S(1)}, f32[8,128,128]{2,1,0:T(8,128)S(1)}, u32[]{:S(2)}, u32[]{:S(2)}) collective-permute-start(f32[8,128,128]{2,1,0:T(8,128)S(1)} %get-tuple-element.27), channel_id=1, source_target_pairs={{0,240},{16,0},{32,16},{48,32},{64,48},{80,64},{96,80},{112,96},{1... | collective-permute-start | bytes 1572872 | tf_op jit(solution)/shard_map/ppermute | solution.py:42
  250.8 22.2 %collective-permute-start.8 = (f32[4,128,128]{2,1,0:T(8,128)S(1)}, f32[4,128,128]{2,1,0:T(8,128)}, u32[]{:S(2)}, u32[]{:S(2)}) collective-permute-start(f32[4,128,128]{2,1,0:T(8,128)S(1)} %get-tuple-element.28), channel_id=1, source_target_pairs={{0,32},{16,48},{32,64},{48,80},{64,96},{80,112},{96,128},{112,144}... | collective-permute-start | bytes 786440 | tf_op jit(solution)/shard_map/ppermute | solution.py:42
  255.9 17.1 %collective-permute-start.9 = (f32[4,128,128]{2,1,0:T(8,128)S(1)}, f32[4,128,128]{2,1,0:T(8,128)}, u32[]{:S(2)}, u32[]{:S(2)}) collective-permute-start(f32[4,128,128]{2,1,0:T(8,128)S(1)} %get-tuple-element.29), channel_id=1, source_target_pairs={{0,224},{16,240},{32,0},{48,16},{64,32},{80,48},{96,64},{112,80},{... | collective-permute-start | bytes 786440 | tf_op jit(solution)/shard_map/ppermute | solution.py:42
  275.0 47.0 %all-to-all-start.7 = ((f32[8,128,128]{2,1,0:T(8,128)}), f32[8,128,128]{2,1,0:T(8,128)S(1)}, u32[]{:S(2)}, u32[]{:S(2)}) async-start(f32[8,128,128]{2,1,0:T(8,128)} %fusion), calls=%async_computation.8 | async-start | bytes 1048576 | tf_op jit(solution)/shard_map/all_to_all | solution.py:50
Sparse Core Ops, SparseCore 0:
  11.0 66.9 all-gather.2
  103.6 53.8 reduce-scatter.1
  183.6 47.5 all-gather.4

commit v6 on v5

v6 whole, which is shorter than its diff:
```python
import functools

import jax
import jax.numpy as jnp
from jax import lax
from jax.experimental import pallas as pl
from jax.experimental.pallas import tpu as pltpu
from jax.sharding import PartitionSpec as P

BLOCK = 128
NX = 4
NZ = 16
NY = 8
HALF = 128
SLOTS = 16
CB = 64
PAIRS = 64
ENTRIES = 2 * NX * SLOTS
VMEM_LIMIT = 48 * 1024 * 1024

precise = lax.Precision.HIGHEST

BOTH = ("row", "col")
X_GROUPS = [[x * NZ + z for x in range(NX)] for z in range(NZ)]
Y_GROUPS = [[y * 2 + k for y in range(NY)] for k in range(2)]
X_CORE = [
    [(x * NZ + z) * 2 * NY + 2 * y + k for x in range(NX) for k in range(2)]
    for z in range(NZ)
    for y in range(NY)
]
Z_CORE = [
    [(x * NZ + 4 * a + b) * 2 * NY + 2 * y + k for a in range(4) for k in range(2)]
    for x in range(NX)
    for b in range(4)
    for y in range(NY)
]
CORE_SWAP = [(i, i ^ 1) for i in range(2 * NY)]


def send_z(values, step):
    pairs = [(x * NZ + z, x * NZ + (z + step) % NZ) for x in range(NX) for z in range(NZ)]
    return lax.ppermute(values, "row", pairs)


def swap_cores(values):
    return lax.ppermute(values, "col", CORE_SWAP)


def exchange(values, axis, groups):
    return lax.all_to_all(
        values, axis, split_axis=0, concat_axis=0, tiled=True, axis_index_groups=groups
    )


def split_bf16(values):
    high = values.astype(jnp.bfloat16)
    low = (values - high.astype(jnp.float32)).astype(jnp.bfloat16)
    return high, low


def product(left, right, contract):
    left_high, left_low = split_bf16(left)
    right_high, right_low = split_bf16(right)
    rows = jnp.concatenate([left_high, left_low, left_high], axis=contract)
    columns = jnp.concatenate([right_high, right_high, right_low], axis=0)
    dims = (((contract,), (0,)), ((), ()))
    return lax.dot_general(rows, columns, dims, preferred_element_type=jnp.float32)


def copy_block(entry, place, source_ref, blocks_ref, arrived):
    rows = source_ref.at[jnp.bitwise_and(entry, ENTRIES - 1)]
    return pltpu.make_async_copy(rows, blocks_ref.at[place], arrived.at[place])


def start_copies(first, last, list_ref, source_ref, blocks_ref, arrived):
    @pl.loop(first, last)
    def _(index):
        copy_block(list_ref[index], index, source_ref, blocks_ref, arrived).start()


def for_live_blocks(first, last, place_ref, list_ref, source_ref, blocks_ref, arrived, body):
    @pl.loop(first, last)
    def _(index):
        entry = list_ref[index]
        number, position = jnp.bitwise_and(entry, ENTRIES - 1), entry // ENTRIES
        z = jnp.bitwise_and(position, NZ - 1)
        near = jnp.bitwise_and(z - place_ref[0], 3) * 8 + (z // 4) * 2
        near = near + jnp.bitwise_and(number // SLOTS, 1)
        copy_block(entry, index, source_ref, blocks_ref, arrived).wait()
        body(number // (2 * SLOTS), blocks_ref[index], position // (2 * CB), near, index)


def forward_kernel(odd, place_ref, list_ref, source_ref, *refs):
    parts, out_ref, rows_ref, rest = refs[:5], refs[5], refs[6], refs[7:]
    first = place_ref[1] if odd else 0
    last = place_ref[2] if odd else place_ref[1]
    start_copies(first, last, list_ref, source_ref, *rest)
    out_ref[...] = jnp.zeros_like(out_ref)
    start = 0
    for part in parts:
        rows_ref[pl.ds(start, part.shape[0])] = part[...]
        start += part.shape[0]

    def body(x, block, y, near, index):
        place = x * NY + y if odd else y * NX + x
        out_ref[place] += product(block, rows_ref[near], 1)

    for_live_blocks(first, last, place_ref, list_ref, source_ref, *rest, body)


def backward_kernel(place_ref, list_ref, source_ref, even, odd, *refs):
    outs, total_ref, rest = refs[:5], refs[5], refs[6:]
    start_copies(0, place_ref[2], list_ref, source_ref, *rest)
    total_ref[...] = jnp.zeros_like(total_ref)

    def body(x, block, y, near, index):
        rows = jnp.where(index < place_ref[1], even[y * NX + x], odd[x * NY + y])
        total_ref[near] += product(block, rows, 0)

    for_live_blocks(0, place_ref[2], place_ref, list_ref, source_ref, *rest, body)
    start = 0
    for out in outs:
        out[...] = total_ref[pl.ds(start, out.shape[0])]
        start += out.shape[0]


def call_kernel(body, place, entries, source, arrays, out_blocks):
    whole = pl.BlockSpec(memory_space=pltpu.VMEM)
    scalars = pl.BlockSpec(memory_space=pltpu.SMEM)
    return pl.pallas_call(
        body,
        out_shape=[jax.ShapeDtypeStruct((n, BLOCK, HALF), jnp.float32) for n in out_blocks],
        in_specs=[scalars, scalars, pl.BlockSpec(memory_space=pl.ANY)] + [whole] * len(arrays),
        out_specs=[whole] * len(out_blocks),
        scratch_shapes=[
            pltpu.VMEM((2 * NZ, BLOCK, HALF), jnp.float32),
            pltpu.VMEM((ENTRIES, BLOCK, BLOCK), jnp.float32),
            pltpu.SemaphoreType.DMA((ENTRIES,)),
        ],
        compiler_params=pltpu.CompilerParams(vmem_limit_bytes=VMEM_LIMIT),
    )(place, entries, source, *arrays)


def live_list(ids, own_x, own_z):
    numbers = jnp.arange(ENTRIES, dtype=jnp.int32)
    live = (ids >= 0) & (jnp.bitwise_and(ids, CB - 1) // NZ == own_x)
    odd = jnp.bitwise_and(ids // CB, 1) == 1
    even_live, odd_live = live & ~odd, live & odd
    before = numbers[None, :] < numbers[:, None]
    even_end = jnp.sum(even_live.astype(jnp.int32))
    rank = jnp.where(
        odd,
        even_end + jnp.sum((before & odd_live[None, :]).astype(jnp.int32), axis=1),
        jnp.sum((before & even_live[None, :]).astype(jnp.int32), axis=1),
    )
    hit = live[None, :] & (rank[None, :] == numbers[:, None])
    entries = jnp.sum(jnp.where(hit, (ids * ENTRIES + numbers)[None, :], 0), axis=1)
    return entries, jnp.stack([own_z, even_end, jnp.sum(live.astype(jnp.int32))])


def one_hot(indices, span_rows):
    return (indices[..., None] == jnp.arange(span_rows, dtype=jnp.int32)).astype(jnp.float32)


def per_device(table, blocks, block_ids, counts, users, positives, neg_index, popular):
    own_row = lax.axis_index("row")
    core = jnp.bitwise_and(lax.axis_index("col"), 1)
    own_z = jnp.bitwise_and(own_row, NZ - 1)
    source = lax.all_gather(blocks[0], BOTH, axis=0, tiled=True, axis_index_groups=X_CORE)

    halves = jnp.stack([table[:, :HALF], table[:, HALF:]])
    halves = jnp.broadcast_to(halves[None], (4, 2, BLOCK, HALF)).reshape(8, BLOCK, HALF)
    far = exchange(halves, BOTH, Z_CORE)
    span_table = lax.dynamic_slice_in_dim(far, own_z // 4 * 2, 2)
    parts = [far, send_z(far, -1), send_z(far[:4], -2), send_z(far[4:], 2), send_z(far, 1)]
    picks = jnp.stack([users[0], positives[0], jnp.take(positives[0], neg_index[0]), popular[0]])
    other_picks = swap_cores(picks)
    live = jnp.arange(SLOTS, dtype=jnp.int32) < counts[0]
    marked, _ = lax.optimization_barrier((jnp.where(live, block_ids[0], -1), far))
    ids = exchange(jnp.broadcast_to(marked[None], (2 * NX, SLOTS)), BOTH, X_CORE)
    entries, place = live_list(ids.reshape(-1), own_row // NZ, own_z)
    source, other_picks, entries, place, *parts = lax.optimization_barrier(
        (source, other_picks, entries, place, *parts)
    )
    even, odd = (functools.partial(forward_kernel, odd) for odd in (False, True))
    (first,) = call_kernel(even, place, entries, source, parts, [NX * NY])
    entries, first = lax.optimization_barrier((entries, first))
    (second,) = call_kernel(odd, place, entries, source, parts, [NX * NY])

    first = lax.psum_scatter(
        first, "col", scatter_dimension=0, tiled=True, axis_index_groups=Y_GROUPS
    )
    second = second.reshape(NX, NY, BLOCK, HALF)
    second = jnp.sum(exchange(second, "row", X_GROUPS), axis=0)
    second = jnp.sum(exchange(second, "col", Y_GROUPS), axis=0)
    first = jnp.sum(exchange(first, "row", X_GROUPS), axis=0)
    current = jnp.stack([first, second])

    is_first = core == 0
    span_picks = [jnp.where(is_first, picks, other_picks), jnp.where(is_first, other_picks, picks)]
    final_rows = (span_table + current) / 2
    hot = one_hot(jnp.stack(span_picks), BLOCK)
    rows = jnp.einsum("hpij,hjd->hpid", hot, final_rows, precision=precise)
    user_rows, item_rows, batch_rows, popular_rows = (rows[:, i] for i in range(4))
    scores = jnp.stack(
        [
            jnp.sum(user_rows * item_rows, axis=-1),
            jnp.sum(user_rows * batch_rows, axis=-1),
            jnp.sum(user_rows * popular_rows, axis=-1),
        ],
        axis=1,
    )
    scores = scores + swap_cores(scores)
    first = scores[:, 1] - scores[:, 0]
    second = scores[:, 2] - scores[:, 0]
    losses = jax.nn.softplus(first) + jax.nn.softplus(second)
    span_losses = jnp.sum(losses, axis=1) / PAIRS
    span_loss = jnp.where(is_first, span_losses[0], span_losses[1]).reshape(1)
    pull_first = jax.nn.sigmoid(first)[..., None] / 2
    pull_second = jax.nn.sigmoid(second)[..., None] / 2
    pull_item = -(pull_first + pull_second)
    row_grads = jnp.stack(
        [
            pull_item * item_rows + pull_first * batch_rows + pull_second * popular_rows,
            pull_item * user_rows,
            pull_first * user_rows,
            pull_second * user_rows,
        ],
        axis=1,
    )
    scaled = jnp.einsum("hpij,hpid->hjd", hot, row_grads, precision=precise)

    first = exchange(jnp.broadcast_to(scaled[0][None], (NX, BLOCK, HALF)), "row", X_GROUPS)
    first = lax.all_gather(first, "col", axis=0, tiled=True, axis_index_groups=Y_GROUPS)
    second = exchange(jnp.broadcast_to(scaled[1][None], (NY, BLOCK, HALF)), "col", Y_GROUPS)
    second = jnp.broadcast_to(second[None], (NX, NY, BLOCK, HALF))
    second = exchange(second, "row", X_GROUPS).reshape(NX * NY, BLOCK, HALF)
    own, after, two, two_far, before = call_kernel(
        backward_kernel, place, entries, source, [first, second], [8, 8, 4, 4, 8]
    )
    two = jnp.concatenate([send_z(two, 2), send_z(two_far, -2)])
    near = (own + send_z(after, 1) + send_z(before, -1) + two).reshape(4, 2, BLOCK, HALF)
    is_own = (jnp.arange(4) == own_z // 4)[:, None, None, None]
    near = near + jnp.where(is_own, scaled[None], 0.0)
    halves = exchange(near.reshape(8, BLOCK, HALF), BOTH, Z_CORE)
    halves = jnp.sum(halves.reshape(4, 2, BLOCK, HALF), axis=0)
    gradient = jnp.concatenate([halves[0], halves[1]], axis=1)
    return (gradient, span_loss)


def solution(mesh):
    in_specs = (
        P(("row", "col"), None),
        P(("row", "col"), None, None, None),
        P(("row", "col"), None),
        P(("row", "col")),
        P(("row", "col"), None),
        P(("row", "col"), None),
        P(("row", "col"), None),
        P(("row", "col"), None),
    )
    out_specs = (P(("row", "col"), None), P(("row", "col")))
    return jax.shard_map(
        per_device, mesh=mesh, in_specs=in_specs, out_specs=out_specs, check_vma=False
    )
```

time: 332 us -> 325 us (0.979)
  the two profiles are of different devices: /device:TPU:112 before, /device:TPU:1 now
where the time goes in v6:
time: 325 us; the launch traced here: 319 us
  starting transfers between devices  104 us (32%)
  blocking collectives  82.8 us (25%)
  waiting for transfers between devices  82.4 us (25%)
  Pallas kernels  18 us (6%)
  between operations  17.2 us (5%)
  other arithmetic  7.68 us (2%)
  local copies, waits for them, and re-layouts  6.43 us (2%)
    all_to_all x4, blocking collectives, exchange(): lax.all_to_all(values, axis, split_axis=0, concat_axis=0, tiled=True, axi...  82.8 us
    all_to_all x5, starting transfers between devices, exchange(): lax.all_to_all(values, axis, split_axis=0, concat_axis=0, tiled=True, axi...  66.3 us
    all_to_all x5, waiting for transfers between devices, exchange(): lax.all_to_all(values, axis, split_axis=0, concat_axis=0, tiled=True, axi...  61.3 us
    ppermute x8, starting transfers between devices, send_z(): return lax.ppermute(values, 'row', pairs)  28.9 us
    ppermute x8, waiting for transfers between devices, send_z(): return lax.ppermute(values, 'row', pairs)  19.5 us
    pallas_call x3, Pallas kernels, call_kernel(): pl.pallas_call(body, out_shape=[jax.ShapeDtypeStruct((n, BLOCK, HALF), jn...  18 us
    ppermute x2, starting transfers between devices, swap_cores(): return lax.ppermute(values, 'col', CORE_SWAP)  8.16 us
  transfers between devices with their start and end apart: 18, of which 9 were waited for; matrix products, arithmetic and copies ran while one was open for 3% of the time, Pallas kernels for 1%

profile of v6, /device:TPU:1, one launch (start us, length us, event | category | flops | bytes accessed | tf_op | source)
XLA Modules:
  0.0 318.8 jit_solution(12471827826826145847)
XLA Ops:
  7.3 0.7 all-gather.6.cloned.1.call-update
  7.9 0.9 slice_bitcast_fusion.5
  8.9 0.9 broadcast_in_dim.96
  9.7 20.2 %all-to-all-start = ((f32[8,128,128]{2,1,0:T(8,128)}), f32[8,128,128]{2,1,0:T(8,128)S(1)}, u32[]{:S(2)}, u32[]{:S(2)}) async-start(f32[8,128,128]{2,1,0:T(8,128)} %bitcast.10), calls=%async_computation | async-start | bytes 1048576 | tf_op jit(solution)/shard_map/all_to_all | solution.py:50
  30.0 0.8 gather_fusion
  30.8 1.9 collective-permute-start
  33.4 17.3 %all-to-all-done.refs_0_ = f32[8,128,128]{2,1,0:T(8,128)S(1)} async-done(((f32[8,128,128]{2,1,0:T(8,128)}), f32[8,128,128]{2,1,0:T(8,128)S(1)}, u32[]{:S(2)}, u32[]{:S(2)}) %all-to-all-start) | async-done | bytes 524320 | tf_op jit(solution)/shard_map/all_to_all | solution.py:50
  50.7 0.6 broadcast_in_dim.97
  51.3 17.9 %all-to-all-start.1 = ((s32[8,1,16]{2,1,0:T(1,128)}), s32[8,1,16]{2,1,0:T(1,128)S(1)}, u32[]{:S(2)}, u32[]{:S(2)}) async-start(s32[8,1,16]{2,1,0:T(1,128)} %broadcast_in_dim.97), calls=%async_computation.1 | async-start | bytes 8192 | tf_op jit(solution)/shard_map/all_to_all | solution.py:50
  69.3 1.9 collective-permute-start.3
  71.3 5.5 %collective-permute-start.2 = (f32[4,128,128]{2,1,0:T(8,128)S(1)}, f32[4,128,128]{2,1,0:T(8,128)S(1)}, u32[]{:S(2)}, u32[]{:S(2)}) collective-permute-start(f32[4,128,128]{2,1,0:T(8,128)S(1)} %get-tuple-element.48), channel_id=1, source_target_pairs={{0,224},{16,240},{32,0},{48,16},{64,32},{80,48},{96,64},{112,80},{... | collective-permute-start | bytes 786440 | tf_op jit(solution)/shard_map/ppermute | solution.py:42
  76.7 1.9 collective-permute-start.4
  78.7 4.6 %collective-permute-start.1 = (f32[8,128,128]{2,1,0:T(8,128)S(1)}, f32[8,128,128]{2,1,0:T(8,128)S(1)}, u32[]{:S(2)}, u32[]{:S(2)}) collective-permute-start(f32[8,128,128]{2,1,0:T(8,128)S(1)} %all-to-all-done.refs_0_), channel_id=1, source_target_pairs={{0,240},{16,0},{32,16},{48,32},{64,48},{80,64},{96,80},{112,96},{1... | collective-permute-start | bytes 1572872 | tf_op jit(solution)/shard_map/ppermute | solution.py:42
  83.2 0.5 broadcast.358
  83.8 0.7 reduce.8
  84.5 0.6 convert_reduce_fusion.2
  85.3 0.7 add_select_fusion.2
  86.1 1.4 pad_add_fusion.2.place_ref
  87.5 10.8 %collective-permute-done.4.refs_4_ = f32[8,128,128]{2,1,0:T(8,128)S(1)} collective-permute-done((f32[8,128,128]{2,1,0:T(8,128)S(1)}, f32[8,128,128]{2,1,0:T(8,128)S(1)}, u32[]{:S(2)}, u32[]{:S(2)}) %collective-permute-start.4) | collective-permute-done | bytes 524320 | tf_op jit(solution)/shard_map/ppermute | solution.py:42
  98.3 0.5 collective-permute-done.1.refs_1_
  98.8 5.6 %shard_map.95 = f32[32,128,128]{2,1,0:T(8,128)} custom-call(s32[3]{0:T(128)S(1)} %pad_add_fusion.2.place_ref, s32[128]{0:T(128)S(1)} %select_reduce_fusion.list_ref, f32[128,128,128]{2,1,0:T(8,128)} %bitcast.73, f32[8,128,128]{2,1,0:T(8,128)S(1)} %all-to-all-done.refs_0_, f32[8,128,128]{2,1,0:T(8,128)S(1)} %collective-permute-done.1.refs_1_, ...), custom_call_target="tpu_custom_call" | custom-call | tf_op jit(solution)/shard_map/pallas_call | solution.py:130
  104.4 4.4 %shard_map.96 = f32[32,128,128]{2,1,0:T(8,128)S(1)} custom-call(s32[3]{0:T(128)S(1)} %pad_add_fusion.2.place_ref, s32[128]{0:T(128)S(1)} %select_reduce_fusion.list_ref, f32[128,128,128]{2,1,0:T(8,128)} %bitcast.74, f32[8,128,128]{2,1,0:T(8,128)S(1)} %all-to-all-done.refs_0_, f32[8,128,128]{2,1,0:T(8,128)S(1)} %collective-permute-done.1.refs_1_, ...), custom_call_target="tpu_custom_call" | custom-call | tf_op jit(solution)/shard_map/pallas_call | solution.py:130
  108.7 28.6 %all_to_all.49 = f32[4,8,128,128]{3,2,1,0:T(8,128)S(1)} all-to-all(f32[4,8,128,128]{3,2,1,0:T(8,128)S(1)} %bitcast.71), channel_id=1, replica_groups={{0,256,512,768},{16,272,528,784},{32,288,544,800},{48,304,560,816},{64,..., dimensions={0} | all-to-all | bytes 4194304 | tf_op jit(solution)/shard_map/all_to_all | solution.py:50
  137.4 1.0 reduce_sum.123
  138.4 7.9 %all-to-all-start.4 = ((f32[8,128,128]{2,1,0:T(8,128)}), f32[8,128,128]{2,1,0:T(8,128)S(1)}, u32[]{:S(2)}, u32[]{:S(2)}) async-start(f32[8,128,128]{2,1,0:T(8,128)} %reduce_sum.123), calls=%async_computation.5 | async-start | bytes 1048576 | tf_op jit(solution)/shard_map/all_to_all | solution.py:50
  146.3 15.3 %all-to-all-done.4 = f32[8,128,128]{2,1,0:T(8,128)S(1)} async-done(((f32[8,128,128]{2,1,0:T(8,128)}), f32[8,128,128]{2,1,0:T(8,128)S(1)}, u32[]{:S(2)}, u32[]{:S(2)}) %all-to-all-start.4) | async-done | bytes 524320 | tf_op jit(solution)/shard_map/all_to_all | solution.py:50
  161.6 3.4 %all-to-all-start.2 = ((f32[4,128,128]{2,1,0:T(8,128)}), f32[4,128,128]{2,1,0:T(8,128)S(1)}, u32[]{:S(2)}, u32[]{:S(2)}) async-start(f32[4,128,128]{2,1,0:T(8,128)} %reduce-scatter.2.cloned.1.call-done), calls=%async_computation.3 | async-start | bytes 524288 | tf_op jit(solution)/shard_map/all_to_all | solution.py:50
  165.1 5.4 %all-to-all-done.2 = f32[4,128,128]{2,1,0:T(8,128)S(1)} async-done(((f32[4,128,128]{2,1,0:T(8,128)}), f32[4,128,128]{2,1,0:T(8,128)S(1)}, u32[]{:S(2)}, u32[]{:S(2)}) %all-to-all-start.2) | async-done | bytes 262176 | tf_op jit(solution)/shard_map/all_to_all | solution.py:50
  170.5 0.3 fusion.8
  171.0 6.2 %collective-permute-start.5 = (f32[2,3,64]{2,0,1:T(2,128)S(1)}, f32[2,3,64]{2,0,1:T(2,128)S(1)}, u32[]{:S(2)}, u32[]{:S(2)}) collective-permute-start(f32[2,3,64]{2,0,1:T(2,128)S(1)} %pad_maximum_fusion.2), channel_id=1, source_target_pairs={{0,1},{1,0},{2,3},{3,2},{4,5},{5,4},{6,7},{7,6},{8,9},{9,8},{10,11... | collective-permute-start | bytes 4616 | tf_op jit(solution)/shard_map/ppermute | solution.py:46
  177.2 0.8 collective-permute-done.5
  178.3 0.5 convolution_bitcast_fusion
  178.8 9.5 %all_to_all.50 = f32[4,128,128]{2,1,0:T(8,128)} all-to-all(f32[4,128,128]{2,1,0:T(8,128)S(1)} %broadcast_in_dim.101), channel_id=1, replica_groups={{0,256,512,768},{16,272,528,784},{32,288,544,800},{48,304,560,816},{64,..., dimensions={0} | all-to-all | bytes 524288 | tf_op jit(solution)/shard_map/all_to_all | solution.py:50
  188.4 18.1 %all_to_all.51 = f32[8,128,128]{2,1,0:T(8,128)S(1)} all-to-all(f32[8,128,128]{2,1,0:T(8,128)S(1)} %broadcast_in_dim.103), channel_id=1, replica_groups={{0,2,4,6,8,10,12,14},{1,3,5,7,9,11,13,15},{16,18,20,22,24,26,28,30},{17..., dimensions={0} | all-to-all | bytes 1048576 | tf_op jit(solution)/shard_map/all_to_all | solution.py:50
  206.8 26.5 %all_to_all.52 = f32[4,8,128,128]{3,2,1,0:T(8,128)} all-to-all(f32[4,8,128,128]{3,2,1,0:T(8,128)S(1)} %broadcast_in_dim.104), channel_id=1, replica_groups={{0,256,512,768},{16,272,528,784},{32,288,544,800},{48,304,560,816},{64,..., dimensions={0} | all-to-all | bytes 4194304 | tf_op jit(solution)/shard_map/all_to_all | solution.py:50
  233.3 1.6 copy-done
  234.9 8.1 %shard_map.97 = (f32[8,128,128]{2,1,0:T(8,128)S(1)}, f32[8,128,128]{2,1,0:T(8,128)S(1)}, f32[4,128,128]{2,1,0:T(8,128)S(1)}, f32[4,128,128]{2,1,0:T(8,128)S(1)}, f32[8,128,128]{2,1,0:T(8,128)S(1)}) custom-call(s32[3]{0:T(128)S(1)} %pad_add_fusion.2.place_ref, s32[128]{0:T(128)S(1)} %select_reduce_fusion.list_ref, f32[128,128,128]{2,1,0:T(8,128)} %bitcast.75, ...), custom_call_target="tpu_custom_call" | custom-call | tf_op jit(solution)/shard_map/pallas_call | solution.py:130
  242.9 1.9 collective-permute-start.6
  244.9 5.7 %collective-permute-start.7 = (f32[8,128,128]{2,1,0:T(8,128)S(1)}, f32[8,128,128]{2,1,0:T(8,128)S(1)}, u32[]{:S(2)}, u32[]{:S(2)}) collective-permute-start(f32[8,128,128]{2,1,0:T(8,128)S(1)} %get-tuple-element.33), channel_id=1, source_target_pairs={{0,240},{16,0},{32,16},{48,32},{64,48},{80,64},{96,80},{112,96},{1... | collective-permute-start | bytes 1572872 | tf_op jit(solution)/shard_map/ppermute | solution.py:42
  250.6 1.9 collective-permute-start.8
  252.5 5.5 %collective-permute-start.9 = (f32[4,128,128]{2,1,0:T(8,128)S(1)}, f32[4,128,128]{2,1,0:T(8,128)}, u32[]{:S(2)}, u32[]{:S(2)}) collective-permute-start(f32[4,128,128]{2,1,0:T(8,128)S(1)} %get-tuple-element.35), channel_id=1, source_target_pairs={{0,224},{16,240},{32,0},{48,16},{64,32},{80,48},{96,64},{112,80},{... | collective-permute-start | bytes 786440 | tf_op jit(solution)/shard_map/ppermute | solution.py:42
  258.2 7.8 %collective-permute-done.8 = f32[4,128,128]{2,1,0:T(8,128)S(1)} collective-permute-done((f32[4,128,128]{2,1,0:T(8,128)S(1)}, f32[4,128,128]{2,1,0:T(8,128)S(1)}, u32[]{:S(2)}, u32[]{:S(2)}) %collective-permute-start.8) | collective-permute-done | bytes 262176 | tf_op jit(solution)/shard_map/ppermute | solution.py:42
  266.0 0.5 collective-permute-done.9
  266.4 1.9 fusion
  268.4 16.9 %all-to-all-start.8 = ((f32[8,128,128]{2,1,0:T(8,128)}), f32[8,128,128]{2,1,0:T(8,128)S(1)}, u32[]{:S(2)}, u32[]{:S(2)}) async-start(f32[8,128,128]{2,1,0:T(8,128)} %fusion), calls=%async_computation.9 | async-start | bytes 1048576 | tf_op jit(solution)/shard_map/all_to_all | solution.py:50
  285.2 0.6 fusion.40
  287.1 23.3 %all-to-all-done.8 = f32[8,128,128]{2,1,0:T(8,128)S(1)} async-done(((f32[8,128,128]{2,1,0:T(8,128)}), f32[8,128,128]{2,1,0:T(8,128)S(1)}, u32[]{:S(2)}, u32[]{:S(2)}) %all-to-all-start.8) | async-done | bytes 524320 | tf_op jit(solution)/shard_map/all_to_all | solution.py:50
  310.5 0.7 pad_maximum_fusion.1
  (57 shorter events, 1.5 us)
Async XLA Ops:
  7.2 22.8 %copy-start.4 = (s32[1,64]{1,0:T(1,128)S(1)}, s32[1,64]{1,0:T(1,128)}, u32[]{:S(2)}) copy-start(s32[1,64]{1,0:T(1,128)} %param.14) | copy-start | bytes 772
  7.2 22.8 %copy-start.1 = (s32[1,64]{1,0:T(1,128)S(1)}, s32[1,64]{1,0:T(1,128)}, u32[]{:S(2)}) copy-start(s32[1,64]{1,0:T(1,128)} %param.13) | copy-start | bytes 772
  7.2 23.6 %copy-start.2 = (s32[1,64]{1,0:T(1,128)S(1)}, s32[1,64]{1,0:T(1,128)}, u32[]{:S(2)}) copy-start(s32[1,64]{1,0:T(1,128)} %param.15) | copy-start | bytes 772
  7.2 23.6 %copy-start.3 = (s32[1,64]{1,0:T(1,128)S(1)}, s32[1,64]{1,0:T(1,128)}, u32[]{:S(2)}) copy-start(s32[1,64]{1,0:T(1,128)} %param.12) | copy-start | bytes 772
  7.2 26.2 %copy-start.5 = (s32[1,16]{1,0:T(1,128)S(1)}, s32[1,16]{1,0:T(1,128)}, u32[]{:S(2)}) copy-start(s32[1,16]{1,0:T(1,128)} %param.10) | copy-start | bytes 196
  7.2 91.6 %all-gather.6.cloned.1.call-start = ((), (), s32[]{:S(2)}) async-start(), calls=%async_computation.12 | async-start | bytes 9437184 | tf_op jit(solution)/shard_map/all_gather | solution.py:169
  9.7 41.0 %all-to-all-start = ((f32[8,128,128]{2,1,0:T(8,128)}), f32[8,128,128]{2,1,0:T(8,128)S(1)}, u32[]{:S(2)}, u32[]{:S(2)}) async-start(f32[8,128,128]{2,1,0:T(8,128)} %bitcast.10), calls=%async_computation | async-start | bytes 1048576 | tf_op jit(solution)/shard_map/all_to_all | solution.py:50
  30.8 56.7 %collective-permute-start = (s32[4,64]{1,0:T(4,128)S(1)}, s32[4,64]{1,0:T(4,128)S(1)}, u32[]{:S(2)}, u32[]{:S(2)}) collective-permute-start(s32[4,64]{1,0:T(4,128)S(1)} %pad_add_fusion.1), channel_id=1, source_target_pairs={{0,1},{1,0},{2,3},{3,2},{4,5},{5,4},{6,7},{7,6},{8,9},{9,8},{10,11... | collective-permute-start | bytes 3080 | tf_op jit(solution)/shard_map/ppermute | solution.py:46
  51.3 31.9 %all-to-all-start.1 = ((s32[8,1,16]{2,1,0:T(1,128)}), s32[8,1,16]{2,1,0:T(1,128)S(1)}, u32[]{:S(2)}, u32[]{:S(2)}) async-start(s32[8,1,16]{2,1,0:T(1,128)} %broadcast_in_dim.97), calls=%async_computation.1 | async-start | bytes 8192 | tf_op jit(solution)/shard_map/all_to_all | solution.py:50
  69.3 92.3 %reduce-scatter.2.cloned.1.call-start = ((), (), s32[]{:S(2)}) async-start(), calls=%async_computation.10 | async-start | bytes 2359296 | tf_op jit(solution)/shard_map/reduce_scatter | solution.py:190
  69.3 18.1 %collective-permute-start.3 = (f32[4,128,128]{2,1,0:T(8,128)S(1)}, f32[4,128,128]{2,1,0:T(8,128)S(1)}, u32[]{:S(2)}, u32[]{:S(2)}) collective-permute-start(f32[4,128,128]{2,1,0:T(8,128)S(1)} %get-tuple-element.47), channel_id=1, source_target_pairs={{0,32},{16,48},{32,64},{48,80},{64,96},{80,112},{96,128},{112,144}... | collective-permute-start | bytes 786440 | tf_op jit(solution)/shard_map/ppermute | solution.py:42
  71.3 16.2 %collective-permute-start.2 = (f32[4,128,128]{2,1,0:T(8,128)S(1)}, f32[4,128,128]{2,1,0:T(8,128)S(1)}, u32[]{:S(2)}, u32[]{:S(2)}) collective-permute-start(f32[4,128,128]{2,1,0:T(8,128)S(1)} %get-tuple-element.48), channel_id=1, source_target_pairs={{0,224},{16,240},{32,0},{48,16},{64,32},{80,48},{96,64},{112,80},{... | collective-permute-start | bytes 786440 | tf_op jit(solution)/shard_map/ppermute | solution.py:42
  76.7 21.6 %collective-permute-start.4 = (f32[8,128,128]{2,1,0:T(8,128)S(1)}, f32[8,128,128]{2,1,0:T(8,128)S(1)}, u32[]{:S(2)}, u32[]{:S(2)}) collective-permute-start(f32[8,128,128]{2,1,0:T(8,128)S(1)} %all-to-all-done.refs_0_), channel_id=1, source_target_pairs={{0,16},{16,32},{32,48},{48,64},{64,80},{80,96},{96,112},{112,128},... | collective-permute-start | bytes 1572872 | tf_op jit(solution)/shard_map/ppermute | solution.py:42
  78.7 20.1 %collective-permute-start.1 = (f32[8,128,128]{2,1,0:T(8,128)S(1)}, f32[8,128,128]{2,1,0:T(8,128)S(1)}, u32[]{:S(2)}, u32[]{:S(2)}) collective-permute-start(f32[8,128,128]{2,1,0:T(8,128)S(1)} %all-to-all-done.refs_0_), channel_id=1, source_target_pairs={{0,240},{16,0},{32,16},{48,32},{64,48},{80,64},{96,80},{112,96},{1... | collective-permute-start | bytes 1572872 | tf_op jit(solution)/shard_map/ppermute | solution.py:42
  138.4 23.2 %all-to-all-start.4 = ((f32[8,128,128]{2,1,0:T(8,128)}), f32[8,128,128]{2,1,0:T(8,128)S(1)}, u32[]{:S(2)}, u32[]{:S(2)}) async-start(f32[8,128,128]{2,1,0:T(8,128)} %reduce_sum.123), calls=%async_computation.5 | async-start | bytes 1048576 | tf_op jit(solution)/shard_map/all_to_all | solution.py:50
  161.6 8.9 %all-to-all-start.2 = ((f32[4,128,128]{2,1,0:T(8,128)}), f32[4,128,128]{2,1,0:T(8,128)S(1)}, u32[]{:S(2)}, u32[]{:S(2)}) async-start(f32[4,128,128]{2,1,0:T(8,128)} %reduce-scatter.2.cloned.1.call-done), calls=%async_computation.3 | async-start | bytes 524288 | tf_op jit(solution)/shard_map/all_to_all | solution.py:50
  165.0 68.3 %all-gather.4.cloned.1.call-start = ((), (), s32[]{:S(2)}) async-start(), calls=%async_computation.11 | async-start | bytes 2359296 | tf_op jit(solution)/shard_map/all_gather | solution.py:234
  171.0 7.0 %collective-permute-start.5 = (f32[2,3,64]{2,0,1:T(2,128)S(1)}, f32[2,3,64]{2,0,1:T(2,128)S(1)}, u32[]{:S(2)}, u32[]{:S(2)}) collective-permute-start(f32[2,3,64]{2,0,1:T(2,128)S(1)} %pad_maximum_fusion.2), channel_id=1, source_target_pairs={{0,1},{1,0},{2,3},{3,2},{4,5},{5,4},{6,7},{7,6},{8,9},{9,8},{10,11... | collective-permute-start | bytes 4616 | tf_op jit(solution)/shard_map/ppermute | solution.py:46
  233.3 1.6 copy-start
  242.9 23.5 %collective-permute-start.6 = (f32[8,128,128]{2,1,0:T(8,128)S(1)}, f32[8,128,128]{2,1,0:T(8,128)S(1)}, u32[]{:S(2)}, u32[]{:S(2)}) collective-permute-start(f32[8,128,128]{2,1,0:T(8,128)S(1)} %get-tuple-element.32), channel_id=1, source_target_pairs={{0,16},{16,32},{32,48},{48,64},{64,80},{80,96},{96,112},{112,128},... | collective-permute-start | bytes 1572872 | tf_op jit(solution)/shard_map/ppermute | solution.py:42
  244.9 21.6 %collective-permute-start.7 = (f32[8,128,128]{2,1,0:T(8,128)S(1)}, f32[8,128,128]{2,1,0:T(8,128)S(1)}, u32[]{:S(2)}, u32[]{:S(2)}) collective-permute-start(f32[8,128,128]{2,1,0:T(8,128)S(1)} %get-tuple-element.33), channel_id=1, source_target_pairs={{0,240},{16,0},{32,16},{48,32},{64,48},{80,64},{96,80},{112,96},{1... | collective-permute-start | bytes 1572872 | tf_op jit(solution)/shard_map/ppermute | solution.py:42
  250.6 15.4 %collective-permute-start.8 = (f32[4,128,128]{2,1,0:T(8,128)S(1)}, f32[4,128,128]{2,1,0:T(8,128)S(1)}, u32[]{:S(2)}, u32[]{:S(2)}) collective-permute-start(f32[4,128,128]{2,1,0:T(8,128)S(1)} %get-tuple-element.34), channel_id=1, source_target_pairs={{0,32},{16,48},{32,64},{48,80},{64,96},{80,112},{96,128},{112,144}... | collective-permute-start | bytes 786440 | tf_op jit(solution)/shard_map/ppermute | solution.py:42
  252.5 13.9 %collective-permute-start.9 = (f32[4,128,128]{2,1,0:T(8,128)S(1)}, f32[4,128,128]{2,1,0:T(8,128)}, u32[]{:S(2)}, u32[]{:S(2)}) collective-permute-start(f32[4,128,128]{2,1,0:T(8,128)S(1)} %get-tuple-element.35), channel_id=1, source_target_pairs={{0,224},{16,240},{32,0},{48,16},{64,32},{80,48},{96,64},{112,80},{... | collective-permute-start | bytes 786440 | tf_op jit(solution)/shard_map/ppermute | solution.py:42
  268.4 42.1 %all-to-all-start.8 = ((f32[8,128,128]{2,1,0:T(8,128)}), f32[8,128,128]{2,1,0:T(8,128)S(1)}, u32[]{:S(2)}, u32[]{:S(2)}) async-start(f32[8,128,128]{2,1,0:T(8,128)} %fusion), calls=%async_computation.9 | async-start | bytes 1048576 | tf_op jit(solution)/shard_map/all_to_all | solution.py:50
Sparse Core Ops, SparseCore 0:
  10.8 69.4 all-gather.5
  104.5 40.8 reduce-scatter.1
  188.5 40.2 all-gather.3

commit v7 on v6

--- a/solution.py
+++ b/solution.py
@@ -16,6 +16,7 @@
 CB = 64
 PAIRS = 64
 ENTRIES = 2 * NX * SLOTS
+EXTRA = 32
 VMEM_LIMIT = 48 * 1024 * 1024
 
 precise = lax.Precision.HIGHEST
@@ -67,76 +68,136 @@
     return lax.dot_general(rows, columns, dims, preferred_element_type=jnp.float32)
 
 
-def copy_block(entry, place, source_ref, blocks_ref, arrived):
-    rows = source_ref.at[jnp.bitwise_and(entry, ENTRIES - 1)]
-    return pltpu.make_async_copy(rows, blocks_ref.at[place], arrived.at[place])
-
-
-def start_copies(first, last, list_ref, source_ref, blocks_ref, arrived):
-    @pl.loop(first, last)
-    def _(index):
-        copy_block(list_ref[index], index, source_ref, blocks_ref, arrived).start()
-
-
-def for_live_blocks(first, last, place_ref, list_ref, source_ref, blocks_ref, arrived, body):
-    @pl.loop(first, last)
-    def _(index):
-        entry = list_ref[index]
-        number, position = jnp.bitwise_and(entry, ENTRIES - 1), entry // ENTRIES
-        z = jnp.bitwise_and(position, NZ - 1)
-        near = jnp.bitwise_and(z - place_ref[0], 3) * 8 + (z // 4) * 2
-        near = near + jnp.bitwise_and(number // SLOTS, 1)
-        copy_block(entry, index, source_ref, blocks_ref, arrived).wait()
-        body(number // (2 * SLOTS), blocks_ref[index], position // (2 * CB), near, index)
+def copy_block(entry, place, source_ref, blocks_ref, arrived, rows=slice(0, BLOCK)):
+    window = pl.ds(rows.start, rows.stop - rows.start)
+    block = source_ref.at[jnp.bitwise_and(entry, ENTRIES - 1), window]
+    return pltpu.make_async_copy(block, blocks_ref.at[place, window], arrived.at[place])
+
+
+def decode(entry, own_z):
+    number, position = jnp.bitwise_and(entry, ENTRIES - 1), entry // ENTRIES
+    z = jnp.bitwise_and(position, NZ - 1)
+    near = jnp.bitwise_and(z - own_z, 3) * 8 + (z // 4) * 2
+    near = near + jnp.bitwise_and(number // SLOTS, 1)
+    return number // (2 * SLOTS), position // (2 * CB), near
+
+
+def for_pairs(first, last, wait, compute, add):
+    @pl.loop(0, (last - first + 1) // 2)
+    def _(step):
+        index = first + 2 * step
+        both = index + 1 < last
+        other = jnp.where(both, index + 1, index)
+        wait(index)
+
+        @pl.when(both)
+        def _():
+            wait(other)
+
+        value, other_value = compute(index), compute(other)
+        add(index, value)
+        add(other, jnp.where(both, other_value, 0.0))
 
 
 def forward_kernel(odd, place_ref, list_ref, source_ref, *refs):
-    parts, out_ref, rows_ref, rest = refs[:5], refs[5], refs[6], refs[7:]
-    first = place_ref[1] if odd else 0
-    last = place_ref[2] if odd else place_ref[1]
-    start_copies(first, last, list_ref, source_ref, *rest)
+    parts, out_ref, rows_ref, blocks_ref, arrived = refs[:5], refs[5], refs[6], refs[7], refs[8]
+    own_z, even_end, end = place_ref[0], place_ref[1], place_ref[2]
+
+    def copy(index, rows):
+        return copy_block(list_ref[index], index, source_ref, blocks_ref, arrived, rows)
+
+    top, rest, whole = slice(0, EXTRA), slice(EXTRA, BLOCK), slice(0, BLOCK)
+    if odd:
+        spans = [(even_end, end, rest, slice(0, BLOCK - EXTRA))]
+    else:
+        spans = [(0, even_end, whole, whole), (even_end, end, top, slice(BLOCK, BLOCK + EXTRA))]
+    for first, last, rows, _ in spans:
+
+        @pl.loop(first, last)
+        def _(index):
+            copy(index, rows).start()
+
     out_ref[...] = jnp.zeros_like(out_ref)
     start = 0
     for part in parts:
         rows_ref[pl.ds(start, part.shape[0])] = part[...]
         start += part.shape[0]
 
-    def body(x, block, y, near, index):
-        place = x * NY + y if odd else y * NX + x
-        out_ref[place] += product(block, rows_ref[near], 1)
-
-    for_live_blocks(first, last, place_ref, list_ref, source_ref, *rest, body)
-
-
-def backward_kernel(place_ref, list_ref, source_ref, even, odd, *refs):
-    outs, total_ref, rest = refs[:5], refs[5], refs[6:]
-    start_copies(0, place_ref[2], list_ref, source_ref, *rest)
+    for first, last, rows, out_rows in spans:
+
+        def compute(index):
+            _, _, near = decode(list_ref[index], own_z)
+            return product(blocks_ref[index, rows], rows_ref[near], 1)
+
+        def add(index, value):
+            x, y, _ = decode(list_ref[index], own_z)
+            out_ref[x * NY + y if odd else y * NX + x, out_rows] += value
+
+        for_pairs(first, last, lambda index: copy(index, rows).wait(), compute, add)
+
+
+def backward_kernel(place_ref, list_ref, source_ref, even_ref, odd_ref, *refs):
+    outs, total_ref, blocks_ref, arrived, rows_ref, rows_arrived = refs[:5], *refs[5:]
+    own_z, even_end, end = place_ref[0], place_ref[1], place_ref[2]
+
+    def copy(index):
+        return copy_block(list_ref[index], index, source_ref, blocks_ref, arrived)
+
+    def copy_rows(index, source, place, source_rows, rows):
+        return pltpu.make_async_copy(
+            source.at[place, pl.ds(source_rows, rows.stop - rows.start)],
+            rows_ref.at[index, pl.ds(rows.start, rows.stop - rows.start)],
+            rows_arrived.at[index],
+        )
+
+    @pl.loop(0, even_end)
+    def _(index):
+        x, y, _ = decode(list_ref[index], own_z)
+        copy(index).start()
+        copy_rows(index, even_ref, y * NX + x, 0, slice(0, BLOCK)).start()
+
+    @pl.loop(even_end, end)
+    def _(index):
+        x, y, _ = decode(list_ref[index], own_z)
+        copy(index).start()
+        copy_rows(index, even_ref, y * NX + x, BLOCK, slice(0, EXTRA)).start()
+        copy_rows(index, odd_ref, x * NY + y, 0, slice(EXTRA, BLOCK)).start()
+
     total_ref[...] = jnp.zeros_like(total_ref)
 
-    def body(x, block, y, near, index):
-        rows = jnp.where(index < place_ref[1], even[y * NX + x], odd[x * NY + y])
-        total_ref[near] += product(block, rows, 0)
-
-    for_live_blocks(0, place_ref[2], place_ref, list_ref, source_ref, *rest, body)
+    def wait(index):
+        copy(index).wait()
+        copy_rows(index, even_ref, 0, 0, slice(0, BLOCK)).wait()
+
+    def compute(index):
+        return product(blocks_ref[index], rows_ref[index], 0)
+
+    def add(index, value):
+        _, _, near = decode(list_ref[index], own_z)
+        total_ref[near] += value
+
+    for_pairs(0, end, wait, compute, add)
     start = 0
     for out in outs:
         out[...] = total_ref[pl.ds(start, out.shape[0])]
         start += out.shape[0]
 
 
-def call_kernel(body, place, entries, source, arrays, out_blocks):
+def call_kernel(body, place, entries, source, arrays, out_shapes, in_place=True):
     whole = pl.BlockSpec(memory_space=pltpu.VMEM)
     scalars = pl.BlockSpec(memory_space=pltpu.SMEM)
+    anywhere = pl.BlockSpec(memory_space=pl.ANY)
+    copies = [
+        pltpu.VMEM((ENTRIES, BLOCK, BLOCK), jnp.float32),
+        pltpu.SemaphoreType.DMA((ENTRIES,)),
+    ]
     return pl.pallas_call(
         body,
-        out_shape=[jax.ShapeDtypeStruct((n, BLOCK, HALF), jnp.float32) for n in out_blocks],
-        in_specs=[scalars, scalars, pl.BlockSpec(memory_space=pl.ANY)] + [whole] * len(arrays),
-        out_specs=[whole] * len(out_blocks),
-        scratch_shapes=[
-            pltpu.VMEM((2 * NZ, BLOCK, HALF), jnp.float32),
-            pltpu.VMEM((ENTRIES, BLOCK, BLOCK), jnp.float32),
-            pltpu.SemaphoreType.DMA((ENTRIES,)),
-        ],
+        out_shape=[jax.ShapeDtypeStruct((*shape, HALF), jnp.float32) for shape in out_shapes],
+        in_specs=[scalars, scalars, anywhere] + [whole if in_place else anywhere] * len(arrays),
+        out_specs=[whole] * len(out_shapes),
+        scratch_shapes=[pltpu.VMEM((2 * NZ, BLOCK, HALF), jnp.float32)]
+        + copies * (1 if in_place else 2),
         compiler_params=pltpu.CompilerParams(vmem_limit_bytes=VMEM_LIMIT),
     )(place, entries, source, *arrays)
 
@@ -183,18 +244,19 @@
         (source, other_picks, entries, place, *parts)
     )
     even, odd = (functools.partial(forward_kernel, odd) for odd in (False, True))
-    (first,) = call_kernel(even, place, entries, source, parts, [NX * NY])
+    (first,) = call_kernel(even, place, entries, source, parts, [(NX * NY, BLOCK + EXTRA)])
     entries, first = lax.optimization_barrier((entries, first))
-    (second,) = call_kernel(odd, place, entries, source, parts, [NX * NY])
+    (second,) = call_kernel(odd, place, entries, source, parts, [(NX * NY, BLOCK - EXTRA)])
 
     first = lax.psum_scatter(
         first, "col", scatter_dimension=0, tiled=True, axis_index_groups=Y_GROUPS
     )
-    second = second.reshape(NX, NY, BLOCK, HALF)
+    second = second.reshape(NX, NY * (BLOCK - EXTRA), HALF)
     second = jnp.sum(exchange(second, "row", X_GROUPS), axis=0)
-    second = jnp.sum(exchange(second, "col", Y_GROUPS), axis=0)
+    second = exchange(second.reshape(NY, BLOCK - EXTRA, HALF), "col", Y_GROUPS)
+    second = jnp.sum(second, axis=0)
     first = jnp.sum(exchange(first, "row", X_GROUPS), axis=0)
-    current = jnp.stack([first, second])
+    current = jnp.concatenate([first, second]).reshape(2, BLOCK, HALF)
 
     is_first = core == 0
     span_picks = [jnp.where(is_first, picks, other_picks), jnp.where(is_first, other_picks, picks)]
@@ -230,13 +292,17 @@
     )
     scaled = jnp.einsum("hpij,hpid->hjd", hot, row_grads, precision=precise)
 
-    first = exchange(jnp.broadcast_to(scaled[0][None], (NX, BLOCK, HALF)), "row", X_GROUPS)
+    all_rows = scaled.reshape(2 * BLOCK, HALF)
+    first, second = all_rows[: BLOCK + EXTRA], all_rows[BLOCK + EXTRA :]
+    first = exchange(jnp.broadcast_to(first[None], (NX, *first.shape)), "row", X_GROUPS)
     first = lax.all_gather(first, "col", axis=0, tiled=True, axis_index_groups=Y_GROUPS)
-    second = exchange(jnp.broadcast_to(scaled[1][None], (NY, BLOCK, HALF)), "col", Y_GROUPS)
-    second = jnp.broadcast_to(second[None], (NX, NY, BLOCK, HALF))
-    second = exchange(second, "row", X_GROUPS).reshape(NX * NY, BLOCK, HALF)
+    second = exchange(jnp.broadcast_to(second[None], (NY, *second.shape)), "col", Y_GROUPS)
+    second = second.reshape(NY * (BLOCK - EXTRA), HALF)
+    second = exchange(jnp.broadcast_to(second[None], (NX, *second.shape)), "row", X_GROUPS)
+    second = second.reshape(NX * NY, BLOCK - EXTRA, HALF)
+    shapes = [(n, BLOCK) for n in (8, 8, 4, 4, 8)]
     own, after, two, two_far, before = call_kernel(
-        backward_kernel, place, entries, source, [first, second], [8, 8, 4, 4, 8]
+        backward_kernel, place, entries, source, [first, second], shapes, in_place=False
     )
     two = jnp.concatenate([send_z(two, 2), send_z(two_far, -2)])
     near = (own + send_z(after, 1) + send_z(before, -1) + two).reshape(4, 2, BLOCK, HALF)

time: 325 us -> 325 us (level)
  waiting for transfers between devices: 82.4 us -> 102 us
  blocking collectives: 82.8 us -> 70.6 us
    all_to_all x4, blocking collectives: 82.8 us -> 70.6 us  [exchange(): lax.all_to_all(values, axis, split_axis=0, concat_axis=0, tiled=True, axi...]
    all_gather x1, waiting for transfers between devices: 0.01 us -> 10.7 us  [per_device(): lax.all_gather(first, 'col', axis=0, tiled=True, axis_index_groups=Y_GROUPS)]
    all_to_all x5, waiting for transfers between devices: 61.3 us -> 67.1 us  [exchange(): lax.all_to_all(values, axis, split_axis=0, concat_axis=0, tiled=True, axi...]
  transfers between devices with their start and end apart: 18 -> 18, of which waited for: 9 -> 10; matrix products, arithmetic and copies ran while one was open for 3% -> 3% of each run, Pallas kernels for 1% -> 1%
where the time goes in v7:
time: 325 us; the launch traced here: 322 us
  starting transfers between devices  105 us (32%)
  waiting for transfers between devices  102 us (31%)
  blocking collectives  70.6 us (22%)
  between operations  17.2 us (5%)
  Pallas kernels  15.7 us (5%)
  other arithmetic  6.58 us (2%)
  local copies, waits for them, and re-layouts  4.73 us (1%)
    all_to_all x4, blocking collectives, exchange(): lax.all_to_all(values, axis, split_axis=0, concat_axis=0, tiled=True, axi...  70.6 us
    all_to_all x5, waiting for transfers between devices, exchange(): lax.all_to_all(values, axis, split_axis=0, concat_axis=0, tiled=True, axi...  67.1 us
    all_to_all x5, starting transfers between devices, exchange(): lax.all_to_all(values, axis, split_axis=0, concat_axis=0, tiled=True, axi...  65.7 us
    ppermute x8, starting transfers between devices, send_z(): return lax.ppermute(values, 'row', pairs)  31.3 us
    ppermute x8, waiting for transfers between devices, send_z(): return lax.ppermute(values, 'row', pairs)  22.5 us
    pallas_call x3, Pallas kernels, call_kernel(): pl.pallas_call(body, out_shape=[jax.ShapeDtypeStruct((*shape, HALF), jnp....  15.7 us
    all_gather x1, waiting for transfers between devices, per_device(): lax.all_gather(first, 'col', axis=0, tiled=True, axis_index_groups=Y_GROUPS)  10.7 us
    ppermute x2, starting transfers between devices, swap_cores(): return lax.ppermute(values, 'col', CORE_SWAP)  7.41 us
  transfers between devices with their start and end apart: 18, of which 10 were waited for; matrix products, arithmetic and copies ran while one was open for 3% of the time, Pallas kernels for 1%

profile of v7, /device:TPU:1, one launch (start us, length us, event | category | flops | bytes accessed | tf_op | source)
XLA Modules:
  0.0 322.0 jit_solution(15049115546729943369)
XLA Ops:
  7.2 0.7 all-gather.6.cloned.1.call-update
  7.9 0.9 slice_bitcast_fusion.3
  8.8 0.9 broadcast_in_dim.95
  9.7 20.2 %all-to-all-start = ((f32[8,128,128]{2,1,0:T(8,128)}), f32[8,128,128]{2,1,0:T(8,128)S(1)}, u32[]{:S(2)}, u32[]{:S(2)}) async-start(f32[8,128,128]{2,1,0:T(8,128)} %bitcast.10), calls=%async_computation | async-start | bytes 1048576 | tf_op jit(solution)/shard_map/all_to_all | solution.py:51
  30.0 0.8 gather_fusion
  30.8 1.9 collective-permute-start
  33.4 17.3 %all-to-all-done.refs_0_ = f32[8,128,128]{2,1,0:T(8,128)S(1)} async-done(((f32[8,128,128]{2,1,0:T(8,128)}), f32[8,128,128]{2,1,0:T(8,128)S(1)}, u32[]{:S(2)}, u32[]{:S(2)}) %all-to-all-start) | async-done | bytes 524320 | tf_op jit(solution)/shard_map/all_to_all | solution.py:51
  50.8 0.6 broadcast_in_dim.96
  51.3 17.9 %all-to-all-start.1 = ((s32[8,1,16]{2,1,0:T(1,128)}), s32[8,1,16]{2,1,0:T(1,128)S(1)}, u32[]{:S(2)}, u32[]{:S(2)}) async-start(s32[8,1,16]{2,1,0:T(1,128)} %broadcast_in_dim.96), calls=%async_computation.1 | async-start | bytes 8192 | tf_op jit(solution)/shard_map/all_to_all | solution.py:51
  69.3 1.9 collective-permute-start.3
  71.3 5.5 %collective-permute-start.2 = (f32[4,128,128]{2,1,0:T(8,128)S(1)}, f32[4,128,128]{2,1,0:T(8,128)S(1)}, u32[]{:S(2)}, u32[]{:S(2)}) collective-permute-start(f32[4,128,128]{2,1,0:T(8,128)S(1)} %get-tuple-element.48), channel_id=1, source_target_pairs={{0,224},{16,240},{32,0},{48,16},{64,32},{80,48},{96,64},{112,80},{... | collective-permute-start | bytes 786440 | tf_op jit(solution)/shard_map/ppermute | solution.py:43
  76.7 1.9 collective-permute-start.4
  78.7 4.6 %collective-permute-start.1 = (f32[8,128,128]{2,1,0:T(8,128)S(1)}, f32[8,128,128]{2,1,0:T(8,128)S(1)}, u32[]{:S(2)}, u32[]{:S(2)}) collective-permute-start(f32[8,128,128]{2,1,0:T(8,128)S(1)} %all-to-all-done.refs_0_), channel_id=1, source_target_pairs={{0,240},{16,0},{32,16},{48,32},{64,48},{80,64},{96,80},{112,96},{1... | collective-permute-start | bytes 1572872 | tf_op jit(solution)/shard_map/ppermute | solution.py:43
  83.3 0.5 broadcast.359
  83.8 0.7 reduce.8
  84.5 0.6 convert_reduce_fusion.2
  85.3 0.7 add_select_fusion.2
  86.1 1.4 pad_add_fusion.2.place_ref
  87.5 10.8 %collective-permute-done.4.refs_4_ = f32[8,128,128]{2,1,0:T(8,128)S(1)} collective-permute-done((f32[8,128,128]{2,1,0:T(8,128)S(1)}, f32[8,128,128]{2,1,0:T(8,128)S(1)}, u32[]{:S(2)}, u32[]{:S(2)}) %collective-permute-start.4) | collective-permute-done | bytes 524320 | tf_op jit(solution)/shard_map/ppermute | solution.py:43
  98.3 0.5 collective-permute-done.1.refs_1_
  98.8 5.7 %shard_map.95 = f32[32,160,128]{2,1,0:T(8,128)} custom-call(s32[3]{0:T(128)S(1)} %pad_add_fusion.2.place_ref, s32[128]{0:T(128)S(1)} %select_reduce_fusion.list_ref, f32[128,128,128]{2,1,0:T(8,128)} %bitcast.72, f32[8,128,128]{2,1,0:T(8,128)S(1)} %all-to-all-done.refs_0_, f32[8,128,128]{2,1,0:T(8,128)S(1)} %collective-permute-done.1.refs_1_, ...), custom_call_target="tpu_custom_call" | custom-call | tf_op jit(solution)/shard_map/pallas_call | solution.py:194
  104.5 3.4 %shard_map.96 = f32[32,96,128]{2,1,0:T(8,128)S(1)} custom-call(s32[3]{0:T(128)S(1)} %pad_add_fusion.2.place_ref, s32[128]{0:T(128)S(1)} %select_reduce_fusion.list_ref, f32[128,128,128]{2,1,0:T(8,128)} %bitcast.73, f32[8,128,128]{2,1,0:T(8,128)S(1)} %all-to-all-done.refs_0_, f32[8,128,128]{2,1,0:T(8,128)S(1)} %collective-permute-done.1.refs_1_, ...), custom_call_target="tpu_custom_call" | custom-call | tf_op jit(solution)/shard_map/pallas_call | solution.py:194
  107.9 24.0 %all_to_all.49 = f32[4,768,128]{2,1,0:T(8,128)S(1)} all-to-all(f32[4,768,128]{2,1,0:T(8,128)S(1)} %bitcast.70), channel_id=1, replica_groups={{0,256,512,768},{16,272,528,784},{32,288,544,800},{48,304,560,816},{64,..., dimensions={0} | all-to-all | bytes 3145728 | tf_op jit(solution)/shard_map/all_to_all | solution.py:51
  131.9 0.9 reduce_sum.123
  132.8 8.3 %all-to-all-start.4 = ((f32[8,96,128]{2,1,0:T(8,128)}), f32[8,96,128]{2,1,0:T(8,128)S(1)}, u32[]{:S(2)}, u32[]{:S(2)}) async-start(f32[8,96,128]{2,1,0:T(8,128)} %bitcast.18), calls=%async_computation.5 | async-start | bytes 786432 | tf_op jit(solution)/shard_map/all_to_all | solution.py:51
  141.1 16.2 %all-to-all-done.4 = f32[8,96,128]{2,1,0:T(8,128)S(1)} async-done(((f32[8,96,128]{2,1,0:T(8,128)}), f32[8,96,128]{2,1,0:T(8,128)S(1)}, u32[]{:S(2)}, u32[]{:S(2)}) %all-to-all-start.4) | async-done | bytes 393248 | tf_op jit(solution)/shard_map/all_to_all | solution.py:51
  157.3 3.5 %all-to-all-start.2 = ((f32[4,160,128]{2,1,0:T(8,128)}), f32[4,160,128]{2,1,0:T(8,128)S(1)}, u32[]{:S(2)}, u32[]{:S(2)}) async-start(f32[4,160,128]{2,1,0:T(8,128)} %reduce-scatter.2.cloned.1.call-done), calls=%async_computation.3 | async-start | bytes 655360 | tf_op jit(solution)/shard_map/all_to_all | solution.py:51
  160.9 5.7 %all-to-all-done.2 = f32[4,160,128]{2,1,0:T(8,128)S(1)} async-done(((f32[4,160,128]{2,1,0:T(8,128)}), f32[4,160,128]{2,1,0:T(8,128)S(1)}, u32[]{:S(2)}, u32[]{:S(2)}) %all-to-all-start.2) | async-done | bytes 327712 | tf_op jit(solution)/shard_map/all_to_all | solution.py:51
  166.6 0.3 fusion.9
  167.1 5.5 %collective-permute-start.5 = (f32[2,3,64]{2,0,1:T(2,128)S(1)}, f32[2,3,64]{2,0,1:T(2,128)S(1)}, u32[]{:S(2)}, u32[]{:S(2)}) collective-permute-start(f32[2,3,64]{2,0,1:T(2,128)S(1)} %pad_maximum_fusion.3), channel_id=1, source_target_pairs={{0,1},{1,0},{2,3},{3,2},{4,5},{5,4},{6,7},{7,6},{8,9},{9,8},{10,11... | collective-permute-start | bytes 4616 | tf_op jit(solution)/shard_map/ppermute | solution.py:47
  172.6 0.8 collective-permute-done.5
  173.7 0.5 fusion.1
  174.3 9.9 %all_to_all.50 = f32[4,160,128]{2,1,0:T(8,128)} all-to-all(f32[4,160,128]{2,1,0:T(8,128)S(1)} %broadcast_in_dim.99), channel_id=1, replica_groups={{0,256,512,768},{16,272,528,784},{32,288,544,800},{48,304,560,816},{64,..., dimensions={0} | all-to-all | bytes 655360 | tf_op jit(solution)/shard_map/all_to_all | solution.py:51
  184.3 16.6 %all_to_all.51 = f32[8,96,128]{2,1,0:T(8,128)S(1)} all-to-all(f32[8,96,128]{2,1,0:T(8,128)S(1)} %broadcast_in_dim.100), channel_id=1, replica_groups={{0,2,4,6,8,10,12,14},{1,3,5,7,9,11,13,15},{16,18,20,22,24,26,28,30},{17..., dimensions={0} | all-to-all | bytes 786432 | tf_op jit(solution)/shard_map/all_to_all | solution.py:51
  201.0 20.0 %all_to_all.52 = f32[4,768,128]{2,1,0:T(8,128)S(1)} all-to-all(f32[4,768,128]{2,1,0:T(8,128)S(1)} %broadcast_in_dim.102), channel_id=1, replica_groups={{0,256,512,768},{16,272,528,784},{32,288,544,800},{48,304,560,816},{64,..., dimensions={0} | all-to-all | bytes 3145728 | tf_op jit(solution)/shard_map/all_to_all | solution.py:51
  221.0 10.7 %all-gather.4.cloned.1.call-done.even_ref = f32[32,160,128]{2,1,0:T(8,128)} async-done(((f32[4,160,128]{2,1,0:T(8,128)}), f32[32,160,128]{2,1,0:T(8,128)}) %all-gather.4.cloned.1.call-update) | async-done | bytes 2621456 | tf_op jit(solution)/shard_map/all_gather | solution.py:298
  231.7 6.6 %shard_map.97 = (f32[8,128,128]{2,1,0:T(8,128)S(1)}, f32[8,128,128]{2,1,0:T(8,128)S(1)}, f32[4,128,128]{2,1,0:T(8,128)}, f32[4,128,128]{2,1,0:T(8,128)S(1)}, f32[8,128,128]{2,1,0:T(8,128)S(1)}) custom-call(s32[3]{0:T(128)S(1)} %pad_add_fusion.2.place_ref, s32[128]{0:T(128)S(1)} %select_reduce_fusion.list_ref, f32[128,128,128]{2,1,0:T(8,128)} %bitcast.74, ...), custom_call_target="tpu_custom_call" | custom-call | tf_op jit(solution)/shard_map/pallas_call | solution.py:194
  238.3 2.9 collective-permute-start.6
  241.3 7.1 %collective-permute-start.7 = (f32[8,128,128]{2,1,0:T(8,128)S(1)}, f32[8,128,128]{2,1,0:T(8,128)S(1)}, u32[]{:S(2)}, u32[]{:S(2)}) collective-permute-start(f32[8,128,128]{2,1,0:T(8,128)S(1)} %get-tuple-element.33), channel_id=1, source_target_pairs={{0,240},{16,0},{32,16},{48,32},{64,48},{80,64},{96,80},{112,96},{1... | collective-permute-start | bytes 1572872 | tf_op jit(solution)/shard_map/ppermute | solution.py:43
  248.4 1.9 collective-permute-start.8
  250.3 5.5 %collective-permute-start.9 = (f32[4,128,128]{2,1,0:T(8,128)S(1)}, f32[4,128,128]{2,1,0:T(8,128)S(1)}, u32[]{:S(2)}, u32[]{:S(2)}) collective-permute-start(f32[4,128,128]{2,1,0:T(8,128)S(1)} %get-tuple-element.35), channel_id=1, source_target_pairs={{0,224},{16,240},{32,0},{48,16},{64,32},{80,48},{96,64},{112,80},{... | collective-permute-start | bytes 786440 | tf_op jit(solution)/shard_map/ppermute | solution.py:43
  256.0 8.1 %collective-permute-done.8 = f32[4,128,128]{2,1,0:T(8,128)S(1)} collective-permute-done((f32[4,128,128]{2,1,0:T(8,128)}, f32[4,128,128]{2,1,0:T(8,128)S(1)}, u32[]{:S(2)}, u32[]{:S(2)}) %collective-permute-start.8) | collective-permute-done | bytes 262176 | tf_op jit(solution)/shard_map/ppermute | solution.py:43
  264.1 3.1 collective-permute-done.9
  267.2 0.9 fusion
  268.1 15.8 %all-to-all-start.8 = ((f32[8,128,128]{2,1,0:T(8,128)}), f32[8,128,128]{2,1,0:T(8,128)S(1)}, u32[]{:S(2)}, u32[]{:S(2)}) async-start(f32[8,128,128]{2,1,0:T(8,128)} %fusion), calls=%async_computation.9 | async-start | bytes 1048576 | tf_op jit(solution)/shard_map/all_to_all | solution.py:51
  283.9 0.6 fusion.38
  285.8 27.9 %all-to-all-done.8 = f32[8,128,128]{2,1,0:T(8,128)S(1)} async-done(((f32[8,128,128]{2,1,0:T(8,128)}), f32[8,128,128]{2,1,0:T(8,128)S(1)}, u32[]{:S(2)}, u32[]{:S(2)}) %all-to-all-start.8) | async-done | bytes 524320 | tf_op jit(solution)/shard_map/all_to_all | solution.py:51
  313.7 0.7 pad_maximum_fusion.2
  (57 shorter events, 1.4 us)
Async XLA Ops:
  7.2 91.6 %all-gather.6.cloned.1.call-start = ((), (), s32[]{:S(2)}) async-start(), calls=%async_computation.12 | async-start | bytes 9437184 | tf_op jit(solution)/shard_map/all_gather | solution.py:230
  7.2 22.8 %copy-start.3 = (s32[1,64]{1,0:T(1,128)S(1)}, s32[1,64]{1,0:T(1,128)}, u32[]{:S(2)}) copy-start(s32[1,64]{1,0:T(1,128)} %param.14) | copy-start | bytes 772
  7.2 22.8 %copy-start = (s32[1,64]{1,0:T(1,128)S(1)}, s32[1,64]{1,0:T(1,128)}, u32[]{:S(2)}) copy-start(s32[1,64]{1,0:T(1,128)} %param.13) | copy-start | bytes 772
  7.9 22.9 %copy-start.1 = (s32[1,64]{1,0:T(1,128)S(1)}, s32[1,64]{1,0:T(1,128)}, u32[]{:S(2)}) copy-start(s32[1,64]{1,0:T(1,128)} %param.15) | copy-start | bytes 772
  7.9 22.9 %copy-start.2 = (s32[1,64]{1,0:T(1,128)S(1)}, s32[1,64]{1,0:T(1,128)}, u32[]{:S(2)}) copy-start(s32[1,64]{1,0:T(1,128)} %param.12) | copy-start | bytes 772
  7.9 25.5 %copy-start.4 = (s32[1,16]{1,0:T(1,128)S(1)}, s32[1,16]{1,0:T(1,128)}, u32[]{:S(2)}) copy-start(s32[1,16]{1,0:T(1,128)} %param.10) | copy-start | bytes 196
  9.7 41.0 %all-to-all-start = ((f32[8,128,128]{2,1,0:T(8,128)}), f32[8,128,128]{2,1,0:T(8,128)S(1)}, u32[]{:S(2)}, u32[]{:S(2)}) async-start(f32[8,128,128]{2,1,0:T(8,128)} %bitcast.10), calls=%async_computation | async-start | bytes 1048576 | tf_op jit(solution)/shard_map/all_to_all | solution.py:51
  30.8 56.7 %collective-permute-start = (s32[4,64]{1,0:T(4,128)S(1)}, s32[4,64]{1,0:T(4,128)S(1)}, u32[]{:S(2)}, u32[]{:S(2)}) collective-permute-start(s32[4,64]{1,0:T(4,128)S(1)} %pad_add_fusion.1), channel_id=1, source_target_pairs={{0,1},{1,0},{2,3},{3,2},{4,5},{5,4},{6,7},{7,6},{8,9},{9,8},{10,11... | collective-permute-start | bytes 3080 | tf_op jit(solution)/shard_map/ppermute | solution.py:47
  51.3 31.9 %all-to-all-start.1 = ((s32[8,1,16]{2,1,0:T(1,128)}), s32[8,1,16]{2,1,0:T(1,128)S(1)}, u32[]{:S(2)}, u32[]{:S(2)}) async-start(s32[8,1,16]{2,1,0:T(1,128)} %broadcast_in_dim.96), calls=%async_computation.1 | async-start | bytes 8192 | tf_op jit(solution)/shard_map/all_to_all | solution.py:51
  69.3 88.0 %reduce-scatter.2.cloned.1.call-start = ((), (), s32[]{:S(2)}) async-start(), calls=%async_computation.10 | async-start | bytes 2949120 | tf_op jit(solution)/shard_map/reduce_scatter | solution.py:251
  69.3 18.1 %collective-permute-start.3 = (f32[4,128,128]{2,1,0:T(8,128)S(1)}, f32[4,128,128]{2,1,0:T(8,128)S(1)}, u32[]{:S(2)}, u32[]{:S(2)}) collective-permute-start(f32[4,128,128]{2,1,0:T(8,128)S(1)} %get-tuple-element.47), channel_id=1, source_target_pairs={{0,32},{16,48},{32,64},{48,80},{64,96},{80,112},{96,128},{112,144}... | collective-permute-start | bytes 786440 | tf_op jit(solution)/shard_map/ppermute | solution.py:43
  71.3 16.2 %collective-permute-start.2 = (f32[4,128,128]{2,1,0:T(8,128)S(1)}, f32[4,128,128]{2,1,0:T(8,128)S(1)}, u32[]{:S(2)}, u32[]{:S(2)}) collective-permute-start(f32[4,128,128]{2,1,0:T(8,128)S(1)} %get-tuple-element.48), channel_id=1, source_target_pairs={{0,224},{16,240},{32,0},{48,16},{64,32},{80,48},{96,64},{112,80},{... | collective-permute-start | bytes 786440 | tf_op jit(solution)/shard_map/ppermute | solution.py:43
  76.7 21.6 %collective-permute-start.4 = (f32[8,128,128]{2,1,0:T(8,128)S(1)}, f32[8,128,128]{2,1,0:T(8,128)S(1)}, u32[]{:S(2)}, u32[]{:S(2)}) collective-permute-start(f32[8,128,128]{2,1,0:T(8,128)S(1)} %all-to-all-done.refs_0_), channel_id=1, source_target_pairs={{0,16},{16,32},{32,48},{48,64},{64,80},{80,96},{96,112},{112,128},... | collective-permute-start | bytes 1572872 | tf_op jit(solution)/shard_map/ppermute | solution.py:43
  78.7 20.1 %collective-permute-start.1 = (f32[8,128,128]{2,1,0:T(8,128)S(1)}, f32[8,128,128]{2,1,0:T(8,128)S(1)}, u32[]{:S(2)}, u32[]{:S(2)}) collective-permute-start(f32[8,128,128]{2,1,0:T(8,128)S(1)} %all-to-all-done.refs_0_), channel_id=1, source_target_pairs={{0,240},{16,0},{32,16},{48,32},{64,48},{80,64},{96,80},{112,96},{1... | collective-permute-start | bytes 1572872 | tf_op jit(solution)/shard_map/ppermute | solution.py:43
  132.8 24.5 %all-to-all-start.4 = ((f32[8,96,128]{2,1,0:T(8,128)}), f32[8,96,128]{2,1,0:T(8,128)S(1)}, u32[]{:S(2)}, u32[]{:S(2)}) async-start(f32[8,96,128]{2,1,0:T(8,128)} %bitcast.18), calls=%async_computation.5 | async-start | bytes 786432 | tf_op jit(solution)/shard_map/all_to_all | solution.py:51
  157.3 9.3 %all-to-all-start.2 = ((f32[4,160,128]{2,1,0:T(8,128)}), f32[4,160,128]{2,1,0:T(8,128)S(1)}, u32[]{:S(2)}, u32[]{:S(2)}) async-start(f32[4,160,128]{2,1,0:T(8,128)} %reduce-scatter.2.cloned.1.call-done), calls=%async_computation.3 | async-start | bytes 655360 | tf_op jit(solution)/shard_map/all_to_all | solution.py:51
  160.8 71.0 %all-gather.4.cloned.1.call-start = ((), (), s32[]{:S(2)}) async-start(), calls=%async_computation.11 | async-start | bytes 2949120 | tf_op jit(solution)/shard_map/all_gather | solution.py:298
  167.1 6.3 %collective-permute-start.5 = (f32[2,3,64]{2,0,1:T(2,128)S(1)}, f32[2,3,64]{2,0,1:T(2,128)S(1)}, u32[]{:S(2)}, u32[]{:S(2)}) collective-permute-start(f32[2,3,64]{2,0,1:T(2,128)S(1)} %pad_maximum_fusion.3), channel_id=1, source_target_pairs={{0,1},{1,0},{2,3},{3,2},{4,5},{5,4},{6,7},{7,6},{8,9},{9,8},{10,11... | collective-permute-start | bytes 4616 | tf_op jit(solution)/shard_map/ppermute | solution.py:47
  238.3 28.9 %collective-permute-start.6 = (f32[8,128,128]{2,1,0:T(8,128)S(1)}, f32[8,128,128]{2,1,0:T(8,128)S(1)}, u32[]{:S(2)}, u32[]{:S(2)}) collective-permute-start(f32[8,128,128]{2,1,0:T(8,128)S(1)} %get-tuple-element.32), channel_id=1, source_target_pairs={{0,16},{16,32},{32,48},{48,64},{64,80},{80,96},{96,112},{112,128},... | collective-permute-start | bytes 1572872 | tf_op jit(solution)/shard_map/ppermute | solution.py:43
  241.3 25.9 %collective-permute-start.7 = (f32[8,128,128]{2,1,0:T(8,128)S(1)}, f32[8,128,128]{2,1,0:T(8,128)S(1)}, u32[]{:S(2)}, u32[]{:S(2)}) collective-permute-start(f32[8,128,128]{2,1,0:T(8,128)S(1)} %get-tuple-element.33), channel_id=1, source_target_pairs={{0,240},{16,0},{32,16},{48,32},{64,48},{80,64},{96,80},{112,96},{1... | collective-permute-start | bytes 1572872 | tf_op jit(solution)/shard_map/ppermute | solution.py:43
  248.4 15.7 %collective-permute-start.8 = (f32[4,128,128]{2,1,0:T(8,128)}, f32[4,128,128]{2,1,0:T(8,128)S(1)}, u32[]{:S(2)}, u32[]{:S(2)}) collective-permute-start(f32[4,128,128]{2,1,0:T(8,128)} %get-tuple-element.34), channel_id=1, source_target_pairs={{0,32},{16,48},{32,64},{48,80},{64,96},{80,112},{96,128},{112,144}... | collective-permute-start | bytes 786440 | tf_op jit(solution)/shard_map/ppermute | solution.py:43
  250.3 16.9 %collective-permute-start.9 = (f32[4,128,128]{2,1,0:T(8,128)S(1)}, f32[4,128,128]{2,1,0:T(8,128)S(1)}, u32[]{:S(2)}, u32[]{:S(2)}) collective-permute-start(f32[4,128,128]{2,1,0:T(8,128)S(1)} %get-tuple-element.35), channel_id=1, source_target_pairs={{0,224},{16,240},{32,0},{48,16},{64,32},{80,48},{96,64},{112,80},{... | collective-permute-start | bytes 786440 | tf_op jit(solution)/shard_map/ppermute | solution.py:43
  268.1 45.5 %all-to-all-start.8 = ((f32[8,128,128]{2,1,0:T(8,128)}), f32[8,128,128]{2,1,0:T(8,128)S(1)}, u32[]{:S(2)}, u32[]{:S(2)}) async-start(f32[8,128,128]{2,1,0:T(8,128)} %fusion), calls=%async_computation.9 | async-start | bytes 1048576 | tf_op jit(solution)/shard_map/all_to_all | solution.py:51
Sparse Core Ops, SparseCore 0:
  10.7 69.4 all-gather.5
  104.6 45.7 reduce-scatter.1
  184.3 47.3 all-gather.3

commit v8 on v7

--- a/solution.py
+++ b/solution.py
@@ -16,7 +16,7 @@
 CB = 64
 PAIRS = 64
 ENTRIES = 2 * NX * SLOTS
-EXTRA = 32
+EXTRA = 16
 VMEM_LIMIT = 48 * 1024 * 1024
 
 precise = lax.Precision.HIGHEST
@@ -131,75 +131,104 @@
 
         def add(index, value):
             x, y, _ = decode(list_ref[index], own_z)
-            out_ref[x * NY + y if odd else y * NX + x, out_rows] += value
+            out_ref[y * NX + x, out_rows] += value
 
         for_pairs(first, last, lambda index: copy(index, rows).wait(), compute, add)
 
 
-def backward_kernel(place_ref, list_ref, source_ref, even_ref, odd_ref, *refs):
-    outs, total_ref, blocks_ref, arrived, rows_ref, rows_arrived = refs[:5], *refs[5:]
+def backward_kernel(odd, place_ref, list_ref, source_ref, slab_ref, *refs):
+    total_ref, blocks_ref, arrived, rows_ref, rows_arrived = refs[-5:]
     own_z, even_end, end = place_ref[0], place_ref[1], place_ref[2]
 
-    def copy(index):
-        return copy_block(list_ref[index], index, source_ref, blocks_ref, arrived)
-
-    def copy_rows(index, source, place, source_rows, rows):
+    def copy(index, rows):
+        return copy_block(list_ref[index], index, source_ref, blocks_ref, arrived, rows)
+
+    def copy_rows(index, rows, slab_start):
+        x, y, _ = decode(list_ref[index], own_z)
+        place = x * NY + y if odd else y * NX + x
+        length = rows.stop - rows.start
         return pltpu.make_async_copy(
-            source.at[place, pl.ds(source_rows, rows.stop - rows.start)],
-            rows_ref.at[index, pl.ds(rows.start, rows.stop - rows.start)],
+            slab_ref.at[place, pl.ds(slab_start, length)],
+            rows_ref.at[index, pl.ds(rows.start, length)],
             rows_arrived.at[index],
         )
 
-    @pl.loop(0, even_end)
-    def _(index):
-        x, y, _ = decode(list_ref[index], own_z)
-        copy(index).start()
-        copy_rows(index, even_ref, y * NX + x, 0, slice(0, BLOCK)).start()
-
-    @pl.loop(even_end, end)
-    def _(index):
-        x, y, _ = decode(list_ref[index], own_z)
-        copy(index).start()
-        copy_rows(index, even_ref, y * NX + x, BLOCK, slice(0, EXTRA)).start()
-        copy_rows(index, odd_ref, x * NY + y, 0, slice(EXTRA, BLOCK)).start()
-
-    total_ref[...] = jnp.zeros_like(total_ref)
-
-    def wait(index):
-        copy(index).wait()
-        copy_rows(index, even_ref, 0, 0, slice(0, BLOCK)).wait()
-
-    def compute(index):
-        return product(blocks_ref[index], rows_ref[index], 0)
-
-    def add(index, value):
-        _, _, near = decode(list_ref[index], own_z)
-        total_ref[near] += value
-
-    for_pairs(0, end, wait, compute, add)
-    start = 0
-    for out in outs:
-        out[...] = total_ref[pl.ds(start, out.shape[0])]
-        start += out.shape[0]
-
-
-def call_kernel(body, place, entries, source, arrays, out_shapes, in_place=True):
+    if odd:
+        spans = [(even_end, end, slice(EXTRA, BLOCK), 0)]
+    else:
+        spans = [(0, even_end, slice(0, BLOCK), 0), (even_end, end, slice(0, EXTRA), BLOCK)]
+    for first, last, rows, slab_start in spans:
+
+        @pl.loop(first, last)
+        def _(index):
+            copy(index, rows).start()
+            copy_rows(index, rows, slab_start).start()
+
+    if odd:
+        total_ref[...] = jnp.zeros_like(total_ref)
+    else:
+        total_ref[...] = refs[0][...]
+
+    for first, last, rows, slab_start in spans:
+
+        def wait(index):
+            copy(index, rows).wait()
+            copy_rows(index, rows, slab_start).wait()
+
+        def compute(index):
+            return product(blocks_ref[index, rows], rows_ref[index, rows], 0)
+
+        def add(index, value):
+            _, _, near = decode(list_ref[index], own_z)
+            total_ref[near] += value
+
+        for_pairs(first, last, wait, compute, add)
+
+    if not odd:
+        start = 0
+        for out in refs[1:-5]:
+            out[...] = total_ref[pl.ds(start, out.shape[0])]
+            start += out.shape[0]
+
+
+def call_kernel(body, place, entries, source, arrays, specs, out_shapes, scratch):
     whole = pl.BlockSpec(memory_space=pltpu.VMEM)
     scalars = pl.BlockSpec(memory_space=pltpu.SMEM)
     anywhere = pl.BlockSpec(memory_space=pl.ANY)
-    copies = [
+    return pl.pallas_call(
+        body,
+        out_shape=[jax.ShapeDtypeStruct((*shape, HALF), jnp.float32) for shape in out_shapes],
+        in_specs=[scalars, scalars, anywhere] + [anywhere if s else whole for s in specs],
+        out_specs=[whole] * len(out_shapes),
+        scratch_shapes=scratch,
+        compiler_params=pltpu.CompilerParams(vmem_limit_bytes=VMEM_LIMIT),
+    )(place, entries, source, *arrays)
+
+
+def copies():
+    return [
         pltpu.VMEM((ENTRIES, BLOCK, BLOCK), jnp.float32),
         pltpu.SemaphoreType.DMA((ENTRIES,)),
     ]
-    return pl.pallas_call(
-        body,
-        out_shape=[jax.ShapeDtypeStruct((*shape, HALF), jnp.float32) for shape in out_shapes],
-        in_specs=[scalars, scalars, anywhere] + [whole if in_place else anywhere] * len(arrays),
-        out_specs=[whole] * len(out_shapes),
-        scratch_shapes=[pltpu.VMEM((2 * NZ, BLOCK, HALF), jnp.float32)]
-        + copies * (1 if in_place else 2),
-        compiler_params=pltpu.CompilerParams(vmem_limit_bytes=VMEM_LIMIT),
-    )(place, entries, source, *arrays)
+
+
+def forward_products(odd, place, entries, source, parts):
+    rows = BLOCK - EXTRA if odd else BLOCK + EXTRA
+    scratch = [pltpu.VMEM((2 * NZ, BLOCK, HALF), jnp.float32)] + copies()
+    body = functools.partial(forward_kernel, odd)
+    specs = [False] * len(parts)
+    return call_kernel(body, place, entries, source, parts, specs, [(NX * NY, rows)], scratch)[0]
+
+
+def backward_products(odd, place, entries, source, slab, total=None):
+    body = functools.partial(backward_kernel, odd)
+    if odd:
+        shapes, arrays, scratch = [(2 * NZ, BLOCK)], [slab], []
+    else:
+        shapes, arrays = [(n, BLOCK) for n in (8, 8, 4, 4, 8)], [slab, total]
+        scratch = [pltpu.VMEM((2 * NZ, BLOCK, HALF), jnp.float32)]
+    scratch = scratch + copies() + copies()
+    return call_kernel(body, place, entries, source, arrays, [True, False][: len(arrays)], shapes, scratch)
 
 
 def live_list(ids, own_x, own_z):
@@ -243,20 +272,17 @@
     source, other_picks, entries, place, *parts = lax.optimization_barrier(
         (source, other_picks, entries, place, *parts)
     )
-    even, odd = (functools.partial(forward_kernel, odd) for odd in (False, True))
-    (first,) = call_kernel(even, place, entries, source, parts, [(NX * NY, BLOCK + EXTRA)])
+    first = forward_products(False, place, entries, source, parts)
     entries, first = lax.optimization_barrier((entries, first))
-    (second,) = call_kernel(odd, place, entries, source, parts, [(NX * NY, BLOCK - EXTRA)])
+    second = forward_products(True, place, entries, source, parts)
 
     first = lax.psum_scatter(
         first, "col", scatter_dimension=0, tiled=True, axis_index_groups=Y_GROUPS
     )
-    second = second.reshape(NX, NY * (BLOCK - EXTRA), HALF)
-    second = jnp.sum(exchange(second, "row", X_GROUPS), axis=0)
-    second = exchange(second.reshape(NY, BLOCK - EXTRA, HALF), "col", Y_GROUPS)
-    second = jnp.sum(second, axis=0)
-    first = jnp.sum(exchange(first, "row", X_GROUPS), axis=0)
-    current = jnp.concatenate([first, second]).reshape(2, BLOCK, HALF)
+    second = second.reshape(NY, NX * (BLOCK - EXTRA), HALF)
+    second = jnp.sum(exchange(second, "col", Y_GROUPS), axis=0)
+    both = jnp.concatenate([first, second.reshape(NX, BLOCK - EXTRA, HALF)], axis=1)
+    current = jnp.sum(exchange(both, "row", X_GROUPS), axis=0).reshape(2, BLOCK, HALF)
 
     is_first = core == 0
     span_picks = [jnp.where(is_first, picks, other_picks), jnp.where(is_first, other_picks, picks)]
@@ -300,9 +326,9 @@
     second = second.reshape(NY * (BLOCK - EXTRA), HALF)
     second = exchange(jnp.broadcast_to(second[None], (NX, *second.shape)), "row", X_GROUPS)
     second = second.reshape(NX * NY, BLOCK - EXTRA, HALF)
-    shapes = [(n, BLOCK) for n in (8, 8, 4, 4, 8)]
-    own, after, two, two_far, before = call_kernel(
-        backward_kernel, place, entries, source, [first, second], shapes, in_place=False
+    (total,) = backward_products(True, place, entries, source, second)
+    own, after, two, two_far, before = backward_products(
+        False, place, entries, source, first, total
     )
     two = jnp.concatenate([send_z(two, 2), send_z(two_far, -2)])
     near = (own + send_z(after, 1) + send_z(before, -1) + two).reshape(4, 2, BLOCK, HALF)

time: 325 us -> 345 us (1.062)
  the two profiles are of different devices: /device:TPU:1 before, /device:TPU:66 now
where the time goes in v8:
time: 345 us; the launch traced here: 344 us
  blocking collectives  125 us (36%)
  waiting for transfers between devices  94.7 us (27%)
  starting transfers between devices  68.9 us (20%)
  Pallas kernels  25 us (7%)
  between operations  17.2 us (5%)
  other arithmetic  7.67 us (2%)
  local copies, waits for them, and re-layouts  4.72 us (1%)
    all_to_all x4, blocking collectives, exchange(): lax.all_to_all(values, axis, split_axis=0, concat_axis=0, tiled=True, axi...  125 us
    all_to_all x4, waiting for transfers between devices, exchange(): lax.all_to_all(values, axis, split_axis=0, concat_axis=0, tiled=True, axi...  68 us
    all_to_all x4, starting transfers between devices, exchange(): lax.all_to_all(values, axis, split_axis=0, concat_axis=0, tiled=True, axi...  35.8 us
    ppermute x8, starting transfers between devices, send_z(): return lax.ppermute(values, 'row', pairs)  28.7 us
    pallas_call x4, Pallas kernels, call_kernel(): pl.pallas_call(body, out_shape=[jax.ShapeDtypeStruct((*shape, HALF), jnp....  25 us
    ppermute x8, waiting for transfers between devices, send_z(): return lax.ppermute(values, 'row', pairs)  22.6 us
  transfers between devices with their start and end apart: 17, of which 10 were waited for; matrix products, arithmetic and copies ran while one was open for 2% of the time, Pallas kernels for 3%

profile of v8, /device:TPU:66, one launch (start us, length us, event | category | flops | bytes accessed | tf_op | source)
XLA Modules:
  0.0 343.9 jit_solution(204344545472731948)
XLA Ops:
  7.3 0.7 all-gather.6.cloned.1.call-update
  7.9 0.9 slice_bitcast_fusion.3
  8.9 0.9 broadcast_in_dim.95
  9.7 17.8 %all-to-all-start = ((f32[8,128,128]{2,1,0:T(8,128)}), f32[8,128,128]{2,1,0:T(8,128)S(1)}, u32[]{:S(2)}, u32[]{:S(2)}) async-start(f32[8,128,128]{2,1,0:T(8,128)} %bitcast.10), calls=%async_computation | async-start | bytes 1048576 | tf_op jit(solution)/shard_map/all_to_all | solution.py:51
  27.6 0.8 gather_fusion
  28.4 2.4 collective-permute-start
  31.5 27.9 %all-to-all-done.refs_0_ = f32[8,128,128]{2,1,0:T(8,128)S(1)} async-done(((f32[8,128,128]{2,1,0:T(8,128)}), f32[8,128,128]{2,1,0:T(8,128)S(1)}, u32[]{:S(2)}, u32[]{:S(2)}) %all-to-all-start) | async-done | bytes 524320 | tf_op jit(solution)/shard_map/all_to_all | solution.py:51
  59.4 0.6 broadcast_in_dim.96
  60.0 4.8 %all-to-all-start.1 = ((s32[8,1,16]{2,1,0:T(1,128)}), s32[8,1,16]{2,1,0:T(1,128)S(1)}, u32[]{:S(2)}, u32[]{:S(2)}) async-start(s32[8,1,16]{2,1,0:T(1,128)} %broadcast_in_dim.96), calls=%async_computation.1 | async-start | bytes 8192 | tf_op jit(solution)/shard_map/all_to_all | solution.py:51
  64.9 4.5 %collective-permute-start.3 = (f32[4,128,128]{2,1,0:T(8,128)S(1)}, f32[4,128,128]{2,1,0:T(8,128)S(1)}, u32[]{:S(2)}, u32[]{:S(2)}) collective-permute-start(f32[4,128,128]{2,1,0:T(8,128)S(1)} %get-tuple-element.47), channel_id=1, source_target_pairs={{0,32},{16,48},{32,64},{48,80},{64,96},{80,112},{96,128},{112,144}... | collective-permute-start | bytes 786440 | tf_op jit(solution)/shard_map/ppermute | solution.py:43
  69.4 3.5 %collective-permute-start.2 = (f32[4,128,128]{2,1,0:T(8,128)S(1)}, f32[4,128,128]{2,1,0:T(8,128)S(1)}, u32[]{:S(2)}, u32[]{:S(2)}) collective-permute-start(f32[4,128,128]{2,1,0:T(8,128)S(1)} %get-tuple-element.48), channel_id=1, source_target_pairs={{0,224},{16,240},{32,0},{48,16},{64,32},{80,48},{96,64},{112,80},{... | collective-permute-start | bytes 786440 | tf_op jit(solution)/shard_map/ppermute | solution.py:43
  72.9 2.6 collective-permute-start.4
  75.4 4.4 %collective-permute-start.1 = (f32[8,128,128]{2,1,0:T(8,128)S(1)}, f32[8,128,128]{2,1,0:T(8,128)S(1)}, u32[]{:S(2)}, u32[]{:S(2)}) collective-permute-start(f32[8,128,128]{2,1,0:T(8,128)S(1)} %all-to-all-done.refs_0_), channel_id=1, source_target_pairs={{0,240},{16,0},{32,16},{48,32},{64,48},{80,64},{96,80},{112,96},{1... | collective-permute-start | bytes 1572872 | tf_op jit(solution)/shard_map/ppermute | solution.py:43
  79.8 0.5 broadcast.359
  80.4 0.7 reduce.8
  81.1 0.6 convert_reduce_fusion.2
  81.9 0.7 add_select_fusion.2
  82.7 1.4 pad_add_fusion.2.place_ref
  84.1 1.6 collective-permute-done.2.refs_2_
  85.6 7.8 %collective-permute-done.4.refs_4_ = f32[8,128,128]{2,1,0:T(8,128)S(1)} collective-permute-done((f32[8,128,128]{2,1,0:T(8,128)S(1)}, f32[8,128,128]{2,1,0:T(8,128)S(1)}, u32[]{:S(2)}, u32[]{:S(2)}) %collective-permute-start.4) | collective-permute-done | bytes 524320 | tf_op jit(solution)/shard_map/ppermute | solution.py:43
  93.4 3.1 collective-permute-done.1.refs_1_
  96.5 6.5 %shard_map.95 = f32[32,144,128]{2,1,0:T(8,128)} custom-call(s32[3]{0:T(128)S(1)} %pad_add_fusion.2.place_ref, s32[128]{0:T(128)S(1)} %select_reduce_fusion.list_ref, f32[128,128,128]{2,1,0:T(8,128)} %bitcast.72, f32[8,128,128]{2,1,0:T(8,128)S(1)} %all-to-all-done.refs_0_, f32[8,128,128]{2,1,0:T(8,128)S(1)} %collective-permute-done.1.refs_1_, ...), custom_call_target="tpu_custom_call" | custom-call | tf_op jit(solution)/shard_map/pallas_call | solution.py:198
  103.0 4.4 %shard_map.96 = f32[32,112,128]{2,1,0:T(8,128)S(1)} custom-call(s32[3]{0:T(128)S(1)} %pad_add_fusion.2.place_ref, s32[128]{0:T(128)S(1)} %select_reduce_fusion.list_ref, f32[128,128,128]{2,1,0:T(8,128)} %bitcast.73, f32[8,128,128]{2,1,0:T(8,128)S(1)} %all-to-all-done.refs_0_, f32[8,128,128]{2,1,0:T(8,128)S(1)} %collective-permute-done.1.refs_1_, ...), custom_call_target="tpu_custom_call" | custom-call | tf_op jit(solution)/shard_map/pallas_call | solution.py:198
  107.4 69.1 %all_to_all.44 = f32[8,448,128]{2,1,0:T(8,128)S(1)} all-to-all(f32[8,448,128]{2,1,0:T(8,128)S(1)} %bitcast.69), channel_id=1, replica_groups={{0,2,4,6,8,10,12,14},{1,3,5,7,9,11,13,15},{16,18,20,22,24,26,28,30},{17..., dimensions={0} | all-to-all | bytes 3670016 | tf_op jit(solution)/shard_map/all_to_all | solution.py:51
  176.6 2.2 reduce-scatter.2.cloned.1.call-done
  178.8 1.8 pad_maximum_fusion
  180.6 5.1 %all-to-all-start.3 = ((f32[4,256,128]{2,1,0:T(8,128)}), f32[4,256,128]{2,1,0:T(8,128)S(1)}, u32[]{:S(2)}, u32[]{:S(2)}) async-start(f32[4,256,128]{2,1,0:T(8,128)} %pad_maximum_fusion), calls=%async_computation.4 | async-start | bytes 1048576 | tf_op jit(solution)/shard_map/all_to_all | solution.py:51
  185.8 7.6 %all-to-all-done.3 = f32[4,256,128]{2,1,0:T(8,128)S(1)} async-done(((f32[4,256,128]{2,1,0:T(8,128)}), f32[4,256,128]{2,1,0:T(8,128)S(1)}, u32[]{:S(2)}, u32[]{:S(2)}) %all-to-all-start.3) | async-done | bytes 524320 | tf_op jit(solution)/shard_map/all_to_all | solution.py:51
  193.5 0.3 fusion.9
  193.9 1.9 collective-permute-start.5
  195.9 1.1 collective-permute-done.5
  197.3 0.5 fusion.1
  197.8 10.7 %all_to_all.45 = f32[4,144,128]{2,1,0:T(8,128)} all-to-all(f32[4,144,128]{2,1,0:T(8,128)S(1)} %broadcast_in_dim.99), channel_id=1, replica_groups={{0,256,512,768},{16,272,528,784},{32,288,544,800},{48,304,560,816},{64,..., dimensions={0} | all-to-all | bytes 589824 | tf_op jit(solution)/shard_map/all_to_all | solution.py:51
  208.6 21.9 %all_to_all.46 = f32[8,112,128]{2,1,0:T(8,128)S(1)} all-to-all(f32[8,112,128]{2,1,0:T(8,128)S(1)} %broadcast_in_dim.100), channel_id=1, replica_groups={{0,2,4,6,8,10,12,14},{1,3,5,7,9,11,13,15},{16,18,20,22,24,26,28,30},{17..., dimensions={0} | all-to-all | bytes 917504 | tf_op jit(solution)/shard_map/all_to_all | solution.py:51
  230.6 23.3 %all_to_all.47 = f32[4,896,128]{2,1,0:T(8,128)S(1)} all-to-all(f32[4,896,128]{2,1,0:T(8,128)S(1)} %broadcast_in_dim.102), channel_id=1, replica_groups={{0,256,512,768},{16,272,528,784},{32,288,544,800},{48,304,560,816},{64,..., dimensions={0} | all-to-all | bytes 3670016 | tf_op jit(solution)/shard_map/all_to_all | solution.py:51
  253.9 6.5 %shard_map.97.refs_0_ = f32[32,128,128]{2,1,0:T(8,128)S(1)} custom-call(s32[3]{0:T(128)S(1)} %pad_add_fusion.2.place_ref, s32[128]{0:T(128)S(1)} %select_reduce_fusion.list_ref, f32[128,128,128]{2,1,0:T(8,128)} %bitcast.74, f32[32,112,128]{2,1,0:T(8,128)S(1)} %bitcast.70), custom_call_target="tpu_custom_call" | custom-call | tf_op jit(solution)/shard_map/pallas_call | solution.py:198
  260.4 7.6 %shard_map.98 = (f32[8,128,128]{2,1,0:T(8,128)S(1)}, f32[8,128,128]{2,1,0:T(8,128)}, f32[4,128,128]{2,1,0:T(8,128)}, f32[4,128,128]{2,1,0:T(8,128)S(1)}, f32[8,128,128]{2,1,0:T(8,128)S(1)}) custom-call(s32[3]{0:T(128)S(1)} %pad_add_fusion.2.place_ref, s32[128]{0:T(128)S(1)} %select_reduce_fusion.list_ref, f32[128,128,128]{2,1,0:T(8,128)} %bitcast.75, ...), custom_call_target="tpu_custom_call" | custom-call | tf_op jit(solution)/shard_map/pallas_call | solution.py:198
  268.0 1.9 collective-permute-start.6
  270.0 3.9 %collective-permute-start.7 = (f32[8,128,128]{2,1,0:T(8,128)S(1)}, f32[8,128,128]{2,1,0:T(8,128)S(1)}, u32[]{:S(2)}, u32[]{:S(2)}) collective-permute-start(f32[8,128,128]{2,1,0:T(8,128)S(1)} %get-tuple-element.33), channel_id=1, source_target_pairs={{0,240},{16,0},{32,16},{48,32},{64,48},{80,64},{96,80},{112,96},{1... | collective-permute-start | bytes 1572872 | tf_op jit(solution)/shard_map/ppermute | solution.py:43
  273.9 2.0 collective-permute-start.8
  275.9 6.0 %collective-permute-start.9 = (f32[4,128,128]{2,1,0:T(8,128)S(1)}, f32[4,128,128]{2,1,0:T(8,128)S(1)}, u32[]{:S(2)}, u32[]{:S(2)}) collective-permute-start(f32[4,128,128]{2,1,0:T(8,128)S(1)} %get-tuple-element.35), channel_id=1, source_target_pairs={{0,224},{16,240},{32,0},{48,16},{64,32},{80,48},{96,64},{112,80},{... | collective-permute-start | bytes 786440 | tf_op jit(solution)/shard_map/ppermute | solution.py:43
  282.1 8.6 %collective-permute-done.8 = f32[4,128,128]{2,1,0:T(8,128)S(1)} collective-permute-done((f32[4,128,128]{2,1,0:T(8,128)}, f32[4,128,128]{2,1,0:T(8,128)S(1)}, u32[]{:S(2)}, u32[]{:S(2)}) %collective-permute-start.8) | collective-permute-done | bytes 262176 | tf_op jit(solution)/shard_map/ppermute | solution.py:43
  290.6 1.6 collective-permute-done.9
  292.2 1.0 fusion
  293.2 8.0 %all-to-all-start.7 = ((f32[8,128,128]{2,1,0:T(8,128)}), f32[8,128,128]{2,1,0:T(8,128)S(1)}, u32[]{:S(2)}, u32[]{:S(2)}) async-start(f32[8,128,128]{2,1,0:T(8,128)} %fusion), calls=%async_computation.8 | async-start | bytes 1048576 | tf_op jit(solution)/shard_map/all_to_all | solution.py:51
  301.1 0.6 fusion.38
  303.0 32.5 %all-to-all-done.7 = f32[8,128,128]{2,1,0:T(8,128)S(1)} async-done(((f32[8,128,128]{2,1,0:T(8,128)}), f32[8,128,128]{2,1,0:T(8,128)S(1)}, u32[]{:S(2)}, u32[]{:S(2)}) %all-to-all-start.7) | async-done | bytes 524320 | tf_op jit(solution)/shard_map/all_to_all | solution.py:51
  335.6 0.7 pad_maximum_fusion.2
  (55 shorter events, 1.5 us)
Async XLA Ops:
  7.2 20.4 %copy-start.3 = (s32[1,64]{1,0:T(1,128)S(1)}, s32[1,64]{1,0:T(1,128)}, u32[]{:S(2)}) copy-start(s32[1,64]{1,0:T(1,128)} %param.14) | copy-start | bytes 772
  7.2 20.4 %copy-start = (s32[1,64]{1,0:T(1,128)S(1)}, s32[1,64]{1,0:T(1,128)}, u32[]{:S(2)}) copy-start(s32[1,64]{1,0:T(1,128)} %param.13) | copy-start | bytes 772
  7.2 21.2 %copy-start.1 = (s32[1,64]{1,0:T(1,128)S(1)}, s32[1,64]{1,0:T(1,128)}, u32[]{:S(2)}) copy-start(s32[1,64]{1,0:T(1,128)} %param.15) | copy-start | bytes 772
  7.2 21.2 %copy-start.2 = (s32[1,64]{1,0:T(1,128)S(1)}, s32[1,64]{1,0:T(1,128)}, u32[]{:S(2)}) copy-start(s32[1,64]{1,0:T(1,128)} %param.12) | copy-start | bytes 772
  7.2 24.3 %copy-start.4 = (s32[1,16]{1,0:T(1,128)S(1)}, s32[1,16]{1,0:T(1,128)}, u32[]{:S(2)}) copy-start(s32[1,16]{1,0:T(1,128)} %param.10) | copy-start | bytes 196
  7.2 89.3 %all-gather.6.cloned.1.call-start = ((), (), s32[]{:S(2)}) async-start(), calls=%async_computation.11 | async-start | bytes 9437184 | tf_op jit(solution)/shard_map/all_gather | solution.py:259
  9.7 49.7 %all-to-all-start = ((f32[8,128,128]{2,1,0:T(8,128)}), f32[8,128,128]{2,1,0:T(8,128)S(1)}, u32[]{:S(2)}, u32[]{:S(2)}) async-start(f32[8,128,128]{2,1,0:T(8,128)} %bitcast.10), calls=%async_computation | async-start | bytes 1048576 | tf_op jit(solution)/shard_map/all_to_all | solution.py:51
  28.4 55.6 %collective-permute-start = (s32[4,64]{1,0:T(4,128)S(1)}, s32[4,64]{1,0:T(4,128)S(1)}, u32[]{:S(2)}, u32[]{:S(2)}) collective-permute-start(s32[4,64]{1,0:T(4,128)S(1)} %pad_add_fusion.1), channel_id=1, source_target_pairs={{0,1},{1,0},{2,3},{3,2},{4,5},{5,4},{6,7},{7,6},{8,9},{9,8},{10,11... | collective-permute-start | bytes 3080 | tf_op jit(solution)/shard_map/ppermute | solution.py:47
  60.0 19.8 %all-to-all-start.1 = ((s32[8,1,16]{2,1,0:T(1,128)}), s32[8,1,16]{2,1,0:T(1,128)S(1)}, u32[]{:S(2)}, u32[]{:S(2)}) async-start(s32[8,1,16]{2,1,0:T(1,128)} %broadcast_in_dim.96), calls=%async_computation.1 | async-start | bytes 8192 | tf_op jit(solution)/shard_map/all_to_all | solution.py:51
  64.9 113.9 %reduce-scatter.2.cloned.1.call-start = ((), (), s32[]{:S(2)}) async-start(), calls=%async_computation.9 | async-start | bytes 2654208 | tf_op jit(solution)/shard_map/reduce_scatter | solution.py:279
  64.9 19.2 %collective-permute-start.3 = (f32[4,128,128]{2,1,0:T(8,128)S(1)}, f32[4,128,128]{2,1,0:T(8,128)S(1)}, u32[]{:S(2)}, u32[]{:S(2)}) collective-permute-start(f32[4,128,128]{2,1,0:T(8,128)S(1)} %get-tuple-element.47), channel_id=1, source_target_pairs={{0,32},{16,48},{32,64},{48,80},{64,96},{80,112},{96,128},{112,144}... | collective-permute-start | bytes 786440 | tf_op jit(solution)/shard_map/ppermute | solution.py:43
  69.4 16.3 %collective-permute-start.2 = (f32[4,128,128]{2,1,0:T(8,128)S(1)}, f32[4,128,128]{2,1,0:T(8,128)S(1)}, u32[]{:S(2)}, u32[]{:S(2)}) collective-permute-start(f32[4,128,128]{2,1,0:T(8,128)S(1)} %get-tuple-element.48), channel_id=1, source_target_pairs={{0,224},{16,240},{32,0},{48,16},{64,32},{80,48},{96,64},{112,80},{... | collective-permute-start | bytes 786440 | tf_op jit(solution)/shard_map/ppermute | solution.py:43
  72.9 20.6 %collective-permute-start.4 = (f32[8,128,128]{2,1,0:T(8,128)S(1)}, f32[8,128,128]{2,1,0:T(8,128)S(1)}, u32[]{:S(2)}, u32[]{:S(2)}) collective-permute-start(f32[8,128,128]{2,1,0:T(8,128)S(1)} %all-to-all-done.refs_0_), channel_id=1, source_target_pairs={{0,16},{16,32},{32,48},{48,64},{64,80},{80,96},{96,112},{112,128},... | collective-permute-start | bytes 1572872 | tf_op jit(solution)/shard_map/ppermute | solution.py:43
  75.4 21.1 %collective-permute-start.1 = (f32[8,128,128]{2,1,0:T(8,128)S(1)}, f32[8,128,128]{2,1,0:T(8,128)S(1)}, u32[]{:S(2)}, u32[]{:S(2)}) collective-permute-start(f32[8,128,128]{2,1,0:T(8,128)S(1)} %all-to-all-done.refs_0_), channel_id=1, source_target_pairs={{0,240},{16,0},{32,16},{48,32},{64,48},{80,64},{96,80},{112,96},{1... | collective-permute-start | bytes 1572872 | tf_op jit(solution)/shard_map/ppermute | solution.py:43
  180.6 12.8 %all-to-all-start.3 = ((f32[4,256,128]{2,1,0:T(8,128)}), f32[4,256,128]{2,1,0:T(8,128)S(1)}, u32[]{:S(2)}, u32[]{:S(2)}) async-start(f32[4,256,128]{2,1,0:T(8,128)} %pad_maximum_fusion), calls=%async_computation.4 | async-start | bytes 1048576 | tf_op jit(solution)/shard_map/all_to_all | solution.py:51
  185.8 74.6 %all-gather.4.cloned.1.call-start = ((), (), s32[]{:S(2)}) async-start(), calls=%async_computation.10 | async-start | bytes 2654208 | tf_op jit(solution)/shard_map/all_gather | solution.py:324
  193.9 3.1 collective-permute-start.5
  268.0 24.2 %collective-permute-start.6 = (f32[8,128,128]{2,1,0:T(8,128)}, f32[8,128,128]{2,1,0:T(8,128)S(1)}, u32[]{:S(2)}, u32[]{:S(2)}) collective-permute-start(f32[8,128,128]{2,1,0:T(8,128)} %get-tuple-element.32), channel_id=1, source_target_pairs={{0,16},{16,32},{32,48},{48,64},{64,80},{80,96},{96,112},{112,128},... | collective-permute-start | bytes 1572872 | tf_op jit(solution)/shard_map/ppermute | solution.py:43
  270.0 22.2 %collective-permute-start.7 = (f32[8,128,128]{2,1,0:T(8,128)S(1)}, f32[8,128,128]{2,1,0:T(8,128)S(1)}, u32[]{:S(2)}, u32[]{:S(2)}) collective-permute-start(f32[8,128,128]{2,1,0:T(8,128)S(1)} %get-tuple-element.33), channel_id=1, source_target_pairs={{0,240},{16,0},{32,16},{48,32},{64,48},{80,64},{96,80},{112,96},{1... | collective-permute-start | bytes 1572872 | tf_op jit(solution)/shard_map/ppermute | solution.py:43
  273.9 16.7 %collective-permute-start.8 = (f32[4,128,128]{2,1,0:T(8,128)}, f32[4,128,128]{2,1,0:T(8,128)S(1)}, u32[]{:S(2)}, u32[]{:S(2)}) collective-permute-start(f32[4,128,128]{2,1,0:T(8,128)} %get-tuple-element.34), channel_id=1, source_target_pairs={{0,32},{16,48},{32,64},{48,80},{64,96},{80,112},{96,128},{112,144}... | collective-permute-start | bytes 786440 | tf_op jit(solution)/shard_map/ppermute | solution.py:43
  275.9 16.3 %collective-permute-start.9 = (f32[4,128,128]{2,1,0:T(8,128)S(1)}, f32[4,128,128]{2,1,0:T(8,128)S(1)}, u32[]{:S(2)}, u32[]{:S(2)}) collective-permute-start(f32[4,128,128]{2,1,0:T(8,128)S(1)} %get-tuple-element.35), channel_id=1, source_target_pairs={{0,224},{16,240},{32,0},{48,16},{64,32},{80,48},{96,64},{112,80},{... | collective-permute-start | bytes 786440 | tf_op jit(solution)/shard_map/ppermute | solution.py:43
  293.2 42.4 %all-to-all-start.7 = ((f32[8,128,128]{2,1,0:T(8,128)}), f32[8,128,128]{2,1,0:T(8,128)S(1)}, u32[]{:S(2)}, u32[]{:S(2)}) async-start(f32[8,128,128]{2,1,0:T(8,128)} %fusion), calls=%async_computation.8 | async-start | bytes 1048576 | tf_op jit(solution)/shard_map/all_to_all | solution.py:51
Sparse Core Ops, SparseCore 0:
  10.8 66.6 all-gather.5
  103.2 75.5 reduce-scatter.1
  208.7 45.0 all-gather.3

commit v9 on v7

--- a/solution.py
+++ b/solution.py
@@ -16,7 +16,8 @@
 CB = 64
 PAIRS = 64
 ENTRIES = 2 * NX * SLOTS
-EXTRA = 32
+EXTRA = 48
+EXTRA_BACK = 16
 VMEM_LIMIT = 48 * 1024 * 1024
 
 precise = lax.Precision.HIGHEST
@@ -160,8 +161,8 @@
     def _(index):
         x, y, _ = decode(list_ref[index], own_z)
         copy(index).start()
-        copy_rows(index, even_ref, y * NX + x, BLOCK, slice(0, EXTRA)).start()
-        copy_rows(index, odd_ref, x * NY + y, 0, slice(EXTRA, BLOCK)).start()
+        copy_rows(index, even_ref, y * NX + x, BLOCK, slice(0, EXTRA_BACK)).start()
+        copy_rows(index, odd_ref, x * NY + y, 0, slice(EXTRA_BACK, BLOCK)).start()
 
     total_ref[...] = jnp.zeros_like(total_ref)
 
@@ -293,13 +294,13 @@
     scaled = jnp.einsum("hpij,hpid->hjd", hot, row_grads, precision=precise)
 
     all_rows = scaled.reshape(2 * BLOCK, HALF)
-    first, second = all_rows[: BLOCK + EXTRA], all_rows[BLOCK + EXTRA :]
+    first, second = all_rows[: BLOCK + EXTRA_BACK], all_rows[BLOCK + EXTRA_BACK :]
     first = exchange(jnp.broadcast_to(first[None], (NX, *first.shape)), "row", X_GROUPS)
     first = lax.all_gather(first, "col", axis=0, tiled=True, axis_index_groups=Y_GROUPS)
     second = exchange(jnp.broadcast_to(second[None], (NY, *second.shape)), "col", Y_GROUPS)
-    second = second.reshape(NY * (BLOCK - EXTRA), HALF)
+    second = second.reshape(NY * (BLOCK - EXTRA_BACK), HALF)
     second = exchange(jnp.broadcast_to(second[None], (NX, *second.shape)), "row", X_GROUPS)
-    second = second.reshape(NX * NY, BLOCK - EXTRA, HALF)
+    second = second.reshape(NX * NY, BLOCK - EXTRA_BACK, HALF)
     shapes = [(n, BLOCK) for n in (8, 8, 4, 4, 8)]
     own, after, two, two_far, before = call_kernel(
         backward_kernel, place, entries, source, [first, second], shapes, in_place=False

time: 325 us -> 322 us (level)
  the two profiles are of different devices: /device:TPU:1 before, /device:TPU:68 now
where the time goes in v9:
time: 322 us; the launch traced here: 321 us
  waiting for transfers between devices  120 us (37%)
  starting transfers between devices  79.6 us (25%)
  blocking collectives  75.5 us (23%)
  between operations  17.2 us (5%)
  Pallas kernels  17.1 us (5%)
  other arithmetic  6.53 us (2%)
  local copies, waits for them, and re-layouts  4.73 us (1%)
    all_to_all x5, waiting for transfers between devices, exchange(): lax.all_to_all(values, axis, split_axis=0, concat_axis=0, tiled=True, axi...  81.1 us
    all_to_all x4, blocking collectives, exchange(): lax.all_to_all(values, axis, split_axis=0, concat_axis=0, tiled=True, axi...  75.5 us
    all_to_all x5, starting transfers between devices, exchange(): lax.all_to_all(values, axis, split_axis=0, concat_axis=0, tiled=True, axi...  46 us
    ppermute x8, starting transfers between devices, send_z(): return lax.ppermute(values, 'row', pairs)  29.2 us
    ppermute x8, waiting for transfers between devices, send_z(): return lax.ppermute(values, 'row', pairs)  25.6 us
    pallas_call x3, Pallas kernels, call_kernel(): pl.pallas_call(body, out_shape=[jax.ShapeDtypeStruct((*shape, HALF), jnp....  17.1 us
  transfers between devices with their start and end apart: 18, of which 12 were waited for; matrix products, arithmetic and copies ran while one was open for 3% of the time, Pallas kernels for 1%

profile of v9, /device:TPU:68, one launch (start us, length us, event | category | flops | bytes accessed | tf_op | source)
XLA Modules:
  0.0 321.3 jit_solution(6569112502353112858)
XLA Ops:
  7.3 0.7 all-gather.6.cloned.1.call-update
  7.9 0.9 slice_bitcast_fusion.3
  8.8 0.9 broadcast_in_dim.95
  9.7 17.8 %all-to-all-start = ((f32[8,128,128]{2,1,0:T(8,128)}), f32[8,128,128]{2,1,0:T(8,128)S(1)}, u32[]{:S(2)}, u32[]{:S(2)}) async-start(f32[8,128,128]{2,1,0:T(8,128)} %bitcast.10), calls=%async_computation | async-start | bytes 1048576 | tf_op jit(solution)/shard_map/all_to_all | solution.py:52
  27.6 0.8 gather_fusion
  28.4 2.4 collective-permute-start
  31.5 27.9 %all-to-all-done.refs_0_ = f32[8,128,128]{2,1,0:T(8,128)S(1)} async-done(((f32[8,128,128]{2,1,0:T(8,128)}), f32[8,128,128]{2,1,0:T(8,128)S(1)}, u32[]{:S(2)}, u32[]{:S(2)}) %all-to-all-start) | async-done | bytes 524320 | tf_op jit(solution)/shard_map/all_to_all | solution.py:52
  59.4 0.6 broadcast_in_dim.96
  60.0 4.8 %all-to-all-start.1 = ((s32[8,1,16]{2,1,0:T(1,128)}), s32[8,1,16]{2,1,0:T(1,128)S(1)}, u32[]{:S(2)}, u32[]{:S(2)}) async-start(s32[8,1,16]{2,1,0:T(1,128)} %broadcast_in_dim.96), calls=%async_computation.1 | async-start | bytes 8192 | tf_op jit(solution)/shard_map/all_to_all | solution.py:52
  64.8 4.5 %collective-permute-start.3 = (f32[4,128,128]{2,1,0:T(8,128)S(1)}, f32[4,128,128]{2,1,0:T(8,128)S(1)}, u32[]{:S(2)}, u32[]{:S(2)}) collective-permute-start(f32[4,128,128]{2,1,0:T(8,128)S(1)} %get-tuple-element.47), channel_id=1, source_target_pairs={{0,32},{16,48},{32,64},{48,80},{64,96},{80,112},{96,128},{112,144}... | collective-permute-start | bytes 786440 | tf_op jit(solution)/shard_map/ppermute | solution.py:44
  69.3 3.5 %collective-permute-start.2 = (f32[4,128,128]{2,1,0:T(8,128)S(1)}, f32[4,128,128]{2,1,0:T(8,128)S(1)}, u32[]{:S(2)}, u32[]{:S(2)}) collective-permute-start(f32[4,128,128]{2,1,0:T(8,128)S(1)} %get-tuple-element.48), channel_id=1, source_target_pairs={{0,224},{16,240},{32,0},{48,16},{64,32},{80,48},{96,64},{112,80},{... | collective-permute-start | bytes 786440 | tf_op jit(solution)/shard_map/ppermute | solution.py:44
  72.8 2.6 collective-permute-start.4
  75.4 4.4 %collective-permute-start.1 = (f32[8,128,128]{2,1,0:T(8,128)S(1)}, f32[8,128,128]{2,1,0:T(8,128)S(1)}, u32[]{:S(2)}, u32[]{:S(2)}) collective-permute-start(f32[8,128,128]{2,1,0:T(8,128)S(1)} %all-to-all-done.refs_0_), channel_id=1, source_target_pairs={{0,240},{16,0},{32,16},{48,32},{64,48},{80,64},{96,80},{112,96},{1... | collective-permute-start | bytes 1572872 | tf_op jit(solution)/shard_map/ppermute | solution.py:44
  80.3 0.7 reduce.8
  81.1 0.6 convert_reduce_fusion.2
  81.8 0.7 add_select_fusion.2
  82.6 1.4 pad_add_fusion.2.place_ref
  84.0 1.6 collective-permute-done.2.refs_2_
  85.6 7.8 %collective-permute-done.4.refs_4_ = f32[8,128,128]{2,1,0:T(8,128)S(1)} collective-permute-done((f32[8,128,128]{2,1,0:T(8,128)S(1)}, f32[8,128,128]{2,1,0:T(8,128)S(1)}, u32[]{:S(2)}, u32[]{:S(2)}) %collective-permute-start.4) | collective-permute-done | bytes 524320 | tf_op jit(solution)/shard_map/ppermute | solution.py:44
  93.4 3.1 collective-permute-done.1.refs_1_
  96.4 6.0 %shard_map.95 = f32[32,176,128]{2,1,0:T(8,128)} custom-call(s32[3]{0:T(128)S(1)} %pad_add_fusion.2.place_ref, s32[128]{0:T(128)S(1)} %select_reduce_fusion.list_ref, f32[128,128,128]{2,1,0:T(8,128)} %bitcast.72, f32[8,128,128]{2,1,0:T(8,128)S(1)} %all-to-all-done.refs_0_, f32[8,128,128]{2,1,0:T(8,128)S(1)} %collective-permute-done.1.refs_1_, ...), custom_call_target="tpu_custom_call" | custom-call | tf_op jit(solution)/shard_map/pallas_call | solution.py:195
  102.5 3.8 %shard_map.96 = f32[32,80,128]{2,1,0:T(8,128)S(1)} custom-call(s32[3]{0:T(128)S(1)} %pad_add_fusion.2.place_ref, s32[128]{0:T(128)S(1)} %select_reduce_fusion.list_ref, f32[128,128,128]{2,1,0:T(8,128)} %bitcast.73, f32[8,128,128]{2,1,0:T(8,128)S(1)} %all-to-all-done.refs_0_, f32[8,128,128]{2,1,0:T(8,128)S(1)} %collective-permute-done.1.refs_1_, ...), custom_call_target="tpu_custom_call" | custom-call | tf_op jit(solution)/shard_map/pallas_call | solution.py:195
  106.3 19.5 %all_to_all.49 = f32[4,640,128]{2,1,0:T(8,128)S(1)} all-to-all(f32[4,640,128]{2,1,0:T(8,128)S(1)} %bitcast.70), channel_id=1, replica_groups={{0,256,512,768},{16,272,528,784},{32,288,544,800},{48,304,560,816},{64,..., dimensions={0} | all-to-all | bytes 2621440 | tf_op jit(solution)/shard_map/all_to_all | solution.py:52
  125.8 0.8 reduce_sum.123
  126.6 7.6 %all-to-all-start.4 = ((f32[8,80,128]{2,1,0:T(8,128)}), f32[8,80,128]{2,1,0:T(8,128)S(1)}, u32[]{:S(2)}, u32[]{:S(2)}) async-start(f32[8,80,128]{2,1,0:T(8,128)} %bitcast.18), calls=%async_computation.5 | async-start | bytes 655360 | tf_op jit(solution)/shard_map/all_to_all | solution.py:52
  134.2 16.5 %all-to-all-done.4 = f32[8,80,128]{2,1,0:T(8,128)S(1)} async-done(((f32[8,80,128]{2,1,0:T(8,128)}), f32[8,80,128]{2,1,0:T(8,128)S(1)}, u32[]{:S(2)}, u32[]{:S(2)}) %all-to-all-start.4) | async-done | bytes 327712 | tf_op jit(solution)/shard_map/all_to_all | solution.py:52
  150.7 6.0 %reduce-scatter.2.cloned.1.call-done = f32[4,176,128]{2,1,0:T(8,128)} async-done(((f32[32,176,128]{2,1,0:T(8,128)}), f32[4,176,128]{2,1,0:T(8,128)}) %reduce-scatter.2.cloned.1.call-update) | async-done | bytes 360464 | tf_op jit(solution)/shard_map/reduce_scatter | solution.py:252
  156.8 4.8 %all-to-all-start.2 = ((f32[4,176,128]{2,1,0:T(8,128)}), f32[4,176,128]{2,1,0:T(8,128)S(1)}, u32[]{:S(2)}, u32[]{:S(2)}) async-start(f32[4,176,128]{2,1,0:T(8,128)} %reduce-scatter.2.cloned.1.call-done), calls=%async_computation.3 | async-start | bytes 720896 | tf_op jit(solution)/shard_map/all_to_all | solution.py:52
  161.6 4.2 %all-to-all-done.2 = f32[4,176,128]{2,1,0:T(8,128)S(1)} async-done(((f32[4,176,128]{2,1,0:T(8,128)}), f32[4,176,128]{2,1,0:T(8,128)S(1)}, u32[]{:S(2)}, u32[]{:S(2)}) %all-to-all-start.2) | async-done | bytes 360480 | tf_op jit(solution)/shard_map/all_to_all | solution.py:52
  166.3 1.9 collective-permute-start.5
  168.2 1.1 collective-permute-done.5
  169.6 0.5 fusion.1
  170.2 11.2 %all_to_all.50 = f32[4,144,128]{2,1,0:T(8,128)} all-to-all(f32[4,144,128]{2,1,0:T(8,128)S(1)} %broadcast_in_dim.99), channel_id=1, replica_groups={{0,256,512,768},{16,272,528,784},{32,288,544,800},{48,304,560,816},{64,..., dimensions={0} | all-to-all | bytes 589824 | tf_op jit(solution)/shard_map/all_to_all | solution.py:52
  181.5 21.1 %all_to_all.51 = f32[8,112,128]{2,1,0:T(8,128)S(1)} all-to-all(f32[8,112,128]{2,1,0:T(8,128)S(1)} %broadcast_in_dim.100), channel_id=1, replica_groups={{0,2,4,6,8,10,12,14},{1,3,5,7,9,11,13,15},{16,18,20,22,24,26,28,30},{17..., dimensions={0} | all-to-all | bytes 917504 | tf_op jit(solution)/shard_map/all_to_all | solution.py:52
  202.7 23.7 %all_to_all.52 = f32[4,896,128]{2,1,0:T(8,128)S(1)} all-to-all(f32[4,896,128]{2,1,0:T(8,128)S(1)} %broadcast_in_dim.102), channel_id=1, replica_groups={{0,256,512,768},{16,272,528,784},{32,288,544,800},{48,304,560,816},{64,..., dimensions={0} | all-to-all | bytes 3670016 | tf_op jit(solution)/shard_map/all_to_all | solution.py:52
  226.4 5.3 %all-gather.4.cloned.1.call-done.even_ref = f32[32,144,128]{2,1,0:T(8,128)} async-done(((f32[4,144,128]{2,1,0:T(8,128)}), f32[32,144,128]{2,1,0:T(8,128)}) %all-gather.4.cloned.1.call-update) | async-done | bytes 2359312 | tf_op jit(solution)/shard_map/all_gather | solution.py:299
  231.7 7.3 %shard_map.97 = (f32[8,128,128]{2,1,0:T(8,128)S(1)}, f32[8,128,128]{2,1,0:T(8,128)S(1)}, f32[4,128,128]{2,1,0:T(8,128)}, f32[4,128,128]{2,1,0:T(8,128)}, f32[8,128,128]{2,1,0:T(8,128)S(1)}) custom-call(s32[3]{0:T(128)S(1)} %pad_add_fusion.2.place_ref, s32[128]{0:T(128)S(1)} %select_reduce_fusion.list_ref, f32[128,128,128]{2,1,0:T(8,128)} %bitcast.74, ...), custom_call_target="tpu_custom_call" | custom-call | tf_op jit(solution)/shard_map/pallas_call | solution.py:195
  239.0 3.1 collective-permute-start.6
  242.1 2.7 collective-permute-start.7
  244.9 5.8 %collective-permute-start.8 = (f32[4,128,128]{2,1,0:T(8,128)}, f32[4,128,128]{2,1,0:T(8,128)S(1)}, u32[]{:S(2)}, u32[]{:S(2)}) collective-permute-start(f32[4,128,128]{2,1,0:T(8,128)} %get-tuple-element.34), channel_id=1, source_target_pairs={{0,32},{16,48},{32,64},{48,80},{64,96},{80,112},{96,128},{112,144}... | collective-permute-start | bytes 786440 | tf_op jit(solution)/shard_map/ppermute | solution.py:44
  250.7 2.6 collective-permute-start.9
  253.5 11.0 %collective-permute-done.8 = f32[4,128,128]{2,1,0:T(8,128)S(1)} collective-permute-done((f32[4,128,128]{2,1,0:T(8,128)}, f32[4,128,128]{2,1,0:T(8,128)S(1)}, u32[]{:S(2)}, u32[]{:S(2)}) %collective-permute-start.8) | collective-permute-done | bytes 262176 | tf_op jit(solution)/shard_map/ppermute | solution.py:44
  264.5 2.2 collective-permute-done.9
  266.7 0.9 fusion
  267.6 10.9 %all-to-all-start.8 = ((f32[8,128,128]{2,1,0:T(8,128)}), f32[8,128,128]{2,1,0:T(8,128)S(1)}, u32[]{:S(2)}, u32[]{:S(2)}) async-start(f32[8,128,128]{2,1,0:T(8,128)} %fusion), calls=%async_computation.9 | async-start | bytes 1048576 | tf_op jit(solution)/shard_map/all_to_all | solution.py:52
  278.5 0.6 fusion.38
  280.4 32.5 %all-to-all-done.8 = f32[8,128,128]{2,1,0:T(8,128)S(1)} async-done(((f32[8,128,128]{2,1,0:T(8,128)}), f32[8,128,128]{2,1,0:T(8,128)S(1)}, u32[]{:S(2)}, u32[]{:S(2)}) %all-to-all-start.8) | async-done | bytes 524320 | tf_op jit(solution)/shard_map/all_to_all | solution.py:52
  313.0 0.7 pad_maximum_fusion.2
  (57 shorter events, 2.2 us)
Async XLA Ops:
  7.2 20.4 %copy-start.3 = (s32[1,64]{1,0:T(1,128)S(1)}, s32[1,64]{1,0:T(1,128)}, u32[]{:S(2)}) copy-start(s32[1,64]{1,0:T(1,128)} %param.14) | copy-start | bytes 772
  7.2 20.4 %copy-start = (s32[1,64]{1,0:T(1,128)S(1)}, s32[1,64]{1,0:T(1,128)}, u32[]{:S(2)}) copy-start(s32[1,64]{1,0:T(1,128)} %param.13) | copy-start | bytes 772
  7.2 89.3 %all-gather.6.cloned.1.call-start = ((), (), s32[]{:S(2)}) async-start(), calls=%async_computation.12 | async-start | bytes 9437184 | tf_op jit(solution)/shard_map/all_gather | solution.py:231
  7.2 21.1 %copy-start.1 = (s32[1,64]{1,0:T(1,128)S(1)}, s32[1,64]{1,0:T(1,128)}, u32[]{:S(2)}) copy-start(s32[1,64]{1,0:T(1,128)} %param.15) | copy-start | bytes 772
  7.2 21.1 %copy-start.2 = (s32[1,64]{1,0:T(1,128)S(1)}, s32[1,64]{1,0:T(1,128)}, u32[]{:S(2)}) copy-start(s32[1,64]{1,0:T(1,128)} %param.12) | copy-start | bytes 772
  7.3 24.2 %copy-start.4 = (s32[1,16]{1,0:T(1,128)S(1)}, s32[1,16]{1,0:T(1,128)}, u32[]{:S(2)}) copy-start(s32[1,16]{1,0:T(1,128)} %param.10) | copy-start | bytes 196
  9.7 49.7 %all-to-all-start = ((f32[8,128,128]{2,1,0:T(8,128)}), f32[8,128,128]{2,1,0:T(8,128)S(1)}, u32[]{:S(2)}, u32[]{:S(2)}) async-start(f32[8,128,128]{2,1,0:T(8,128)} %bitcast.10), calls=%async_computation | async-start | bytes 1048576 | tf_op jit(solution)/shard_map/all_to_all | solution.py:52
  28.4 55.6 %collective-permute-start = (s32[4,64]{1,0:T(4,128)S(1)}, s32[4,64]{1,0:T(4,128)S(1)}, u32[]{:S(2)}, u32[]{:S(2)}) collective-permute-start(s32[4,64]{1,0:T(4,128)S(1)} %pad_add_fusion.1), channel_id=1, source_target_pairs={{0,1},{1,0},{2,3},{3,2},{4,5},{5,4},{6,7},{7,6},{8,9},{9,8},{10,11... | collective-permute-start | bytes 3080 | tf_op jit(solution)/shard_map/ppermute | solution.py:48
  60.0 19.8 %all-to-all-start.1 = ((s32[8,1,16]{2,1,0:T(1,128)}), s32[8,1,16]{2,1,0:T(1,128)S(1)}, u32[]{:S(2)}, u32[]{:S(2)}) async-start(s32[8,1,16]{2,1,0:T(1,128)} %broadcast_in_dim.96), calls=%async_computation.1 | async-start | bytes 8192 | tf_op jit(solution)/shard_map/all_to_all | solution.py:52
  64.8 92.0 %reduce-scatter.2.cloned.1.call-start = ((), (), s32[]{:S(2)}) async-start(), calls=%async_computation.10 | async-start | bytes 3244032 | tf_op jit(solution)/shard_map/reduce_scatter | solution.py:252
  64.8 19.2 %collective-permute-start.3 = (f32[4,128,128]{2,1,0:T(8,128)S(1)}, f32[4,128,128]{2,1,0:T(8,128)S(1)}, u32[]{:S(2)}, u32[]{:S(2)}) collective-permute-start(f32[4,128,128]{2,1,0:T(8,128)S(1)} %get-tuple-element.47), channel_id=1, source_target_pairs={{0,32},{16,48},{32,64},{48,80},{64,96},{80,112},{96,128},{112,144}... | collective-permute-start | bytes 786440 | tf_op jit(solution)/shard_map/ppermute | solution.py:44
  69.3 16.3 %collective-permute-start.2 = (f32[4,128,128]{2,1,0:T(8,128)S(1)}, f32[4,128,128]{2,1,0:T(8,128)S(1)}, u32[]{:S(2)}, u32[]{:S(2)}) collective-permute-start(f32[4,128,128]{2,1,0:T(8,128)S(1)} %get-tuple-element.48), channel_id=1, source_target_pairs={{0,224},{16,240},{32,0},{48,16},{64,32},{80,48},{96,64},{112,80},{... | collective-permute-start | bytes 786440 | tf_op jit(solution)/shard_map/ppermute | solution.py:44
  72.8 20.6 %collective-permute-start.4 = (f32[8,128,128]{2,1,0:T(8,128)S(1)}, f32[8,128,128]{2,1,0:T(8,128)S(1)}, u32[]{:S(2)}, u32[]{:S(2)}) collective-permute-start(f32[8,128,128]{2,1,0:T(8,128)S(1)} %all-to-all-done.refs_0_), channel_id=1, source_target_pairs={{0,16},{16,32},{32,48},{48,64},{64,80},{80,96},{96,112},{112,128},... | collective-permute-start | bytes 1572872 | tf_op jit(solution)/shard_map/ppermute | solution.py:44
  75.4 21.1 %collective-permute-start.1 = (f32[8,128,128]{2,1,0:T(8,128)S(1)}, f32[8,128,128]{2,1,0:T(8,128)S(1)}, u32[]{:S(2)}, u32[]{:S(2)}) collective-permute-start(f32[8,128,128]{2,1,0:T(8,128)S(1)} %all-to-all-done.refs_0_), channel_id=1, source_target_pairs={{0,240},{16,0},{32,16},{48,32},{64,48},{80,64},{96,80},{112,96},{1... | collective-permute-start | bytes 1572872 | tf_op jit(solution)/shard_map/ppermute | solution.py:44
  126.6 24.1 %all-to-all-start.4 = ((f32[8,80,128]{2,1,0:T(8,128)}), f32[8,80,128]{2,1,0:T(8,128)S(1)}, u32[]{:S(2)}, u32[]{:S(2)}) async-start(f32[8,80,128]{2,1,0:T(8,128)} %bitcast.18), calls=%async_computation.5 | async-start | bytes 655360 | tf_op jit(solution)/shard_map/all_to_all | solution.py:52
  156.8 9.0 %all-to-all-start.2 = ((f32[4,176,128]{2,1,0:T(8,128)}), f32[4,176,128]{2,1,0:T(8,128)S(1)}, u32[]{:S(2)}, u32[]{:S(2)}) async-start(f32[4,176,128]{2,1,0:T(8,128)} %reduce-scatter.2.cloned.1.call-done), calls=%async_computation.3 | async-start | bytes 720896 | tf_op jit(solution)/shard_map/all_to_all | solution.py:52
  161.6 70.2 %all-gather.4.cloned.1.call-start = ((), (), s32[]{:S(2)}) async-start(), calls=%async_computation.11 | async-start | bytes 2654208 | tf_op jit(solution)/shard_map/all_gather | solution.py:299
  166.3 3.1 collective-permute-start.5
  239.0 27.7 %collective-permute-start.6 = (f32[8,128,128]{2,1,0:T(8,128)S(1)}, f32[8,128,128]{2,1,0:T(8,128)S(1)}, u32[]{:S(2)}, u32[]{:S(2)}) collective-permute-start(f32[8,128,128]{2,1,0:T(8,128)S(1)} %get-tuple-element.32), channel_id=1, source_target_pairs={{0,16},{16,32},{32,48},{48,64},{64,80},{80,96},{96,112},{112,128},... | collective-permute-start | bytes 1572872 | tf_op jit(solution)/shard_map/ppermute | solution.py:44
  242.1 24.6 %collective-permute-start.7 = (f32[8,128,128]{2,1,0:T(8,128)S(1)}, f32[8,128,128]{2,1,0:T(8,128)S(1)}, u32[]{:S(2)}, u32[]{:S(2)}) collective-permute-start(f32[8,128,128]{2,1,0:T(8,128)S(1)} %get-tuple-element.33), channel_id=1, source_target_pairs={{0,240},{16,0},{32,16},{48,32},{64,48},{80,64},{96,80},{112,96},{1... | collective-permute-start | bytes 1572872 | tf_op jit(solution)/shard_map/ppermute | solution.py:44
  244.9 19.6 %collective-permute-start.8 = (f32[4,128,128]{2,1,0:T(8,128)}, f32[4,128,128]{2,1,0:T(8,128)S(1)}, u32[]{:S(2)}, u32[]{:S(2)}) collective-permute-start(f32[4,128,128]{2,1,0:T(8,128)} %get-tuple-element.34), channel_id=1, source_target_pairs={{0,32},{16,48},{32,64},{48,80},{64,96},{80,112},{96,128},{112,144}... | collective-permute-start | bytes 786440 | tf_op jit(solution)/shard_map/ppermute | solution.py:44
  250.7 16.0 %collective-permute-start.9 = (f32[4,128,128]{2,1,0:T(8,128)}, f32[4,128,128]{2,1,0:T(8,128)S(1)}, u32[]{:S(2)}, u32[]{:S(2)}) collective-permute-start(f32[4,128,128]{2,1,0:T(8,128)} %get-tuple-element.35), channel_id=1, source_target_pairs={{0,224},{16,240},{32,0},{48,16},{64,32},{80,48},{96,64},{112,80},{... | collective-permute-start | bytes 786440 | tf_op jit(solution)/shard_map/ppermute | solution.py:44
  267.6 45.3 %all-to-all-start.8 = ((f32[8,128,128]{2,1,0:T(8,128)}), f32[8,128,128]{2,1,0:T(8,128)S(1)}, u32[]{:S(2)}, u32[]{:S(2)}) async-start(f32[8,128,128]{2,1,0:T(8,128)} %fusion), calls=%async_computation.9 | async-start | bytes 1048576 | tf_op jit(solution)/shard_map/all_to_all | solution.py:52
Sparse Core Ops, SparseCore 0:
  10.8 66.3 all-gather.5
  102.6 54.0 reduce-scatter.1
  181.6 50.0 all-gather.3

commit v10 on v9

--- a/solution.py
+++ b/solution.py
@@ -37,6 +37,11 @@
     for y in range(NY)
 ]
 CORE_SWAP = [(i, i ^ 1) for i in range(2 * NY)]
+
+
+def send_x(values, step):
+    pairs = [(x * NZ + z, ((x + step) % NX) * NZ + z) for x in range(NX) for z in range(NZ)]
+    return lax.ppermute(values, "row", pairs)
 
 
 def send_z(values, step):
@@ -203,6 +208,18 @@
     )(place, entries, source, *arrays)
 
 
+def halves_kernel(table_ref, out_ref):
+    for index in range(out_ref.shape[0]):
+        half = slice(index % 2 * HALF, (index % 2 + 1) * HALF)
+        out_ref[index] = table_ref[:, half]
+
+
+def repeat_halves(table):
+    whole = pl.BlockSpec(memory_space=pltpu.VMEM)
+    shape = jax.ShapeDtypeStruct((8, BLOCK, HALF), jnp.float32)
+    return pl.pallas_call(halves_kernel, out_shape=shape, in_specs=[whole], out_specs=whole)(table)
+
+
 def live_list(ids, own_x, own_z):
     numbers = jnp.arange(ENTRIES, dtype=jnp.int32)
     live = (ids >= 0) & (jnp.bitwise_and(ids, CB - 1) // NZ == own_x)
@@ -216,7 +233,9 @@
         jnp.sum((before & even_live[None, :]).astype(jnp.int32), axis=1),
     )
     hit = live[None, :] & (rank[None, :] == numbers[:, None])
-    entries = jnp.sum(jnp.where(hit, (ids * ENTRIES + numbers)[None, :], 0), axis=1)
+    x = jnp.bitwise_and(own_x - numbers // (2 * SLOTS), NX - 1)
+    gathered = x * (2 * SLOTS) + jnp.bitwise_and(numbers, 2 * SLOTS - 1)
+    entries = jnp.sum(jnp.where(hit, (ids * ENTRIES + gathered)[None, :], 0), axis=1)
     return entries, jnp.stack([own_z, even_end, jnp.sum(live.astype(jnp.int32))])
 
 
@@ -230,19 +249,23 @@
     own_z = jnp.bitwise_and(own_row, NZ - 1)
     source = lax.all_gather(blocks[0], BOTH, axis=0, tiled=True, axis_index_groups=X_CORE)
 
-    halves = jnp.stack([table[:, :HALF], table[:, HALF:]])
-    halves = jnp.broadcast_to(halves[None], (4, 2, BLOCK, HALF)).reshape(8, BLOCK, HALF)
-    far = exchange(halves, BOTH, Z_CORE)
+    far = exchange(repeat_halves(table), BOTH, Z_CORE)
     span_table = lax.dynamic_slice_in_dim(far, own_z // 4 * 2, 2)
     parts = [far, send_z(far, -1), send_z(far[:4], -2), send_z(far[4:], 2), send_z(far, 1)]
-    picks = jnp.stack([users[0], positives[0], jnp.take(positives[0], neg_index[0]), popular[0]])
+    live = jnp.arange(PAIRS, dtype=jnp.int32) < counts[0]
+    marked = jnp.where(live, jnp.pad(block_ids[0], (0, PAIRS - SLOTS), constant_values=-1), -1)
+    batch = jnp.take(positives[0], neg_index[0])
+    picks = jnp.stack([users[0], positives[0], batch, popular[0], marked])
     other_picks = swap_cores(picks)
-    live = jnp.arange(SLOTS, dtype=jnp.int32) < counts[0]
-    marked, _ = lax.optimization_barrier((jnp.where(live, block_ids[0], -1), far))
-    ids = exchange(jnp.broadcast_to(marked[None], (2 * NX, SLOTS)), BOTH, X_CORE)
-    entries, place = live_list(ids.reshape(-1), own_row // NZ, own_z)
-    source, other_picks, entries, place, *parts = lax.optimization_barrier(
-        (source, other_picks, entries, place, *parts)
+    is_first = core == 0
+    span_picks = jnp.where(
+        is_first, jnp.stack([picks, other_picks]), jnp.stack([other_picks, picks])
+    )
+    ids = span_picks[:, 4, :SLOTS]
+    ids = jnp.stack([ids] + [send_x(ids, step) for step in range(1, NX)]).reshape(-1)
+    entries, place = live_list(ids, own_row // NZ, own_z)
+    source, span_picks, entries, place, *parts = lax.optimization_barrier(
+        (source, span_picks, entries, place, *parts)
     )
     even, odd = (functools.partial(forward_kernel, odd) for odd in (False, True))
     (first,) = call_kernel(even, place, entries, source, parts, [(NX * NY, BLOCK + EXTRA)])
@@ -259,10 +282,8 @@
     first = jnp.sum(exchange(first, "row", X_GROUPS), axis=0)
     current = jnp.concatenate([first, second]).reshape(2, BLOCK, HALF)
 
-    is_first = core == 0
-    span_picks = [jnp.where(is_first, picks, other_picks), jnp.where(is_first, other_picks, picks)]
     final_rows = (span_table + current) / 2
-    hot = one_hot(jnp.stack(span_picks), BLOCK)
+    hot = one_hot(span_picks[:, :4], BLOCK)
     rows = jnp.einsum("hpij,hjd->hpid", hot, final_rows, precision=precise)
     user_rows, item_rows, batch_rows, popular_rows = (rows[:, i] for i in range(4))
     scores = jnp.stack(

time: 322 us -> 316 us (0.981)
  the two profiles are of different devices: /device:TPU:68 before, /device:TPU:64 now
where the time goes in v10:
time: 316 us; the launch traced here: 314 us
  waiting for transfers between devices  96.6 us (31%)
  blocking collectives  95.8 us (30%)
  starting transfers between devices  77.7 us (25%)
  Pallas kernels  19.1 us (6%)
  between operations  17.2 us (5%)
  other arithmetic  5.19 us (2%)
    all_to_all x5, blocking collectives, exchange(): lax.all_to_all(values, axis, split_axis=0, concat_axis=0, tiled=True, axi...  95.8 us
    all_to_all x3, waiting for transfers between devices, exchange(): lax.all_to_all(values, axis, split_axis=0, concat_axis=0, tiled=True, axi...  51.1 us
    all_to_all x3, starting transfers between devices, exchange(): lax.all_to_all(values, axis, split_axis=0, concat_axis=0, tiled=True, axi...  32.2 us
    ppermute x8, starting transfers between devices, send_z(): return lax.ppermute(values, 'row', pairs)  31 us
    ppermute x8, waiting for transfers between devices, send_z(): return lax.ppermute(values, 'row', pairs)  25.8 us
    pallas_call x3, Pallas kernels, call_kernel(): pl.pallas_call(body, out_shape=[jax.ShapeDtypeStruct((*shape, HALF), jnp....  17.4 us
    ppermute x3, starting transfers between devices, send_x(): return lax.ppermute(values, 'row', pairs)  10.2 us
    reduce_scatter x1, waiting for transfers between devices, per_device(): lax.psum_scatter(first, 'col', scatter_dimension=0, tiled=True, axis_inde...  9.9 us
  transfers between devices with their start and end apart: 19, of which 13 were waited for; matrix products, arithmetic and copies ran while one was open for 2% of the time, Pallas kernels for 2%

profile of v10, /device:TPU:64, one launch (start us, length us, event | category | flops | bytes accessed | tf_op | source)
XLA Modules:
  0.0 314.4 jit_solution(13884824791513567728)
XLA Ops:
  7.3 0.7 all-gather.6.cloned.1.call-update
  7.9 1.8 shard_map.95
  9.7 17.8 %all-to-all-start = ((f32[8,128,128]{2,1,0:T(8,128)}), f32[8,128,128]{2,1,0:T(8,128)S(1)}, u32[]{:S(2)}, u32[]{:S(2)}) async-start(f32[8,128,128]{2,1,0:T(8,128)} %shard_map.95), calls=%async_computation | async-start | bytes 1048576 | tf_op jit(solution)/shard_map/all_to_all | solution.py:57
  28.3 0.8 gather_fusion
  29.2 2.4 collective-permute-start
  31.6 0.8 collective-permute-done
  32.3 4.7 %collective-permute-start.3 = (s32[2,16]{1,0:T(2,128)S(1)}, s32[2,16]{1,0:T(2,128)S(1)}, u32[]{:S(2)}, u32[]{:S(2)}) collective-permute-start(s32[2,16]{1,0:T(2,128)S(1)} %bitcast.89), channel_id=1, source_target_pairs={{0,768},{16,784},{32,800},{48,816},{64,832},{80,848},{96,864},{112... | collective-permute-start | bytes 392 | tf_op jit(solution)/shard_map/ppermute | solution.py:44
  37.0 2.7 collective-permute-start.2
  39.7 2.8 collective-permute-start.1
  42.5 1.4 collective-permute-done.2
  44.0 2.4 collective-permute-done.1
  46.7 0.7 convert_reduce_fusion.2
  47.3 0.6 add_select_fusion.1
  48.0 11.4 %all-to-all-done.refs_0_ = f32[8,128,128]{2,1,0:T(8,128)S(1)} async-done(((f32[8,128,128]{2,1,0:T(8,128)}), f32[8,128,128]{2,1,0:T(8,128)S(1)}, u32[]{:S(2)}, u32[]{:S(2)}) %all-to-all-start) | async-done | bytes 524320 | tf_op jit(solution)/shard_map/all_to_all | solution.py:57
  59.4 3.8 %collective-permute-start.7 = (f32[8,128,128]{2,1,0:T(8,128)S(1)}, f32[8,128,128]{2,1,0:T(8,128)S(1)}, u32[]{:S(2)}, u32[]{:S(2)}) collective-permute-start(f32[8,128,128]{2,1,0:T(8,128)S(1)} %all-to-all-done.refs_0_), channel_id=1, source_target_pairs={{0,16},{16,32},{32,48},{48,64},{64,80},{80,96},{96,112},{112,128},... | collective-permute-start | bytes 1572872 | tf_op jit(solution)/shard_map/ppermute | solution.py:49
  63.2 3.2 %collective-permute-start.4 = (f32[8,128,128]{2,1,0:T(8,128)S(1)}, f32[8,128,128]{2,1,0:T(8,128)S(1)}, u32[]{:S(2)}, u32[]{:S(2)}) collective-permute-start(f32[8,128,128]{2,1,0:T(8,128)S(1)} %all-to-all-done.refs_0_), channel_id=1, source_target_pairs={{0,240},{16,0},{32,16},{48,32},{64,48},{80,64},{96,80},{112,96},{1... | collective-permute-start | bytes 1572872 | tf_op jit(solution)/shard_map/ppermute | solution.py:49
  66.4 3.4 %collective-permute-start.6 = (f32[4,128,128]{2,1,0:T(8,128)S(1)}, f32[4,128,128]{2,1,0:T(8,128)S(1)}, u32[]{:S(2)}, u32[]{:S(2)}) collective-permute-start(f32[4,128,128]{2,1,0:T(8,128)S(1)} %get-tuple-element.47), channel_id=1, source_target_pairs={{0,32},{16,48},{32,64},{48,80},{64,96},{80,112},{96,128},{112,144}... | collective-permute-start | bytes 786440 | tf_op jit(solution)/shard_map/ppermute | solution.py:49
  69.8 4.6 %collective-permute-start.5 = (f32[4,128,128]{2,1,0:T(8,128)S(1)}, f32[4,128,128]{2,1,0:T(8,128)S(1)}, u32[]{:S(2)}, u32[]{:S(2)}) collective-permute-start(f32[4,128,128]{2,1,0:T(8,128)S(1)} %get-tuple-element.48), channel_id=1, source_target_pairs={{0,224},{16,240},{32,0},{48,16},{64,32},{80,48},{96,64},{112,80},{... | collective-permute-start | bytes 786440 | tf_op jit(solution)/shard_map/ppermute | solution.py:49
  74.4 1.4 pad_add_fusion.1.place_ref
  75.9 9.8 %collective-permute-done.6.refs_3_ = f32[4,128,128]{2,1,0:T(8,128)S(1)} collective-permute-done((f32[4,128,128]{2,1,0:T(8,128)S(1)}, f32[4,128,128]{2,1,0:T(8,128)S(1)}, u32[]{:S(2)}, u32[]{:S(2)}) %collective-permute-start.6) | collective-permute-done | bytes 262176 | tf_op jit(solution)/shard_map/ppermute | solution.py:49
  85.7 3.9 %collective-permute-done.5.refs_2_ = f32[4,128,128]{2,1,0:T(8,128)S(1)} collective-permute-done((f32[4,128,128]{2,1,0:T(8,128)S(1)}, f32[4,128,128]{2,1,0:T(8,128)S(1)}, u32[]{:S(2)}, u32[]{:S(2)}) %collective-permute-start.5) | collective-permute-done | bytes 262176 | tf_op jit(solution)/shard_map/ppermute | solution.py:49
  89.6 6.3 %shard_map.96 = f32[32,176,128]{2,1,0:T(8,128)} custom-call(s32[3]{0:T(128)S(1)} %pad_add_fusion.1.place_ref, s32[128]{0:T(128)S(1)} %select_reduce_fusion.list_ref, f32[128,128,128]{2,1,0:T(8,128)} %bitcast.70, f32[8,128,128]{2,1,0:T(8,128)S(1)} %all-to-all-done.refs_0_, f32[8,128,128]{2,1,0:T(8,128)S(1)} %collective-permute-done.4.refs_1_, ...), custom_call_target="tpu_custom_call" | custom-call | tf_op jit(solution)/shard_map/pallas_call | solution.py:200
  95.9 3.8 %shard_map.97 = f32[32,80,128]{2,1,0:T(8,128)S(1)} custom-call(s32[3]{0:T(128)S(1)} %pad_add_fusion.1.place_ref, s32[128]{0:T(128)S(1)} %select_reduce_fusion.list_ref, f32[128,128,128]{2,1,0:T(8,128)} %bitcast.71, f32[8,128,128]{2,1,0:T(8,128)S(1)} %all-to-all-done.refs_0_, f32[8,128,128]{2,1,0:T(8,128)S(1)} %collective-permute-done.4.refs_1_, ...), custom_call_target="tpu_custom_call" | custom-call | tf_op jit(solution)/shard_map/pallas_call | solution.py:200
  99.7 18.8 %all_to_all.40 = f32[4,640,128]{2,1,0:T(8,128)S(1)} all-to-all(f32[4,640,128]{2,1,0:T(8,128)S(1)} %bitcast.68), channel_id=1, replica_groups={{0,256,512,768},{16,272,528,784},{32,288,544,800},{48,304,560,816},{64,..., dimensions={0} | all-to-all | bytes 2621440 | tf_op jit(solution)/shard_map/all_to_all | solution.py:57
  118.6 21.2 %all_to_all.41 = f32[8,80,128]{2,1,0:T(8,128)S(1)} all-to-all(f32[8,80,128]{2,1,0:T(8,128)S(1)} %bitcast.75), channel_id=1, replica_groups={{0,2,4,6,8,10,12,14},{1,3,5,7,9,11,13,15},{16,18,20,22,24,26,28,30},{17..., dimensions={0} | all-to-all | bytes 655360 | tf_op jit(solution)/shard_map/all_to_all | solution.py:57
  139.8 9.9 %reduce-scatter.2.cloned.1.call-done = f32[4,176,128]{2,1,0:T(8,128)} async-done(((f32[32,176,128]{2,1,0:T(8,128)}), f32[4,176,128]{2,1,0:T(8,128)}) %reduce-scatter.2.cloned.1.call-update) | async-done | bytes 360464 | tf_op jit(solution)/shard_map/reduce_scatter | solution.py:275
  149.7 4.2 %all-to-all-start.1 = ((f32[4,176,128]{2,1,0:T(8,128)}), f32[4,176,128]{2,1,0:T(8,128)S(1)}, u32[]{:S(2)}, u32[]{:S(2)}) async-start(f32[4,176,128]{2,1,0:T(8,128)} %reduce-scatter.2.cloned.1.call-done), calls=%async_computation.2 | async-start | bytes 720896 | tf_op jit(solution)/shard_map/all_to_all | solution.py:57
  154.0 7.2 %all-to-all-done.1 = f32[4,176,128]{2,1,0:T(8,128)S(1)} async-done(((f32[4,176,128]{2,1,0:T(8,128)}), f32[4,176,128]{2,1,0:T(8,128)S(1)}, u32[]{:S(2)}, u32[]{:S(2)}) %all-to-all-start.1) | async-done | bytes 360480 | tf_op jit(solution)/shard_map/all_to_all | solution.py:57
  161.2 0.3 fusion.9
  161.7 1.9 collective-permute-start.8
  163.6 1.1 collective-permute-done.8
  165.0 0.5 fusion.1
  165.6 10.7 %all_to_all.42 = f32[4,144,128]{2,1,0:T(8,128)} all-to-all(f32[4,144,128]{2,1,0:T(8,128)S(1)} %broadcast_in_dim.85), channel_id=1, replica_groups={{0,256,512,768},{16,272,528,784},{32,288,544,800},{48,304,560,816},{64,..., dimensions={0} | all-to-all | bytes 589824 | tf_op jit(solution)/shard_map/all_to_all | solution.py:57
  176.3 21.0 %all_to_all.43 = f32[8,112,128]{2,1,0:T(8,128)S(1)} all-to-all(f32[8,112,128]{2,1,0:T(8,128)S(1)} %broadcast_in_dim.86), channel_id=1, replica_groups={{0,2,4,6,8,10,12,14},{1,3,5,7,9,11,13,15},{16,18,20,22,24,26,28,30},{17..., dimensions={0} | all-to-all | bytes 917504 | tf_op jit(solution)/shard_map/all_to_all | solution.py:57
  197.5 24.1 %all_to_all.44 = f32[4,896,128]{2,1,0:T(8,128)S(1)} all-to-all(f32[4,896,128]{2,1,0:T(8,128)S(1)} %broadcast_in_dim.88), channel_id=1, replica_groups={{0,256,512,768},{16,272,528,784},{32,288,544,800},{48,304,560,816},{64,..., dimensions={0} | all-to-all | bytes 3670016 | tf_op jit(solution)/shard_map/all_to_all | solution.py:57
  221.5 3.2 %all-gather.4.cloned.1.call-done.even_ref = f32[32,144,128]{2,1,0:T(8,128)} async-done(((f32[4,144,128]{2,1,0:T(8,128)}), f32[32,144,128]{2,1,0:T(8,128)}) %all-gather.4.cloned.1.call-update) | async-done | bytes 2359312 | tf_op jit(solution)/shard_map/all_gather | solution.py:320
  224.7 7.3 %shard_map.98 = (f32[8,128,128]{2,1,0:T(8,128)S(1)}, f32[8,128,128]{2,1,0:T(8,128)S(1)}, f32[4,128,128]{2,1,0:T(8,128)}, f32[4,128,128]{2,1,0:T(8,128)}, f32[8,128,128]{2,1,0:T(8,128)S(1)}) custom-call(s32[3]{0:T(128)S(1)} %pad_add_fusion.1.place_ref, s32[128]{0:T(128)S(1)} %select_reduce_fusion.list_ref, f32[128,128,128]{2,1,0:T(8,128)} %bitcast.72, ...), custom_call_target="tpu_custom_call" | custom-call | tf_op jit(solution)/shard_map/pallas_call | solution.py:200
  232.0 3.8 %collective-permute-start.9 = (f32[8,128,128]{2,1,0:T(8,128)S(1)}, f32[8,128,128]{2,1,0:T(8,128)S(1)}, u32[]{:S(2)}, u32[]{:S(2)}) collective-permute-start(f32[8,128,128]{2,1,0:T(8,128)S(1)} %get-tuple-element.30), channel_id=1, source_target_pairs={{0,16},{16,32},{32,48},{48,64},{64,80},{80,96},{96,112},{112,128},... | collective-permute-start | bytes 1572872 | tf_op jit(solution)/shard_map/ppermute | solution.py:49
  235.8 2.1 collective-permute-start.10
  237.9 8.4 %collective-permute-start.11 = (f32[4,128,128]{2,1,0:T(8,128)}, f32[4,128,128]{2,1,0:T(8,128)S(1)}, u32[]{:S(2)}, u32[]{:S(2)}) collective-permute-start(f32[4,128,128]{2,1,0:T(8,128)} %get-tuple-element.32), channel_id=1, source_target_pairs={{0,32},{16,48},{32,64},{48,80},{64,96},{80,112},{96,128},{112,144}... | collective-permute-start | bytes 786440 | tf_op jit(solution)/shard_map/ppermute | solution.py:49
  246.3 1.9 collective-permute-start.12
  248.4 10.2 %collective-permute-done.11 = f32[4,128,128]{2,1,0:T(8,128)S(1)} collective-permute-done((f32[4,128,128]{2,1,0:T(8,128)}, f32[4,128,128]{2,1,0:T(8,128)S(1)}, u32[]{:S(2)}, u32[]{:S(2)}) %collective-permute-start.11) | collective-permute-done | bytes 262176 | tf_op jit(solution)/shard_map/ppermute | solution.py:49
  258.6 1.9 collective-permute-done.12
  260.5 1.0 fusion
  261.5 10.2 %all-to-all-start.7 = ((f32[8,128,128]{2,1,0:T(8,128)}), f32[8,128,128]{2,1,0:T(8,128)S(1)}, u32[]{:S(2)}, u32[]{:S(2)}) async-start(f32[8,128,128]{2,1,0:T(8,128)} %fusion), calls=%async_computation.8 | async-start | bytes 1048576 | tf_op jit(solution)/shard_map/all_to_all | solution.py:57
  271.7 0.6 fusion.38
  273.5 32.5 %all-to-all-done.7 = f32[8,128,128]{2,1,0:T(8,128)S(1)} async-done(((f32[8,128,128]{2,1,0:T(8,128)}), f32[8,128,128]{2,1,0:T(8,128)S(1)}, u32[]{:S(2)}, u32[]{:S(2)}) %all-to-all-start.7) | async-done | bytes 524320 | tf_op jit(solution)/shard_map/all_to_all | solution.py:57
  306.1 0.7 pad_maximum_fusion.1
  (57 shorter events, 1.5 us)
Async XLA Ops:
  7.2 21.1 %copy-start.4 = (s32[1,64]{1,0:T(1,128)S(1)}, s32[1,64]{1,0:T(1,128)}, u32[]{:S(2)}) copy-start(s32[1,64]{1,0:T(1,128)} %param.14) | copy-start | bytes 772
  7.2 21.1 %copy-start = (s32[1,64]{1,0:T(1,128)S(1)}, s32[1,64]{1,0:T(1,128)}, u32[]{:S(2)}) copy-start(s32[1,64]{1,0:T(1,128)} %param.13) | copy-start | bytes 772
  7.2 21.9 %copy-start.3 = (s32[1,16]{1,0:T(1,128)S(1)}, s32[1,16]{1,0:T(1,128)}, u32[]{:S(2)}) copy-start(s32[1,16]{1,0:T(1,128)} %param.10) | copy-start | bytes 196
  7.2 21.9 %copy-start.2 = (s32[1,64]{1,0:T(1,128)S(1)}, s32[1,64]{1,0:T(1,128)}, u32[]{:S(2)}) copy-start(s32[1,64]{1,0:T(1,128)} %param.15) | copy-start | bytes 772
  7.2 21.9 %copy-start.1 = (s32[1,64]{1,0:T(1,128)S(1)}, s32[1,64]{1,0:T(1,128)}, u32[]{:S(2)}) copy-start(s32[1,64]{1,0:T(1,128)} %param.12) | copy-start | bytes 772
  7.2 82.4 %all-gather.6.cloned.1.call-start = ((), (), s32[]{:S(2)}) async-start(), calls=%async_computation.11 | async-start | bytes 9437184 | tf_op jit(solution)/shard_map/all_gather | solution.py:250
  9.7 49.7 %all-to-all-start = ((f32[8,128,128]{2,1,0:T(8,128)}), f32[8,128,128]{2,1,0:T(8,128)S(1)}, u32[]{:S(2)}, u32[]{:S(2)}) async-start(f32[8,128,128]{2,1,0:T(8,128)} %shard_map.95), calls=%async_computation | async-start | bytes 1048576 | tf_op jit(solution)/shard_map/all_to_all | solution.py:57
  27.6 122.2 %reduce-scatter.2.cloned.1.call-start = ((), (), s32[]{:S(2)}) async-start(), calls=%async_computation.9 | async-start | bytes 3244032 | tf_op jit(solution)/shard_map/reduce_scatter | solution.py:275
  29.2 3.2 %collective-permute-start = (s32[5,64]{1,0:T(8,128)S(1)}, s32[5,64]{1,0:T(8,128)S(1)}, u32[]{:S(2)}, u32[]{:S(2)}) collective-permute-start(s32[5,64]{1,0:T(8,128)S(1)} %stack.65), channel_id=1, source_target_pairs={{0,1},{1,0},{2,3},{3,2},{4,5},{5,4},{6,7},{7,6},{8,9},{9,8},{10,11... | collective-permute-start | bytes 3848 | tf_op jit(solution)/shard_map/ppermute | solution.py:53
  32.3 10.2 %collective-permute-start.3 = (s32[2,16]{1,0:T(2,128)S(1)}, s32[2,16]{1,0:T(2,128)S(1)}, u32[]{:S(2)}, u32[]{:S(2)}) collective-permute-start(s32[2,16]{1,0:T(2,128)S(1)} %bitcast.89), channel_id=1, source_target_pairs={{0,768},{16,784},{32,800},{48,816},{64,832},{80,848},{96,864},{112... | collective-permute-start | bytes 392 | tf_op jit(solution)/shard_map/ppermute | solution.py:44
  37.0 7.0 %collective-permute-start.2 = (s32[2,16]{1,0:T(2,128)S(1)}, s32[2,16]{1,0:T(2,128)S(1)}, u32[]{:S(2)}, u32[]{:S(2)}) collective-permute-start(s32[2,16]{1,0:T(2,128)S(1)} %bitcast.90), channel_id=1, source_target_pairs={{0,512},{16,528},{32,544},{48,560},{64,576},{80,592},{96,608},{112... | collective-permute-start | bytes 392 | tf_op jit(solution)/shard_map/ppermute | solution.py:44
  39.7 6.7 %collective-permute-start.1 = (s32[2,16]{1,0:T(2,128)S(1)}, s32[2,16]{1,0:T(2,128)S(1)}, u32[]{:S(2)}, u32[]{:S(2)}) collective-permute-start(s32[2,16]{1,0:T(2,128)S(1)} %bitcast.91), channel_id=1, source_target_pairs={{0,256},{16,272},{32,288},{48,304},{64,320},{80,336},{96,352},{112... | collective-permute-start | bytes 392 | tf_op jit(solution)/shard_map/ppermute | solution.py:44
  59.4 30.2 %collective-permute-start.7 = (f32[8,128,128]{2,1,0:T(8,128)S(1)}, f32[8,128,128]{2,1,0:T(8,128)S(1)}, u32[]{:S(2)}, u32[]{:S(2)}) collective-permute-start(f32[8,128,128]{2,1,0:T(8,128)S(1)} %all-to-all-done.refs_0_), channel_id=1, source_target_pairs={{0,16},{16,32},{32,48},{48,64},{64,80},{80,96},{96,112},{112,128},... | collective-permute-start | bytes 1572872 | tf_op jit(solution)/shard_map/ppermute | solution.py:49
  63.2 26.4 %collective-permute-start.4 = (f32[8,128,128]{2,1,0:T(8,128)S(1)}, f32[8,128,128]{2,1,0:T(8,128)S(1)}, u32[]{:S(2)}, u32[]{:S(2)}) collective-permute-start(f32[8,128,128]{2,1,0:T(8,128)S(1)} %all-to-all-done.refs_0_), channel_id=1, source_target_pairs={{0,240},{16,0},{32,16},{48,32},{64,48},{80,64},{96,80},{112,96},{1... | collective-permute-start | bytes 1572872 | tf_op jit(solution)/shard_map/ppermute | solution.py:49
  66.4 19.2 %collective-permute-start.6 = (f32[4,128,128]{2,1,0:T(8,128)S(1)}, f32[4,128,128]{2,1,0:T(8,128)S(1)}, u32[]{:S(2)}, u32[]{:S(2)}) collective-permute-start(f32[4,128,128]{2,1,0:T(8,128)S(1)} %get-tuple-element.47), channel_id=1, source_target_pairs={{0,32},{16,48},{32,64},{48,80},{64,96},{80,112},{96,128},{112,144}... | collective-permute-start | bytes 786440 | tf_op jit(solution)/shard_map/ppermute | solution.py:49
  69.8 19.8 %collective-permute-start.5 = (f32[4,128,128]{2,1,0:T(8,128)S(1)}, f32[4,128,128]{2,1,0:T(8,128)S(1)}, u32[]{:S(2)}, u32[]{:S(2)}) collective-permute-start(f32[4,128,128]{2,1,0:T(8,128)S(1)} %get-tuple-element.48), channel_id=1, source_target_pairs={{0,224},{16,240},{32,0},{48,16},{64,32},{80,48},{96,64},{112,80},{... | collective-permute-start | bytes 786440 | tf_op jit(solution)/shard_map/ppermute | solution.py:49
  149.7 11.4 %all-to-all-start.1 = ((f32[4,176,128]{2,1,0:T(8,128)}), f32[4,176,128]{2,1,0:T(8,128)S(1)}, u32[]{:S(2)}, u32[]{:S(2)}) async-start(f32[4,176,128]{2,1,0:T(8,128)} %reduce-scatter.2.cloned.1.call-done), calls=%async_computation.2 | async-start | bytes 720896 | tf_op jit(solution)/shard_map/all_to_all | solution.py:57
  153.9 70.8 %all-gather.4.cloned.1.call-start = ((), (), s32[]{:S(2)}) async-start(), calls=%async_computation.10 | async-start | bytes 2654208 | tf_op jit(solution)/shard_map/all_gather | solution.py:320
  161.7 3.1 collective-permute-start.8
  232.0 28.5 %collective-permute-start.9 = (f32[8,128,128]{2,1,0:T(8,128)S(1)}, f32[8,128,128]{2,1,0:T(8,128)S(1)}, u32[]{:S(2)}, u32[]{:S(2)}) collective-permute-start(f32[8,128,128]{2,1,0:T(8,128)S(1)} %get-tuple-element.30), channel_id=1, source_target_pairs={{0,16},{16,32},{32,48},{48,64},{64,80},{80,96},{96,112},{112,128},... | collective-permute-start | bytes 1572872 | tf_op jit(solution)/shard_map/ppermute | solution.py:49
  235.8 24.7 %collective-permute-start.10 = (f32[8,128,128]{2,1,0:T(8,128)S(1)}, f32[8,128,128]{2,1,0:T(8,128)S(1)}, u32[]{:S(2)}, u32[]{:S(2)}) collective-permute-start(f32[8,128,128]{2,1,0:T(8,128)S(1)} %get-tuple-element.31), channel_id=1, source_target_pairs={{0,240},{16,0},{32,16},{48,32},{64,48},{80,64},{96,80},{112,96},{1... | collective-permute-start | bytes 1572872 | tf_op jit(solution)/shard_map/ppermute | solution.py:49
  237.9 20.7 %collective-permute-start.11 = (f32[4,128,128]{2,1,0:T(8,128)}, f32[4,128,128]{2,1,0:T(8,128)S(1)}, u32[]{:S(2)}, u32[]{:S(2)}) collective-permute-start(f32[4,128,128]{2,1,0:T(8,128)} %get-tuple-element.32), channel_id=1, source_target_pairs={{0,32},{16,48},{32,64},{48,80},{64,96},{80,112},{96,128},{112,144}... | collective-permute-start | bytes 786440 | tf_op jit(solution)/shard_map/ppermute | solution.py:49
  246.3 14.2 %collective-permute-start.12 = (f32[4,128,128]{2,1,0:T(8,128)}, f32[4,128,128]{2,1,0:T(8,128)S(1)}, u32[]{:S(2)}, u32[]{:S(2)}) collective-permute-start(f32[4,128,128]{2,1,0:T(8,128)} %get-tuple-element.33), channel_id=1, source_target_pairs={{0,224},{16,240},{32,0},{48,16},{64,32},{80,48},{96,64},{112,80},{... | collective-permute-start | bytes 786440 | tf_op jit(solution)/shard_map/ppermute | solution.py:49
  261.5 44.6 %all-to-all-start.7 = ((f32[8,128,128]{2,1,0:T(8,128)}), f32[8,128,128]{2,1,0:T(8,128)S(1)}, u32[]{:S(2)}, u32[]{:S(2)}) async-start(f32[8,128,128]{2,1,0:T(8,128)} %fusion), calls=%async_computation.8 | async-start | bytes 1048576 | tf_op jit(solution)/shard_map/all_to_all | solution.py:57
Sparse Core Ops, SparseCore 0:
  10.8 67.4 all-gather.5
  96.1 53.6 reduce-scatter.1
  176.4 48.2 all-gather.3

commit v11 on v10

--- a/solution.py
+++ b/solution.py
@@ -16,8 +16,9 @@
 CB = 64
 PAIRS = 64
 ENTRIES = 2 * NX * SLOTS
-EXTRA = 48
+EXTRA = 32
 EXTRA_BACK = 16
+GROUP = 4
 VMEM_LIMIT = 48 * 1024 * 1024
 
 precise = lax.Precision.HIGHEST
@@ -88,21 +89,21 @@
     return number // (2 * SLOTS), position // (2 * CB), near
 
 
-def for_pairs(first, last, wait, compute, add):
-    @pl.loop(0, (last - first + 1) // 2)
+def for_groups(first, last, wait, compute, add):
+    @pl.loop(0, (last - first + GROUP - 1) // GROUP)
     def _(step):
-        index = first + 2 * step
-        both = index + 1 < last
-        other = jnp.where(both, index + 1, index)
-        wait(index)
-
-        @pl.when(both)
-        def _():
-            wait(other)
-
-        value, other_value = compute(index), compute(other)
-        add(index, value)
-        add(other, jnp.where(both, other_value, 0.0))
+        start = first + GROUP * step
+        wait(start)
+        for index in range(1, GROUP):
+
+            @pl.when(start + index < last)
+            def _():
+                wait(start + index)
+
+        places = [jnp.minimum(start + index, last - 1) for index in range(GROUP)]
+        values = [compute(place) for place in places]
+        for index, (place, value) in enumerate(zip(places, values)):
+            add(place, value if index == 0 else jnp.where(start + index < last, value, 0.0))
 
 
 def forward_kernel(odd, place_ref, list_ref, source_ref, *refs):
@@ -139,7 +140,7 @@
             x, y, _ = decode(list_ref[index], own_z)
             out_ref[x * NY + y if odd else y * NX + x, out_rows] += value
 
-        for_pairs(first, last, lambda index: copy(index, rows).wait(), compute, add)
+        for_groups(first, last, lambda index: copy(index, rows).wait(), compute, add)
 
 
 def backward_kernel(place_ref, list_ref, source_ref, even_ref, odd_ref, *refs):
@@ -182,7 +183,7 @@
         _, _, near = decode(list_ref[index], own_z)
         total_ref[near] += value
 
-    for_pairs(0, end, wait, compute, add)
+    for_groups(0, end, wait, compute, add)
     start = 0
     for out in outs:
         out[...] = total_ref[pl.ds(start, out.shape[0])]

time: 316 us -> 313 us (level)
  the two profiles are of different devices: /device:TPU:64 before, /device:TPU:2 now
where the time goes in v11:
time: 313 us; the launch traced here: 312 us
  blocking collectives  103 us (33%)
  starting transfers between devices  84.3 us (27%)
  waiting for transfers between devices  83 us (27%)
  between operations  17.3 us (6%)
  Pallas kernels  16.4 us (5%)
  other arithmetic  5.2 us (2%)
    all_to_all x5, blocking collectives, exchange(): lax.all_to_all(values, axis, split_axis=0, concat_axis=0, tiled=True, axi...  103 us
    all_to_all x3, waiting for transfers between devices, exchange(): lax.all_to_all(values, axis, split_axis=0, concat_axis=0, tiled=True, axi...  51.2 us
    all_to_all x3, starting transfers between devices, exchange(): lax.all_to_all(values, axis, split_axis=0, concat_axis=0, tiled=True, axi...  35.1 us
    ppermute x8, starting transfers between devices, send_z(): return lax.ppermute(values, 'row', pairs)  34.3 us
    ppermute x8, waiting for transfers between devices, send_z(): return lax.ppermute(values, 'row', pairs)  22.5 us
    pallas_call x3, Pallas kernels, call_kernel(): pl.pallas_call(body, out_shape=[jax.ShapeDtypeStruct((*shape, HALF), jnp....  14.6 us
    ppermute x3, starting transfers between devices, send_x(): return lax.ppermute(values, 'row', pairs)  10.5 us
  transfers between devices with their start and end apart: 19, of which 12 were waited for; matrix products, arithmetic and copies ran while one was open for 2% of the time, Pallas kernels for 2%

profile of v11, /device:TPU:2, one launch (start us, length us, event | category | flops | bytes accessed | tf_op | source)
XLA Modules:
  0.0 311.9 jit_solution(7417129931614986435)
XLA Ops:
  7.3 0.7 all-gather.6.cloned.1.call-update
  7.9 1.8 shard_map.95
  9.7 18.7 %all-to-all-start = ((f32[8,128,128]{2,1,0:T(8,128)}), f32[8,128,128]{2,1,0:T(8,128)S(1)}, u32[]{:S(2)}, u32[]{:S(2)}) async-start(f32[8,128,128]{2,1,0:T(8,128)} %shard_map.95), calls=%async_computation | async-start | bytes 1048576 | tf_op jit(solution)/shard_map/all_to_all | solution.py:58
  29.2 0.8 gather_fusion
  30.0 2.4 collective-permute-start
  32.5 0.8 collective-permute-done
  33.2 2.4 collective-permute-start.3
  35.7 4.3 %collective-permute-start.2 = (s32[2,16]{1,0:T(2,128)S(1)}, s32[2,16]{1,0:T(2,128)S(1)}, u32[]{:S(2)}, u32[]{:S(2)}) collective-permute-start(s32[2,16]{1,0:T(2,128)S(1)} %bitcast.90), channel_id=1, source_target_pairs={{0,512},{16,528},{32,544},{48,560},{64,576},{80,592},{96,608},{112... | collective-permute-start | bytes 392 | tf_op jit(solution)/shard_map/ppermute | solution.py:45
  40.0 3.7 %collective-permute-start.1 = (s32[2,16]{1,0:T(2,128)S(1)}, s32[2,16]{1,0:T(2,128)S(1)}, u32[]{:S(2)}, u32[]{:S(2)}) collective-permute-start(s32[2,16]{1,0:T(2,128)S(1)} %bitcast.91), channel_id=1, source_target_pairs={{0,256},{16,272},{32,288},{48,304},{64,320},{80,336},{96,352},{112... | collective-permute-start | bytes 392 | tf_op jit(solution)/shard_map/ppermute | solution.py:45
  43.8 1.7 collective-permute-done.1
  45.7 0.7 convert_reduce_fusion.2
  46.4 0.6 add_select_fusion.1
  47.1 15.8 %all-to-all-done.refs_0_ = f32[8,128,128]{2,1,0:T(8,128)S(1)} async-done(((f32[8,128,128]{2,1,0:T(8,128)}), f32[8,128,128]{2,1,0:T(8,128)S(1)}, u32[]{:S(2)}, u32[]{:S(2)}) %all-to-all-start) | async-done | bytes 524320 | tf_op jit(solution)/shard_map/all_to_all | solution.py:58
  62.9 1.9 collective-permute-start.7
  64.8 5.1 %collective-permute-start.4 = (f32[8,128,128]{2,1,0:T(8,128)S(1)}, f32[8,128,128]{2,1,0:T(8,128)S(1)}, u32[]{:S(2)}, u32[]{:S(2)}) collective-permute-start(f32[8,128,128]{2,1,0:T(8,128)S(1)} %all-to-all-done.refs_0_), channel_id=1, source_target_pairs={{0,240},{16,0},{32,16},{48,32},{64,48},{80,64},{96,80},{112,96},{1... | collective-permute-start | bytes 1572872 | tf_op jit(solution)/shard_map/ppermute | solution.py:50
  70.0 1.9 collective-permute-start.6
  71.9 6.0 %collective-permute-start.5 = (f32[4,128,128]{2,1,0:T(8,128)S(1)}, f32[4,128,128]{2,1,0:T(8,128)S(1)}, u32[]{:S(2)}, u32[]{:S(2)}) collective-permute-start(f32[4,128,128]{2,1,0:T(8,128)S(1)} %get-tuple-element.48), channel_id=1, source_target_pairs={{0,224},{16,240},{32,0},{48,16},{64,32},{80,48},{96,64},{112,80},{... | collective-permute-start | bytes 786440 | tf_op jit(solution)/shard_map/ppermute | solution.py:50
  78.0 1.4 pad_add_fusion.1.place_ref
  79.5 6.6 %collective-permute-done.6.refs_3_ = f32[4,128,128]{2,1,0:T(8,128)S(1)} collective-permute-done((f32[4,128,128]{2,1,0:T(8,128)S(1)}, f32[4,128,128]{2,1,0:T(8,128)S(1)}, u32[]{:S(2)}, u32[]{:S(2)}) %collective-permute-start.6) | collective-permute-done | bytes 262176 | tf_op jit(solution)/shard_map/ppermute | solution.py:50
  86.1 5.5 %collective-permute-done.5.refs_2_ = f32[4,128,128]{2,1,0:T(8,128)S(1)} collective-permute-done((f32[4,128,128]{2,1,0:T(8,128)S(1)}, f32[4,128,128]{2,1,0:T(8,128)S(1)}, u32[]{:S(2)}, u32[]{:S(2)}) %collective-permute-start.5) | collective-permute-done | bytes 262176 | tf_op jit(solution)/shard_map/ppermute | solution.py:50
  91.6 5.5 %shard_map.96 = f32[32,160,128]{2,1,0:T(8,128)} custom-call(s32[3]{0:T(128)S(1)} %pad_add_fusion.1.place_ref, s32[128]{0:T(128)S(1)} %select_reduce_fusion.list_ref, f32[128,128,128]{2,1,0:T(8,128)} %bitcast.70, f32[8,128,128]{2,1,0:T(8,128)S(1)} %all-to-all-done.refs_0_, f32[8,128,128]{2,1,0:T(8,128)S(1)} %collective-permute-done.4.refs_1_, ...), custom_call_target="tpu_custom_call" | custom-call | tf_op jit(solution)/shard_map/pallas_call | solution.py:201
  97.1 3.1 shard_map.97
  100.2 21.6 %all_to_all.40 = f32[4,768,128]{2,1,0:T(8,128)S(1)} all-to-all(f32[4,768,128]{2,1,0:T(8,128)S(1)} %bitcast.68), channel_id=1, replica_groups={{0,256,512,768},{16,272,528,784},{32,288,544,800},{48,304,560,816},{64,..., dimensions={0} | all-to-all | bytes 3145728 | tf_op jit(solution)/shard_map/all_to_all | solution.py:58
  121.9 26.6 %all_to_all.41 = f32[8,96,128]{2,1,0:T(8,128)S(1)} all-to-all(f32[8,96,128]{2,1,0:T(8,128)S(1)} %bitcast.75), channel_id=1, replica_groups={{0,2,4,6,8,10,12,14},{1,3,5,7,9,11,13,15},{16,18,20,22,24,26,28,30},{17..., dimensions={0} | all-to-all | bytes 786432 | tf_op jit(solution)/shard_map/all_to_all | solution.py:58
  148.5 0.2 reduce-scatter.2.cloned.1.call-done
  148.7 5.2 %all-to-all-start.1 = ((f32[4,160,128]{2,1,0:T(8,128)}), f32[4,160,128]{2,1,0:T(8,128)S(1)}, u32[]{:S(2)}, u32[]{:S(2)}) async-start(f32[4,160,128]{2,1,0:T(8,128)} %reduce-scatter.2.cloned.1.call-done), calls=%async_computation.2 | async-start | bytes 655360 | tf_op jit(solution)/shard_map/all_to_all | solution.py:58
  153.9 5.5 %all-to-all-done.1 = f32[4,160,128]{2,1,0:T(8,128)S(1)} async-done(((f32[4,160,128]{2,1,0:T(8,128)}), f32[4,160,128]{2,1,0:T(8,128)S(1)}, u32[]{:S(2)}, u32[]{:S(2)}) %all-to-all-start.1) | async-done | bytes 327712 | tf_op jit(solution)/shard_map/all_to_all | solution.py:58
  159.5 0.3 fusion.9
  160.0 1.9 collective-permute-start.8
  161.9 1.1 collective-permute-done.8
  163.1 0.1 add_negate_fusion
  163.3 0.5 fusion.1
  163.9 10.7 %all_to_all.42 = f32[4,144,128]{2,1,0:T(8,128)} all-to-all(f32[4,144,128]{2,1,0:T(8,128)S(1)} %broadcast_in_dim.85), channel_id=1, replica_groups={{0,256,512,768},{16,272,528,784},{32,288,544,800},{48,304,560,816},{64,..., dimensions={0} | all-to-all | bytes 589824 | tf_op jit(solution)/shard_map/all_to_all | solution.py:58
  174.7 20.1 %all_to_all.43 = f32[8,112,128]{2,1,0:T(8,128)S(1)} all-to-all(f32[8,112,128]{2,1,0:T(8,128)S(1)} %broadcast_in_dim.86), channel_id=1, replica_groups={{0,2,4,6,8,10,12,14},{1,3,5,7,9,11,13,15},{16,18,20,22,24,26,28,30},{17..., dimensions={0} | all-to-all | bytes 917504 | tf_op jit(solution)/shard_map/all_to_all | solution.py:58
  194.9 24.1 %all_to_all.44 = f32[4,896,128]{2,1,0:T(8,128)S(1)} all-to-all(f32[4,896,128]{2,1,0:T(8,128)S(1)} %broadcast_in_dim.88), channel_id=1, replica_groups={{0,256,512,768},{16,272,528,784},{32,288,544,800},{48,304,560,816},{64,..., dimensions={0} | all-to-all | bytes 3670016 | tf_op jit(solution)/shard_map/all_to_all | solution.py:58
  218.9 4.8 %all-gather.4.cloned.1.call-done.even_ref = f32[32,144,128]{2,1,0:T(8,128)} async-done(((f32[4,144,128]{2,1,0:T(8,128)}), f32[32,144,128]{2,1,0:T(8,128)}) %all-gather.4.cloned.1.call-update) | async-done | bytes 2359312 | tf_op jit(solution)/shard_map/all_gather | solution.py:321
  223.7 6.0 %shard_map.98 = (f32[8,128,128]{2,1,0:T(8,128)S(1)}, f32[8,128,128]{2,1,0:T(8,128)S(1)}, f32[4,128,128]{2,1,0:T(8,128)}, f32[4,128,128]{2,1,0:T(8,128)}, f32[8,128,128]{2,1,0:T(8,128)S(1)}) custom-call(s32[3]{0:T(128)S(1)} %pad_add_fusion.1.place_ref, s32[128]{0:T(128)S(1)} %select_reduce_fusion.list_ref, f32[128,128,128]{2,1,0:T(8,128)} %bitcast.72, ...), custom_call_target="tpu_custom_call" | custom-call | tf_op jit(solution)/shard_map/pallas_call | solution.py:201
  229.7 4.2 %collective-permute-start.9 = (f32[8,128,128]{2,1,0:T(8,128)S(1)}, f32[8,128,128]{2,1,0:T(8,128)S(1)}, u32[]{:S(2)}, u32[]{:S(2)}) collective-permute-start(f32[8,128,128]{2,1,0:T(8,128)S(1)} %get-tuple-element.30), channel_id=1, source_target_pairs={{0,16},{16,32},{32,48},{48,64},{64,80},{80,96},{96,112},{112,128},... | collective-permute-start | bytes 1572872 | tf_op jit(solution)/shard_map/ppermute | solution.py:50
  233.9 7.2 %collective-permute-start.10 = (f32[8,128,128]{2,1,0:T(8,128)S(1)}, f32[8,128,128]{2,1,0:T(8,128)S(1)}, u32[]{:S(2)}, u32[]{:S(2)}) collective-permute-start(f32[8,128,128]{2,1,0:T(8,128)S(1)} %get-tuple-element.31), channel_id=1, source_target_pairs={{0,240},{16,0},{32,16},{48,32},{64,48},{80,64},{96,80},{112,96},{1... | collective-permute-start | bytes 1572872 | tf_op jit(solution)/shard_map/ppermute | solution.py:50
  241.1 1.9 collective-permute-start.11
  243.0 6.0 %collective-permute-start.12 = (f32[4,128,128]{2,1,0:T(8,128)}, f32[4,128,128]{2,1,0:T(8,128)S(1)}, u32[]{:S(2)}, u32[]{:S(2)}) collective-permute-start(f32[4,128,128]{2,1,0:T(8,128)} %get-tuple-element.33), channel_id=1, source_target_pairs={{0,224},{16,240},{32,0},{48,16},{64,32},{80,48},{96,64},{112,80},{... | collective-permute-start | bytes 786440 | tf_op jit(solution)/shard_map/ppermute | solution.py:50
  249.2 9.8 %collective-permute-done.11 = f32[4,128,128]{2,1,0:T(8,128)S(1)} collective-permute-done((f32[4,128,128]{2,1,0:T(8,128)}, f32[4,128,128]{2,1,0:T(8,128)S(1)}, u32[]{:S(2)}, u32[]{:S(2)}) %collective-permute-start.11) | collective-permute-done | bytes 262176 | tf_op jit(solution)/shard_map/ppermute | solution.py:50
  259.1 0.6 collective-permute-done.12
  259.7 1.0 fusion
  260.7 11.2 %all-to-all-start.7 = ((f32[8,128,128]{2,1,0:T(8,128)}), f32[8,128,128]{2,1,0:T(8,128)S(1)}, u32[]{:S(2)}, u32[]{:S(2)}) async-start(f32[8,128,128]{2,1,0:T(8,128)} %fusion), calls=%async_computation.8 | async-start | bytes 1048576 | tf_op jit(solution)/shard_map/all_to_all | solution.py:58
  271.8 0.6 fusion.38
  273.7 29.8 %all-to-all-done.7 = f32[8,128,128]{2,1,0:T(8,128)S(1)} async-done(((f32[8,128,128]{2,1,0:T(8,128)}), f32[8,128,128]{2,1,0:T(8,128)S(1)}, u32[]{:S(2)}, u32[]{:S(2)}) %all-to-all-start.7) | async-done | bytes 524320 | tf_op jit(solution)/shard_map/all_to_all | solution.py:58
  303.6 0.7 pad_maximum_fusion.1
  (57 shorter events, 1.4 us)
Async XLA Ops:
  7.2 22.0 %copy-start.4 = (s32[1,64]{1,0:T(1,128)S(1)}, s32[1,64]{1,0:T(1,128)}, u32[]{:S(2)}) copy-start(s32[1,64]{1,0:T(1,128)} %param.14) | copy-start | bytes 772
  7.2 22.0 %copy-start = (s32[1,64]{1,0:T(1,128)S(1)}, s32[1,64]{1,0:T(1,128)}, u32[]{:S(2)}) copy-start(s32[1,64]{1,0:T(1,128)} %param.13) | copy-start | bytes 772
  7.2 22.8 %copy-start.3 = (s32[1,16]{1,0:T(1,128)S(1)}, s32[1,16]{1,0:T(1,128)}, u32[]{:S(2)}) copy-start(s32[1,16]{1,0:T(1,128)} %param.10) | copy-start | bytes 196
  7.2 22.8 %copy-start.2 = (s32[1,64]{1,0:T(1,128)S(1)}, s32[1,64]{1,0:T(1,128)}, u32[]{:S(2)}) copy-start(s32[1,64]{1,0:T(1,128)} %param.15) | copy-start | bytes 772
  7.2 22.8 %copy-start.1 = (s32[1,64]{1,0:T(1,128)S(1)}, s32[1,64]{1,0:T(1,128)}, u32[]{:S(2)}) copy-start(s32[1,64]{1,0:T(1,128)} %param.12) | copy-start | bytes 772
  7.2 84.4 %all-gather.6.cloned.1.call-start = ((), (), s32[]{:S(2)}) async-start(), calls=%async_computation.11 | async-start | bytes 9437184 | tf_op jit(solution)/shard_map/all_gather | solution.py:251
  9.7 53.2 %all-to-all-start = ((f32[8,128,128]{2,1,0:T(8,128)}), f32[8,128,128]{2,1,0:T(8,128)S(1)}, u32[]{:S(2)}, u32[]{:S(2)}) async-start(f32[8,128,128]{2,1,0:T(8,128)} %shard_map.95), calls=%async_computation | async-start | bytes 1048576 | tf_op jit(solution)/shard_map/all_to_all | solution.py:58
  28.5 120.2 %reduce-scatter.2.cloned.1.call-start = ((), (), s32[]{:S(2)}) async-start(), calls=%async_computation.9 | async-start | bytes 2949120 | tf_op jit(solution)/shard_map/reduce_scatter | solution.py:276
  30.0 3.2 %collective-permute-start = (s32[5,64]{1,0:T(8,128)S(1)}, s32[5,64]{1,0:T(8,128)S(1)}, u32[]{:S(2)}, u32[]{:S(2)}) collective-permute-start(s32[5,64]{1,0:T(8,128)S(1)} %stack.65), channel_id=1, source_target_pairs={{0,1},{1,0},{2,3},{3,2},{4,5},{5,4},{6,7},{7,6},{8,9},{9,8},{10,11... | collective-permute-start | bytes 3848 | tf_op jit(solution)/shard_map/ppermute | solution.py:54
  33.2 10.5 %collective-permute-start.3 = (s32[2,16]{1,0:T(2,128)S(1)}, s32[2,16]{1,0:T(2,128)S(1)}, u32[]{:S(2)}, u32[]{:S(2)}) collective-permute-start(s32[2,16]{1,0:T(2,128)S(1)} %bitcast.89), channel_id=1, source_target_pairs={{0,768},{16,784},{32,800},{48,816},{64,832},{80,848},{96,864},{112... | collective-permute-start | bytes 392 | tf_op jit(solution)/shard_map/ppermute | solution.py:45
  35.7 8.1 %collective-permute-start.2 = (s32[2,16]{1,0:T(2,128)S(1)}, s32[2,16]{1,0:T(2,128)S(1)}, u32[]{:S(2)}, u32[]{:S(2)}) collective-permute-start(s32[2,16]{1,0:T(2,128)S(1)} %bitcast.90), channel_id=1, source_target_pairs={{0,512},{16,528},{32,544},{48,560},{64,576},{80,592},{96,608},{112... | collective-permute-start | bytes 392 | tf_op jit(solution)/shard_map/ppermute | solution.py:45
  40.0 5.5 %collective-permute-start.1 = (s32[2,16]{1,0:T(2,128)S(1)}, s32[2,16]{1,0:T(2,128)S(1)}, u32[]{:S(2)}, u32[]{:S(2)}) collective-permute-start(s32[2,16]{1,0:T(2,128)S(1)} %bitcast.91), channel_id=1, source_target_pairs={{0,256},{16,272},{32,288},{48,304},{64,320},{80,336},{96,352},{112... | collective-permute-start | bytes 392 | tf_op jit(solution)/shard_map/ppermute | solution.py:45
  62.9 28.7 %collective-permute-start.7 = (f32[8,128,128]{2,1,0:T(8,128)S(1)}, f32[8,128,128]{2,1,0:T(8,128)S(1)}, u32[]{:S(2)}, u32[]{:S(2)}) collective-permute-start(f32[8,128,128]{2,1,0:T(8,128)S(1)} %all-to-all-done.refs_0_), channel_id=1, source_target_pairs={{0,16},{16,32},{32,48},{48,64},{64,80},{80,96},{96,112},{112,128},... | collective-permute-start | bytes 1572872 | tf_op jit(solution)/shard_map/ppermute | solution.py:50
  64.8 26.7 %collective-permute-start.4 = (f32[8,128,128]{2,1,0:T(8,128)S(1)}, f32[8,128,128]{2,1,0:T(8,128)S(1)}, u32[]{:S(2)}, u32[]{:S(2)}) collective-permute-start(f32[8,128,128]{2,1,0:T(8,128)S(1)} %all-to-all-done.refs_0_), channel_id=1, source_target_pairs={{0,240},{16,0},{32,16},{48,32},{64,48},{80,64},{96,80},{112,96},{1... | collective-permute-start | bytes 1572872 | tf_op jit(solution)/shard_map/ppermute | solution.py:50
  70.0 16.1 %collective-permute-start.6 = (f32[4,128,128]{2,1,0:T(8,128)S(1)}, f32[4,128,128]{2,1,0:T(8,128)S(1)}, u32[]{:S(2)}, u32[]{:S(2)}) collective-permute-start(f32[4,128,128]{2,1,0:T(8,128)S(1)} %get-tuple-element.47), channel_id=1, source_target_pairs={{0,32},{16,48},{32,64},{48,80},{64,96},{80,112},{96,128},{112,144}... | collective-permute-start | bytes 786440 | tf_op jit(solution)/shard_map/ppermute | solution.py:50
  71.9 19.6 %collective-permute-start.5 = (f32[4,128,128]{2,1,0:T(8,128)S(1)}, f32[4,128,128]{2,1,0:T(8,128)S(1)}, u32[]{:S(2)}, u32[]{:S(2)}) collective-permute-start(f32[4,128,128]{2,1,0:T(8,128)S(1)} %get-tuple-element.48), channel_id=1, source_target_pairs={{0,224},{16,240},{32,0},{48,16},{64,32},{80,48},{96,64},{112,80},{... | collective-permute-start | bytes 786440 | tf_op jit(solution)/shard_map/ppermute | solution.py:50
  148.7 10.8 %all-to-all-start.1 = ((f32[4,160,128]{2,1,0:T(8,128)}), f32[4,160,128]{2,1,0:T(8,128)S(1)}, u32[]{:S(2)}, u32[]{:S(2)}) async-start(f32[4,160,128]{2,1,0:T(8,128)} %reduce-scatter.2.cloned.1.call-done), calls=%async_computation.2 | async-start | bytes 655360 | tf_op jit(solution)/shard_map/all_to_all | solution.py:58
  153.9 69.8 %all-gather.4.cloned.1.call-start = ((), (), s32[]{:S(2)}) async-start(), calls=%async_computation.10 | async-start | bytes 2654208 | tf_op jit(solution)/shard_map/all_gather | solution.py:321
  160.0 3.1 collective-permute-start.8
  229.7 30.0 %collective-permute-start.9 = (f32[8,128,128]{2,1,0:T(8,128)S(1)}, f32[8,128,128]{2,1,0:T(8,128)S(1)}, u32[]{:S(2)}, u32[]{:S(2)}) collective-permute-start(f32[8,128,128]{2,1,0:T(8,128)S(1)} %get-tuple-element.30), channel_id=1, source_target_pairs={{0,16},{16,32},{32,48},{48,64},{64,80},{80,96},{96,112},{112,128},... | collective-permute-start | bytes 1572872 | tf_op jit(solution)/shard_map/ppermute | solution.py:50
  233.9 25.8 %collective-permute-start.10 = (f32[8,128,128]{2,1,0:T(8,128)S(1)}, f32[8,128,128]{2,1,0:T(8,128)S(1)}, u32[]{:S(2)}, u32[]{:S(2)}) collective-permute-start(f32[8,128,128]{2,1,0:T(8,128)S(1)} %get-tuple-element.31), channel_id=1, source_target_pairs={{0,240},{16,0},{32,16},{48,32},{64,48},{80,64},{96,80},{112,96},{1... | collective-permute-start | bytes 1572872 | tf_op jit(solution)/shard_map/ppermute | solution.py:50
  241.1 18.0 %collective-permute-start.11 = (f32[4,128,128]{2,1,0:T(8,128)}, f32[4,128,128]{2,1,0:T(8,128)S(1)}, u32[]{:S(2)}, u32[]{:S(2)}) collective-permute-start(f32[4,128,128]{2,1,0:T(8,128)} %get-tuple-element.32), channel_id=1, source_target_pairs={{0,32},{16,48},{32,64},{48,80},{64,96},{80,112},{96,128},{112,144}... | collective-permute-start | bytes 786440 | tf_op jit(solution)/shard_map/ppermute | solution.py:50
  243.0 16.7 %collective-permute-start.12 = (f32[4,128,128]{2,1,0:T(8,128)}, f32[4,128,128]{2,1,0:T(8,128)S(1)}, u32[]{:S(2)}, u32[]{:S(2)}) collective-permute-start(f32[4,128,128]{2,1,0:T(8,128)} %get-tuple-element.33), channel_id=1, source_target_pairs={{0,224},{16,240},{32,0},{48,16},{64,32},{80,48},{96,64},{112,80},{... | collective-permute-start | bytes 786440 | tf_op jit(solution)/shard_map/ppermute | solution.py:50
  260.7 42.9 %all-to-all-start.7 = ((f32[8,128,128]{2,1,0:T(8,128)}), f32[8,128,128]{2,1,0:T(8,128)S(1)}, u32[]{:S(2)}, u32[]{:S(2)}) async-start(f32[8,128,128]{2,1,0:T(8,128)} %fusion), calls=%async_computation.8 | async-start | bytes 1048576 | tf_op jit(solution)/shard_map/all_to_all | solution.py:58
Sparse Core Ops, SparseCore 0:
  10.8 67.3 all-gather.5
  97.2 51.4 reduce-scatter.1
  174.7 48.9 all-gather.3

commit v12 on v11

--- a/solution.py
+++ b/solution.py
@@ -18,7 +18,7 @@
 ENTRIES = 2 * NX * SLOTS
 EXTRA = 32
 EXTRA_BACK = 16
-GROUP = 4
+GROUP = 8
 VMEM_LIMIT = 48 * 1024 * 1024
 
 precise = lax.Precision.HIGHEST

time: 313 us -> 313 us (level)
  the two profiles are of different devices: /device:TPU:2 before, /device:TPU:4 now
where the time goes in v12:
time: 313 us; the launch traced here: 312 us
  blocking collectives  99.8 us (32%)
  waiting for transfers between devices  88.9 us (28%)
  starting transfers between devices  78.2 us (25%)
  Pallas kernels  19.7 us (6%)
  between operations  17.2 us (5%)
  other arithmetic  5.2 us (2%)
    all_to_all x5, blocking collectives, exchange(): lax.all_to_all(values, axis, split_axis=0, concat_axis=0, tiled=True, axi...  99.8 us
    all_to_all x3, waiting for transfers between devices, exchange(): lax.all_to_all(values, axis, split_axis=0, concat_axis=0, tiled=True, axi...  50.6 us
    all_to_all x3, starting transfers between devices, exchange(): lax.all_to_all(values, axis, split_axis=0, concat_axis=0, tiled=True, axi...  33.9 us
    ppermute x8, starting transfers between devices, send_z(): return lax.ppermute(values, 'row', pairs)  30.9 us
    ppermute x8, waiting for transfers between devices, send_z(): return lax.ppermute(values, 'row', pairs)  23.6 us
    pallas_call x3, Pallas kernels, call_kernel(): pl.pallas_call(body, out_shape=[jax.ShapeDtypeStruct((*shape, HALF), jnp....  17.9 us
    ppermute x3, starting transfers between devices, send_x(): return lax.ppermute(values, 'row', pairs)  8.99 us
  transfers between devices with their start and end apart: 19, of which 13 were waited for; matrix products, arithmetic and copies ran while one was open for 2% of the time, Pallas kernels for 2%

profile of v12, /device:TPU:4, one launch (start us, length us, event | category | flops | bytes accessed | tf_op | source)
XLA Modules:
  0.0 311.6 jit_solution(13907597965413965896)
XLA Ops:
  7.3 0.7 all-gather.6.cloned.1.call-update
  7.9 1.8 shard_map.95
  9.7 18.7 %all-to-all-start = ((f32[8,128,128]{2,1,0:T(8,128)}), f32[8,128,128]{2,1,0:T(8,128)S(1)}, u32[]{:S(2)}, u32[]{:S(2)}) async-start(f32[8,128,128]{2,1,0:T(8,128)} %shard_map.95), calls=%async_computation | async-start | bytes 1048576 | tf_op jit(solution)/shard_map/all_to_all | solution.py:58
  29.2 0.8 gather_fusion
  30.0 2.4 collective-permute-start
  32.5 0.8 collective-permute-done
  33.2 2.4 collective-permute-start.3
  35.7 4.6 %collective-permute-start.2 = (s32[2,16]{1,0:T(2,128)S(1)}, s32[2,16]{1,0:T(2,128)S(1)}, u32[]{:S(2)}, u32[]{:S(2)}) collective-permute-start(s32[2,16]{1,0:T(2,128)S(1)} %bitcast.90), channel_id=1, source_target_pairs={{0,512},{16,528},{32,544},{48,560},{64,576},{80,592},{96,608},{112... | collective-permute-start | bytes 392 | tf_op jit(solution)/shard_map/ppermute | solution.py:45
  40.3 1.9 collective-permute-start.1
  42.3 0.4 collective-permute-done.2
  42.7 3.1 %collective-permute-done.1 = s32[2,16]{1,0:T(2,128)S(1)} collective-permute-done((s32[2,16]{1,0:T(2,128)S(1)}, s32[2,16]{1,0:T(2,128)S(1)}, u32[]{:S(2)}, u32[]{:S(2)}) %collective-permute-start.1) | collective-permute-done | bytes 160 | tf_op jit(solution)/shard_map/ppermute | solution.py:45
  46.1 0.7 convert_reduce_fusion.2
  46.7 0.6 add_select_fusion.1
  47.4 15.5 %all-to-all-done.refs_0_ = f32[8,128,128]{2,1,0:T(8,128)S(1)} async-done(((f32[8,128,128]{2,1,0:T(8,128)}), f32[8,128,128]{2,1,0:T(8,128)S(1)}, u32[]{:S(2)}, u32[]{:S(2)}) %all-to-all-start) | async-done | bytes 524320 | tf_op jit(solution)/shard_map/all_to_all | solution.py:58
  62.9 1.9 collective-permute-start.7
  64.8 5.1 %collective-permute-start.4 = (f32[8,128,128]{2,1,0:T(8,128)S(1)}, f32[8,128,128]{2,1,0:T(8,128)S(1)}, u32[]{:S(2)}, u32[]{:S(2)}) collective-permute-start(f32[8,128,128]{2,1,0:T(8,128)S(1)} %all-to-all-done.refs_0_), channel_id=1, source_target_pairs={{0,240},{16,0},{32,16},{48,32},{64,48},{80,64},{96,80},{112,96},{1... | collective-permute-start | bytes 1572872 | tf_op jit(solution)/shard_map/ppermute | solution.py:50
  70.0 1.9 collective-permute-start.6
  71.9 6.0 %collective-permute-start.5 = (f32[4,128,128]{2,1,0:T(8,128)S(1)}, f32[4,128,128]{2,1,0:T(8,128)S(1)}, u32[]{:S(2)}, u32[]{:S(2)}) collective-permute-start(f32[4,128,128]{2,1,0:T(8,128)S(1)} %get-tuple-element.48), channel_id=1, source_target_pairs={{0,224},{16,240},{32,0},{48,16},{64,32},{80,48},{96,64},{112,80},{... | collective-permute-start | bytes 786440 | tf_op jit(solution)/shard_map/ppermute | solution.py:50
  78.0 1.4 pad_add_fusion.1.place_ref
  79.5 6.6 %collective-permute-done.6.refs_3_ = f32[4,128,128]{2,1,0:T(8,128)S(1)} collective-permute-done((f32[4,128,128]{2,1,0:T(8,128)S(1)}, f32[4,128,128]{2,1,0:T(8,128)S(1)}, u32[]{:S(2)}, u32[]{:S(2)}) %collective-permute-start.6) | collective-permute-done | bytes 262176 | tf_op jit(solution)/shard_map/ppermute | solution.py:50
  86.1 5.5 %collective-permute-done.5.refs_2_ = f32[4,128,128]{2,1,0:T(8,128)S(1)} collective-permute-done((f32[4,128,128]{2,1,0:T(8,128)S(1)}, f32[4,128,128]{2,1,0:T(8,128)S(1)}, u32[]{:S(2)}, u32[]{:S(2)}) %collective-permute-start.5) | collective-permute-done | bytes 262176 | tf_op jit(solution)/shard_map/ppermute | solution.py:50
  91.6 6.2 %shard_map.96 = f32[32,160,128]{2,1,0:T(8,128)} custom-call(s32[3]{0:T(128)S(1)} %pad_add_fusion.1.place_ref, s32[128]{0:T(128)S(1)} %select_reduce_fusion.list_ref, f32[128,128,128]{2,1,0:T(8,128)} %bitcast.70, f32[8,128,128]{2,1,0:T(8,128)S(1)} %all-to-all-done.refs_0_, f32[8,128,128]{2,1,0:T(8,128)S(1)} %collective-permute-done.4.refs_1_, ...), custom_call_target="tpu_custom_call" | custom-call | tf_op jit(solution)/shard_map/pallas_call | solution.py:201
  97.8 4.0 %shard_map.97 = f32[32,96,128]{2,1,0:T(8,128)S(1)} custom-call(s32[3]{0:T(128)S(1)} %pad_add_fusion.1.place_ref, s32[128]{0:T(128)S(1)} %select_reduce_fusion.list_ref, f32[128,128,128]{2,1,0:T(8,128)} %bitcast.71, f32[8,128,128]{2,1,0:T(8,128)S(1)} %all-to-all-done.refs_0_, f32[8,128,128]{2,1,0:T(8,128)S(1)} %collective-permute-done.4.refs_1_, ...), custom_call_target="tpu_custom_call" | custom-call | tf_op jit(solution)/shard_map/pallas_call | solution.py:201
  101.8 20.6 %all_to_all.40 = f32[4,768,128]{2,1,0:T(8,128)S(1)} all-to-all(f32[4,768,128]{2,1,0:T(8,128)S(1)} %bitcast.68), channel_id=1, replica_groups={{0,256,512,768},{16,272,528,784},{32,288,544,800},{48,304,560,816},{64,..., dimensions={0} | all-to-all | bytes 3145728 | tf_op jit(solution)/shard_map/all_to_all | solution.py:58
  122.5 23.5 %all_to_all.41 = f32[8,96,128]{2,1,0:T(8,128)S(1)} all-to-all(f32[8,96,128]{2,1,0:T(8,128)S(1)} %bitcast.75), channel_id=1, replica_groups={{0,2,4,6,8,10,12,14},{1,3,5,7,9,11,13,15},{16,18,20,22,24,26,28,30},{17..., dimensions={0} | all-to-all | bytes 786432 | tf_op jit(solution)/shard_map/all_to_all | solution.py:58
  145.9 3.2 %reduce-scatter.2.cloned.1.call-done = f32[4,160,128]{2,1,0:T(8,128)} async-done(((f32[32,160,128]{2,1,0:T(8,128)}), f32[4,160,128]{2,1,0:T(8,128)}) %reduce-scatter.2.cloned.1.call-update) | async-done | bytes 327696 | tf_op jit(solution)/shard_map/reduce_scatter | solution.py:276
  149.2 4.8 %all-to-all-start.1 = ((f32[4,160,128]{2,1,0:T(8,128)}), f32[4,160,128]{2,1,0:T(8,128)S(1)}, u32[]{:S(2)}, u32[]{:S(2)}) async-start(f32[4,160,128]{2,1,0:T(8,128)} %reduce-scatter.2.cloned.1.call-done), calls=%async_computation.2 | async-start | bytes 655360 | tf_op jit(solution)/shard_map/all_to_all | solution.py:58
  154.0 4.0 %all-to-all-done.1 = f32[4,160,128]{2,1,0:T(8,128)S(1)} async-done(((f32[4,160,128]{2,1,0:T(8,128)}), f32[4,160,128]{2,1,0:T(8,128)S(1)}, u32[]{:S(2)}, u32[]{:S(2)}) %all-to-all-start.1) | async-done | bytes 327712 | tf_op jit(solution)/shard_map/all_to_all | solution.py:58
  158.1 0.3 fusion.9
  158.6 1.9 collective-permute-start.8
  160.5 1.1 collective-permute-done.8
  161.9 0.5 fusion.1
  162.5 11.2 %all_to_all.42 = f32[4,144,128]{2,1,0:T(8,128)} all-to-all(f32[4,144,128]{2,1,0:T(8,128)S(1)} %broadcast_in_dim.85), channel_id=1, replica_groups={{0,256,512,768},{16,272,528,784},{32,288,544,800},{48,304,560,816},{64,..., dimensions={0} | all-to-all | bytes 589824 | tf_op jit(solution)/shard_map/all_to_all | solution.py:58
  173.8 20.9 %all_to_all.43 = f32[8,112,128]{2,1,0:T(8,128)S(1)} all-to-all(f32[8,112,128]{2,1,0:T(8,128)S(1)} %broadcast_in_dim.86), channel_id=1, replica_groups={{0,2,4,6,8,10,12,14},{1,3,5,7,9,11,13,15},{16,18,20,22,24,26,28,30},{17..., dimensions={0} | all-to-all | bytes 917504 | tf_op jit(solution)/shard_map/all_to_all | solution.py:58
  194.8 23.6 %all_to_all.44 = f32[4,896,128]{2,1,0:T(8,128)S(1)} all-to-all(f32[4,896,128]{2,1,0:T(8,128)S(1)} %broadcast_in_dim.88), channel_id=1, replica_groups={{0,256,512,768},{16,272,528,784},{32,288,544,800},{48,304,560,816},{64,..., dimensions={0} | all-to-all | bytes 3670016 | tf_op jit(solution)/shard_map/all_to_all | solution.py:58
  218.4 5.2 %all-gather.4.cloned.1.call-done.even_ref = f32[32,144,128]{2,1,0:T(8,128)} async-done(((f32[4,144,128]{2,1,0:T(8,128)}), f32[32,144,128]{2,1,0:T(8,128)}) %all-gather.4.cloned.1.call-update) | async-done | bytes 2359312 | tf_op jit(solution)/shard_map/all_gather | solution.py:321
  223.6 7.7 %shard_map.98 = (f32[8,128,128]{2,1,0:T(8,128)S(1)}, f32[8,128,128]{2,1,0:T(8,128)S(1)}, f32[4,128,128]{2,1,0:T(8,128)}, f32[4,128,128]{2,1,0:T(8,128)}, f32[8,128,128]{2,1,0:T(8,128)S(1)}) custom-call(s32[3]{0:T(128)S(1)} %pad_add_fusion.1.place_ref, s32[128]{0:T(128)S(1)} %select_reduce_fusion.list_ref, f32[128,128,128]{2,1,0:T(8,128)} %bitcast.72, ...), custom_call_target="tpu_custom_call" | custom-call | tf_op jit(solution)/shard_map/pallas_call | solution.py:201
  231.4 1.9 collective-permute-start.9
  233.3 6.0 %collective-permute-start.10 = (f32[8,128,128]{2,1,0:T(8,128)S(1)}, f32[8,128,128]{2,1,0:T(8,128)S(1)}, u32[]{:S(2)}, u32[]{:S(2)}) collective-permute-start(f32[8,128,128]{2,1,0:T(8,128)S(1)} %get-tuple-element.31), channel_id=1, source_target_pairs={{0,240},{16,0},{32,16},{48,32},{64,48},{80,64},{96,80},{112,96},{1... | collective-permute-start | bytes 1572872 | tf_op jit(solution)/shard_map/ppermute | solution.py:50
  239.4 2.2 collective-permute-start.11
  241.5 5.8 %collective-permute-start.12 = (f32[4,128,128]{2,1,0:T(8,128)}, f32[4,128,128]{2,1,0:T(8,128)S(1)}, u32[]{:S(2)}, u32[]{:S(2)}) collective-permute-start(f32[4,128,128]{2,1,0:T(8,128)} %get-tuple-element.33), channel_id=1, source_target_pairs={{0,224},{16,240},{32,0},{48,16},{64,32},{80,48},{96,64},{112,80},{... | collective-permute-start | bytes 786440 | tf_op jit(solution)/shard_map/ppermute | solution.py:50
  247.5 10.8 %collective-permute-done.11 = f32[4,128,128]{2,1,0:T(8,128)S(1)} collective-permute-done((f32[4,128,128]{2,1,0:T(8,128)}, f32[4,128,128]{2,1,0:T(8,128)S(1)}, u32[]{:S(2)}, u32[]{:S(2)}) %collective-permute-start.11) | collective-permute-done | bytes 262176 | tf_op jit(solution)/shard_map/ppermute | solution.py:50
  258.3 0.7 collective-permute-done.12
  259.0 1.0 fusion
  260.0 10.3 %all-to-all-start.7 = ((f32[8,128,128]{2,1,0:T(8,128)}), f32[8,128,128]{2,1,0:T(8,128)S(1)}, u32[]{:S(2)}, u32[]{:S(2)}) async-start(f32[8,128,128]{2,1,0:T(8,128)} %fusion), calls=%async_computation.8 | async-start | bytes 1048576 | tf_op jit(solution)/shard_map/all_to_all | solution.py:58
  270.3 0.6 fusion.38
  272.2 31.1 %all-to-all-done.7 = f32[8,128,128]{2,1,0:T(8,128)S(1)} async-done(((f32[8,128,128]{2,1,0:T(8,128)}), f32[8,128,128]{2,1,0:T(8,128)S(1)}, u32[]{:S(2)}, u32[]{:S(2)}) %all-to-all-start.7) | async-done | bytes 524320 | tf_op jit(solution)/shard_map/all_to_all | solution.py:58
  303.3 0.7 pad_maximum_fusion.1
  (57 shorter events, 1.6 us)
Async XLA Ops:
  7.2 22.0 %copy-start.4 = (s32[1,64]{1,0:T(1,128)S(1)}, s32[1,64]{1,0:T(1,128)}, u32[]{:S(2)}) copy-start(s32[1,64]{1,0:T(1,128)} %param.14) | copy-start | bytes 772
  7.2 22.0 %copy-start = (s32[1,64]{1,0:T(1,128)S(1)}, s32[1,64]{1,0:T(1,128)}, u32[]{:S(2)}) copy-start(s32[1,64]{1,0:T(1,128)} %param.13) | copy-start | bytes 772
  7.2 22.8 %copy-start.3 = (s32[1,16]{1,0:T(1,128)S(1)}, s32[1,16]{1,0:T(1,128)}, u32[]{:S(2)}) copy-start(s32[1,16]{1,0:T(1,128)} %param.10) | copy-start | bytes 196
  7.2 22.8 %copy-start.2 = (s32[1,64]{1,0:T(1,128)S(1)}, s32[1,64]{1,0:T(1,128)}, u32[]{:S(2)}) copy-start(s32[1,64]{1,0:T(1,128)} %param.15) | copy-start | bytes 772
  7.2 22.8 %copy-start.1 = (s32[1,64]{1,0:T(1,128)S(1)}, s32[1,64]{1,0:T(1,128)}, u32[]{:S(2)}) copy-start(s32[1,64]{1,0:T(1,128)} %param.12) | copy-start | bytes 772
  7.2 84.4 %all-gather.6.cloned.1.call-start = ((), (), s32[]{:S(2)}) async-start(), calls=%async_computation.11 | async-start | bytes 9437184 | tf_op jit(solution)/shard_map/all_gather | solution.py:251
  9.7 53.2 %all-to-all-start = ((f32[8,128,128]{2,1,0:T(8,128)}), f32[8,128,128]{2,1,0:T(8,128)S(1)}, u32[]{:S(2)}, u32[]{:S(2)}) async-start(f32[8,128,128]{2,1,0:T(8,128)} %shard_map.95), calls=%async_computation | async-start | bytes 1048576 | tf_op jit(solution)/shard_map/all_to_all | solution.py:58
  28.5 120.7 %reduce-scatter.2.cloned.1.call-start = ((), (), s32[]{:S(2)}) async-start(), calls=%async_computation.9 | async-start | bytes 2949120 | tf_op jit(solution)/shard_map/reduce_scatter | solution.py:276
  30.0 3.2 %collective-permute-start = (s32[5,64]{1,0:T(8,128)S(1)}, s32[5,64]{1,0:T(8,128)S(1)}, u32[]{:S(2)}, u32[]{:S(2)}) collective-permute-start(s32[5,64]{1,0:T(8,128)S(1)} %stack.65), channel_id=1, source_target_pairs={{0,1},{1,0},{2,3},{3,2},{4,5},{5,4},{6,7},{7,6},{8,9},{9,8},{10,11... | collective-permute-start | bytes 3848 | tf_op jit(solution)/shard_map/ppermute | solution.py:54
  33.2 9.0 %collective-permute-start.3 = (s32[2,16]{1,0:T(2,128)S(1)}, s32[2,16]{1,0:T(2,128)S(1)}, u32[]{:S(2)}, u32[]{:S(2)}) collective-permute-start(s32[2,16]{1,0:T(2,128)S(1)} %bitcast.89), channel_id=1, source_target_pairs={{0,768},{16,784},{32,800},{48,816},{64,832},{80,848},{96,864},{112... | collective-permute-start | bytes 392 | tf_op jit(solution)/shard_map/ppermute | solution.py:45
  35.7 7.0 %collective-permute-start.2 = (s32[2,16]{1,0:T(2,128)S(1)}, s32[2,16]{1,0:T(2,128)S(1)}, u32[]{:S(2)}, u32[]{:S(2)}) collective-permute-start(s32[2,16]{1,0:T(2,128)S(1)} %bitcast.90), channel_id=1, source_target_pairs={{0,512},{16,528},{32,544},{48,560},{64,576},{80,592},{96,608},{112... | collective-permute-start | bytes 392 | tf_op jit(solution)/shard_map/ppermute | solution.py:45
  40.3 5.5 %collective-permute-start.1 = (s32[2,16]{1,0:T(2,128)S(1)}, s32[2,16]{1,0:T(2,128)S(1)}, u32[]{:S(2)}, u32[]{:S(2)}) collective-permute-start(s32[2,16]{1,0:T(2,128)S(1)} %bitcast.91), channel_id=1, source_target_pairs={{0,256},{16,272},{32,288},{48,304},{64,320},{80,336},{96,352},{112... | collective-permute-start | bytes 392 | tf_op jit(solution)/shard_map/ppermute | solution.py:45
  62.9 28.7 %collective-permute-start.7 = (f32[8,128,128]{2,1,0:T(8,128)S(1)}, f32[8,128,128]{2,1,0:T(8,128)S(1)}, u32[]{:S(2)}, u32[]{:S(2)}) collective-permute-start(f32[8,128,128]{2,1,0:T(8,128)S(1)} %all-to-all-done.refs_0_), channel_id=1, source_target_pairs={{0,16},{16,32},{32,48},{48,64},{64,80},{80,96},{96,112},{112,128},... | collective-permute-start | bytes 1572872 | tf_op jit(solution)/shard_map/ppermute | solution.py:50
  64.8 26.7 %collective-permute-start.4 = (f32[8,128,128]{2,1,0:T(8,128)S(1)}, f32[8,128,128]{2,1,0:T(8,128)S(1)}, u32[]{:S(2)}, u32[]{:S(2)}) collective-permute-start(f32[8,128,128]{2,1,0:T(8,128)S(1)} %all-to-all-done.refs_0_), channel_id=1, source_target_pairs={{0,240},{16,0},{32,16},{48,32},{64,48},{80,64},{96,80},{112,96},{1... | collective-permute-start | bytes 1572872 | tf_op jit(solution)/shard_map/ppermute | solution.py:50
  70.0 16.1 %collective-permute-start.6 = (f32[4,128,128]{2,1,0:T(8,128)S(1)}, f32[4,128,128]{2,1,0:T(8,128)S(1)}, u32[]{:S(2)}, u32[]{:S(2)}) collective-permute-start(f32[4,128,128]{2,1,0:T(8,128)S(1)} %get-tuple-element.47), channel_id=1, source_target_pairs={{0,32},{16,48},{32,64},{48,80},{64,96},{80,112},{96,128},{112,144}... | collective-permute-start | bytes 786440 | tf_op jit(solution)/shard_map/ppermute | solution.py:50
  71.9 19.6 %collective-permute-start.5 = (f32[4,128,128]{2,1,0:T(8,128)S(1)}, f32[4,128,128]{2,1,0:T(8,128)S(1)}, u32[]{:S(2)}, u32[]{:S(2)}) collective-permute-start(f32[4,128,128]{2,1,0:T(8,128)S(1)} %get-tuple-element.48), channel_id=1, source_target_pairs={{0,224},{16,240},{32,0},{48,16},{64,32},{80,48},{96,64},{112,80},{... | collective-permute-start | bytes 786440 | tf_op jit(solution)/shard_map/ppermute | solution.py:50
  149.2 8.9 %all-to-all-start.1 = ((f32[4,160,128]{2,1,0:T(8,128)}), f32[4,160,128]{2,1,0:T(8,128)S(1)}, u32[]{:S(2)}, u32[]{:S(2)}) async-start(f32[4,160,128]{2,1,0:T(8,128)} %reduce-scatter.2.cloned.1.call-done), calls=%async_computation.2 | async-start | bytes 655360 | tf_op jit(solution)/shard_map/all_to_all | solution.py:58
  154.0 69.6 %all-gather.4.cloned.1.call-start = ((), (), s32[]{:S(2)}) async-start(), calls=%async_computation.10 | async-start | bytes 2654208 | tf_op jit(solution)/shard_map/all_gather | solution.py:321
  158.6 3.1 collective-permute-start.8
  231.4 27.6 %collective-permute-start.9 = (f32[8,128,128]{2,1,0:T(8,128)S(1)}, f32[8,128,128]{2,1,0:T(8,128)S(1)}, u32[]{:S(2)}, u32[]{:S(2)}) collective-permute-start(f32[8,128,128]{2,1,0:T(8,128)S(1)} %get-tuple-element.30), channel_id=1, source_target_pairs={{0,16},{16,32},{32,48},{48,64},{64,80},{80,96},{96,112},{112,128},... | collective-permute-start | bytes 1572872 | tf_op jit(solution)/shard_map/ppermute | solution.py:50
  233.3 25.7 %collective-permute-start.10 = (f32[8,128,128]{2,1,0:T(8,128)S(1)}, f32[8,128,128]{2,1,0:T(8,128)S(1)}, u32[]{:S(2)}, u32[]{:S(2)}) collective-permute-start(f32[8,128,128]{2,1,0:T(8,128)S(1)} %get-tuple-element.31), channel_id=1, source_target_pairs={{0,240},{16,0},{32,16},{48,32},{64,48},{80,64},{96,80},{112,96},{1... | collective-permute-start | bytes 1572872 | tf_op jit(solution)/shard_map/ppermute | solution.py:50
  239.4 18.9 %collective-permute-start.11 = (f32[4,128,128]{2,1,0:T(8,128)}, f32[4,128,128]{2,1,0:T(8,128)S(1)}, u32[]{:S(2)}, u32[]{:S(2)}) collective-permute-start(f32[4,128,128]{2,1,0:T(8,128)} %get-tuple-element.32), channel_id=1, source_target_pairs={{0,32},{16,48},{32,64},{48,80},{64,96},{80,112},{96,128},{112,144}... | collective-permute-start | bytes 786440 | tf_op jit(solution)/shard_map/ppermute | solution.py:50
  241.5 17.5 %collective-permute-start.12 = (f32[4,128,128]{2,1,0:T(8,128)}, f32[4,128,128]{2,1,0:T(8,128)S(1)}, u32[]{:S(2)}, u32[]{:S(2)}) collective-permute-start(f32[4,128,128]{2,1,0:T(8,128)} %get-tuple-element.33), channel_id=1, source_target_pairs={{0,224},{16,240},{32,0},{48,16},{64,32},{80,48},{96,64},{112,80},{... | collective-permute-start | bytes 786440 | tf_op jit(solution)/shard_map/ppermute | solution.py:50
  260.0 43.3 %all-to-all-start.7 = ((f32[8,128,128]{2,1,0:T(8,128)}), f32[8,128,128]{2,1,0:T(8,128)S(1)}, u32[]{:S(2)}, u32[]{:S(2)}) async-start(f32[8,128,128]{2,1,0:T(8,128)} %fusion), calls=%async_computation.8 | async-start | bytes 1048576 | tf_op jit(solution)/shard_map/all_to_all | solution.py:58
Sparse Core Ops, SparseCore 0:
  10.8 67.0 all-gather.5
  97.9 51.2 reduce-scatter.1
  173.9 49.7 all-gather.3

commit v13 on v12

--- a/solution.py
+++ b/solution.py
@@ -329,11 +329,17 @@
     )
     two = jnp.concatenate([send_z(two, 2), send_z(two_far, -2)])
     near = (own + send_z(after, 1) + send_z(before, -1) + two).reshape(4, 2, BLOCK, HALF)
-    is_own = (jnp.arange(4) == own_z // 4)[:, None, None, None]
-    near = near + jnp.where(is_own, scaled[None], 0.0)
-    halves = exchange(near.reshape(8, BLOCK, HALF), BOTH, Z_CORE)
-    halves = jnp.sum(halves.reshape(4, 2, BLOCK, HALF), axis=0)
-    gradient = jnp.concatenate([halves[0], halves[1]], axis=1)
+    at_stride = [
+        lax.dynamic_index_in_dim(near, jnp.bitwise_and(own_z // 4 + m, 3), keepdims=False)
+        for m in range(4)
+    ]
+    halves = scaled + at_stride[0] + send_z(at_stride[2], 8)
+    halves = halves + send_z(at_stride[1], 4) + send_z(at_stride[3], -4)
+    own_half = jnp.where(is_first, halves[0], halves[1])
+    other_half = swap_cores(jnp.where(is_first, halves[1], halves[0]))
+    gradient = jnp.concatenate(
+        [jnp.where(is_first, own_half, other_half), jnp.where(is_first, other_half, own_half)], axis=1
+    )
     return (gradient, span_loss)
 
 

time: 313 us -> 307 us (0.981)
  the two profiles are of different devices: /device:TPU:4 before, /device:TPU:1 now
where the time goes in v13:
time: 307 us; the launch traced here: 305 us
  starting transfers between devices  103 us (34%)
  blocking collectives  91.3 us (30%)
  waiting for transfers between devices  69.6 us (23%)
  between operations  17.3 us (6%)
  Pallas kernels  16.6 us (5%)
  other arithmetic  4.42 us (1%)
    all_to_all x5, blocking collectives, exchange(): lax.all_to_all(values, axis, split_axis=0, concat_axis=0, tiled=True, axi...  91.3 us
    ppermute x11, starting transfers between devices, send_z(): return lax.ppermute(values, 'row', pairs)  57.7 us
    ppermute x11, waiting for transfers between devices, send_z(): return lax.ppermute(values, 'row', pairs)  39.1 us
    all_to_all x2, starting transfers between devices, exchange(): lax.all_to_all(values, axis, split_axis=0, concat_axis=0, tiled=True, axi...  24 us
    pallas_call x3, Pallas kernels, call_kernel(): pl.pallas_call(body, out_shape=[jax.ShapeDtypeStruct((*shape, HALF), jnp....  14.8 us
    reduce_scatter x1, waiting for transfers between devices, per_device(): lax.psum_scatter(first, 'col', scatter_dimension=0, tiled=True, axis_inde...  14.2 us
    ppermute x3, starting transfers between devices, swap_cores(): return lax.ppermute(values, 'col', CORE_SWAP)  10.6 us
    ppermute x3, starting transfers between devices, send_x(): return lax.ppermute(values, 'row', pairs)  10.5 us
  transfers between devices with their start and end apart: 22, of which 13 were waited for; matrix products, arithmetic and copies ran while one was open for 2% of the time, Pallas kernels for 2%

profile of v13, /device:TPU:1, one launch (start us, length us, event | category | flops | bytes accessed | tf_op | source)
XLA Modules:
  0.0 304.7 jit_solution(3879964861718847716)
XLA Ops:
  7.3 0.7 all-gather.6.cloned.1.call-update
  7.9 1.8 shard_map.95
  9.7 20.2 %all-to-all-start = ((f32[8,128,128]{2,1,0:T(8,128)}), f32[8,128,128]{2,1,0:T(8,128)S(1)}, u32[]{:S(2)}, u32[]{:S(2)}) async-start(f32[8,128,128]{2,1,0:T(8,128)} %shard_map.95), calls=%async_computation | async-start | bytes 1048576 | tf_op jit(solution)/shard_map/all_to_all | solution.py:58
  30.6 0.8 gather_fusion
  31.5 1.9 collective-permute-start
  33.5 1.1 collective-permute-done
  34.6 3.1 %collective-permute-start.1 = (s32[2,16]{1,0:T(2,128)S(1)}, s32[2,16]{1,0:T(2,128)S(1)}, u32[]{:S(2)}, u32[]{:S(2)}) collective-permute-start(s32[2,16]{1,0:T(2,128)S(1)} %bitcast.101), channel_id=1, source_target_pairs={{0,256},{16,272},{32,288},{48,304},{64,320},{80,336},{96,352},{112... | collective-permute-start | bytes 392 | tf_op jit(solution)/shard_map/ppermute | solution.py:45
  37.7 4.4 %collective-permute-start.2 = (s32[2,16]{1,0:T(2,128)S(1)}, s32[2,16]{1,0:T(2,128)S(1)}, u32[]{:S(2)}, u32[]{:S(2)}) collective-permute-start(s32[2,16]{1,0:T(2,128)S(1)} %bitcast.102), channel_id=1, source_target_pairs={{0,512},{16,528},{32,544},{48,560},{64,576},{80,592},{96,608},{112... | collective-permute-start | bytes 392 | tf_op jit(solution)/shard_map/ppermute | solution.py:45
  42.1 3.1 %collective-permute-start.3 = (s32[2,16]{1,0:T(2,128)S(1)}, s32[2,16]{1,0:T(2,128)S(1)}, u32[]{:S(2)}, u32[]{:S(2)}) collective-permute-start(s32[2,16]{1,0:T(2,128)S(1)} %bitcast.103), channel_id=1, source_target_pairs={{0,768},{16,784},{32,800},{48,816},{64,832},{80,848},{96,864},{112... | collective-permute-start | bytes 392 | tf_op jit(solution)/shard_map/ppermute | solution.py:45
  45.1 1.6 collective-permute-done.3
  47.0 0.7 convert_reduce_fusion.2
  47.7 0.6 add_select_fusion.1
  48.4 2.4 all-to-all-done.refs_0_
  50.7 11.9 %collective-permute-start.4 = (f32[8,128,128]{2,1,0:T(8,128)S(1)}, f32[8,128,128]{2,1,0:T(8,128)S(1)}, u32[]{:S(2)}, u32[]{:S(2)}) collective-permute-start(f32[8,128,128]{2,1,0:T(8,128)S(1)} %all-to-all-done.refs_0_), channel_id=1, source_target_pairs={{0,240},{16,0},{32,16},{48,32},{64,48},{80,64},{96,80},{112,96},{1... | collective-permute-start | bytes 1572872 | tf_op jit(solution)/shard_map/ppermute | solution.py:50
  62.6 3.5 %collective-permute-start.7 = (f32[8,128,128]{2,1,0:T(8,128)S(1)}, f32[8,128,128]{2,1,0:T(8,128)S(1)}, u32[]{:S(2)}, u32[]{:S(2)}) collective-permute-start(f32[8,128,128]{2,1,0:T(8,128)S(1)} %all-to-all-done.refs_0_), channel_id=1, source_target_pairs={{0,16},{16,32},{32,48},{48,64},{64,80},{80,96},{96,112},{112,128},... | collective-permute-start | bytes 1572872 | tf_op jit(solution)/shard_map/ppermute | solution.py:50
  66.2 5.0 %collective-permute-start.5 = (f32[4,128,128]{2,1,0:T(8,128)S(1)}, f32[4,128,128]{2,1,0:T(8,128)S(1)}, u32[]{:S(2)}, u32[]{:S(2)}) collective-permute-start(f32[4,128,128]{2,1,0:T(8,128)S(1)} %get-tuple-element.51), channel_id=1, source_target_pairs={{0,224},{16,240},{32,0},{48,16},{64,32},{80,48},{96,64},{112,80},{... | collective-permute-start | bytes 786440 | tf_op jit(solution)/shard_map/ppermute | solution.py:50
  71.2 1.9 collective-permute-start.6
  73.1 1.4 pad_add_fusion.1.place_ref
  74.6 11.3 %collective-permute-done.5.refs_2_ = f32[4,128,128]{2,1,0:T(8,128)S(1)} collective-permute-done((f32[4,128,128]{2,1,0:T(8,128)S(1)}, f32[4,128,128]{2,1,0:T(8,128)S(1)}, u32[]{:S(2)}, u32[]{:S(2)}) %collective-permute-start.5) | collective-permute-done | bytes 262176 | tf_op jit(solution)/shard_map/ppermute | solution.py:50
  85.9 0.5 collective-permute-done.6.refs_3_
  86.5 5.6 %shard_map.96 = f32[32,160,128]{2,1,0:T(8,128)} custom-call(s32[3]{0:T(128)S(1)} %pad_add_fusion.1.place_ref, s32[128]{0:T(128)S(1)} %select_reduce_fusion.list_ref, f32[128,128,128]{2,1,0:T(8,128)} %bitcast.82, f32[8,128,128]{2,1,0:T(8,128)S(1)} %all-to-all-done.refs_0_, f32[8,128,128]{2,1,0:T(8,128)S(1)} %collective-permute-done.4.refs_1_, ...), custom_call_target="tpu_custom_call" | custom-call | tf_op jit(solution)/shard_map/pallas_call | solution.py:201
  92.1 3.1 %shard_map.97 = f32[32,96,128]{2,1,0:T(8,128)S(1)} custom-call(s32[3]{0:T(128)S(1)} %pad_add_fusion.1.place_ref, s32[128]{0:T(128)S(1)} %select_reduce_fusion.list_ref, f32[128,128,128]{2,1,0:T(8,128)} %bitcast.83, f32[8,128,128]{2,1,0:T(8,128)S(1)} %all-to-all-done.refs_0_, f32[8,128,128]{2,1,0:T(8,128)S(1)} %collective-permute-done.4.refs_1_, ...), custom_call_target="tpu_custom_call" | custom-call | tf_op jit(solution)/shard_map/pallas_call | solution.py:201
  95.2 17.6 %all_to_all.35 = f32[4,768,128]{2,1,0:T(8,128)S(1)} all-to-all(f32[4,768,128]{2,1,0:T(8,128)S(1)} %bitcast.80), channel_id=1, replica_groups={{0,256,512,768},{16,272,528,784},{32,288,544,800},{48,304,560,816},{64,..., dimensions={0} | all-to-all | bytes 3145728 | tf_op jit(solution)/shard_map/all_to_all | solution.py:58
  112.8 21.4 %all_to_all.36 = f32[8,96,128]{2,1,0:T(8,128)S(1)} all-to-all(f32[8,96,128]{2,1,0:T(8,128)S(1)} %bitcast.88), channel_id=1, replica_groups={{0,2,4,6,8,10,12,14},{1,3,5,7,9,11,13,15},{16,18,20,22,24,26,28,30},{17..., dimensions={0} | all-to-all | bytes 786432 | tf_op jit(solution)/shard_map/all_to_all | solution.py:58
  134.2 14.2 %reduce-scatter.2.cloned.1.call-done = f32[4,160,128]{2,1,0:T(8,128)} async-done(((f32[32,160,128]{2,1,0:T(8,128)}), f32[4,160,128]{2,1,0:T(8,128)}) %reduce-scatter.2.cloned.1.call-update) | async-done | bytes 327696 | tf_op jit(solution)/shard_map/reduce_scatter | solution.py:276
  148.4 3.7 %all-to-all-start.1 = ((f32[4,160,128]{2,1,0:T(8,128)}), f32[4,160,128]{2,1,0:T(8,128)S(1)}, u32[]{:S(2)}, u32[]{:S(2)}) async-start(f32[4,160,128]{2,1,0:T(8,128)} %reduce-scatter.2.cloned.1.call-done), calls=%async_computation.2 | async-start | bytes 655360 | tf_op jit(solution)/shard_map/all_to_all | solution.py:58
  152.2 5.8 %all-to-all-done.1 = f32[4,160,128]{2,1,0:T(8,128)S(1)} async-done(((f32[4,160,128]{2,1,0:T(8,128)}), f32[4,160,128]{2,1,0:T(8,128)S(1)}, u32[]{:S(2)}, u32[]{:S(2)}) %all-to-all-start.1) | async-done | bytes 327712 | tf_op jit(solution)/shard_map/all_to_all | solution.py:58
  158.5 6.3 %collective-permute-start.8 = (f32[2,3,64]{2,0,1:T(2,128)S(1)}, f32[2,3,64]{2,0,1:T(2,128)S(1)}, u32[]{:S(2)}, u32[]{:S(2)}) collective-permute-start(f32[2,3,64]{2,0,1:T(2,128)S(1)} %pad_maximum_fusion.2), channel_id=1, source_target_pairs={{0,1},{1,0},{2,3},{3,2},{4,5},{5,4},{6,7},{7,6},{8,9},{9,8},{10,11... | collective-permute-start | bytes 4616 | tf_op jit(solution)/shard_map/ppermute | solution.py:54
  164.8 0.8 collective-permute-done.8
  165.9 0.5 fusion
  166.4 9.7 %all_to_all.37 = f32[4,144,128]{2,1,0:T(8,128)} all-to-all(f32[4,144,128]{2,1,0:T(8,128)S(1)} %broadcast_in_dim.34), channel_id=1, replica_groups={{0,256,512,768},{16,272,528,784},{32,288,544,800},{48,304,560,816},{64,..., dimensions={0} | all-to-all | bytes 589824 | tf_op jit(solution)/shard_map/all_to_all | solution.py:58
  176.2 19.8 %all_to_all.38 = f32[8,112,128]{2,1,0:T(8,128)S(1)} all-to-all(f32[8,112,128]{2,1,0:T(8,128)S(1)} %broadcast_in_dim.35), channel_id=1, replica_groups={{0,2,4,6,8,10,12,14},{1,3,5,7,9,11,13,15},{16,18,20,22,24,26,28,30},{17..., dimensions={0} | all-to-all | bytes 917504 | tf_op jit(solution)/shard_map/all_to_all | solution.py:58
  196.1 22.9 %all_to_all.39 = f32[4,896,128]{2,1,0:T(8,128)S(1)} all-to-all(f32[4,896,128]{2,1,0:T(8,128)S(1)} %broadcast_in_dim.60), channel_id=1, replica_groups={{0,256,512,768},{16,272,528,784},{32,288,544,800},{48,304,560,816},{64,..., dimensions={0} | all-to-all | bytes 3670016 | tf_op jit(solution)/shard_map/all_to_all | solution.py:58
  219.0 3.8 %all-gather.4.cloned.1.call-done.even_ref = f32[32,144,128]{2,1,0:T(8,128)} async-done(((f32[4,144,128]{2,1,0:T(8,128)}), f32[32,144,128]{2,1,0:T(8,128)}) %all-gather.4.cloned.1.call-update) | async-done | bytes 2359312 | tf_op jit(solution)/shard_map/all_gather | solution.py:321
  222.8 6.2 %shard_map.98 = (f32[8,128,128]{2,1,0:T(8,128)S(1)}, f32[8,128,128]{2,1,0:T(8,128)S(1)}, f32[4,128,128]{2,1,0:T(8,128)}, f32[4,128,128]{2,1,0:T(8,128)}, f32[8,128,128]{2,1,0:T(8,128)S(1)}) custom-call(s32[3]{0:T(128)S(1)} %pad_add_fusion.1.place_ref, s32[128]{0:T(128)S(1)} %select_reduce_fusion.list_ref, f32[128,128,128]{2,1,0:T(8,128)} %bitcast.84, ...), custom_call_target="tpu_custom_call" | custom-call | tf_op jit(solution)/shard_map/pallas_call | solution.py:201
  229.0 6.8 %collective-permute-start.10 = (f32[8,128,128]{2,1,0:T(8,128)S(1)}, f32[8,128,128]{2,1,0:T(8,128)S(1)}, u32[]{:S(2)}, u32[]{:S(2)}) collective-permute-start(f32[8,128,128]{2,1,0:T(8,128)S(1)} %get-tuple-element.31), channel_id=1, source_target_pairs={{0,240},{16,0},{32,16},{48,32},{64,48},{80,64},{96,80},{112,96},{1... | collective-permute-start | bytes 1572872 | tf_op jit(solution)/shard_map/ppermute | solution.py:50
  235.8 1.9 collective-permute-start.9
  237.7 1.9 collective-permute-start.11
  239.7 5.5 %collective-permute-start.12 = (f32[4,128,128]{2,1,0:T(8,128)}, f32[4,128,128]{2,1,0:T(8,128)S(1)}, u32[]{:S(2)}, u32[]{:S(2)}) collective-permute-start(f32[4,128,128]{2,1,0:T(8,128)} %get-tuple-element.33), channel_id=1, source_target_pairs={{0,224},{16,240},{32,0},{48,16},{64,32},{80,48},{96,64},{112,80},{... | collective-permute-start | bytes 786440 | tf_op jit(solution)/shard_map/ppermute | solution.py:50
  245.2 11.8 %collective-permute-done.11 = f32[4,128,128]{2,1,0:T(8,128)S(1)} collective-permute-done((f32[4,128,128]{2,1,0:T(8,128)}, f32[4,128,128]{2,1,0:T(8,128)S(1)}, u32[]{:S(2)}, u32[]{:S(2)}) %collective-permute-start.11) | collective-permute-done | bytes 262176 | tf_op jit(solution)/shard_map/ppermute | solution.py:50
  257.4 10.1 %collective-permute-start.13 = (f32[2,128,128]{2,1,0:T(8,128)S(1)}, f32[2,128,128]{2,1,0:T(8,128)S(1)}, u32[]{:S(2)}, u32[]{:S(2)}) collective-permute-start(f32[2,128,128]{2,1,0:T(8,128)S(1)} %get-tuple-element.47), channel_id=1, source_target_pairs={{0,128},{16,144},{32,160},{48,176},{64,192},{80,208},{96,224},{112... | collective-permute-start | bytes 393224 | tf_op jit(solution)/shard_map/ppermute | solution.py:50
  267.6 3.3 %collective-permute-start.14 = (f32[2,128,128]{2,1,0:T(8,128)S(1)}, f32[2,128,128]{2,1,0:T(8,128)S(1)}, u32[]{:S(2)}, u32[]{:S(2)}) collective-permute-start(f32[2,128,128]{2,1,0:T(8,128)S(1)} %get-tuple-element.49), channel_id=1, source_target_pairs={{0,64},{16,80},{32,96},{48,112},{64,128},{80,144},{96,160},{112,17... | collective-permute-start | bytes 393224 | tf_op jit(solution)/shard_map/ppermute | solution.py:50
  270.9 5.9 %collective-permute-start.15 = (f32[2,128,128]{2,1,0:T(8,128)S(1)}, f32[2,128,128]{2,1,0:T(8,128)S(1)}, u32[]{:S(2)}, u32[]{:S(2)}) collective-permute-start(f32[2,128,128]{2,1,0:T(8,128)S(1)} %get-tuple-element.48), channel_id=1, source_target_pairs={{0,192},{16,208},{32,224},{48,240},{64,0},{80,16},{96,32},{112,48}... | collective-permute-start | bytes 393224 | tf_op jit(solution)/shard_map/ppermute | solution.py:50
  276.8 4.9 %collective-permute-done.14 = f32[2,128,128]{2,1,0:T(8,128)S(1)} collective-permute-done((f32[2,128,128]{2,1,0:T(8,128)S(1)}, f32[2,128,128]{2,1,0:T(8,128)S(1)}, u32[]{:S(2)}, u32[]{:S(2)}) %collective-permute-start.14) | collective-permute-done | bytes 131104 | tf_op jit(solution)/shard_map/ppermute | solution.py:50
  281.7 10.3 %collective-permute-done.15 = f32[2,128,128]{2,1,0:T(8,128)S(1)} collective-permute-done((f32[2,128,128]{2,1,0:T(8,128)S(1)}, f32[2,128,128]{2,1,0:T(8,128)S(1)}, u32[]{:S(2)}, u32[]{:S(2)}) %collective-permute-start.15) | collective-permute-done | bytes 131104 | tf_op jit(solution)/shard_map/ppermute | solution.py:50
  292.0 2.4 collective-permute-start.16
  294.5 0.6 fusion.40
  296.4 0.7 pad_maximum_fusion.1
  (62 shorter events, 2.2 us)
Async XLA Ops:
  7.2 23.4 %copy-start.4 = (s32[1,64]{1,0:T(1,128)S(1)}, s32[1,64]{1,0:T(1,128)}, u32[]{:S(2)}) copy-start(s32[1,64]{1,0:T(1,128)} %param.14) | copy-start | bytes 772
  7.2 23.5 %copy-start = (s32[1,64]{1,0:T(1,128)S(1)}, s32[1,64]{1,0:T(1,128)}, u32[]{:S(2)}) copy-start(s32[1,64]{1,0:T(1,128)} %param.13) | copy-start | bytes 772
  7.2 24.2 %copy-start.3 = (s32[1,16]{1,0:T(1,128)S(1)}, s32[1,16]{1,0:T(1,128)}, u32[]{:S(2)}) copy-start(s32[1,16]{1,0:T(1,128)} %param.10) | copy-start | bytes 196
  7.2 24.3 %copy-start.1 = (s32[1,64]{1,0:T(1,128)S(1)}, s32[1,64]{1,0:T(1,128)}, u32[]{:S(2)}) copy-start(s32[1,64]{1,0:T(1,128)} %param.12) | copy-start | bytes 772
  7.2 24.3 %copy-start.2 = (s32[1,64]{1,0:T(1,128)S(1)}, s32[1,64]{1,0:T(1,128)}, u32[]{:S(2)}) copy-start(s32[1,64]{1,0:T(1,128)} %param.15) | copy-start | bytes 772
  7.2 79.3 %all-gather.6.cloned.1.call-start = ((), (), s32[]{:S(2)}) async-start(), calls=%async_computation.10 | async-start | bytes 9437184 | tf_op jit(solution)/shard_map/all_gather | solution.py:251
  9.7 41.0 %all-to-all-start = ((f32[8,128,128]{2,1,0:T(8,128)}), f32[8,128,128]{2,1,0:T(8,128)S(1)}, u32[]{:S(2)}, u32[]{:S(2)}) async-start(f32[8,128,128]{2,1,0:T(8,128)} %shard_map.95), calls=%async_computation | async-start | bytes 1048576 | tf_op jit(solution)/shard_map/all_to_all | solution.py:58
  29.9 118.4 %reduce-scatter.2.cloned.1.call-start = ((), (), s32[]{:S(2)}) async-start(), calls=%async_computation.8 | async-start | bytes 2949120 | tf_op jit(solution)/shard_map/reduce_scatter | solution.py:276
  31.5 3.1 %collective-permute-start = (s32[5,64]{1,0:T(8,128)S(1)}, s32[5,64]{1,0:T(8,128)S(1)}, u32[]{:S(2)}, u32[]{:S(2)}) collective-permute-start(s32[5,64]{1,0:T(8,128)S(1)} %stack.65), channel_id=1, source_target_pairs={{0,1},{1,0},{2,3},{3,2},{4,5},{5,4},{6,7},{7,6},{8,9},{9,8},{10,11... | collective-permute-start | bytes 3848 | tf_op jit(solution)/shard_map/ppermute | solution.py:54
  34.6 10.6 %collective-permute-start.1 = (s32[2,16]{1,0:T(2,128)S(1)}, s32[2,16]{1,0:T(2,128)S(1)}, u32[]{:S(2)}, u32[]{:S(2)}) collective-permute-start(s32[2,16]{1,0:T(2,128)S(1)} %bitcast.101), channel_id=1, source_target_pairs={{0,256},{16,272},{32,288},{48,304},{64,320},{80,336},{96,352},{112... | collective-permute-start | bytes 392 | tf_op jit(solution)/shard_map/ppermute | solution.py:45
  37.7 7.4 %collective-permute-start.2 = (s32[2,16]{1,0:T(2,128)S(1)}, s32[2,16]{1,0:T(2,128)S(1)}, u32[]{:S(2)}, u32[]{:S(2)}) collective-permute-start(s32[2,16]{1,0:T(2,128)S(1)} %bitcast.102), channel_id=1, source_target_pairs={{0,512},{16,528},{32,544},{48,560},{64,576},{80,592},{96,608},{112... | collective-permute-start | bytes 392 | tf_op jit(solution)/shard_map/ppermute | solution.py:45
  42.1 4.7 %collective-permute-start.3 = (s32[2,16]{1,0:T(2,128)S(1)}, s32[2,16]{1,0:T(2,128)S(1)}, u32[]{:S(2)}, u32[]{:S(2)}) collective-permute-start(s32[2,16]{1,0:T(2,128)S(1)} %bitcast.103), channel_id=1, source_target_pairs={{0,768},{16,784},{32,800},{48,816},{64,832},{80,848},{96,864},{112... | collective-permute-start | bytes 392 | tf_op jit(solution)/shard_map/ppermute | solution.py:45
  50.7 35.7 %collective-permute-start.4 = (f32[8,128,128]{2,1,0:T(8,128)S(1)}, f32[8,128,128]{2,1,0:T(8,128)S(1)}, u32[]{:S(2)}, u32[]{:S(2)}) collective-permute-start(f32[8,128,128]{2,1,0:T(8,128)S(1)} %all-to-all-done.refs_0_), channel_id=1, source_target_pairs={{0,240},{16,0},{32,16},{48,32},{64,48},{80,64},{96,80},{112,96},{1... | collective-permute-start | bytes 1572872 | tf_op jit(solution)/shard_map/ppermute | solution.py:50
  62.6 23.9 %collective-permute-start.7 = (f32[8,128,128]{2,1,0:T(8,128)S(1)}, f32[8,128,128]{2,1,0:T(8,128)S(1)}, u32[]{:S(2)}, u32[]{:S(2)}) collective-permute-start(f32[8,128,128]{2,1,0:T(8,128)S(1)} %all-to-all-done.refs_0_), channel_id=1, source_target_pairs={{0,16},{16,32},{32,48},{48,64},{64,80},{80,96},{96,112},{112,128},... | collective-permute-start | bytes 1572872 | tf_op jit(solution)/shard_map/ppermute | solution.py:50
  66.2 19.7 %collective-permute-start.5 = (f32[4,128,128]{2,1,0:T(8,128)S(1)}, f32[4,128,128]{2,1,0:T(8,128)S(1)}, u32[]{:S(2)}, u32[]{:S(2)}) collective-permute-start(f32[4,128,128]{2,1,0:T(8,128)S(1)} %get-tuple-element.51), channel_id=1, source_target_pairs={{0,224},{16,240},{32,0},{48,16},{64,32},{80,48},{96,64},{112,80},{... | collective-permute-start | bytes 786440 | tf_op jit(solution)/shard_map/ppermute | solution.py:50
  71.2 15.3 %collective-permute-start.6 = (f32[4,128,128]{2,1,0:T(8,128)S(1)}, f32[4,128,128]{2,1,0:T(8,128)S(1)}, u32[]{:S(2)}, u32[]{:S(2)}) collective-permute-start(f32[4,128,128]{2,1,0:T(8,128)S(1)} %get-tuple-element.50), channel_id=1, source_target_pairs={{0,32},{16,48},{32,64},{48,80},{64,96},{80,112},{96,128},{112,144}... | collective-permute-start | bytes 786440 | tf_op jit(solution)/shard_map/ppermute | solution.py:50
  148.4 9.6 %all-to-all-start.1 = ((f32[4,160,128]{2,1,0:T(8,128)}), f32[4,160,128]{2,1,0:T(8,128)S(1)}, u32[]{:S(2)}, u32[]{:S(2)}) async-start(f32[4,160,128]{2,1,0:T(8,128)} %reduce-scatter.2.cloned.1.call-done), calls=%async_computation.2 | async-start | bytes 655360 | tf_op jit(solution)/shard_map/all_to_all | solution.py:58
  152.1 70.7 %all-gather.4.cloned.1.call-start = ((), (), s32[]{:S(2)}) async-start(), calls=%async_computation.9 | async-start | bytes 2654208 | tf_op jit(solution)/shard_map/all_gather | solution.py:321
  158.5 7.1 %collective-permute-start.8 = (f32[2,3,64]{2,0,1:T(2,128)S(1)}, f32[2,3,64]{2,0,1:T(2,128)S(1)}, u32[]{:S(2)}, u32[]{:S(2)}) collective-permute-start(f32[2,3,64]{2,0,1:T(2,128)S(1)} %pad_maximum_fusion.2), channel_id=1, source_target_pairs={{0,1},{1,0},{2,3},{3,2},{4,5},{5,4},{6,7},{7,6},{8,9},{9,8},{10,11... | collective-permute-start | bytes 4616 | tf_op jit(solution)/shard_map/ppermute | solution.py:54
  229.0 28.2 %collective-permute-start.10 = (f32[8,128,128]{2,1,0:T(8,128)S(1)}, f32[8,128,128]{2,1,0:T(8,128)S(1)}, u32[]{:S(2)}, u32[]{:S(2)}) collective-permute-start(f32[8,128,128]{2,1,0:T(8,128)S(1)} %get-tuple-element.31), channel_id=1, source_target_pairs={{0,240},{16,0},{32,16},{48,32},{64,48},{80,64},{96,80},{112,96},{1... | collective-permute-start | bytes 1572872 | tf_op jit(solution)/shard_map/ppermute | solution.py:50
  235.8 21.4 %collective-permute-start.9 = (f32[8,128,128]{2,1,0:T(8,128)S(1)}, f32[8,128,128]{2,1,0:T(8,128)S(1)}, u32[]{:S(2)}, u32[]{:S(2)}) collective-permute-start(f32[8,128,128]{2,1,0:T(8,128)S(1)} %get-tuple-element.30), channel_id=1, source_target_pairs={{0,16},{16,32},{32,48},{48,64},{64,80},{80,96},{96,112},{112,128},... | collective-permute-start | bytes 1572872 | tf_op jit(solution)/shard_map/ppermute | solution.py:50
  237.7 19.3 %collective-permute-start.11 = (f32[4,128,128]{2,1,0:T(8,128)}, f32[4,128,128]{2,1,0:T(8,128)S(1)}, u32[]{:S(2)}, u32[]{:S(2)}) collective-permute-start(f32[4,128,128]{2,1,0:T(8,128)} %get-tuple-element.32), channel_id=1, source_target_pairs={{0,32},{16,48},{32,64},{48,80},{64,96},{80,112},{96,128},{112,144}... | collective-permute-start | bytes 786440 | tf_op jit(solution)/shard_map/ppermute | solution.py:50
  239.7 17.6 %collective-permute-start.12 = (f32[4,128,128]{2,1,0:T(8,128)}, f32[4,128,128]{2,1,0:T(8,128)S(1)}, u32[]{:S(2)}, u32[]{:S(2)}) collective-permute-start(f32[4,128,128]{2,1,0:T(8,128)} %get-tuple-element.33), channel_id=1, source_target_pairs={{0,224},{16,240},{32,0},{48,16},{64,32},{80,48},{96,64},{112,80},{... | collective-permute-start | bytes 786440 | tf_op jit(solution)/shard_map/ppermute | solution.py:50
  257.4 19.4 %collective-permute-start.13 = (f32[2,128,128]{2,1,0:T(8,128)S(1)}, f32[2,128,128]{2,1,0:T(8,128)S(1)}, u32[]{:S(2)}, u32[]{:S(2)}) collective-permute-start(f32[2,128,128]{2,1,0:T(8,128)S(1)} %get-tuple-element.47), channel_id=1, source_target_pairs={{0,128},{16,144},{32,160},{48,176},{64,192},{80,208},{96,224},{112... | collective-permute-start | bytes 393224 | tf_op jit(solution)/shard_map/ppermute | solution.py:50
  267.6 14.1 %collective-permute-start.14 = (f32[2,128,128]{2,1,0:T(8,128)S(1)}, f32[2,128,128]{2,1,0:T(8,128)S(1)}, u32[]{:S(2)}, u32[]{:S(2)}) collective-permute-start(f32[2,128,128]{2,1,0:T(8,128)S(1)} %get-tuple-element.49), channel_id=1, source_target_pairs={{0,64},{16,80},{32,96},{48,112},{64,128},{80,144},{96,160},{112,17... | collective-permute-start | bytes 393224 | tf_op jit(solution)/shard_map/ppermute | solution.py:50
  270.9 21.1 %collective-permute-start.15 = (f32[2,128,128]{2,1,0:T(8,128)S(1)}, f32[2,128,128]{2,1,0:T(8,128)S(1)}, u32[]{:S(2)}, u32[]{:S(2)}) collective-permute-start(f32[2,128,128]{2,1,0:T(8,128)S(1)} %get-tuple-element.48), channel_id=1, source_target_pairs={{0,192},{16,208},{32,224},{48,240},{64,0},{80,16},{96,32},{112,48}... | collective-permute-start | bytes 393224 | tf_op jit(solution)/shard_map/ppermute | solution.py:50
  292.0 4.3 %collective-permute-start.16 = (f32[128,128]{1,0:T(8,128)S(1)}, f32[128,128]{1,0:T(8,128)S(1)}, u32[]{:S(2)}, u32[]{:S(2)}) collective-permute-start(f32[128,128]{1,0:T(8,128)S(1)} %select_bitcast_fusion), channel_id=1, source_target_pairs={{0,1},{1,0},{2,3},{3,2},{4,5},{5,4},{6,7},{7,6},{8,9},{9,8},{10,11... | collective-permute-start | bytes 196616 | tf_op jit(solution)/shard_map/ppermute | solution.py:54
Sparse Core Ops, SparseCore 0:
  10.8 69.3 all-gather.5
  92.2 56.1 reduce-scatter.1
  176.3 46.5 all-gather.3

commit v14 on v13

--- a/solution.py
+++ b/solution.py
@@ -16,7 +16,7 @@
 CB = 64
 PAIRS = 64
 ENTRIES = 2 * NX * SLOTS
-EXTRA = 32
+EXTRA = 16
 EXTRA_BACK = 16
 GROUP = 8
 VMEM_LIMIT = 48 * 1024 * 1024

time: 307 us -> 317 us (1.033)
  the two profiles are of different devices: /device:TPU:1 before, /device:TPU:177 now
where the time goes in v14:
time: 317 us
  starting transfers between devices  111 us (35%)
  blocking collectives  96.2 us (30%)
  waiting for transfers between devices  68.1 us (21%)
  Pallas kernels  17.5 us (6%)
  between operations  17.3 us (5%)
  other arithmetic  4.43 us (1%)
    all_to_all x5, blocking collectives, exchange(): lax.all_to_all(values, axis, split_axis=0, concat_axis=0, tiled=True, axi...  96.2 us
    ppermute x11, starting transfers between devices, send_z(): return lax.ppermute(values, 'row', pairs)  45.2 us
    ppermute x3, starting transfers between devices, swap_cores(): return lax.ppermute(values, 'col', CORE_SWAP)  34.7 us
    ppermute x11, waiting for transfers between devices, send_z(): return lax.ppermute(values, 'row', pairs)  34.2 us
    all_to_all x2, starting transfers between devices, exchange(): lax.all_to_all(values, axis, split_axis=0, concat_axis=0, tiled=True, axi...  21.5 us
    all_to_all x2, waiting for transfers between devices, exchange(): lax.all_to_all(values, axis, split_axis=0, concat_axis=0, tiled=True, axi...  18.3 us
    pallas_call x3, Pallas kernels, call_kernel(): pl.pallas_call(body, out_shape=[jax.ShapeDtypeStruct((*shape, HALF), jnp....  15.7 us
    ppermute x3, starting transfers between devices, send_x(): return lax.ppermute(values, 'row', pairs)  9.33 us
  transfers between devices with their start and end apart: 22, of which 13 were waited for; matrix products, arithmetic and copies ran while one was open for 2% of the time, Pallas kernels for 2%

profile of v14, /device:TPU:177, one launch (start us, length us, event | category | flops | bytes accessed | tf_op | source)
XLA Modules:
  0.0 316.9 jit_solution(18000897638730051894)
XLA Ops:
  7.3 0.7 all-gather.6.cloned.1.call-update
  7.9 1.8 shard_map.95
  9.7 17.6 %all-to-all-start = ((f32[8,128,128]{2,1,0:T(8,128)}), f32[8,128,128]{2,1,0:T(8,128)S(1)}, u32[]{:S(2)}, u32[]{:S(2)}) async-start(f32[8,128,128]{2,1,0:T(8,128)} %shard_map.95), calls=%async_computation | async-start | bytes 1048576 | tf_op jit(solution)/shard_map/all_to_all | solution.py:58
  28.0 0.8 gather_fusion
  28.9 1.9 collective-permute-start
  30.8 1.1 collective-permute-done
  31.9 4.4 %collective-permute-start.3 = (s32[2,16]{1,0:T(2,128)S(1)}, s32[2,16]{1,0:T(2,128)S(1)}, u32[]{:S(2)}, u32[]{:S(2)}) collective-permute-start(s32[2,16]{1,0:T(2,128)S(1)} %bitcast.101), channel_id=1, source_target_pairs={{0,768},{16,784},{32,800},{48,816},{64,832},{80,848},{96,864},{112... | collective-permute-start | bytes 392 | tf_op jit(solution)/shard_map/ppermute | solution.py:45
  36.3 2.4 collective-permute-start.2
  38.8 2.5 collective-permute-start.1
  41.3 1.1 collective-permute-done.2
  42.4 2.2 collective-permute-done.1
  45.0 0.7 convert_reduce_fusion.2
  45.6 0.6 add_select_fusion.1
  46.3 12.7 %all-to-all-done.refs_0_ = f32[8,128,128]{2,1,0:T(8,128)S(1)} async-done(((f32[8,128,128]{2,1,0:T(8,128)}), f32[8,128,128]{2,1,0:T(8,128)S(1)}, u32[]{:S(2)}, u32[]{:S(2)}) %all-to-all-start) | async-done | bytes 524320 | tf_op jit(solution)/shard_map/all_to_all | solution.py:58
  58.9 1.9 collective-permute-start.7
  60.9 3.4 %collective-permute-start.4 = (f32[8,128,128]{2,1,0:T(8,128)S(1)}, f32[8,128,128]{2,1,0:T(8,128)S(1)}, u32[]{:S(2)}, u32[]{:S(2)}) collective-permute-start(f32[8,128,128]{2,1,0:T(8,128)S(1)} %all-to-all-done.refs_0_), channel_id=1, source_target_pairs={{0,240},{16,0},{32,16},{48,32},{64,48},{80,64},{96,80},{112,96},{1... | collective-permute-start | bytes 1572872 | tf_op jit(solution)/shard_map/ppermute | solution.py:50
  64.3 1.9 collective-permute-start.6
  66.2 4.3 %collective-permute-start.5 = (f32[4,128,128]{2,1,0:T(8,128)S(1)}, f32[4,128,128]{2,1,0:T(8,128)S(1)}, u32[]{:S(2)}, u32[]{:S(2)}) collective-permute-start(f32[4,128,128]{2,1,0:T(8,128)S(1)} %get-tuple-element.51), channel_id=1, source_target_pairs={{0,224},{16,240},{32,0},{48,16},{64,32},{80,48},{96,64},{112,80},{... | collective-permute-start | bytes 786440 | tf_op jit(solution)/shard_map/ppermute | solution.py:50
  70.5 1.4 pad_add_fusion.1.place_ref
  72.0 10.6 %collective-permute-done.6.refs_3_ = f32[4,128,128]{2,1,0:T(8,128)S(1)} collective-permute-done((f32[4,128,128]{2,1,0:T(8,128)S(1)}, f32[4,128,128]{2,1,0:T(8,128)S(1)}, u32[]{:S(2)}, u32[]{:S(2)}) %collective-permute-start.6) | collective-permute-done | bytes 262176 | tf_op jit(solution)/shard_map/ppermute | solution.py:50
  82.6 1.0 collective-permute-done.5.refs_2_
  83.6 5.8 %shard_map.96 = f32[32,144,128]{2,1,0:T(8,128)} custom-call(s32[3]{0:T(128)S(1)} %pad_add_fusion.1.place_ref, s32[128]{0:T(128)S(1)} %select_reduce_fusion.list_ref, f32[128,128,128]{2,1,0:T(8,128)} %bitcast.82, f32[8,128,128]{2,1,0:T(8,128)S(1)} %all-to-all-done.refs_0_, f32[8,128,128]{2,1,0:T(8,128)S(1)} %collective-permute-done.4.refs_1_, ...), custom_call_target="tpu_custom_call" | custom-call | tf_op jit(solution)/shard_map/pallas_call | solution.py:201
  89.4 3.6 %shard_map.97 = f32[32,112,128]{2,1,0:T(8,128)S(1)} custom-call(s32[3]{0:T(128)S(1)} %pad_add_fusion.1.place_ref, s32[128]{0:T(128)S(1)} %select_reduce_fusion.list_ref, f32[128,128,128]{2,1,0:T(8,128)} %bitcast.83, f32[8,128,128]{2,1,0:T(8,128)S(1)} %all-to-all-done.refs_0_, f32[8,128,128]{2,1,0:T(8,128)S(1)} %collective-permute-done.4.refs_1_, ...), custom_call_target="tpu_custom_call" | custom-call | tf_op jit(solution)/shard_map/pallas_call | solution.py:201
  93.0 22.6 %all_to_all.35 = f32[4,896,128]{2,1,0:T(8,128)S(1)} all-to-all(f32[4,896,128]{2,1,0:T(8,128)S(1)} %bitcast.80), channel_id=1, replica_groups={{0,256,512,768},{16,272,528,784},{32,288,544,800},{48,304,560,816},{64,..., dimensions={0} | all-to-all | bytes 3670016 | tf_op jit(solution)/shard_map/all_to_all | solution.py:58
  115.8 20.6 %all_to_all.36 = f32[8,112,128]{2,1,0:T(8,128)S(1)} all-to-all(f32[8,112,128]{2,1,0:T(8,128)S(1)} %bitcast.87), channel_id=1, replica_groups={{0,2,4,6,8,10,12,14},{1,3,5,7,9,11,13,15},{16,18,20,22,24,26,28,30},{17..., dimensions={0} | all-to-all | bytes 917504 | tf_op jit(solution)/shard_map/all_to_all | solution.py:58
  136.4 6.8 %reduce-scatter.2.cloned.1.call-done = f32[4,144,128]{2,1,0:T(8,128)} async-done(((f32[32,144,128]{2,1,0:T(8,128)}), f32[4,144,128]{2,1,0:T(8,128)}) %reduce-scatter.2.cloned.1.call-update) | async-done | bytes 294928 | tf_op jit(solution)/shard_map/reduce_scatter | solution.py:276
  143.2 3.9 %all-to-all-start.1 = ((f32[4,144,128]{2,1,0:T(8,128)}), f32[4,144,128]{2,1,0:T(8,128)S(1)}, u32[]{:S(2)}, u32[]{:S(2)}) async-start(f32[4,144,128]{2,1,0:T(8,128)} %reduce-scatter.2.cloned.1.call-done), calls=%async_computation.2 | async-start | bytes 589824 | tf_op jit(solution)/shard_map/all_to_all | solution.py:58
  147.2 5.7 %all-to-all-done.1 = f32[4,144,128]{2,1,0:T(8,128)S(1)} async-done(((f32[4,144,128]{2,1,0:T(8,128)}), f32[4,144,128]{2,1,0:T(8,128)S(1)}, u32[]{:S(2)}, u32[]{:S(2)}) %all-to-all-start.1) | async-done | bytes 294944 | tf_op jit(solution)/shard_map/all_to_all | solution.py:58
  153.4 6.2 %collective-permute-start.8 = (f32[2,3,64]{2,0,1:T(2,128)S(1)}, f32[2,3,64]{2,0,1:T(2,128)S(1)}, u32[]{:S(2)}, u32[]{:S(2)}) collective-permute-start(f32[2,3,64]{2,0,1:T(2,128)S(1)} %pad_maximum_fusion.2), channel_id=1, source_target_pairs={{0,1},{1,0},{2,3},{3,2},{4,5},{5,4},{6,7},{7,6},{8,9},{9,8},{10,11... | collective-permute-start | bytes 4616 | tf_op jit(solution)/shard_map/ppermute | solution.py:54
  159.6 0.8 collective-permute-done.8
  161.3 9.7 %all_to_all.37 = f32[4,144,128]{2,1,0:T(8,128)} all-to-all(f32[4,144,128]{2,1,0:T(8,128)S(1)} %broadcast_in_dim.34), channel_id=1, replica_groups={{0,256,512,768},{16,272,528,784},{32,288,544,800},{48,304,560,816},{64,..., dimensions={0} | all-to-all | bytes 589824 | tf_op jit(solution)/shard_map/all_to_all | solution.py:58
  171.0 18.9 %all_to_all.38 = f32[8,112,128]{2,1,0:T(8,128)S(1)} all-to-all(f32[8,112,128]{2,1,0:T(8,128)S(1)} %broadcast_in_dim.35), channel_id=1, replica_groups={{0,2,4,6,8,10,12,14},{1,3,5,7,9,11,13,15},{16,18,20,22,24,26,28,30},{17..., dimensions={0} | all-to-all | bytes 917504 | tf_op jit(solution)/shard_map/all_to_all | solution.py:58
  190.1 24.4 %all_to_all.39 = f32[4,896,128]{2,1,0:T(8,128)S(1)} all-to-all(f32[4,896,128]{2,1,0:T(8,128)S(1)} %broadcast_in_dim.60), channel_id=1, replica_groups={{0,256,512,768},{16,272,528,784},{32,288,544,800},{48,304,560,816},{64,..., dimensions={0} | all-to-all | bytes 3670016 | tf_op jit(solution)/shard_map/all_to_all | solution.py:58
  214.4 2.7 all-gather.4.cloned.1.call-done.even_ref
  217.1 6.3 %shard_map.98 = (f32[8,128,128]{2,1,0:T(8,128)S(1)}, f32[8,128,128]{2,1,0:T(8,128)S(1)}, f32[4,128,128]{2,1,0:T(8,128)}, f32[4,128,128]{2,1,0:T(8,128)}, f32[8,128,128]{2,1,0:T(8,128)S(1)}) custom-call(s32[3]{0:T(128)S(1)} %pad_add_fusion.1.place_ref, s32[128]{0:T(128)S(1)} %select_reduce_fusion.list_ref, f32[128,128,128]{2,1,0:T(8,128)} %bitcast.84, ...), custom_call_target="tpu_custom_call" | custom-call | tf_op jit(solution)/shard_map/pallas_call | solution.py:201
  223.4 2.8 collective-permute-start.9
  226.2 2.5 collective-permute-start.10
  228.7 6.5 %collective-permute-start.11 = (f32[4,128,128]{2,1,0:T(8,128)}, f32[4,128,128]{2,1,0:T(8,128)S(1)}, u32[]{:S(2)}, u32[]{:S(2)}) collective-permute-start(f32[4,128,128]{2,1,0:T(8,128)} %get-tuple-element.32), channel_id=1, source_target_pairs={{0,32},{16,48},{32,64},{48,80},{64,96},{80,112},{96,128},{112,144}... | collective-permute-start | bytes 786440 | tf_op jit(solution)/shard_map/ppermute | solution.py:50
  235.2 1.9 collective-permute-start.12
  237.1 6.8 %collective-permute-done.11 = f32[4,128,128]{2,1,0:T(8,128)S(1)} collective-permute-done((f32[4,128,128]{2,1,0:T(8,128)}, f32[4,128,128]{2,1,0:T(8,128)S(1)}, u32[]{:S(2)}, u32[]{:S(2)}) %collective-permute-start.11) | collective-permute-done | bytes 262176 | tf_op jit(solution)/shard_map/ppermute | solution.py:50
  243.9 6.4 %collective-permute-done.12 = f32[4,128,128]{2,1,0:T(8,128)S(1)} collective-permute-done((f32[4,128,128]{2,1,0:T(8,128)}, f32[4,128,128]{2,1,0:T(8,128)S(1)}, u32[]{:S(2)}, u32[]{:S(2)}) %collective-permute-start.12) | collective-permute-done | bytes 262176 | tf_op jit(solution)/shard_map/ppermute | solution.py:50
  250.5 10.8 %collective-permute-start.13 = (f32[2,128,128]{2,1,0:T(8,128)S(1)}, f32[2,128,128]{2,1,0:T(8,128)S(1)}, u32[]{:S(2)}, u32[]{:S(2)}) collective-permute-start(f32[2,128,128]{2,1,0:T(8,128)S(1)} %get-tuple-element.47), channel_id=1, source_target_pairs={{0,128},{16,144},{32,160},{48,176},{64,192},{80,208},{96,224},{112... | collective-permute-start | bytes 393224 | tf_op jit(solution)/shard_map/ppermute | solution.py:50
  261.4 7.3 %collective-permute-start.15 = (f32[2,128,128]{2,1,0:T(8,128)S(1)}, f32[2,128,128]{2,1,0:T(8,128)S(1)}, u32[]{:S(2)}, u32[]{:S(2)}) collective-permute-start(f32[2,128,128]{2,1,0:T(8,128)S(1)} %get-tuple-element.48), channel_id=1, source_target_pairs={{0,192},{16,208},{32,224},{48,240},{64,0},{80,16},{96,32},{112,48}... | collective-permute-start | bytes 393224 | tf_op jit(solution)/shard_map/ppermute | solution.py:50
  268.7 1.9 collective-permute-start.14
  270.6 9.4 %collective-permute-done.15 = f32[2,128,128]{2,1,0:T(8,128)S(1)} collective-permute-done((f32[2,128,128]{2,1,0:T(8,128)S(1)}, f32[2,128,128]{2,1,0:T(8,128)S(1)}, u32[]{:S(2)}, u32[]{:S(2)}) %collective-permute-start.15) | collective-permute-done | bytes 131104 | tf_op jit(solution)/shard_map/ppermute | solution.py:50
  280.1 26.5 %collective-permute-start.16 = (f32[128,128]{1,0:T(8,128)S(1)}, f32[128,128]{1,0:T(8,128)S(1)}, u32[]{:S(2)}, u32[]{:S(2)}) collective-permute-start(f32[128,128]{1,0:T(8,128)S(1)} %select_bitcast_fusion), channel_id=1, source_target_pairs={{0,1},{1,0},{2,3},{3,2},{4,5},{5,4},{6,7},{7,6},{8,9},{9,8},{10,11... | collective-permute-start | bytes 196616 | tf_op jit(solution)/shard_map/ppermute | solution.py:54
  306.6 0.6 fusion.40
  308.6 0.7 pad_maximum_fusion.1
  (62 shorter events, 2.4 us)
Async XLA Ops:
  7.2 20.8 %copy-start.4 = (s32[1,64]{1,0:T(1,128)S(1)}, s32[1,64]{1,0:T(1,128)}, u32[]{:S(2)}) copy-start(s32[1,64]{1,0:T(1,128)} %param.14) | copy-start | bytes 772
  7.2 20.8 %copy-start = (s32[1,64]{1,0:T(1,128)S(1)}, s32[1,64]{1,0:T(1,128)}, u32[]{:S(2)}) copy-start(s32[1,64]{1,0:T(1,128)} %param.13) | copy-start | bytes 772
  7.2 21.6 %copy-start.3 = (s32[1,16]{1,0:T(1,128)S(1)}, s32[1,16]{1,0:T(1,128)}, u32[]{:S(2)}) copy-start(s32[1,16]{1,0:T(1,128)} %param.10) | copy-start | bytes 196
  7.2 21.6 %copy-start.2 = (s32[1,64]{1,0:T(1,128)S(1)}, s32[1,64]{1,0:T(1,128)}, u32[]{:S(2)}) copy-start(s32[1,64]{1,0:T(1,128)} %param.15) | copy-start | bytes 772
  7.2 21.6 %copy-start.1 = (s32[1,64]{1,0:T(1,128)S(1)}, s32[1,64]{1,0:T(1,128)}, u32[]{:S(2)}) copy-start(s32[1,64]{1,0:T(1,128)} %param.12) | copy-start | bytes 772
  7.2 76.4 %all-gather.6.cloned.1.call-start = ((), (), s32[]{:S(2)}) async-start(), calls=%async_computation.10 | async-start | bytes 9437184 | tf_op jit(solution)/shard_map/all_gather | solution.py:251
  9.7 49.2 %all-to-all-start = ((f32[8,128,128]{2,1,0:T(8,128)}), f32[8,128,128]{2,1,0:T(8,128)S(1)}, u32[]{:S(2)}, u32[]{:S(2)}) async-start(f32[8,128,128]{2,1,0:T(8,128)} %shard_map.95), calls=%async_computation | async-start | bytes 1048576 | tf_op jit(solution)/shard_map/all_to_all | solution.py:58
  27.3 115.9 %reduce-scatter.2.cloned.1.call-start = ((), (), s32[]{:S(2)}) async-start(), calls=%async_computation.8 | async-start | bytes 2654208 | tf_op jit(solution)/shard_map/reduce_scatter | solution.py:276
  28.9 3.1 collective-permute-start
  31.9 9.4 %collective-permute-start.3 = (s32[2,16]{1,0:T(2,128)S(1)}, s32[2,16]{1,0:T(2,128)S(1)}, u32[]{:S(2)}, u32[]{:S(2)}) collective-permute-start(s32[2,16]{1,0:T(2,128)S(1)} %bitcast.101), channel_id=1, source_target_pairs={{0,768},{16,784},{32,800},{48,816},{64,832},{80,848},{96,864},{112... | collective-permute-start | bytes 392 | tf_op jit(solution)/shard_map/ppermute | solution.py:45
  36.3 6.1 %collective-permute-start.2 = (s32[2,16]{1,0:T(2,128)S(1)}, s32[2,16]{1,0:T(2,128)S(1)}, u32[]{:S(2)}, u32[]{:S(2)}) collective-permute-start(s32[2,16]{1,0:T(2,128)S(1)} %bitcast.102), channel_id=1, source_target_pairs={{0,512},{16,528},{32,544},{48,560},{64,576},{80,592},{96,608},{112... | collective-permute-start | bytes 392 | tf_op jit(solution)/shard_map/ppermute | solution.py:45
  38.8 5.9 %collective-permute-start.1 = (s32[2,16]{1,0:T(2,128)S(1)}, s32[2,16]{1,0:T(2,128)S(1)}, u32[]{:S(2)}, u32[]{:S(2)}) collective-permute-start(s32[2,16]{1,0:T(2,128)S(1)} %bitcast.103), channel_id=1, source_target_pairs={{0,256},{16,272},{32,288},{48,304},{64,320},{80,336},{96,352},{112... | collective-permute-start | bytes 392 | tf_op jit(solution)/shard_map/ppermute | solution.py:45
  58.9 24.6 %collective-permute-start.7 = (f32[8,128,128]{2,1,0:T(8,128)S(1)}, f32[8,128,128]{2,1,0:T(8,128)S(1)}, u32[]{:S(2)}, u32[]{:S(2)}) collective-permute-start(f32[8,128,128]{2,1,0:T(8,128)S(1)} %all-to-all-done.refs_0_), channel_id=1, source_target_pairs={{0,16},{16,32},{32,48},{48,64},{64,80},{80,96},{96,112},{112,128},... | collective-permute-start | bytes 1572872 | tf_op jit(solution)/shard_map/ppermute | solution.py:50
  60.9 22.7 %collective-permute-start.4 = (f32[8,128,128]{2,1,0:T(8,128)S(1)}, f32[8,128,128]{2,1,0:T(8,128)S(1)}, u32[]{:S(2)}, u32[]{:S(2)}) collective-permute-start(f32[8,128,128]{2,1,0:T(8,128)S(1)} %all-to-all-done.refs_0_), channel_id=1, source_target_pairs={{0,240},{16,0},{32,16},{48,32},{64,48},{80,64},{96,80},{112,96},{1... | collective-permute-start | bytes 1572872 | tf_op jit(solution)/shard_map/ppermute | solution.py:50
  64.3 18.3 %collective-permute-start.6 = (f32[4,128,128]{2,1,0:T(8,128)S(1)}, f32[4,128,128]{2,1,0:T(8,128)S(1)}, u32[]{:S(2)}, u32[]{:S(2)}) collective-permute-start(f32[4,128,128]{2,1,0:T(8,128)S(1)} %get-tuple-element.50), channel_id=1, source_target_pairs={{0,32},{16,48},{32,64},{48,80},{64,96},{80,112},{96,128},{112,144}... | collective-permute-start | bytes 786440 | tf_op jit(solution)/shard_map/ppermute | solution.py:50
  66.2 17.4 %collective-permute-start.5 = (f32[4,128,128]{2,1,0:T(8,128)S(1)}, f32[4,128,128]{2,1,0:T(8,128)S(1)}, u32[]{:S(2)}, u32[]{:S(2)}) collective-permute-start(f32[4,128,128]{2,1,0:T(8,128)S(1)} %get-tuple-element.51), channel_id=1, source_target_pairs={{0,224},{16,240},{32,0},{48,16},{64,32},{80,48},{96,64},{112,80},{... | collective-permute-start | bytes 786440 | tf_op jit(solution)/shard_map/ppermute | solution.py:50
  143.2 9.6 %all-to-all-start.1 = ((f32[4,144,128]{2,1,0:T(8,128)}), f32[4,144,128]{2,1,0:T(8,128)S(1)}, u32[]{:S(2)}, u32[]{:S(2)}) async-start(f32[4,144,128]{2,1,0:T(8,128)} %reduce-scatter.2.cloned.1.call-done), calls=%async_computation.2 | async-start | bytes 589824 | tf_op jit(solution)/shard_map/all_to_all | solution.py:58
  147.1 70.0 %all-gather.4.cloned.1.call-start = ((), (), s32[]{:S(2)}) async-start(), calls=%async_computation.9 | async-start | bytes 2654208 | tf_op jit(solution)/shard_map/all_gather | solution.py:321
  153.4 7.0 %collective-permute-start.8 = (f32[2,3,64]{2,0,1:T(2,128)S(1)}, f32[2,3,64]{2,0,1:T(2,128)S(1)}, u32[]{:S(2)}, u32[]{:S(2)}) collective-permute-start(f32[2,3,64]{2,0,1:T(2,128)S(1)} %pad_maximum_fusion.2), channel_id=1, source_target_pairs={{0,1},{1,0},{2,3},{3,2},{4,5},{5,4},{6,7},{7,6},{8,9},{9,8},{10,11... | collective-permute-start | bytes 4616 | tf_op jit(solution)/shard_map/ppermute | solution.py:54
  223.4 26.9 %collective-permute-start.9 = (f32[8,128,128]{2,1,0:T(8,128)S(1)}, f32[8,128,128]{2,1,0:T(8,128)S(1)}, u32[]{:S(2)}, u32[]{:S(2)}) collective-permute-start(f32[8,128,128]{2,1,0:T(8,128)S(1)} %get-tuple-element.30), channel_id=1, source_target_pairs={{0,16},{16,32},{32,48},{48,64},{64,80},{80,96},{96,112},{112,128},... | collective-permute-start | bytes 1572872 | tf_op jit(solution)/shard_map/ppermute | solution.py:50
  226.2 24.1 %collective-permute-start.10 = (f32[8,128,128]{2,1,0:T(8,128)S(1)}, f32[8,128,128]{2,1,0:T(8,128)S(1)}, u32[]{:S(2)}, u32[]{:S(2)}) collective-permute-start(f32[8,128,128]{2,1,0:T(8,128)S(1)} %get-tuple-element.31), channel_id=1, source_target_pairs={{0,240},{16,0},{32,16},{48,32},{64,48},{80,64},{96,80},{112,96},{1... | collective-permute-start | bytes 1572872 | tf_op jit(solution)/shard_map/ppermute | solution.py:50
  228.7 15.2 %collective-permute-start.11 = (f32[4,128,128]{2,1,0:T(8,128)}, f32[4,128,128]{2,1,0:T(8,128)S(1)}, u32[]{:S(2)}, u32[]{:S(2)}) collective-permute-start(f32[4,128,128]{2,1,0:T(8,128)} %get-tuple-element.32), channel_id=1, source_target_pairs={{0,32},{16,48},{32,64},{48,80},{64,96},{80,112},{96,128},{112,144}... | collective-permute-start | bytes 786440 | tf_op jit(solution)/shard_map/ppermute | solution.py:50
  235.2 15.1 %collective-permute-start.12 = (f32[4,128,128]{2,1,0:T(8,128)}, f32[4,128,128]{2,1,0:T(8,128)S(1)}, u32[]{:S(2)}, u32[]{:S(2)}) collective-permute-start(f32[4,128,128]{2,1,0:T(8,128)} %get-tuple-element.33), channel_id=1, source_target_pairs={{0,224},{16,240},{32,0},{48,16},{64,32},{80,48},{96,64},{112,80},{... | collective-permute-start | bytes 786440 | tf_op jit(solution)/shard_map/ppermute | solution.py:50
  250.5 20.1 %collective-permute-start.13 = (f32[2,128,128]{2,1,0:T(8,128)S(1)}, f32[2,128,128]{2,1,0:T(8,128)S(1)}, u32[]{:S(2)}, u32[]{:S(2)}) collective-permute-start(f32[2,128,128]{2,1,0:T(8,128)S(1)} %get-tuple-element.47), channel_id=1, source_target_pairs={{0,128},{16,144},{32,160},{48,176},{64,192},{80,208},{96,224},{112... | collective-permute-start | bytes 393224 | tf_op jit(solution)/shard_map/ppermute | solution.py:50
  261.4 18.7 %collective-permute-start.15 = (f32[2,128,128]{2,1,0:T(8,128)S(1)}, f32[2,128,128]{2,1,0:T(8,128)S(1)}, u32[]{:S(2)}, u32[]{:S(2)}) collective-permute-start(f32[2,128,128]{2,1,0:T(8,128)S(1)} %get-tuple-element.48), channel_id=1, source_target_pairs={{0,192},{16,208},{32,224},{48,240},{64,0},{80,16},{96,32},{112,48}... | collective-permute-start | bytes 393224 | tf_op jit(solution)/shard_map/ppermute | solution.py:50
  268.7 11.4 %collective-permute-start.14 = (f32[2,128,128]{2,1,0:T(8,128)S(1)}, f32[2,128,128]{2,1,0:T(8,128)S(1)}, u32[]{:S(2)}, u32[]{:S(2)}) collective-permute-start(f32[2,128,128]{2,1,0:T(8,128)S(1)} %get-tuple-element.49), channel_id=1, source_target_pairs={{0,64},{16,80},{32,96},{48,112},{64,128},{80,144},{96,160},{112,17... | collective-permute-start | bytes 393224 | tf_op jit(solution)/shard_map/ppermute | solution.py:50
  280.1 28.4 %collective-permute-start.16 = (f32[128,128]{1,0:T(8,128)S(1)}, f32[128,128]{1,0:T(8,128)S(1)}, u32[]{:S(2)}, u32[]{:S(2)}) collective-permute-start(f32[128,128]{1,0:T(8,128)S(1)} %select_bitcast_fusion), channel_id=1, source_target_pairs={{0,1},{1,0},{2,3},{3,2},{4,5},{5,4},{6,7},{7,6},{8,9},{9,8},{10,11... | collective-permute-start | bytes 196616 | tf_op jit(solution)/shard_map/ppermute | solution.py:54
Sparse Core Ops, SparseCore 0:
  10.8 66.5 all-gather.5
  89.5 53.7 reduce-scatter.1
  171.1 46.0 all-gather.3
